TPU v7x, 32 devices: a whole 2x2x4 slice. The times are simulated.
32 devices in a mesh: blk: 16 (over z, y, core), rep: 2 (over x).
Axes of the slice: x: 2, y: 2, z: 4, core: 2. Of those that a mesh axis runs over, the one named last changes fastest.
Arguments:
- image_embed: bfloat16 [16384, 1152], P(('rep', 'blk')), parts along dimension 0, may hold values from -6 to 6
- text_embed: bfloat16 [16384, 1152], P(('rep', 'blk')), parts along dimension 0, may hold values from -6 to 6
Outputs:
- image_grad: float32 [16384, 1152], P(('rep', 'blk')), parts along dimension 0
- text_grad: float32 [16384, 1152], P(('rep', 'blk')), parts along dimension 0
There are 2 independent parts, one for each index of `rep`. A program takes and returns all parts, laid end to end along the dimension named above; each array names one. Nothing has to cross between parts.
All inputs are finite; a program needn't handle non-finite values.
Results may differ from a plain program's by a relative error of at most 0.002.
Values may be sent and summed in bfloat16 or wider, within the bound.
No kernel may reach another device: no remote copies, remote signals or barrier semaphores. Data moves between devices by JAX's collectives and lax.ppermute only.
A program may use at most 64 MiB of HBM per device.

v0:
```python
import math

import jax
import jax.numpy as jnp
from jax import lax
from jax.sharding import PartitionSpec as P

STEPS = 4


def from_behind(block, axis, distance):
    devices = range(lax.axis_size(axis))
    route = [((i - distance) % len(devices), i) for i in devices]
    return lax.ppermute(block, axis, route)


def pair_weights(images, visitor, own_block):
    factor = 2.0 / math.sqrt(images.shape[1])
    inner_prod = lax.dot_general(
        images, visitor, (((1,), (1,)), ((), ())), preferred_element_type=jnp.float32
    )
    chances = jax.nn.sigmoid(factor * inner_prod - 1.0)
    if own_block:
        row_ids = jnp.arange(images.shape[0])
        chances = chances - (row_ids[:, None] == row_ids[None, :]).astype(jnp.float32)
    return chances.astype(jnp.bfloat16)


def text_term(weight, images):
    factor = 2.0 / math.sqrt(images.shape[1])
    return factor * lax.dot_general(
        weight, images, (((0,), (0,)), ((), ())), preferred_element_type=jnp.float32
    )


def local(image_embed, text_embed):
    factor = 2.0 / math.sqrt(image_embed.shape[1])
    visiting = [text_embed]
    current = text_embed
    for offset in range(1, STEPS):
        current = from_behind(current, "blk", 1)
        visiting.append(current)
    image_grad = jnp.zeros(image_embed.shape, jnp.float32)
    weights_all = []
    for offset in range(STEPS):
        weight = pair_weights(image_embed, visiting[offset], offset == 0)
        weights_all.append(weight)
        image_grad = image_grad + factor * jnp.dot(
            weight, visiting[offset], preferred_element_type=jnp.float32
        )
    carried = text_term(weights_all[0], image_embed)
    for offset in range(1, STEPS):
        carried = from_behind(carried, "blk", 1)
        carried = carried + text_term(weights_all[offset], image_embed)
    text_grad = from_behind(carried, "blk", -(STEPS - 1))
    return (image_grad, text_grad)


def solution(mesh):
    in_specs = (P(("rep", "blk"), None), P(("rep", "blk"), None))
    out_specs = (P(("rep", "blk"), None), P(("rep", "blk"), None))
    return jax.shard_map(local, mesh=mesh, in_specs=in_specs, out_specs=out_specs, check_vma=False)
```

profile of v0, /device:TPU:0, one launch (start us, length us, event | category | flops | bytes accessed | tf_op | source)
XLA Modules:
  0.0 192.8 jit_solution(16474511636771254046)
XLA Ops:
  0.6 0.0 copy-start
  0.6 1.3 copy-done
  1.9 2.3 %fusion.23 = bf16[512,512]{1,0:T(8,128)(2,1)S(1)} fusion(bf16[512,1152]{1,0:T(8,128)(2,1)S(1)} %copy-done, bf16[512,1152]{1,0:T(8,128)(2,1)} %param.3), kind=kOutput, calls=%fused_computation.34 | convolution fusion | flops 606339072 | bytes 2883584 | tf_op jit(solution)/shard_map/dot_general | solution.py:19
  4.2 0.0 copy-start.1
  4.2 0.9 convolution_multiply_fusion.3
  5.1 0.5 collective-permute-start.3
  5.6 2.6 %collective-permute-start = (bf16[512,1152]{1,0:T(8,128)(2,1)S(1)}, bf16[512,1152]{1,0:T(8,128)(2,1)S(1)}, u32[]{:S(2)}, u32[]{:S(2)}) collective-permute-start(bf16[512,1152]{1,0:T(8,128)(2,1)S(1)} %copy-done.1), channel_id=1, source_target_pairs={{30,0},{0,2},{2,4},{4,6},{6,8},{8,10},{10,12},{12,14},{14,16},{16,... | collective-permute-start | bytes 3538952 | tf_op jit(solution)/shard_map/ppermute | solution.py:14
  8.2 41.5 %collective-permute-done = bf16[512,1152]{1,0:T(8,128)(2,1)S(1)} collective-permute-done((bf16[512,1152]{1,0:T(8,128)(2,1)S(1)}, bf16[512,1152]{1,0:T(8,128)(2,1)S(1)}, u32[]{:S(2)}, u32[]{:S(2)}) %collective-permute-start) | collective-permute-done | bytes 1179680 | tf_op jit(solution)/shard_map/ppermute | solution.py:14
  49.8 1.0 fusion.26
  50.8 0.0 collective-permute-done.3
  50.8 0.9 fusion.1
  51.7 0.1 collective-permute-start.4
  51.8 0.1 collective-permute-start.1
  51.8 43.5 %collective-permute-done.1 = bf16[512,1152]{1,0:T(8,128)(2,1)S(1)} collective-permute-done((bf16[512,1152]{1,0:T(8,128)(2,1)S(1)}, bf16[512,1152]{1,0:T(8,128)(2,1)S(1)}, u32[]{:S(2)}, u32[]{:S(2)}) %collective-permute-start.1) | collective-permute-done | bytes 1179680 | tf_op jit(solution)/shard_map/ppermute | solution.py:14
  95.3 1.0 fusion.25
  96.4 0.9 convolution_multiply_fusion.1
  97.3 0.0 collective-permute-done.4
  97.3 0.2 add.42
  97.5 0.1 collective-permute-start.5
  97.6 0.1 collective-permute-start.2
  97.7 43.6 %collective-permute-done.2 = bf16[512,1152]{1,0:T(8,128)(2,1)S(1)} collective-permute-done((bf16[512,1152]{1,0:T(8,128)(2,1)S(1)}, bf16[512,1152]{1,0:T(8,128)(2,1)S(1)}, u32[]{:S(2)}, u32[]{:S(2)}) %collective-permute-start.2) | collective-permute-done | bytes 1179680 | tf_op jit(solution)/shard_map/ppermute | solution.py:14
  141.2 1.0 fusion.24
  142.2 0.9 convolution_multiply_fusion
  143.1 0.0 collective-permute-done.5
  143.1 0.2 add.43
  143.4 0.1 collective-permute-start.6
  143.5 0.9 fusion.27
  144.3 0.9 convolution_add_fusion.2
  145.2 0.8 convolution_add_fusion.1
  146.1 2.3 %fusion = f32[512,1152]{1,0:T(8,128)} fusion(f32[512,1152]{1,0:T(8,128)S(1)} %convolution_add_fusion.1, bf16[512,512]{1,0:T(8,128)(2,1)S(1)} %fusion.24, bf16[512,1152]{1,0:T(8,128)(2,1)S(1)} %collective-permute-done.2), kind=kOutput, calls=%fused_computation.7 | convolution fusion | flops 605159424 | bytes 6422528 | tf_op jit(solution)/shard_map/dot_general | solution.py:48
  148.3 43.0 %collective-permute-done.6 = f32[512,1152]{1,0:T(8,128)S(1)} collective-permute-done((f32[512,1152]{1,0:T(8,128)S(1)}, f32[512,1152]{1,0:T(8,128)S(1)}, u32[]{:S(2)}, u32[]{:S(2)}) %collective-permute-start.6) | collective-permute-done | bytes 2359328 | tf_op jit(solution)/shard_map/ppermute | solution.py:14
  191.4 1.4 copy.5
  (1 shorter events, 0.0 us)
Async XLA Ops:
  0.6 1.3 copy-start
  4.2 1.4 copy-start.1
  5.1 45.7 %collective-permute-start.3 = (f32[512,1152]{1,0:T(8,128)S(1)}, f32[512,1152]{1,0:T(8,128)S(1)}, u32[]{:S(2)}, u32[]{:S(2)}) collective-permute-start(f32[512,1152]{1,0:T(8,128)S(1)} %convolution_multiply_fusion.3), channel_id=1, source_target_pairs={{30,0},{0,2},{2,4},{4,6},{6,8},{8,10},{10,12},{12,14},{14,16},{16,... | collective-permute-start | bytes 7077896 | tf_op jit(solution)/shard_map/ppermute | solution.py:14
  5.6 44.2 %collective-permute-start = (bf16[512,1152]{1,0:T(8,128)(2,1)S(1)}, bf16[512,1152]{1,0:T(8,128)(2,1)S(1)}, u32[]{:S(2)}, u32[]{:S(2)}) collective-permute-start(bf16[512,1152]{1,0:T(8,128)(2,1)S(1)} %copy-done.1), channel_id=1, source_target_pairs={{30,0},{0,2},{2,4},{4,6},{6,8},{8,10},{10,12},{12,14},{14,16},{16,... | collective-permute-start | bytes 3538952 | tf_op jit(solution)/shard_map/ppermute | solution.py:14
  51.7 45.6 %collective-permute-start.4 = (f32[512,1152]{1,0:T(8,128)S(1)}, f32[512,1152]{1,0:T(8,128)S(1)}, u32[]{:S(2)}, u32[]{:S(2)}) collective-permute-start(f32[512,1152]{1,0:T(8,128)S(1)} %fusion.1), channel_id=1, source_target_pairs={{30,0},{0,2},{2,4},{4,6},{6,8},{8,10},{10,12},{12,14},{14,16},{16,... | collective-permute-start | bytes 7077896 | tf_op jit(solution)/shard_map/ppermute | solution.py:14
  51.8 43.6 %collective-permute-start.1 = (bf16[512,1152]{1,0:T(8,128)(2,1)S(1)}, bf16[512,1152]{1,0:T(8,128)(2,1)S(1)}, u32[]{:S(2)}, u32[]{:S(2)}) collective-permute-start(bf16[512,1152]{1,0:T(8,128)(2,1)S(1)} %collective-permute-done), channel_id=1, source_target_pairs={{30,0},{0,2},{2,4},{4,6},{6,8},{8,10},{10,12},{12,14},{14,16},{16,... | collective-permute-start | bytes 3538952 | tf_op jit(solution)/shard_map/ppermute | solution.py:14
  97.5 45.6 %collective-permute-start.5 = (f32[512,1152]{1,0:T(8,128)S(1)}, f32[512,1152]{1,0:T(8,128)S(1)}, u32[]{:S(2)}, u32[]{:S(2)}) collective-permute-start(f32[512,1152]{1,0:T(8,128)S(1)} %add.42), channel_id=1, source_target_pairs={{30,0},{0,2},{2,4},{4,6},{6,8},{8,10},{10,12},{12,14},{14,16},{16,... | collective-permute-start | bytes 7077896 | tf_op jit(solution)/shard_map/ppermute | solution.py:14
  97.6 43.6 %collective-permute-start.2 = (bf16[512,1152]{1,0:T(8,128)(2,1)S(1)}, bf16[512,1152]{1,0:T(8,128)(2,1)S(1)}, u32[]{:S(2)}, u32[]{:S(2)}) collective-permute-start(bf16[512,1152]{1,0:T(8,128)(2,1)S(1)} %collective-permute-done.1), channel_id=1, source_target_pairs={{30,0},{0,2},{2,4},{4,6},{6,8},{8,10},{10,12},{12,14},{14,16},{16,... | collective-permute-start | bytes 3538952 | tf_op jit(solution)/shard_map/ppermute | solution.py:14
  143.4 48.0 %collective-permute-start.6 = (f32[512,1152]{1,0:T(8,128)S(1)}, f32[512,1152]{1,0:T(8,128)S(1)}, u32[]{:S(2)}, u32[]{:S(2)}) collective-permute-start(f32[512,1152]{1,0:T(8,128)S(1)} %add.43), channel_id=1, source_target_pairs={{6,0},{8,2},{10,4},{12,6},{14,8},{16,10},{18,12},{20,14},{22,16},{... | collective-permute-start | bytes 7077896 | tf_op jit(solution)/shard_map/ppermute | solution.py:14
where the time goes:
time: 193 us
  waiting for transfers between devices  172 us (89%)
  matrix products  13.7 us (7%)
  starting transfers between devices  3.42 us (2%)
  local copies, waits for them, and re-layouts  2.68 us (1%)
    ppermute x7, waiting for transfers between devices, from_behind(): return lax.ppermute(block, axis, route)  172 us
    dot_general x4, matrix products, pair_weights(): lax.dot_general(images, visitor, (((1,), (1,)), ((), ())), preferred_elem...  5.34 us
    dot_general x4, matrix products, local(): jnp.dot(weight, visiting[offset], preferred_element_type=jnp.float32)  4.88 us
  transfers between devices with their start and end apart: 7, of which 4 were waited for; matrix products, arithmetic and copies ran while one was open for 5% of the time, Pallas kernels for 0%

commit v1 on v0

v1 whole, which is shorter than its diff:
```python
import math

import jax
import jax.numpy as jnp
from jax import lax
from jax.sharding import PartitionSpec as P

STEPS = 4
AXIS = "blk"


def send(block, target):
    count = lax.axis_size(AXIS)
    return lax.ppermute(block, AXIS, [(i, target(i) % count) for i in range(count)])


def weights(images, texts):
    factor = 2.0 / math.sqrt(images.shape[1])
    inner_prod = lax.dot_general(
        images, texts, (((1,), (1,)), ((), ())), preferred_element_type=jnp.float32
    )
    return jax.nn.sigmoid(factor * inner_prod - 1.0)


def image_term(weight, texts):
    return jnp.dot(weight, texts, preferred_element_type=jnp.float32)


def text_term(weight, images):
    return lax.dot_general(
        weight, images, (((0,), (0,)), ((), ())), preferred_element_type=jnp.float32
    )


def local(image_embed, text_embed):
    factor = 2.0 / math.sqrt(image_embed.shape[1])
    rows = image_embed.shape[0]

    text_2 = send(text_embed, lambda i: i + 2)
    image_2 = send(image_embed, lambda i: i - 2)
    text_x = send(text_embed, lambda i: i + 3 if i % 2 else i + 1)
    image_x = send(image_embed, lambda i: i - 1 if i % 2 else i - 3)
    text_s = send(text_2, lambda i: i ^ 1)
    image_s = send(image_2, lambda i: i ^ 1)

    row_ids = jnp.arange(rows)
    matched = (row_ids[:, None] == row_ids[None, :]).astype(jnp.float32)
    own = (weights(image_embed, text_embed) - matched).astype(jnp.bfloat16)
    image_grad = image_term(own, text_embed)
    text_grad = text_term(own, image_embed)
    for texts in (text_x, text_2, text_s):
        weight = weights(image_embed, texts).astype(jnp.bfloat16)
        image_grad = image_grad + image_term(weight, texts)
    for images in (image_x, image_2, image_s):
        weight = weights(images, text_embed).astype(jnp.bfloat16)
        text_grad = text_grad + text_term(weight, images)
    return (factor * image_grad, factor * text_grad)


def solution(mesh):
    spec = P(("rep", "blk"), None)
    return jax.shard_map(
        local, mesh=mesh, in_specs=(spec, spec), out_specs=(spec, spec), check_vma=False
    )
```

time: 193 us -> 90.9 us (0.47)
  waiting for transfers between devices: 172 us -> 44.2 us
  matrix products: 13.7 us -> 38.4 us
  starting transfers between devices: 3.42 us -> 6.94 us
  local copies, waits for them, and re-layouts: 2.68 us -> 0.02 us
    ppermute x7 -> x6, waiting for transfers between devices: 172 us -> 44.2 us  [send(): lax.ppermute(block, AXIS, [(i, target(i) % count) for i in range(count)])]
    dot_general x4, matrix products: 3.53 us -> 18.3 us  [text_term(): lax.dot_general(weight, images, (((0,), (0,)), ((), ())), preferred_eleme...]
    dot_general x8 -> x5, matrix products: 10.2 us -> 20.1 us  [the longest x4 17.4 us: image_term(): return jnp.dot(weight, texts, preferred_element_type=jnp.float32)]
    ppermute x7 -> x6, starting transfers between devices: 3.42 us -> 6.94 us  [send(): lax.ppermute(block, AXIS, [(i, target(i) % count) for i in range(count)])]
    unnamed x5 -> x8, local copies, waits for them, and re-layouts: 2.68 us -> 0.02 us
  transfers between devices with their start and end apart: 7 -> 6, of which waited for: 4 -> 3; matrix products, arithmetic and copies ran while one was open for 5% -> 36% of each run, Pallas kernels for 0% -> 0%
where the time goes in v1:
time: 90.9 us; the launch traced here: 90.2 us
  waiting for transfers between devices  44.2 us (49%)
  matrix products  38.4 us (42%)
  starting transfers between devices  6.94 us (8%)
    ppermute x6, waiting for transfers between devices, send(): lax.ppermute(block, AXIS, [(i, target(i) % count) for i in range(count)])  44.2 us
    dot_general x4, matrix products, text_term(): lax.dot_general(weight, images, (((0,), (0,)), ((), ())), preferred_eleme...  18.3 us
    dot_general x4, matrix products, image_term(): return jnp.dot(weight, texts, preferred_element_type=jnp.float32)  17.4 us
    ppermute x6, starting transfers between devices, send(): lax.ppermute(block, AXIS, [(i, target(i) % count) for i in range(count)])  6.94 us
    dot_general x1, matrix products, weights(): lax.dot_general(images, texts, (((1,), (1,)), ((), ())), preferred_elemen...  2.65 us
  transfers between devices with their start and end apart: 6, of which 3 were waited for; matrix products, arithmetic and copies ran while one was open for 36% of the time, Pallas kernels for 0%

profile of v1, /device:TPU:0, one launch (start us, length us, event | category | flops | bytes accessed | tf_op | source)
XLA Modules:
  0.0 90.2 jit_solution(5743802886003315776)
XLA Ops:
  0.6 0.0 copy-start.1
  0.6 6.1 %collective-permute-start.4 = (bf16[512,1152]{1,0:T(8,128)(2,1)}, bf16[512,1152]{1,0:T(8,128)(2,1)}, u32[]{:S(2)}, u32[]{:S(2)}) collective-permute-start(bf16[512,1152]{1,0:T(8,128)(2,1)} %param.2), channel_id=1, source_target_pairs={{0,28},{2,30},{4,0},{6,2},{8,4},{10,6},{12,8},{14,10},{16,12},{18,... | collective-permute-start | bytes 3538952 | tf_op jit(solution)/shard_map/ppermute | solution.py:14
  6.7 0.0 collective-permute-start.1
  6.7 0.0 collective-permute-start.3
  6.7 0.5 collective-permute-start
  7.2 2.6 %fusion.38 = bf16[512,512]{1,0:T(8,128)(2,1)S(1)} fusion(bf16[512,1152]{1,0:T(8,128)(2,1)} %param.2, bf16[512,1152]{1,0:T(8,128)(2,1)} %param.3), kind=kOutput, calls=%fused_computation.51 | convolution fusion | flops 606339072 | bytes 2883584 | tf_op jit(solution)/shard_map/dot_general | solution.py:19
  9.9 0.0 copy-done.1
  9.9 0.0 copy-start
  9.9 2.3 %fusion.82 = f32[512,1152]{1,0:T(8,128)} fusion(bf16[512,512]{1,0:T(8,128)(2,1)S(1)} %fusion.38, bf16[512,1152]{1,0:T(8,128)(2,1)S(1)} %copy-done.1), kind=kOutput, calls=%fused_computation.96 | convolution fusion | flops 603979776 | bytes 4063232 | tf_op jit(solution)/shard_map/dot_general | solution.py:30
  12.2 0.0 copy-done
  12.2 0.9 fusion.81
  13.0 42.2 %collective-permute-done.4 = bf16[512,1152]{1,0:T(8,128)(2,1)} collective-permute-done((bf16[512,1152]{1,0:T(8,128)(2,1)}, bf16[512,1152]{1,0:T(8,128)(2,1)}, u32[]{:S(2)}, u32[]{:S(2)}) %collective-permute-start.4) | collective-permute-done | bytes 1179680 | tf_op jit(solution)/shard_map/ppermute | solution.py:14
  55.2 0.0 collective-permute-start.5
  55.2 0.1 collective-permute-done.1
  55.4 0.4 collective-permute-start.2
  55.7 1.8 %collective-permute-done.3 = bf16[512,1152]{1,0:T(8,128)(2,1)} collective-permute-done((bf16[512,1152]{1,0:T(8,128)(2,1)}, bf16[512,1152]{1,0:T(8,128)(2,1)}, u32[]{:S(2)}, u32[]{:S(2)}) %collective-permute-start.3) | collective-permute-done | bytes 1179680 | tf_op jit(solution)/shard_map/ppermute | solution.py:14
  57.6 5.6 %convolution_add_fusion.2 = f32[512,1152]{1,0:T(8,128)} fusion(f32[512,1152]{1,0:T(8,128)} %fusion.82, bf16[512,1152]{1,0:T(8,128)(2,1)} %collective-permute-done.3, bf16[512,1152]{1,0:T(8,128)(2,1)S(1)} %copy-done), kind=kOutput, calls=%fused_computation.2 | convolution fusion | flops 1210122240 | bytes 7077888 | tf_op jit(solution)/shard_map/dot_general | solution.py:30
  63.2 0.0 collective-permute-done
  63.2 5.1 %convolution_add_fusion.5 = f32[512,1152]{1,0:T(8,128)} fusion(f32[512,1152]{1,0:T(8,128)S(1)} %fusion.81, bf16[512,1152]{1,0:T(8,128)(2,1)} %collective-permute-done, bf16[512,1152]{1,0:T(8,128)(2,1)} %param.2), kind=kOutput, calls=%fused_computation.5 | convolution fusion | flops 1210122240 | bytes 7077888 | tf_op jit(solution)/shard_map/dot_general | solution.py:26
  68.3 0.0 copy-start.3
  68.3 6.0 %convolution_add_fusion.4 = f32[512,1152]{1,0:T(8,128)} fusion(f32[512,1152]{1,0:T(8,128)} %convolution_add_fusion.5, bf16[512,1152]{1,0:T(8,128)(2,1)} %collective-permute-done.1, bf16[512,1152]{1,0:T(8,128)(2,1)} %param.2), kind=kOutput, calls=%fused_computation.4 | convolution fusion | flops 1210122240 | bytes 7077888 | tf_op jit(solution)/shard_map/dot_general | solution.py:26
  74.3 0.0 copy-done.3
  74.3 4.8 %convolution_add_fusion.1 = f32[512,1152]{1,0:T(8,128)} fusion(f32[512,1152]{1,0:T(8,128)S(1)} %copy-done.3, bf16[512,1152]{1,0:T(8,128)(2,1)} %collective-permute-done.4, bf16[512,1152]{1,0:T(8,128)(2,1)S(1)} %copy-done), kind=kOutput, calls=%fused_computation.1 | convolution fusion | flops 1210122240 | bytes 7077888 | tf_op jit(solution)/shard_map/dot_general | solution.py:30
  79.1 0.0 copy-start.2
  79.1 0.0 collective-permute-done.5
  79.1 5.6 %fusion.1 = f32[512,1152]{1,0:T(8,128)} fusion(f32[512,1152]{1,0:T(8,128)} %convolution_add_fusion.1, bf16[512,1152]{1,0:T(8,128)(2,1)} %collective-permute-done.5, bf16[512,1152]{1,0:T(8,128)(2,1)S(1)} %copy-done), kind=kOutput, calls=%fused_computation.7 | convolution fusion | flops 1210712064 | bytes 7077888 | tf_op jit(solution)/shard_map/dot_general | solution.py:30
  84.7 0.0 collective-permute-done.2
  84.7 0.0 copy-done.2
  84.7 5.5 %fusion = f32[512,1152]{1,0:T(8,128)} fusion(f32[512,1152]{1,0:T(8,128)} %convolution_add_fusion.4, bf16[512,1152]{1,0:T(8,128)(2,1)} %collective-permute-done.2, bf16[512,1152]{1,0:T(8,128)(2,1)S(1)} %copy-done.2), kind=kOutput, calls=%fused_computation.6 | convolution fusion | flops 1210712064 | bytes 7077888 | tf_op jit(solution)/shard_map/dot_general | solution.py:26
Async XLA Ops:
  0.6 9.2 %copy-start.1 = (bf16[512,1152]{1,0:T(8,128)(2,1)S(1)}, bf16[512,1152]{1,0:T(8,128)(2,1)}, u32[]{:S(2)}) copy-start(bf16[512,1152]{1,0:T(8,128)(2,1)} %param.2) | copy-start | bytes 3538948
  0.6 54.6 %collective-permute-start.4 = (bf16[512,1152]{1,0:T(8,128)(2,1)}, bf16[512,1152]{1,0:T(8,128)(2,1)}, u32[]{:S(2)}, u32[]{:S(2)}) collective-permute-start(bf16[512,1152]{1,0:T(8,128)(2,1)} %param.2), channel_id=1, source_target_pairs={{0,28},{2,30},{4,0},{6,2},{8,4},{10,6},{12,8},{14,10},{16,12},{18,... | collective-permute-start | bytes 3538952 | tf_op jit(solution)/shard_map/ppermute | solution.py:14
  6.7 48.7 %collective-permute-start.1 = (bf16[512,1152]{1,0:T(8,128)(2,1)}, bf16[512,1152]{1,0:T(8,128)(2,1)}, u32[]{:S(2)}, u32[]{:S(2)}) collective-permute-start(bf16[512,1152]{1,0:T(8,128)(2,1)} %param.3), channel_id=1, source_target_pairs={{0,4},{2,6},{4,8},{6,10},{8,12},{10,14},{12,16},{14,18},{16,20},{1... | collective-permute-start | bytes 3538952 | tf_op jit(solution)/shard_map/ppermute | solution.py:14
  6.7 50.9 %collective-permute-start.3 = (bf16[512,1152]{1,0:T(8,128)(2,1)}, bf16[512,1152]{1,0:T(8,128)(2,1)}, u32[]{:S(2)}, u32[]{:S(2)}) collective-permute-start(bf16[512,1152]{1,0:T(8,128)(2,1)} %param.2), channel_id=1, source_target_pairs={{0,26},{2,0},{4,30},{6,4},{8,2},{10,8},{12,6},{14,12},{16,10},{18,... | collective-permute-start | bytes 3538952 | tf_op jit(solution)/shard_map/ppermute | solution.py:14
  6.7 56.5 %collective-permute-start = (bf16[512,1152]{1,0:T(8,128)(2,1)}, bf16[512,1152]{1,0:T(8,128)(2,1)}, u32[]{:S(2)}, u32[]{:S(2)}) collective-permute-start(bf16[512,1152]{1,0:T(8,128)(2,1)} %param.3), channel_id=1, source_target_pairs={{0,2},{2,8},{4,6},{6,12},{8,10},{10,16},{12,14},{14,20},{16,18},{1... | collective-permute-start | bytes 3538952 | tf_op jit(solution)/shard_map/ppermute | solution.py:14
  9.9 2.3 %copy-start = (bf16[512,1152]{1,0:T(8,128)(2,1)S(1)}, bf16[512,1152]{1,0:T(8,128)(2,1)}, u32[]{:S(2)}) copy-start(bf16[512,1152]{1,0:T(8,128)(2,1)} %param.3) | copy-start | bytes 3538948
  55.2 23.8 %collective-permute-start.5 = (bf16[512,1152]{1,0:T(8,128)(2,1)}, bf16[512,1152]{1,0:T(8,128)(2,1)}, u32[]{:S(2)}, u32[]{:S(2)}) collective-permute-start(bf16[512,1152]{1,0:T(8,128)(2,1)} %collective-permute-done.4), channel_id=1, source_target_pairs={{0,2},{2,0},{4,6},{6,4},{8,10},{10,8},{12,14},{14,12},{16,18},{18,... | collective-permute-start | bytes 3538952 | tf_op jit(solution)/shard_map/ppermute | solution.py:14
  55.4 29.3 %collective-permute-start.2 = (bf16[512,1152]{1,0:T(8,128)(2,1)}, bf16[512,1152]{1,0:T(8,128)(2,1)}, u32[]{:S(2)}, u32[]{:S(2)}) collective-permute-start(bf16[512,1152]{1,0:T(8,128)(2,1)} %collective-permute-done.1), channel_id=1, source_target_pairs={{0,2},{2,0},{4,6},{6,4},{8,10},{10,8},{12,14},{14,12},{16,18},{18,... | collective-permute-start | bytes 3538952 | tf_op jit(solution)/shard_map/ppermute | solution.py:14
  68.3 6.0 %copy-start.3 = (f32[512,1152]{1,0:T(8,128)S(1)}, f32[512,1152]{1,0:T(8,128)}, u32[]{:S(2)}) copy-start(f32[512,1152]{1,0:T(8,128)} %convolution_add_fusion.2) | copy-start | bytes 7077892
  79.1 5.6 %copy-start.2 = (bf16[512,1152]{1,0:T(8,128)(2,1)S(1)}, bf16[512,1152]{1,0:T(8,128)(2,1)}, u32[]{:S(2)}) copy-start(bf16[512,1152]{1,0:T(8,128)(2,1)} %param.2) | copy-start | bytes 3538948

commit v2 on v1

v2 whole, which is shorter than its diff:
```python
import functools
import math

import jax
import jax.numpy as jnp
from jax import lax
from jax.experimental import pallas as pl
from jax.experimental.pallas import tpu as pltpu
from jax.sharding import PartitionSpec as P

AXIS = "blk"
SHARES = (8, 6, 2)
VMEM_MIB = 24
VMEM = pl.BlockSpec(memory_space=pltpu.VMEM)


def send(block, target):
    count = lax.axis_size(AXIS)
    return lax.ppermute(block, AXIS, [(i, target(i) % count) for i in range(count)])


def cut(block):
    rows = block.shape[0]
    ends = [0]
    for share in SHARES:
        ends.append(ends[-1] + rows * share // sum(SHARES))
    return [block[a:b] for a, b in zip(ends, ends[1:])]


def weights(rows, others, factor):
    inner_prod = lax.dot_general(
        rows, others, (((1,), (1,)), ((), ())), preferred_element_type=jnp.float32
    )
    return jax.nn.sigmoid(factor * inner_prod - 1.0)


def product(weight, others):
    return jnp.dot(weight.astype(jnp.bfloat16), others, preferred_element_type=jnp.float32)


def own_kernel(factor, image_ref, text_ref, image_out, text_out):
    images, texts = image_ref[...], text_ref[...]
    shape = (images.shape[0], texts.shape[0])
    matched = lax.broadcasted_iota(jnp.int32, shape, 0) == lax.broadcasted_iota(
        jnp.int32, shape, 1
    )
    matched = matched.astype(jnp.float32)
    image_out[...] = product(weights(images, texts, factor) - matched, texts)
    text_out[...] = product(weights(texts, images, factor) - matched, images)


def window_kernel(factor, n, image_ref, text_ref, *refs):
    texts, images = refs[:n], refs[n : 2 * n]
    image_sum, text_sum, image_out, text_out = refs[2 * n :]
    for own, others, total, out in (
        (image_ref, texts, image_sum, image_out),
        (text_ref, images, text_sum, text_out),
    ):
        rows = own[...]
        result = total[...]
        for other in others:
            block = other[...]
            result = result + product(weights(rows, block, factor), block)
        out[...] = result


def last_kernel(factor, tile, image_ref, text_ref, texts, images, *refs):
    image_sum, text_sum, image_out, text_out, held, sems = refs
    copies = []
    for own, other, total, out in (
        (image_ref, texts, image_sum, image_out),
        (text_ref, images, text_sum, text_out),
    ):
        block = other[...]
        for start in range(0, own.shape[0], tile):
            span = pl.ds(start, tile)
            result = total[span] + product(weights(own[span], block, factor), block)
            slot = len(copies)
            held[slot] = result * factor
            copies.append(pltpu.make_async_copy(held.at[slot], out.at[span], sems.at[slot]))
            copies[-1].start()
    for copy in copies:
        copy.wait()


def params():
    return pltpu.CompilerParams(vmem_limit_bytes=VMEM_MIB << 20)


def local(image_embed, text_embed):
    rows, width = image_embed.shape
    factor = 2.0 / math.sqrt(width)
    shape = (rows, width)
    kept = (pltpu.VMEM(shape, jnp.float32), pltpu.VMEM(shape, jnp.float32))

    def cost(visitors):
        return pl.CostEstimate(
            flops=8 * rows * width * visitors,
            bytes_accessed=8 * (rows + visitors) * width,
            transcendentals=4 * rows * visitors,
        )

    def start():
        return pl.pallas_call(
            functools.partial(own_kernel, factor),
            out_shape=kept,
            in_specs=[VMEM] * 2,
            out_specs=(VMEM, VMEM),
            cost_estimate=cost(rows),
            compiler_params=params(),
        )(image_embed, text_embed)

    def add(sums, texts, images):
        operands = (image_embed, text_embed, *texts, *images, *sums)
        n = len(operands)
        return pl.pallas_call(
            functools.partial(window_kernel, factor, len(texts)),
            out_shape=kept,
            in_specs=[VMEM] * n,
            out_specs=(VMEM, VMEM),
            input_output_aliases={n - 2: 0, n - 1: 1},
            cost_estimate=cost(sum(t.shape[0] for t in texts)),
            compiler_params=params(),
        )(*operands)

    def finish(sums, texts, images):
        tile = rows // 2
        return pl.pallas_call(
            functools.partial(last_kernel, factor, tile),
            out_shape=(jax.ShapeDtypeStruct(shape, jnp.float32),) * 2,
            in_specs=[VMEM] * 6,
            out_specs=(pl.BlockSpec(memory_space=pl.ANY),) * 2,
            scratch_shapes=[
                pltpu.VMEM((2 * rows // tile, tile, width), jnp.float32),
                pltpu.SemaphoreType.DMA((2 * rows // tile,)),
            ],
            cost_estimate=cost(texts.shape[0]),
            compiler_params=params(),
        )(image_embed, text_embed, texts, images, *sums)

    image_parts, text_parts = cut(image_embed), cut(text_embed)
    last = len(SHARES) - 1
    sums = start()
    parts = (text_parts[0], image_parts[0], text_parts[0], image_parts[0])
    targets = (
        lambda i: i + 2,
        lambda i: i - 2,
        lambda i: i + 3 if i % 2 else i + 1,
        lambda i: i - 1 if i % 2 else i - 3,
    )
    for k in range(last + 1):
        following = (text_parts[k + 1], image_parts[k + 1]) * 2 if k < last else parts
        arrived, gated = [], []
        for part, target, later in zip(parts, targets, following):
            piece, later, sums = lax.optimization_barrier((send(part, target), later, sums))
            arrived.append(piece)
            gated.append(later)
        parts = gated
        text_2, image_2, text_x, image_x = arrived
        text_s = send(text_2, lambda i: i ^ 1)
        image_s = send(image_2, lambda i: i ^ 1)
        if k == last:
            sums = add(sums, (text_2, text_x), (image_2, image_x))
            return tuple(finish(sums, text_s, image_s))
        sums = add(sums, (text_2, text_x, text_s), (image_2, image_x, image_s))


def solution(mesh):
    spec = P(("rep", "blk"), None)
    return jax.shard_map(
        local, mesh=mesh, in_specs=(spec, spec), out_specs=(spec, spec), check_vma=False
    )
```

time: 90.9 us -> 80 us (0.88)
  matrix products: 38.4 us -> 0 us
  Pallas kernels: 0 us -> 22.1 us
  starting transfers between devices: 6.94 us -> 26.7 us
  waiting for transfers between devices: 44.2 us -> 27.6 us
  local copies, waits for them, and re-layouts: 0.02 us -> 2.48 us
    dot_general x9 -> x0, matrix products: 38.4 us -> none  [the longest x4 18.3 us: text_term(): lax.dot_general(weight, images, (((0,), (0,)), ((), ())), preferred_eleme...]
    pallas_call x0 -> x5, Pallas kernels: none -> 22.1 us  [the longest x3 16 us: add(): pl.pallas_call(functools.partial(window_kernel, factor, len(texts)), out_...]
    ppermute x6 -> x18, starting transfers between devices: 6.94 us -> 26.7 us  [send(): lax.ppermute(block, AXIS, [(i, target(i) % count) for i in range(count)])]
    ppermute x6 -> x18, waiting for transfers between devices: 44.2 us -> 27.6 us  [send(): lax.ppermute(block, AXIS, [(i, target(i) % count) for i in range(count)])]
    slice x0 -> x6, local copies, waits for them, and re-layouts: none -> 2.47 us  [cut(): return [block[a:b] for a, b in zip(ends, ends[1:])]]
  transfers between devices with their start and end apart: 6 -> 18, of which waited for: 3 -> 7; matrix products, arithmetic and copies ran while one was open for 36% -> 2% of each run, Pallas kernels for 0% -> 24%
where the time goes in v2:
time: 80 us; the launch traced here: 79.8 us
  waiting for transfers between devices  27.6 us (34%)
  starting transfers between devices  26.7 us (33%)
  Pallas kernels  22.1 us (28%)
  local copies, waits for them, and re-layouts  2.48 us (3%)
  between operations  0.94 us (1%)
    ppermute x18, waiting for transfers between devices, send(): lax.ppermute(block, AXIS, [(i, target(i) % count) for i in range(count)])  27.6 us
    ppermute x18, starting transfers between devices, send(): lax.ppermute(block, AXIS, [(i, target(i) % count) for i in range(count)])  26.7 us
    pallas_call x3, Pallas kernels, add(): pl.pallas_call(functools.partial(window_kernel, factor, len(texts)), out_...  16 us
    pallas_call x1, Pallas kernels, start(): pl.pallas_call(functools.partial(own_kernel, factor), out_shape=kept, in_...  3.08 us
    pallas_call x1, Pallas kernels, finish(): pl.pallas_call(functools.partial(last_kernel, factor, tile), out_shape=(j...  3.04 us
    slice x6, local copies, waits for them, and re-layouts, cut(): return [block[a:b] for a, b in zip(ends, ends[1:])]  2.47 us
  transfers between devices with their start and end apart: 18, of which 7 were waited for; matrix products, arithmetic and copies ran while one was open for 2% of the time, Pallas kernels for 24%

profile of v2, /device:TPU:0, one launch (start us, length us, event | category | flops | bytes accessed | tf_op | source)
XLA Modules:
  0.0 79.8 jit_solution(11994308501146681179)
XLA Ops:
  0.6 0.0 copy-start
  0.7 1.3 %slice.18 = bf16[256,1152]{1,0:T(8,128)(2,1)S(1)} slice(bf16[512,1152]{1,0:T(8,128)(2,1)} %text_ref.9), slice={[0:256], [0:1152]} | slice | bytes 1179648 | tf_op jit(solution)/shard_map/slice | solution.py:27
  1.9 3.0 %collective-permute-start = (bf16[256,1152]{1,0:T(8,128)(2,1)S(1)}, bf16[256,1152]{1,0:T(8,128)(2,1)S(1)}, u32[]{:S(2)}, u32[]{:S(2)}) collective-permute-start(bf16[256,1152]{1,0:T(8,128)(2,1)S(1)} %slice.18), channel_id=1, source_target_pairs={{0,4},{2,6},{4,8},{6,10},{8,12},{10,14},{12,16},{14,18},{16,20},{1... | collective-permute-start | bytes 1769480 | tf_op jit(solution)/shard_map/ppermute | solution.py:19
  4.9 1.1 %slice.21 = bf16[256,1152]{1,0:T(8,128)(2,1)S(1)} slice(bf16[512,1152]{1,0:T(8,128)(2,1)} %image_ref.9), slice={[0:256], [0:1152]} | slice | bytes 1179648 | tf_op jit(solution)/shard_map/slice | solution.py:27
  6.0 3.1 %collective-permute-start.3 = (bf16[256,1152]{1,0:T(8,128)(2,1)S(1)}, bf16[256,1152]{1,0:T(8,128)(2,1)S(1)}, u32[]{:S(2)}, u32[]{:S(2)}) collective-permute-start(bf16[256,1152]{1,0:T(8,128)(2,1)S(1)} %slice.21), channel_id=1, source_target_pairs={{0,28},{2,30},{4,0},{6,2},{8,4},{10,6},{12,8},{14,10},{16,12},{18,... | collective-permute-start | bytes 1769480 | tf_op jit(solution)/shard_map/ppermute | solution.py:19
  9.2 0.0 collective-permute-start.2
  9.2 3.5 %collective-permute-start.5 = (bf16[256,1152]{1,0:T(8,128)(2,1)S(1)}, bf16[256,1152]{1,0:T(8,128)(2,1)S(1)}, u32[]{:S(2)}, u32[]{:S(2)}) collective-permute-start(bf16[256,1152]{1,0:T(8,128)(2,1)S(1)} %slice.21), channel_id=1, source_target_pairs={{0,26},{2,0},{4,30},{6,4},{8,2},{10,8},{12,6},{14,12},{16,10},{18,... | collective-permute-start | bytes 1769480 | tf_op jit(solution)/shard_map/ppermute | solution.py:19
  12.7 3.1 %shard_map.41 = (f32[512,1152]{1,0:T(8,128)S(1)}, f32[512,1152]{1,0:T(8,128)S(1)}) custom-call(bf16[512,1152]{1,0:T(8,128)(2,1)S(1)} %copy-done, bf16[512,1152]{1,0:T(8,128)(2,1)S(1)} %copy-done.1), custom_call_target="tpu_custom_call" | custom-call | flops 2415919104 | bytes 9437184 | tf_op jit(solution)/shard_map/pallas_call | solution.py:104
  15.9 14.3 %collective-permute-done.refs_0_ = bf16[256,1152]{1,0:T(8,128)(2,1)S(1)} collective-permute-done((bf16[256,1152]{1,0:T(8,128)(2,1)S(1)}, bf16[256,1152]{1,0:T(8,128)(2,1)S(1)}, u32[]{:S(2)}, u32[]{:S(2)}) %collective-permute-start) | collective-permute-done | bytes 589856 | tf_op jit(solution)/shard_map/ppermute | solution.py:19
  30.2 3.4 %collective-permute-done.3.refs_3_ = bf16[256,1152]{1,0:T(8,128)(2,1)S(1)} collective-permute-done((bf16[256,1152]{1,0:T(8,128)(2,1)S(1)}, bf16[256,1152]{1,0:T(8,128)(2,1)S(1)}, u32[]{:S(2)}, u32[]{:S(2)}) %collective-permute-start.3) | collective-permute-done | bytes 589856 | tf_op jit(solution)/shard_map/ppermute | solution.py:19
  33.5 0.0 collective-permute-start.6
  33.5 0.5 collective-permute-start.4
  34.0 0.0 collective-permute-start.1
  34.0 1.1 %collective-permute-done.2.refs_1_ = bf16[256,1152]{1,0:T(8,128)(2,1)S(1)} collective-permute-done((bf16[256,1152]{1,0:T(8,128)(2,1)S(1)}, bf16[256,1152]{1,0:T(8,128)(2,1)S(1)}, u32[]{:S(2)}, u32[]{:S(2)}) %collective-permute-start.2) | collective-permute-done | bytes 589856 | tf_op jit(solution)/shard_map/ppermute | solution.py:19
  35.1 3.6 %collective-permute-start.9 = (bf16[192,1152]{1,0:T(8,128)(2,1)S(1)}, bf16[192,1152]{1,0:T(8,128)(2,1)S(1)}, u32[]{:S(2)}, u32[]{:S(2)}) collective-permute-start(bf16[192,1152]{1,0:T(8,128)(2,1)S(1)} %slice.22), channel_id=1, source_target_pairs={{0,28},{2,30},{4,0},{6,2},{8,4},{10,6},{12,8},{14,10},{16,12},{18,... | collective-permute-start | bytes 1327112 | tf_op jit(solution)/shard_map/ppermute | solution.py:19
  38.8 0.0 collective-permute-done.5.refs_4_
  38.8 0.1 collective-permute-start.8
  38.9 3.5 %collective-permute-start.11 = (bf16[192,1152]{1,0:T(8,128)(2,1)S(1)}, bf16[192,1152]{1,0:T(8,128)(2,1)S(1)}, u32[]{:S(2)}, u32[]{:S(2)}) collective-permute-start(bf16[192,1152]{1,0:T(8,128)(2,1)S(1)} %slice.22), channel_id=1, source_target_pairs={{0,26},{2,0},{4,30},{6,4},{8,2},{10,8},{12,6},{14,12},{16,10},{18,... | collective-permute-start | bytes 1327112 | tf_op jit(solution)/shard_map/ppermute | solution.py:19
  42.4 5.9 %shard_map.42 = (f32[512,1152]{1,0:T(8,128)S(1)}, f32[512,1152]{1,0:T(8,128)S(1)}) custom-call(bf16[512,1152]{1,0:T(8,128)(2,1)S(1)} %copy-done, bf16[512,1152]{1,0:T(8,128)(2,1)S(1)} %copy-done.1, bf16[256,1152]{1,0:T(8,128)(2,1)S(1)} %collective-permute-done.refs_0_, ...), custom_call_target="tpu_custom_call", output_to_operand_aliasing={{0}: (8, {}), {1}: (9, {})} | custom-call | flops 3623878656 | bytes 11796480 | tf_op jit(solution)/shard_map/pallas_call | solution.py:116
  48.3 5.1 %collective-permute-done.1.refs_0_ = bf16[192,1152]{1,0:T(8,128)(2,1)S(1)} collective-permute-done((bf16[192,1152]{1,0:T(8,128)(2,1)S(1)}, bf16[192,1152]{1,0:T(8,128)(2,1)S(1)}, u32[]{:S(2)}, u32[]{:S(2)}) %collective-permute-start.1) | collective-permute-done | bytes 442400 | tf_op jit(solution)/shard_map/ppermute | solution.py:19
  53.4 2.3 %collective-permute-done.9.refs_3_ = bf16[192,1152]{1,0:T(8,128)(2,1)S(1)} collective-permute-done((bf16[192,1152]{1,0:T(8,128)(2,1)S(1)}, bf16[192,1152]{1,0:T(8,128)(2,1)S(1)}, u32[]{:S(2)}, u32[]{:S(2)}) %collective-permute-start.9) | collective-permute-done | bytes 442400 | tf_op jit(solution)/shard_map/ppermute | solution.py:19
  55.7 0.5 collective-permute-start.10
  56.2 1.0 %collective-permute-done.8.refs_1_ = bf16[192,1152]{1,0:T(8,128)(2,1)S(1)} collective-permute-done((bf16[192,1152]{1,0:T(8,128)(2,1)S(1)}, bf16[192,1152]{1,0:T(8,128)(2,1)S(1)}, u32[]{:S(2)}, u32[]{:S(2)}) %collective-permute-start.8) | collective-permute-done | bytes 442400 | tf_op jit(solution)/shard_map/ppermute | solution.py:19
  57.2 0.5 collective-permute-done.11.refs_4_
  57.6 0.3 collective-permute-start.7
  57.9 4.4 %collective-permute-start.14 = (bf16[64,1152]{1,0:T(8,128)(2,1)S(1)}, bf16[64,1152]{1,0:T(8,128)(2,1)S(1)}, u32[]{:S(2)}, u32[]{:S(2)}) collective-permute-start(bf16[64,1152]{1,0:T(8,128)(2,1)S(1)} %slice.23), channel_id=1, source_target_pairs={{0,28},{2,30},{4,0},{6,2},{8,4},{10,6},{12,8},{14,10},{16,12},{18,... | collective-permute-start | bytes 442376 | tf_op jit(solution)/shard_map/ppermute | solution.py:19
  62.3 3.5 %collective-permute-start.17 = (bf16[64,1152]{1,0:T(8,128)(2,1)S(1)}, bf16[64,1152]{1,0:T(8,128)(2,1)S(1)}, u32[]{:S(2)}, u32[]{:S(2)}) collective-permute-start(bf16[64,1152]{1,0:T(8,128)(2,1)S(1)} %slice.23), channel_id=1, source_target_pairs={{0,26},{2,0},{4,30},{6,4},{8,2},{10,8},{12,6},{14,12},{16,10},{18,... | collective-permute-start | bytes 442376 | tf_op jit(solution)/shard_map/ppermute | solution.py:19
  65.9 5.9 %shard_map.43 = (f32[512,1152]{1,0:T(8,128)S(1)}, f32[512,1152]{1,0:T(8,128)S(1)}) custom-call(bf16[512,1152]{1,0:T(8,128)(2,1)S(1)} %copy-done, bf16[512,1152]{1,0:T(8,128)(2,1)S(1)} %copy-done.1, bf16[192,1152]{1,0:T(8,128)(2,1)S(1)} %collective-permute-done.1.refs_0_, ...), custom_call_target="tpu_custom_call", output_to_operand_aliasing={{0}: (8, {}), {1}: (9, {})} | custom-call | flops 2717908992 | bytes 10027008 | tf_op jit(solution)/shard_map/pallas_call | solution.py:116
  71.8 0.1 collective-permute-start.15
  71.9 0.5 collective-permute-start.13
  72.4 4.2 %shard_map.44 = (f32[512,1152]{1,0:T(8,128)S(1)}, f32[512,1152]{1,0:T(8,128)S(1)}) custom-call(bf16[512,1152]{1,0:T(8,128)(2,1)S(1)} %copy-done, bf16[512,1152]{1,0:T(8,128)(2,1)S(1)} %copy-done.1, bf16[64,1152]{1,0:T(8,128)(2,1)S(1)} %collective-permute-done.7.refs_0_, ...), custom_call_target="tpu_custom_call", output_to_operand_aliasing={{0}: (6, {}), {1}: (7, {})} | custom-call | flops 603979776 | bytes 5898240 | tf_op jit(solution)/shard_map/pallas_call | solution.py:116
  76.6 3.0 %shard_map.45 = (f32[512,1152]{1,0:T(8,128)}, f32[512,1152]{1,0:T(8,128)}) custom-call(bf16[512,1152]{1,0:T(8,128)(2,1)S(1)} %copy-done, bf16[512,1152]{1,0:T(8,128)(2,1)S(1)} %copy-done.1, bf16[64,1152]{1,0:T(8,128)(2,1)S(1)} %collective-permute-done.13.texts, bf16[64,1152]{1,0:T(8,128)(2,1)S(1)} %collective-permute-done.15.images, ...), custom_call_target="tpu_custom_call" | custom-call | flops 301989888 | bytes 5308416 | tf_op jit(solution)/shard_map/pallas_call | solution.py:128
  (19 shorter events, 0.1 us)
Async XLA Ops:
  0.6 12.1 %copy-start.1 = (bf16[512,1152]{1,0:T(8,128)(2,1)S(1)}, bf16[512,1152]{1,0:T(8,128)(2,1)}, u32[]{:S(2)}) copy-start(bf16[512,1152]{1,0:T(8,128)(2,1)} %text_ref.9) | copy-start | bytes 3538948
  0.6 12.1 %copy-start = (bf16[512,1152]{1,0:T(8,128)(2,1)S(1)}, bf16[512,1152]{1,0:T(8,128)(2,1)}, u32[]{:S(2)}) copy-start(bf16[512,1152]{1,0:T(8,128)(2,1)} %image_ref.9) | copy-start | bytes 3538948
  1.9 28.2 %collective-permute-start = (bf16[256,1152]{1,0:T(8,128)(2,1)S(1)}, bf16[256,1152]{1,0:T(8,128)(2,1)S(1)}, u32[]{:S(2)}, u32[]{:S(2)}) collective-permute-start(bf16[256,1152]{1,0:T(8,128)(2,1)S(1)} %slice.18), channel_id=1, source_target_pairs={{0,4},{2,6},{4,8},{6,10},{8,12},{10,14},{12,16},{14,18},{16,20},{1... | collective-permute-start | bytes 1769480 | tf_op jit(solution)/shard_map/ppermute | solution.py:19
  6.0 27.5 %collective-permute-start.3 = (bf16[256,1152]{1,0:T(8,128)(2,1)S(1)}, bf16[256,1152]{1,0:T(8,128)(2,1)S(1)}, u32[]{:S(2)}, u32[]{:S(2)}) collective-permute-start(bf16[256,1152]{1,0:T(8,128)(2,1)S(1)} %slice.21), channel_id=1, source_target_pairs={{0,28},{2,30},{4,0},{6,2},{8,4},{10,6},{12,8},{14,10},{16,12},{18,... | collective-permute-start | bytes 1769480 | tf_op jit(solution)/shard_map/ppermute | solution.py:19
  9.2 26.0 %collective-permute-start.2 = (bf16[256,1152]{1,0:T(8,128)(2,1)S(1)}, bf16[256,1152]{1,0:T(8,128)(2,1)S(1)}, u32[]{:S(2)}, u32[]{:S(2)}) collective-permute-start(bf16[256,1152]{1,0:T(8,128)(2,1)S(1)} %slice.18), channel_id=1, source_target_pairs={{0,2},{2,8},{4,6},{6,12},{8,10},{10,16},{12,14},{14,20},{16,18},{1... | collective-permute-start | bytes 1769480 | tf_op jit(solution)/shard_map/ppermute | solution.py:19
  9.2 29.6 %collective-permute-start.5 = (bf16[256,1152]{1,0:T(8,128)(2,1)S(1)}, bf16[256,1152]{1,0:T(8,128)(2,1)S(1)}, u32[]{:S(2)}, u32[]{:S(2)}) collective-permute-start(bf16[256,1152]{1,0:T(8,128)(2,1)S(1)} %slice.21), channel_id=1, source_target_pairs={{0,26},{2,0},{4,30},{6,4},{8,2},{10,8},{12,6},{14,12},{16,10},{18,... | collective-permute-start | bytes 1769480 | tf_op jit(solution)/shard_map/ppermute | solution.py:19
  33.5 5.4 %collective-permute-start.6 = (bf16[256,1152]{1,0:T(8,128)(2,1)S(1)}, bf16[256,1152]{1,0:T(8,128)(2,1)S(1)}, u32[]{:S(2)}, u32[]{:S(2)}) collective-permute-start(bf16[256,1152]{1,0:T(8,128)(2,1)S(1)} %collective-permute-done.3.refs_3_), channel_id=1, source_target_pairs={{0,2},{2,0},{4,6},{6,4},{8,10},{10,8},{12,14},{14,12},{16,18},{18,... | collective-permute-start | bytes 1769480 | tf_op jit(solution)/shard_map/ppermute | solution.py:19
  33.5 8.9 %collective-permute-start.4 = (bf16[256,1152]{1,0:T(8,128)(2,1)S(1)}, bf16[256,1152]{1,0:T(8,128)(2,1)S(1)}, u32[]{:S(2)}, u32[]{:S(2)}) collective-permute-start(bf16[256,1152]{1,0:T(8,128)(2,1)S(1)} %collective-permute-done.refs_0_), channel_id=1, source_target_pairs={{0,2},{2,0},{4,6},{6,4},{8,10},{10,8},{12,14},{14,12},{16,18},{18,... | collective-permute-start | bytes 1769480 | tf_op jit(solution)/shard_map/ppermute | solution.py:19
  34.0 19.4 %collective-permute-start.1 = (bf16[192,1152]{1,0:T(8,128)(2,1)S(1)}, bf16[192,1152]{1,0:T(8,128)(2,1)S(1)}, u32[]{:S(2)}, u32[]{:S(2)}) collective-permute-start(bf16[192,1152]{1,0:T(8,128)(2,1)S(1)} %slice.19), channel_id=1, source_target_pairs={{0,4},{2,6},{4,8},{6,10},{8,12},{10,14},{12,16},{14,18},{16,20},{1... | collective-permute-start | bytes 1327112 | tf_op jit(solution)/shard_map/ppermute | solution.py:19
  35.1 20.5 %collective-permute-start.9 = (bf16[192,1152]{1,0:T(8,128)(2,1)S(1)}, bf16[192,1152]{1,0:T(8,128)(2,1)S(1)}, u32[]{:S(2)}, u32[]{:S(2)}) collective-permute-start(bf16[192,1152]{1,0:T(8,128)(2,1)S(1)} %slice.22), channel_id=1, source_target_pairs={{0,28},{2,30},{4,0},{6,2},{8,4},{10,6},{12,8},{14,10},{16,12},{18,... | collective-permute-start | bytes 1327112 | tf_op jit(solution)/shard_map/ppermute | solution.py:19
  38.8 18.3 %collective-permute-start.8 = (bf16[192,1152]{1,0:T(8,128)(2,1)S(1)}, bf16[192,1152]{1,0:T(8,128)(2,1)S(1)}, u32[]{:S(2)}, u32[]{:S(2)}) collective-permute-start(bf16[192,1152]{1,0:T(8,128)(2,1)S(1)} %slice.19), channel_id=1, source_target_pairs={{0,2},{2,8},{4,6},{6,12},{8,10},{10,16},{12,14},{14,20},{16,18},{1... | collective-permute-start | bytes 1327112 | tf_op jit(solution)/shard_map/ppermute | solution.py:19
  38.9 18.7 %collective-permute-start.11 = (bf16[192,1152]{1,0:T(8,128)(2,1)S(1)}, bf16[192,1152]{1,0:T(8,128)(2,1)S(1)}, u32[]{:S(2)}, u32[]{:S(2)}) collective-permute-start(bf16[192,1152]{1,0:T(8,128)(2,1)S(1)} %slice.22), channel_id=1, source_target_pairs={{0,26},{2,0},{4,30},{6,4},{8,2},{10,8},{12,6},{14,12},{16,10},{18,... | collective-permute-start | bytes 1327112 | tf_op jit(solution)/shard_map/ppermute | solution.py:19
  55.7 6.7 %collective-permute-start.12 = (bf16[192,1152]{1,0:T(8,128)(2,1)S(1)}, bf16[192,1152]{1,0:T(8,128)(2,1)S(1)}, u32[]{:S(2)}, u32[]{:S(2)}) collective-permute-start(bf16[192,1152]{1,0:T(8,128)(2,1)S(1)} %collective-permute-done.9.refs_3_), channel_id=1, source_target_pairs={{0,2},{2,0},{4,6},{6,4},{8,10},{10,8},{12,14},{14,12},{16,18},{18,... | collective-permute-start | bytes 1327112 | tf_op jit(solution)/shard_map/ppermute | solution.py:19
  55.7 10.2 %collective-permute-start.10 = (bf16[192,1152]{1,0:T(8,128)(2,1)S(1)}, bf16[192,1152]{1,0:T(8,128)(2,1)S(1)}, u32[]{:S(2)}, u32[]{:S(2)}) collective-permute-start(bf16[192,1152]{1,0:T(8,128)(2,1)S(1)} %collective-permute-done.1.refs_0_), channel_id=1, source_target_pairs={{0,2},{2,0},{4,6},{6,4},{8,10},{10,8},{12,14},{14,12},{16,18},{18,... | collective-permute-start | bytes 1327112 | tf_op jit(solution)/shard_map/ppermute | solution.py:19
  57.6 14.2 %collective-permute-start.7 = (bf16[64,1152]{1,0:T(8,128)(2,1)S(1)}, bf16[64,1152]{1,0:T(8,128)(2,1)S(1)}, u32[]{:S(2)}, u32[]{:S(2)}) collective-permute-start(bf16[64,1152]{1,0:T(8,128)(2,1)S(1)} %slice.20), channel_id=1, source_target_pairs={{0,4},{2,6},{4,8},{6,10},{8,12},{10,14},{12,16},{14,18},{16,20},{1... | collective-permute-start | bytes 442376 | tf_op jit(solution)/shard_map/ppermute | solution.py:19
  57.9 13.8 %collective-permute-start.14 = (bf16[64,1152]{1,0:T(8,128)(2,1)S(1)}, bf16[64,1152]{1,0:T(8,128)(2,1)S(1)}, u32[]{:S(2)}, u32[]{:S(2)}) collective-permute-start(bf16[64,1152]{1,0:T(8,128)(2,1)S(1)} %slice.23), channel_id=1, source_target_pairs={{0,28},{2,30},{4,0},{6,2},{8,4},{10,6},{12,8},{14,10},{16,12},{18,... | collective-permute-start | bytes 442376 | tf_op jit(solution)/shard_map/ppermute | solution.py:19
  62.3 10.0 %collective-permute-start.16 = (bf16[64,1152]{1,0:T(8,128)(2,1)S(1)}, bf16[64,1152]{1,0:T(8,128)(2,1)S(1)}, u32[]{:S(2)}, u32[]{:S(2)}) collective-permute-start(bf16[64,1152]{1,0:T(8,128)(2,1)S(1)} %slice.20), channel_id=1, source_target_pairs={{0,2},{2,8},{4,6},{6,12},{8,10},{10,16},{12,14},{14,20},{16,18},{1... | collective-permute-start | bytes 442376 | tf_op jit(solution)/shard_map/ppermute | solution.py:19
  62.3 10.0 %collective-permute-start.17 = (bf16[64,1152]{1,0:T(8,128)(2,1)S(1)}, bf16[64,1152]{1,0:T(8,128)(2,1)S(1)}, u32[]{:S(2)}, u32[]{:S(2)}) collective-permute-start(bf16[64,1152]{1,0:T(8,128)(2,1)S(1)} %slice.23), channel_id=1, source_target_pairs={{0,26},{2,0},{4,30},{6,4},{8,2},{10,8},{12,6},{14,12},{16,10},{18,... | collective-permute-start | bytes 442376 | tf_op jit(solution)/shard_map/ppermute | solution.py:19
  71.8 4.8 %collective-permute-start.15 = (bf16[64,1152]{1,0:T(8,128)(2,1)S(1)}, bf16[64,1152]{1,0:T(8,128)(2,1)S(1)}, u32[]{:S(2)}, u32[]{:S(2)}) collective-permute-start(bf16[64,1152]{1,0:T(8,128)(2,1)S(1)} %collective-permute-done.14.refs_2_), channel_id=1, source_target_pairs={{0,2},{2,0},{4,6},{6,4},{8,10},{10,8},{12,14},{14,12},{16,18},{18,... | collective-permute-start | bytes 442376 | tf_op jit(solution)/shard_map/ppermute | solution.py:19
  71.9 4.7 %collective-permute-start.13 = (bf16[64,1152]{1,0:T(8,128)(2,1)S(1)}, bf16[64,1152]{1,0:T(8,128)(2,1)S(1)}, u32[]{:S(2)}, u32[]{:S(2)}) collective-permute-start(bf16[64,1152]{1,0:T(8,128)(2,1)S(1)} %collective-permute-done.7.refs_0_), channel_id=1, source_target_pairs={{0,2},{2,0},{4,6},{6,4},{8,10},{10,8},{12,14},{14,12},{16,18},{18,... | collective-permute-start | bytes 442376 | tf_op jit(solution)/shard_map/ppermute | solution.py:19

commit v3 on v1

v3 whole, which is shorter than its diff:
```python
import functools
import math

import jax
import jax.numpy as jnp
from jax import lax
from jax.experimental import pallas as pl
from jax.experimental.pallas import tpu as pltpu
from jax.sharding import PartitionSpec as P

AXIS = "blk"
IMAGE_SHARES = (9, 16, 7)
TEXT_SHARES = (13, 12, 7)
DEPTH = 256
TILE = 256
VMEM_MIB = 28
VMEM = pl.BlockSpec(memory_space=pltpu.VMEM)
ANY = pl.BlockSpec(memory_space=pl.ANY)


def send(block, target):
    count = lax.axis_size(AXIS)
    return lax.ppermute(block, AXIS, [(i, target(i) % count) for i in range(count)])


def swap(block):
    return send(block, lambda i: i ^ 1)


def cut(block, shares):
    rows = block.shape[0]
    ends = [0]
    for share in shares:
        ends.append(ends[-1] + rows * share // sum(shares))
    return [block[a:b] for a, b in zip(ends, ends[1:])]


def after(value, *earlier):
    return lax.optimization_barrier((value, *earlier))[0]


def weights(rows, others, factor):
    inner_prod = lax.dot_general(
        rows, others, (((1,), (1,)), ((), ())), preferred_element_type=jnp.float32
    )
    return jax.nn.sigmoid(factor * inner_prod - 1.0)


def product(weight, others):
    return jnp.dot(weight.astype(jnp.bfloat16), others, preferred_element_type=jnp.float32)


def padded(rows):
    return -(-rows // DEPTH) * DEPTH


def join(visitors, joined):
    if len(visitors) == 1 and visitors[0].shape[0] % DEPTH == 0:
        return visitors[0]
    start = 0
    for visitor in visitors:
        joined[pl.ds(start, visitor.shape[0])] = visitor[...]
        start += visitor.shape[0]
    depth = padded(start)
    if start < depth:
        joined[pl.ds(start, depth - start)] = jnp.zeros(
            (depth - start, joined.shape[1]), joined.dtype
        )
    return joined.at[pl.ds(0, depth)]


def own_kernel(factor, image_ref, text_ref, image_out, text_out):
    for rows_ref, others_ref, out in (
        (image_ref, text_ref, image_out),
        (text_ref, image_ref, text_out),
    ):
        others = others_ref[...]
        for start in range(0, rows_ref.shape[0], TILE):
            span = pl.ds(start, TILE)
            shape = (TILE, others.shape[0])
            row = lax.broadcasted_iota(jnp.int32, shape, 0) + start
            matched = (row == lax.broadcasted_iota(jnp.int32, shape, 1)).astype(jnp.float32)
            weight = weights(rows_ref[span], others, factor) - matched
            out[span] = product(weight, others)


def window_kernel(factor, counts, *refs):
    refs = list(refs)
    sides = []
    for count in counts:
        sides.append((refs[0], refs[1 : 1 + count], refs[1 + count]))
        refs = refs[2 + count :]
    joined = refs[len(counts)]
    for (rows_ref, visitors, total), out in zip(sides, refs):
        others = join(visitors, joined)[...]
        for start in range(0, rows_ref.shape[0], TILE):
            span = pl.ds(start, TILE)
            weight = weights(rows_ref[span], others, factor)
            out[span] = total[span] + product(weight, others)


def last_kernel(factor, count, rows_ref, *refs):
    visitors, (total, out, joined, held, sems) = refs[:count], refs[count:]
    others = join(visitors, joined)[...]
    copies = []
    for start in range(0, rows_ref.shape[0], TILE):
        span = pl.ds(start, TILE)
        weight = weights(rows_ref[span], others, factor)
        held[span] = (total[span] + product(weight, others)) * factor
        copies.append(pltpu.make_async_copy(held.at[span], out.at[span], sems.at[len(copies)]))
        copies[-1].start()
    for copy in copies:
        copy.wait()


def params():
    return pltpu.CompilerParams(vmem_limit_bytes=VMEM_MIB << 20)


def local(image_embed, text_embed):
    rows, width = image_embed.shape
    factor = 2.0 / math.sqrt(width)
    shape = (rows, width)
    kept = pltpu.VMEM(shape, jnp.float32)

    cost = pl.CostEstimate(flops=1, bytes_accessed=1, transcendentals=0)

    def joined(sides):
        depth = max(padded(sum(v.shape[0] for v in visitors)) for visitors in sides)
        return pltpu.VMEM((depth, width), jnp.bfloat16)

    def begin():
        return pl.pallas_call(
            functools.partial(own_kernel, factor),
            out_shape=(kept, kept),
            in_specs=[VMEM] * 2,
            out_specs=(VMEM, VMEM),
            cost_estimate=cost,
            compiler_params=params(),
        )(image_embed, text_embed)

    def add(*sides):
        operands, aliases = [], {}
        for number, (own, visitors, total) in enumerate(sides):
            operands += [own, *visitors, total]
            aliases[len(operands) - 1] = number
        return pl.pallas_call(
            functools.partial(window_kernel, factor, [len(side[1]) for side in sides]),
            out_shape=(kept,) * len(sides),
            in_specs=[VMEM] * len(operands),
            out_specs=(VMEM,) * len(sides),
            scratch_shapes=[joined([side[1] for side in sides])],
            input_output_aliases=aliases,
            cost_estimate=cost,
            compiler_params=params(),
        )(*operands)

    def finish(own, visitors, total):
        return pl.pallas_call(
            functools.partial(last_kernel, factor, len(visitors)),
            out_shape=jax.ShapeDtypeStruct(shape, jnp.float32),
            in_specs=[VMEM] * (2 + len(visitors)),
            out_specs=ANY,
            scratch_shapes=[
                joined([visitors]),
                pltpu.VMEM(shape, jnp.float32),
                pltpu.SemaphoreType.DMA((rows // TILE,)),
            ],
            cost_estimate=cost,
            compiler_params=params(),
        )(own, *visitors, total)

    def next_text(piece):
        return send(piece, lambda i: i + 2)

    def next_image(piece):
        return send(piece, lambda i: i - 2)

    def far_text(piece):
        return send(piece, lambda i: i + 3 if i % 2 else i + 1)

    def far_image(piece):
        return send(piece, lambda i: i - 1 if i % 2 else i - 3)

    image_parts, text_parts = cut(image_embed, IMAGE_SHARES), cut(text_embed, TEXT_SHARES)
    text_x, image_x = far_text(text_embed), far_image(image_embed)
    text_piece, image_piece = next_text(text_parts[0]), next_image(image_parts[0])
    image_sum, text_sum = begin()

    image_0 = after(image_piece, image_sum, text_sum)
    image_piece = next_image(after(image_parts[1], image_0))
    image_0s = swap(image_0)
    (text_sum,) = add((text_embed, (image_0,), text_sum))

    text_0 = after(text_piece, text_sum)
    text_piece = next_text(after(text_parts[1], text_0))
    text_0s = swap(text_0)
    (image_sum,) = add((image_embed, (text_0,), image_sum))

    image_1 = after(image_piece, image_sum)
    image_piece = next_image(after(image_parts[2], image_1))
    image_1s = swap(image_1)
    (text_sum,) = add((text_embed, (image_1, image_0s), text_sum))

    text_1 = after(text_piece, text_sum)
    text_piece = next_text(after(text_parts[2], text_1))
    text_1s = swap(text_1)
    (image_sum,) = add((image_embed, (text_1, text_0s), image_sum))

    text_x, image_x = after(text_x, image_sum), after(image_x, image_sum)
    image_sum, text_sum = add(
        (image_embed, (text_x,), image_sum), (text_embed, (image_x,), text_sum)
    )

    image_2 = after(image_piece, image_sum)
    image_2s = swap(image_2)
    image_sum, text_sum = add(
        (image_embed, (text_1s,), image_sum), (text_embed, (image_2, image_1s), text_sum)
    )

    text_2 = after(text_piece, image_sum)
    text_2s = swap(text_2)
    text_grad = finish(text_embed, (after(image_2s, text_2),), text_sum)
    image_grad = finish(image_embed, (text_2, text_2s), image_sum)
    return (image_grad, text_grad)


def solution(mesh):
    spec = P(("rep", "blk"), None)
    return jax.shard_map(
        local, mesh=mesh, in_specs=(spec, spec), out_specs=(spec, spec), check_vma=False
    )
```

time: 90.9 us -> 77.7 us (0.85)
  the two profiles are of different devices: /device:TPU:0 before, /device:TPU:9 now
where the time goes in v3:
time: 77.7 us; the launch traced here: 77.5 us
  starting transfers between devices  29.8 us (38%)
  Pallas kernels  23 us (30%)
  waiting for transfers between devices  20.2 us (26%)
  local copies, waits for them, and re-layouts  3.56 us (5%)
  between operations  0.97 us (1%)
    ppermute x14, starting transfers between devices, send(): lax.ppermute(block, AXIS, [(i, target(i) % count) for i in range(count)])  29.8 us
    ppermute x14, waiting for transfers between devices, send(): lax.ppermute(block, AXIS, [(i, target(i) % count) for i in range(count)])  20.2 us
    pallas_call x6, Pallas kernels, add(): pl.pallas_call(functools.partial(window_kernel, factor, [len(side[1]) for...  14.2 us
    pallas_call x2, Pallas kernels, finish(): pl.pallas_call(functools.partial(last_kernel, factor, len(visitors)), out...  5.38 us
    pallas_call x1, Pallas kernels, begin(): pl.pallas_call(functools.partial(own_kernel, factor), out_shape=(kept, ke...  3.36 us
    slice x6, local copies, waits for them, and re-layouts, cut(): return [block[a:b] for a, b in zip(ends, ends[1:])]  2.28 us
  transfers between devices with their start and end apart: 14, of which 4 were waited for; matrix products, arithmetic and copies ran while one was open for 2% of the time, Pallas kernels for 26%

profile of v3, /device:TPU:9, one launch (start us, length us, event | category | flops | bytes accessed | tf_op | source)
XLA Modules:
  0.0 77.5 jit_solution(14873000210560838971)
XLA Ops:
  0.6 0.0 copy-start
  0.6 1.1 %slice.21 = bf16[144,1152]{1,0:T(8,128)(2,1)S(1)} slice(bf16[512,1152]{1,0:T(8,128)(2,1)} %rows_ref.2), slice={[0:144], [0:1152]} | slice | bytes 663552 | tf_op jit(solution)/shard_map/slice | solution.py:35
  1.7 1.2 %collective-permute-start.1 = (bf16[144,1152]{1,0:T(8,128)(2,1)S(1)}, bf16[144,1152]{1,0:T(8,128)(2,1)S(1)}, u32[]{:S(2)}, u32[]{:S(2)}) collective-permute-start(bf16[144,1152]{1,0:T(8,128)(2,1)S(1)} %slice.21), channel_id=1, source_target_pairs={{0,28},{2,30},{4,0},{6,2},{8,4},{10,6},{12,8},{14,10},{16,12},{18,... | collective-permute-start | bytes 995336 | tf_op jit(solution)/shard_map/ppermute | solution.py:23
  2.9 1.0 %collective-permute-start.9 = (bf16[512,1152]{1,0:T(8,128)(2,1)}, bf16[512,1152]{1,0:T(8,128)(2,1)S(1)}, u32[]{:S(2)}, u32[]{:S(2)}) collective-permute-start(bf16[512,1152]{1,0:T(8,128)(2,1)} %rows_ref.2), channel_id=1, source_target_pairs={{0,26},{2,0},{4,30},{6,4},{8,2},{10,8},{12,6},{14,12},{16,10},{18,... | collective-permute-start | bytes 3538952 | tf_op jit(solution)/shard_map/ppermute | solution.py:23
  3.9 1.1 %slice.20 = bf16[208,1152]{1,0:T(8,128)(2,1)S(1)} slice(bf16[512,1152]{1,0:T(8,128)(2,1)} %rows_ref.3), slice={[0:208], [0:1152]} | slice | bytes 958464 | tf_op jit(solution)/shard_map/slice | solution.py:35
  4.9 0.4 collective-permute-start
  5.3 1.3 %copy-done.1 = bf16[512,1152]{1,0:T(8,128)(2,1)S(1)} copy-done((bf16[512,1152]{1,0:T(8,128)(2,1)S(1)}, bf16[512,1152]{1,0:T(8,128)(2,1)}, u32[]{:S(2)}) %copy-start.1) | copy-done | bytes 1179672
  6.6 3.4 %shard_map.41 = (f32[512,1152]{1,0:T(8,128)S(1)}, f32[512,1152]{1,0:T(8,128)S(1)}) custom-call(bf16[512,1152]{1,0:T(8,128)(2,1)S(1)} %copy-done.1, bf16[512,1152]{1,0:T(8,128)(2,1)S(1)} %copy-done), custom_call_target="tpu_custom_call" | custom-call | flops 1 | bytes 1 | tf_op jit(solution)/shard_map/pallas_call | solution.py:133
  10.0 2.3 %collective-permute-done.1.refs_1_ = bf16[144,1152]{1,0:T(8,128)(2,1)S(1)} collective-permute-done((bf16[144,1152]{1,0:T(8,128)(2,1)S(1)}, bf16[144,1152]{1,0:T(8,128)(2,1)S(1)}, u32[]{:S(2)}, u32[]{:S(2)}) %collective-permute-start.1) | collective-permute-done | bytes 331808 | tf_op jit(solution)/shard_map/ppermute | solution.py:23
  12.3 0.2 collective-permute-start.3
  12.5 3.7 %collective-permute-start.7 = (bf16[512,1152]{1,0:T(8,128)(2,1)S(1)}, bf16[512,1152]{1,0:T(8,128)(2,1)S(1)}, u32[]{:S(2)}, u32[]{:S(2)}) collective-permute-start(bf16[512,1152]{1,0:T(8,128)(2,1)S(1)} %copy-done), channel_id=1, source_target_pairs={{0,2},{2,8},{4,6},{6,12},{8,10},{10,16},{12,14},{14,20},{16,18},{1... | collective-permute-start | bytes 3538952 | tf_op jit(solution)/shard_map/ppermute | solution.py:23
  16.2 1.7 %shard_map.42.refs_3_ = f32[512,1152]{1,0:T(8,128)S(1)} custom-call(bf16[512,1152]{1,0:T(8,128)(2,1)S(1)} %copy-done, bf16[144,1152]{1,0:T(8,128)(2,1)S(1)} %collective-permute-done.1.refs_1_, f32[512,1152]{1,0:T(8,128)S(1)} %get-tuple-element.22.refs_2_), custom_call_target="tpu_custom_call", output_to_operand_aliasing={{}: (2, {})} | custom-call | flops 1 | bytes 1 | tf_op jit(solution)/shard_map/pallas_call | solution.py:147
  18.0 10.1 %collective-permute-done.refs_1_ = bf16[208,1152]{1,0:T(8,128)(2,1)S(1)} collective-permute-done((bf16[208,1152]{1,0:T(8,128)(2,1)S(1)}, bf16[208,1152]{1,0:T(8,128)(2,1)S(1)}, u32[]{:S(2)}, u32[]{:S(2)}) %collective-permute-start) | collective-permute-done | bytes 479264 | tf_op jit(solution)/shard_map/ppermute | solution.py:23
  28.0 2.2 %collective-permute-start.2 = (bf16[192,1152]{1,0:T(8,128)(2,1)S(1)}, bf16[192,1152]{1,0:T(8,128)(2,1)S(1)}, u32[]{:S(2)}, u32[]{:S(2)}) collective-permute-start(bf16[192,1152]{1,0:T(8,128)(2,1)S(1)} %slice.19), channel_id=1, source_target_pairs={{0,4},{2,6},{4,8},{6,10},{8,12},{10,14},{12,16},{14,18},{16,20},{1... | collective-permute-start | bytes 1327112 | tf_op jit(solution)/shard_map/ppermute | solution.py:23
  30.2 0.0 collective-permute-done.3.refs_1_
  30.2 14.0 %collective-permute-start.8 = (bf16[208,1152]{1,0:T(8,128)(2,1)S(1)}, bf16[208,1152]{1,0:T(8,128)(2,1)S(1)}, u32[]{:S(2)}, u32[]{:S(2)}) collective-permute-start(bf16[208,1152]{1,0:T(8,128)(2,1)S(1)} %collective-permute-done.refs_1_), channel_id=1, source_target_pairs={{0,2},{2,0},{4,6},{6,4},{8,10},{10,8},{12,14},{14,12},{16,18},{18,... | collective-permute-start | bytes 1437704 | tf_op jit(solution)/shard_map/ppermute | solution.py:23
  44.2 1.7 %shard_map.43.refs_3_ = f32[512,1152]{1,0:T(8,128)S(1)} custom-call(bf16[512,1152]{1,0:T(8,128)(2,1)S(1)} %copy-done.1, bf16[208,1152]{1,0:T(8,128)(2,1)S(1)} %collective-permute-done.refs_1_, f32[512,1152]{1,0:T(8,128)S(1)} %get-tuple-element.21.refs_2_), custom_call_target="tpu_custom_call", output_to_operand_aliasing={{}: (2, {})} | custom-call | flops 1 | bytes 1 | tf_op jit(solution)/shard_map/pallas_call | solution.py:147
  45.9 0.0 collective-permute-done.4.refs_2_
  45.9 0.1 collective-permute-start.11
  46.0 1.8 %shard_map.44.refs_5_ = f32[512,1152]{1,0:T(8,128)S(1)} custom-call(bf16[512,1152]{1,0:T(8,128)(2,1)S(1)} %copy-done, bf16[256,1152]{1,0:T(8,128)(2,1)S(1)} %collective-permute-done.3.refs_1_, bf16[144,1152]{1,0:T(8,128)(2,1)S(1)} %collective-permute-done.4.refs_2_, f32[512,1152]{1,0:T(8,128)S(1)} %shard_map.42.refs_3_), custom_call_target="tpu_custom_call", output_to_operand_aliasing={{}: (3, {})} | custom-call | flops 1 | bytes 1 | tf_op jit(solution)/shard_map/pallas_call | solution.py:147
  47.8 1.5 %collective-permute-done.2.refs_1_ = bf16[192,1152]{1,0:T(8,128)(2,1)S(1)} collective-permute-done((bf16[192,1152]{1,0:T(8,128)(2,1)S(1)}, bf16[192,1152]{1,0:T(8,128)(2,1)S(1)}, u32[]{:S(2)}, u32[]{:S(2)}) %collective-permute-start.2) | collective-permute-done | bytes 442400 | tf_op jit(solution)/shard_map/ppermute | solution.py:23
  49.4 4.6 %collective-permute-start.6 = (bf16[192,1152]{1,0:T(8,128)(2,1)S(1)}, bf16[192,1152]{1,0:T(8,128)(2,1)S(1)}, u32[]{:S(2)}, u32[]{:S(2)}) collective-permute-start(bf16[192,1152]{1,0:T(8,128)(2,1)S(1)} %collective-permute-done.2.refs_1_), channel_id=1, source_target_pairs={{0,2},{2,0},{4,6},{6,4},{8,10},{10,8},{12,14},{14,12},{16,18},{18,... | collective-permute-start | bytes 1327112 | tf_op jit(solution)/shard_map/ppermute | solution.py:23
  54.0 0.1 collective-permute-start.10
  54.1 1.7 %collective-permute-start.5 = (bf16[112,1152]{1,0:T(8,128)(2,1)S(1)}, bf16[112,1152]{1,0:T(8,128)(2,1)S(1)}, u32[]{:S(2)}, u32[]{:S(2)}) collective-permute-start(bf16[112,1152]{1,0:T(8,128)(2,1)S(1)} %slice.18), channel_id=1, source_target_pairs={{0,4},{2,6},{4,8},{6,10},{8,12},{10,14},{12,16},{14,18},{16,20},{1... | collective-permute-start | bytes 774152 | tf_op jit(solution)/shard_map/ppermute | solution.py:23
  55.7 1.8 %shard_map.45.refs_2_ = f32[512,1152]{1,0:T(8,128)S(1)} custom-call(bf16[512,1152]{1,0:T(8,128)(2,1)S(1)} %copy-done.1, bf16[192,1152]{1,0:T(8,128)(2,1)S(1)} %collective-permute-done.2.refs_1_, bf16[208,1152]{1,0:T(8,128)(2,1)S(1)} %collective-permute-done.8.refs_2_, f32[512,1152]{1,0:T(8,128)S(1)} %shard_map.43.refs_3_), custom_call_target="tpu_custom_call", output_to_operand_aliasing={{}: (3, {})} | custom-call | flops 1 | bytes 1 | tf_op jit(solution)/shard_map/pallas_call | solution.py:147
  57.6 3.6 %shard_map.46 = (f32[512,1152]{1,0:T(8,128)S(1)}, f32[512,1152]{1,0:T(8,128)S(1)}) custom-call(bf16[512,1152]{1,0:T(8,128)(2,1)S(1)} %copy-done.1, bf16[512,1152]{1,0:T(8,128)(2,1)S(1)} %collective-permute-done.7.refs_1_, f32[512,1152]{1,0:T(8,128)S(1)} %shard_map.45.refs_2_, ...), custom_call_target="tpu_custom_call", output_to_operand_aliasing={{0}: (2, {}), {1}: (5, {})} | custom-call | flops 1 | bytes 1 | tf_op jit(solution)/shard_map/pallas_call | solution.py:147
  61.1 6.2 %collective-permute-done.10.refs_4_ = bf16[112,1152]{1,0:T(8,128)(2,1)S(1)} collective-permute-done((bf16[112,1152]{1,0:T(8,128)(2,1)S(1)}, bf16[112,1152]{1,0:T(8,128)(2,1)S(1)}, u32[]{:S(2)}, u32[]{:S(2)}) %collective-permute-start.10) | collective-permute-done | bytes 258080 | tf_op jit(solution)/shard_map/ppermute | solution.py:23
  67.4 0.8 %collective-permute-start.13 = (bf16[112,1152]{1,0:T(8,128)(2,1)S(1)}, bf16[112,1152]{1,0:T(8,128)(2,1)S(1)}, u32[]{:S(2)}, u32[]{:S(2)}) collective-permute-start(bf16[112,1152]{1,0:T(8,128)(2,1)S(1)} %collective-permute-done.10.refs_4_), channel_id=1, source_target_pairs={{0,2},{2,0},{4,6},{6,4},{8,10},{10,8},{12,14},{14,12},{16,18},{18,... | collective-permute-start | bytes 774152 | tf_op jit(solution)/shard_map/ppermute | solution.py:23
  68.2 3.6 %shard_map.47 = (f32[512,1152]{1,0:T(8,128)S(1)}, f32[512,1152]{1,0:T(8,128)S(1)}) custom-call(bf16[512,1152]{1,0:T(8,128)(2,1)S(1)} %copy-done.1, bf16[192,1152]{1,0:T(8,128)(2,1)S(1)} %collective-permute-done.6.refs_1_, f32[512,1152]{1,0:T(8,128)S(1)} %get-tuple-element.32.refs_2_, ...), custom_call_target="tpu_custom_call", output_to_operand_aliasing={{0}: (2, {}), {1}: (6, {})} | custom-call | flops 1 | bytes 1 | tf_op jit(solution)/shard_map/pallas_call | solution.py:147
  71.8 0.1 collective-permute-start.12
  71.9 2.7 %shard_map.49 = f32[512,1152]{1,0:T(8,128)} custom-call(bf16[512,1152]{1,0:T(8,128)(2,1)S(1)} %copy-done, bf16[112,1152]{1,0:T(8,128)(2,1)S(1)} %collective-permute-done.13.refs_0_, f32[512,1152]{1,0:T(8,128)S(1)} %get-tuple-element.39.refs_1_), custom_call_target="tpu_custom_call" | custom-call | flops 1 | bytes 1 | tf_op jit(solution)/shard_map/pallas_call | solution.py:159
  74.6 2.7 %shard_map.48 = f32[512,1152]{1,0:T(8,128)} custom-call(bf16[512,1152]{1,0:T(8,128)(2,1)S(1)} %copy-done.1, bf16[112,1152]{1,0:T(8,128)(2,1)S(1)} %collective-permute-done.5.refs_0_, bf16[112,1152]{1,0:T(8,128)(2,1)S(1)} %collective-permute-done.12.refs_1_, f32[512,1152]{1,0:T(8,128)S(1)} %get-tuple-element.36.refs_2_), custom_call_target="tpu_custom_call" | custom-call | flops 1 | bytes 1 | tf_op jit(solution)/shard_map/pallas_call | solution.py:159
  (15 shorter events, 0.2 us)
Async XLA Ops:
  0.6 4.7 %copy-start = (bf16[512,1152]{1,0:T(8,128)(2,1)S(1)}, bf16[512,1152]{1,0:T(8,128)(2,1)}, u32[]{:S(2)}) copy-start(bf16[512,1152]{1,0:T(8,128)(2,1)} %rows_ref.3) | copy-start | bytes 3538948
  1.7 10.6 %collective-permute-start.1 = (bf16[144,1152]{1,0:T(8,128)(2,1)S(1)}, bf16[144,1152]{1,0:T(8,128)(2,1)S(1)}, u32[]{:S(2)}, u32[]{:S(2)}) collective-permute-start(bf16[144,1152]{1,0:T(8,128)(2,1)S(1)} %slice.21), channel_id=1, source_target_pairs={{0,28},{2,30},{4,0},{6,2},{8,4},{10,6},{12,8},{14,10},{16,12},{18,... | collective-permute-start | bytes 995336 | tf_op jit(solution)/shard_map/ppermute | solution.py:23
  2.9 51.1 %collective-permute-start.9 = (bf16[512,1152]{1,0:T(8,128)(2,1)}, bf16[512,1152]{1,0:T(8,128)(2,1)S(1)}, u32[]{:S(2)}, u32[]{:S(2)}) collective-permute-start(bf16[512,1152]{1,0:T(8,128)(2,1)} %rows_ref.2), channel_id=1, source_target_pairs={{0,26},{2,0},{4,30},{6,4},{8,2},{10,8},{12,6},{14,12},{16,10},{18,... | collective-permute-start | bytes 3538952 | tf_op jit(solution)/shard_map/ppermute | solution.py:23
  4.9 23.1 %collective-permute-start = (bf16[208,1152]{1,0:T(8,128)(2,1)S(1)}, bf16[208,1152]{1,0:T(8,128)(2,1)S(1)}, u32[]{:S(2)}, u32[]{:S(2)}) collective-permute-start(bf16[208,1152]{1,0:T(8,128)(2,1)S(1)} %slice.20), channel_id=1, source_target_pairs={{0,4},{2,6},{4,8},{6,10},{8,12},{10,14},{12,16},{14,18},{16,20},{1... | collective-permute-start | bytes 1437704 | tf_op jit(solution)/shard_map/ppermute | solution.py:23
  5.3 1.3 %copy-start.1 = (bf16[512,1152]{1,0:T(8,128)(2,1)S(1)}, bf16[512,1152]{1,0:T(8,128)(2,1)}, u32[]{:S(2)}) copy-start(bf16[512,1152]{1,0:T(8,128)(2,1)} %rows_ref.2) | copy-start | bytes 3538948
  12.3 17.9 %collective-permute-start.3 = (bf16[256,1152]{1,0:T(8,128)(2,1)S(1)}, bf16[256,1152]{1,0:T(8,128)(2,1)S(1)}, u32[]{:S(2)}, u32[]{:S(2)}) collective-permute-start(bf16[256,1152]{1,0:T(8,128)(2,1)S(1)} %slice.22), channel_id=1, source_target_pairs={{0,28},{2,30},{4,0},{6,2},{8,4},{10,6},{12,8},{14,10},{16,12},{18,... | collective-permute-start | bytes 1769480 | tf_op jit(solution)/shard_map/ppermute | solution.py:23
  12.5 45.1 %collective-permute-start.7 = (bf16[512,1152]{1,0:T(8,128)(2,1)S(1)}, bf16[512,1152]{1,0:T(8,128)(2,1)S(1)}, u32[]{:S(2)}, u32[]{:S(2)}) collective-permute-start(bf16[512,1152]{1,0:T(8,128)(2,1)S(1)} %copy-done), channel_id=1, source_target_pairs={{0,2},{2,8},{4,6},{6,12},{8,10},{10,16},{12,14},{14,20},{16,18},{1... | collective-permute-start | bytes 3538952 | tf_op jit(solution)/shard_map/ppermute | solution.py:23
  16.2 29.7 %collective-permute-start.4 = (bf16[144,1152]{1,0:T(8,128)(2,1)S(1)}, bf16[144,1152]{1,0:T(8,128)(2,1)S(1)}, u32[]{:S(2)}, u32[]{:S(2)}) collective-permute-start(bf16[144,1152]{1,0:T(8,128)(2,1)S(1)} %collective-permute-done.1.refs_1_), channel_id=1, source_target_pairs={{0,2},{2,0},{4,6},{6,4},{8,10},{10,8},{12,14},{14,12},{16,18},{18,... | collective-permute-start | bytes 995336 | tf_op jit(solution)/shard_map/ppermute | solution.py:23
  28.0 21.3 %collective-permute-start.2 = (bf16[192,1152]{1,0:T(8,128)(2,1)S(1)}, bf16[192,1152]{1,0:T(8,128)(2,1)S(1)}, u32[]{:S(2)}, u32[]{:S(2)}) collective-permute-start(bf16[192,1152]{1,0:T(8,128)(2,1)S(1)} %slice.19), channel_id=1, source_target_pairs={{0,4},{2,6},{4,8},{6,10},{8,12},{10,14},{12,16},{14,18},{16,20},{1... | collective-permute-start | bytes 1327112 | tf_op jit(solution)/shard_map/ppermute | solution.py:23
  30.2 23.7 %collective-permute-start.8 = (bf16[208,1152]{1,0:T(8,128)(2,1)S(1)}, bf16[208,1152]{1,0:T(8,128)(2,1)S(1)}, u32[]{:S(2)}, u32[]{:S(2)}) collective-permute-start(bf16[208,1152]{1,0:T(8,128)(2,1)S(1)} %collective-permute-done.refs_1_), channel_id=1, source_target_pairs={{0,2},{2,0},{4,6},{6,4},{8,10},{10,8},{12,14},{14,12},{16,18},{18,... | collective-permute-start | bytes 1437704 | tf_op jit(solution)/shard_map/ppermute | solution.py:23
  45.9 22.2 %collective-permute-start.11 = (bf16[256,1152]{1,0:T(8,128)(2,1)S(1)}, bf16[256,1152]{1,0:T(8,128)(2,1)S(1)}, u32[]{:S(2)}, u32[]{:S(2)}) collective-permute-start(bf16[256,1152]{1,0:T(8,128)(2,1)S(1)} %collective-permute-done.3.refs_1_), channel_id=1, source_target_pairs={{0,2},{2,0},{4,6},{6,4},{8,10},{10,8},{12,14},{14,12},{16,18},{18,... | collective-permute-start | bytes 1769480 | tf_op jit(solution)/shard_map/ppermute | solution.py:23
  49.4 18.8 %collective-permute-start.6 = (bf16[192,1152]{1,0:T(8,128)(2,1)S(1)}, bf16[192,1152]{1,0:T(8,128)(2,1)S(1)}, u32[]{:S(2)}, u32[]{:S(2)}) collective-permute-start(bf16[192,1152]{1,0:T(8,128)(2,1)S(1)} %collective-permute-done.2.refs_1_), channel_id=1, source_target_pairs={{0,2},{2,0},{4,6},{6,4},{8,10},{10,8},{12,14},{14,12},{16,18},{18,... | collective-permute-start | bytes 1327112 | tf_op jit(solution)/shard_map/ppermute | solution.py:23
  54.0 13.4 %collective-permute-start.10 = (bf16[112,1152]{1,0:T(8,128)(2,1)S(1)}, bf16[112,1152]{1,0:T(8,128)(2,1)S(1)}, u32[]{:S(2)}, u32[]{:S(2)}) collective-permute-start(bf16[112,1152]{1,0:T(8,128)(2,1)S(1)} %slice.23), channel_id=1, source_target_pairs={{0,28},{2,30},{4,0},{6,2},{8,4},{10,6},{12,8},{14,10},{16,12},{18,... | collective-permute-start | bytes 774152 | tf_op jit(solution)/shard_map/ppermute | solution.py:23
  54.1 17.7 %collective-permute-start.5 = (bf16[112,1152]{1,0:T(8,128)(2,1)S(1)}, bf16[112,1152]{1,0:T(8,128)(2,1)S(1)}, u32[]{:S(2)}, u32[]{:S(2)}) collective-permute-start(bf16[112,1152]{1,0:T(8,128)(2,1)S(1)} %slice.18), channel_id=1, source_target_pairs={{0,4},{2,6},{4,8},{6,10},{8,12},{10,14},{12,16},{14,18},{16,20},{1... | collective-permute-start | bytes 774152 | tf_op jit(solution)/shard_map/ppermute | solution.py:23
  67.4 4.5 %collective-permute-start.13 = (bf16[112,1152]{1,0:T(8,128)(2,1)S(1)}, bf16[112,1152]{1,0:T(8,128)(2,1)S(1)}, u32[]{:S(2)}, u32[]{:S(2)}) collective-permute-start(bf16[112,1152]{1,0:T(8,128)(2,1)S(1)} %collective-permute-done.10.refs_4_), channel_id=1, source_target_pairs={{0,2},{2,0},{4,6},{6,4},{8,10},{10,8},{12,14},{14,12},{16,18},{18,... | collective-permute-start | bytes 774152 | tf_op jit(solution)/shard_map/ppermute | solution.py:23
  71.8 2.8 %collective-permute-start.12 = (bf16[112,1152]{1,0:T(8,128)(2,1)S(1)}, bf16[112,1152]{1,0:T(8,128)(2,1)S(1)}, u32[]{:S(2)}, u32[]{:S(2)}) collective-permute-start(bf16[112,1152]{1,0:T(8,128)(2,1)S(1)} %collective-permute-done.5.refs_0_), channel_id=1, source_target_pairs={{0,2},{2,0},{4,6},{6,4},{8,10},{10,8},{12,14},{14,12},{16,18},{18,... | collective-permute-start | bytes 774152 | tf_op jit(solution)/shard_map/ppermute | solution.py:23

commit v4 on v1

v4 whole, which is shorter than its diff:
```python
import functools
import math

import jax
import jax.numpy as jnp
from jax import lax
from jax.experimental import pallas as pl
from jax.experimental.pallas import tpu as pltpu
from jax.sharding import PartitionSpec as P

AXIS = "blk"
TILE = 256
NEAR_PARTS = 2
VMEM_MIB = 32
VMEM = pl.BlockSpec(memory_space=pltpu.VMEM)
ANY = pl.BlockSpec(memory_space=pl.ANY)


def send(block, target):
    count = lax.axis_size(AXIS)
    return lax.ppermute(block, AXIS, [(i, target(i) % count) for i in range(count)])


def weights(rows, others, factor):
    inner_prod = lax.dot_general(
        rows, others, (((1,), (1,)), ((), ())), preferred_element_type=jnp.float32
    )
    return jax.nn.sigmoid(factor * inner_prod - 1.0)


def product(weight, others):
    return jnp.dot(weight.astype(jnp.bfloat16), others, preferred_element_type=jnp.float32)


def tiles(rows):
    return [pl.ds(start, TILE) for start in range(0, rows, TILE)]


def core():
    return lax.rem(lax.axis_index(AXIS), 2)


def pick_kernel(image_ref, text_ref, far_ref, near_ref, sems):
    def copy(far, near):
        copies = [
            pltpu.make_async_copy(far, far_ref, sems.at[0]),
            pltpu.make_async_copy(near, near_ref, sems.at[1]),
        ]
        for one in copies:
            one.start()
        for one in copies:
            one.wait()

    @pl.when(core() == 0)
    def _():
        copy(image_ref, text_ref)

    @pl.when(core() == 1)
    def _():
        copy(text_ref, image_ref)


def own_kernel(factor, image_ref, text_ref, near_own, *refs):
    near_parts, sums = refs[:NEAR_PARTS], refs[NEAR_PARTS]
    rows = image_ref.shape[0]
    for side, (own, others) in enumerate(((image_ref, text_ref), (text_ref, image_ref))):
        for span in tiles(rows):
            shape = (TILE, rows)
            row = lax.broadcasted_iota(jnp.int32, shape, 0) + span.start
            matched = (row == lax.broadcasted_iota(jnp.int32, shape, 1)).astype(jnp.float32)
            weight = weights(own[span], others[...], factor) - matched
            sums[side, span] = product(weight, others[...])
    side = 1 - core()
    for span in tiles(rows):
        for near_ref in near_parts:
            weight = weights(near_own[span], near_ref[...], factor)
            sums[side, span] += product(weight, near_ref[...])


def next_kernel(factor, image_ref, text_ref, texts, images, total, sums):
    for side, (own, others) in enumerate(((image_ref, texts), (text_ref, images))):
        for span in tiles(own.shape[0]):
            weight = weights(own[span], others[...], factor)
            sums[side, span] = total[side, span] + product(weight, others[...])


def last_kernel(factor, *refs):
    image_ref, text_ref, far_own, texts, images, far_ref, total = refs[:7]
    image_out, text_out, held, sems = refs[7:]
    rows = image_ref.shape[0]
    side = core()
    for span in tiles(rows):
        weight = weights(far_own[span], far_ref[...], factor)
        held[side, span] = total[side, span] + product(weight, far_ref[...])
        held[1 - side, span] = total[1 - side, span]
    copies = []
    for side, (own, others, out) in enumerate(
        ((image_ref, texts, image_out), (text_ref, images, text_out))
    ):
        for span in tiles(rows):
            weight = weights(own[span], others[...], factor)
            held[side, span] = (held[side, span] + product(weight, others[...])) * factor
            copy = pltpu.make_async_copy(held.at[side, span], out.at[span], sems.at[len(copies)])
            copy.start()
            copies.append(copy)
    for copy in copies:
        copy.wait()


def local(image_embed, text_embed):
    rows, width = image_embed.shape
    factor = 2.0 / math.sqrt(width)
    kept = pltpu.VMEM((2, rows, width), jnp.float32)
    block = pltpu.VMEM((rows, width), image_embed.dtype)
    cost = pl.CostEstimate(flops=1, bytes_accessed=1, transcendentals=0)
    params = pltpu.CompilerParams(vmem_limit_bytes=VMEM_MIB << 20)

    text_2 = send(text_embed, lambda i: i + 2)
    image_2 = send(image_embed, lambda i: i - 2)
    far_own, near_own = pl.pallas_call(
        pick_kernel,
        out_shape=(block, block),
        in_specs=[ANY, ANY],
        out_specs=(VMEM, VMEM),
        scratch_shapes=[pltpu.SemaphoreType.DMA((2,))],
        cost_estimate=cost,
        compiler_params=params,
    )(*(pltpu.with_memory_space_constraint(x, pltpu.HBM) for x in (image_embed, text_embed)))
    far = send(far_own, lambda i: i + 3 if i % 2 else i - 3)
    near = [send(part, lambda i: i ^ 1) for part in jnp.split(near_own, NEAR_PARTS)]
    sums = pl.pallas_call(
        functools.partial(own_kernel, factor),
        out_shape=kept,
        in_specs=[VMEM] * (3 + NEAR_PARTS),
        out_specs=VMEM,
        cost_estimate=cost,
        compiler_params=params,
    )(image_embed, text_embed, near_own, *near)
    text_2, image_2, sums = lax.optimization_barrier((text_2, image_2, sums))
    text_s = send(text_2, lambda i: i ^ 1)
    image_s = send(image_2, lambda i: i ^ 1)
    sums = pl.pallas_call(
        functools.partial(next_kernel, factor),
        out_shape=kept,
        in_specs=[VMEM] * 5,
        out_specs=VMEM,
        input_output_aliases={4: 0},
        cost_estimate=cost,
        compiler_params=params,
    )(image_embed, text_embed, text_2, image_2, sums)
    grad = jax.ShapeDtypeStruct((rows, width), jnp.float32)
    return pl.pallas_call(
        functools.partial(last_kernel, factor),
        out_shape=(grad, grad),
        in_specs=[VMEM] * 7,
        out_specs=(ANY, ANY),
        scratch_shapes=[
            pltpu.VMEM((2, rows, width), jnp.float32),
            pltpu.SemaphoreType.DMA((2 * rows // TILE,)),
        ],
        cost_estimate=cost,
        compiler_params=params,
    )(image_embed, text_embed, far_own, text_s, image_s, far, sums)


def solution(mesh):
    spec = P(("rep", "blk"), None)
    return jax.shard_map(
        local, mesh=mesh, in_specs=(spec, spec), out_specs=(spec, spec), check_vma=False
    )
```

time: 90.9 us -> 66 us (0.73)
  matrix products: 38.4 us -> 0 us
  Pallas kernels: 0 us -> 16.3 us
  waiting for transfers between devices: 44.2 us -> 40.9 us
  starting transfers between devices: 6.94 us -> 7.89 us
    dot_general x9 -> x0, matrix products: 38.4 us -> none  [the longest x4 18.3 us: text_term(): lax.dot_general(weight, images, (((0,), (0,)), ((), ())), preferred_eleme...]
    pallas_call x0 -> x4, Pallas kernels: none -> 16.3 us  [the longest x1 5.99 us: local(): pl.pallas_call(functools.partial(last_kernel, factor), out_shape=(grad, g...]
    ppermute x6 -> x7, waiting for transfers between devices: 44.2 us -> 40.9 us  [send(): lax.ppermute(block, AXIS, [(i, target(i) % count) for i in range(count)])]
    ppermute x6 -> x7, starting transfers between devices: 6.94 us -> 7.89 us  [send(): lax.ppermute(block, AXIS, [(i, target(i) % count) for i in range(count)])]
  transfers between devices with their start and end apart: 6 -> 7, of which waited for: 3 -> 5; matrix products, arithmetic and copies ran while one was open for 36% -> 0% of each run, Pallas kernels for 0% -> 16%
where the time goes in v4:
time: 66 us; the launch traced here: 65.9 us
  waiting for transfers between devices  40.9 us (62%)
  Pallas kernels  16.3 us (25%)
  starting transfers between devices  7.89 us (12%)
  between operations  0.7 us (1%)
    ppermute x7, waiting for transfers between devices, send(): lax.ppermute(block, AXIS, [(i, target(i) % count) for i in range(count)])  40.9 us
    ppermute x7, starting transfers between devices, send(): lax.ppermute(block, AXIS, [(i, target(i) % count) for i in range(count)])  7.89 us
    pallas_call x1, Pallas kernels, local(): pl.pallas_call(functools.partial(last_kernel, factor), out_shape=(grad, g...  5.99 us
    pallas_call x1, Pallas kernels, local(): pl.pallas_call(functools.partial(own_kernel, factor), out_shape=kept, in_...  5.1 us
    pallas_call x1, Pallas kernels, local(): pl.pallas_call(functools.partial(next_kernel, factor), out_shape=kept, in...  3.59 us
    pallas_call x1, Pallas kernels, local(): pl.pallas_call(pick_kernel, out_shape=(block, block), in_specs=[ANY, ANY]...  1.64 us
  transfers between devices with their start and end apart: 7, of which 5 were waited for; matrix products, arithmetic and copies ran while one was open for 0% of the time, Pallas kernels for 16%

profile of v4, /device:TPU:0, one launch (start us, length us, event | category | flops | bytes accessed | tf_op | source)
XLA Modules:
  0.0 65.9 jit_solution(2484992367152153479)
XLA Ops:
  0.6 6.1 %collective-permute-start.1 = (bf16[512,1152]{1,0:T(8,128)(2,1)}, bf16[512,1152]{1,0:T(8,128)(2,1)S(1)}, u32[]{:S(2)}, u32[]{:S(2)}) collective-permute-start(bf16[512,1152]{1,0:T(8,128)(2,1)} %refs_0_.1), channel_id=1, source_target_pairs={{0,28},{2,30},{4,0},{6,2},{8,4},{10,6},{12,8},{14,10},{16,12},{18,... | collective-permute-start | bytes 3538952 | tf_op jit(solution)/shard_map/ppermute | solution.py:21
  6.7 0.0 collective-permute-start
  6.7 1.6 %shard_map.41 = (bf16[512,1152]{1,0:T(8,128)(2,1)S(1)}, bf16[512,1152]{1,0:T(8,128)(2,1)S(1)}) custom-call(bf16[512,1152]{1,0:T(8,128)(2,1)} %refs_0_.1, bf16[512,1152]{1,0:T(8,128)(2,1)} %refs_1_.1), custom_call_target="tpu_custom_call" | custom-call | flops 1 | bytes 1 | tf_op jit(solution)/shard_map/pallas_call | solution.py:120
  8.3 0.0 copy-start
  8.4 0.0 copy-start.1
  8.4 0.1 fusion
  8.5 0.1 collective-permute-start.3
  8.5 0.5 collective-permute-start.2
  9.0 0.8 %collective-permute-start.6 = (bf16[512,1152]{1,0:T(8,128)(2,1)S(1)}, bf16[512,1152]{1,0:T(8,128)(2,1)S(1)}, u32[]{:S(2)}, u32[]{:S(2)}) collective-permute-start(bf16[512,1152]{1,0:T(8,128)(2,1)S(1)} %get-tuple-element.7.refs_2_), channel_id=1, source_target_pairs={{0,26},{2,8},{4,30},{6,12},{8,2},{10,16},{12,6},{14,20},{16,10},{1... | collective-permute-start | bytes 3538952 | tf_op jit(solution)/shard_map/ppermute | solution.py:21
  9.8 0.7 %collective-permute-done.3.refs_1_ = bf16[256,1152]{1,0:T(8,128)(2,1)S(1)} collective-permute-done((bf16[256,1152]{1,0:T(8,128)(2,1)S(1)}, bf16[256,1152]{1,0:T(8,128)(2,1)S(1)}, u32[]{:S(2)}, u32[]{:S(2)}) %collective-permute-start.3) | collective-permute-done | bytes 589856 | tf_op jit(solution)/shard_map/ppermute | solution.py:21
  10.5 0.8 %collective-permute-done.2.refs_0_ = bf16[256,1152]{1,0:T(8,128)(2,1)S(1)} collective-permute-done((bf16[256,1152]{1,0:T(8,128)(2,1)S(1)}, bf16[256,1152]{1,0:T(8,128)(2,1)S(1)}, u32[]{:S(2)}, u32[]{:S(2)}) %collective-permute-start.2) | collective-permute-done | bytes 589856 | tf_op jit(solution)/shard_map/ppermute | solution.py:21
  11.4 0.0 copy-done
  11.4 0.0 copy-done.1
  11.4 5.1 %shard_map.42.total = f32[2,512,1152]{2,1,0:T(8,128)S(1)} custom-call(bf16[512,1152]{1,0:T(8,128)(2,1)S(1)} %copy-done, bf16[512,1152]{1,0:T(8,128)(2,1)S(1)} %copy-done.1, bf16[512,1152]{1,0:T(8,128)(2,1)S(1)} %get-tuple-element.8.near_own, bf16[256,1152]{1,0:T(8,128)(2,1)S(1)} %collective-permute-done.2.refs_0_, ...), custom_call_target="tpu_custom_call" | custom-call | flops 1 | bytes 1 | tf_op jit(solution)/shard_map/pallas_call | solution.py:131
  16.5 38.6 %collective-permute-done.1.images = bf16[512,1152]{1,0:T(8,128)(2,1)S(1)} collective-permute-done((bf16[512,1152]{1,0:T(8,128)(2,1)}, bf16[512,1152]{1,0:T(8,128)(2,1)S(1)}, u32[]{:S(2)}, u32[]{:S(2)}) %collective-permute-start.1) | collective-permute-done | bytes 1179680 | tf_op jit(solution)/shard_map/ppermute | solution.py:21
  55.1 0.3 collective-permute-done.texts
  55.4 0.0 collective-permute-start.4
  55.4 0.5 collective-permute-start.5
  55.9 3.6 %shard_map.43.refs_6_ = f32[2,512,1152]{2,1,0:T(8,128)S(1)} custom-call(bf16[512,1152]{1,0:T(8,128)(2,1)S(1)} %copy-done, bf16[512,1152]{1,0:T(8,128)(2,1)S(1)} %copy-done.1, bf16[512,1152]{1,0:T(8,128)(2,1)S(1)} %collective-permute-done.texts, bf16[512,1152]{1,0:T(8,128)(2,1)S(1)} %collective-permute-done.1.images, ...), custom_call_target="tpu_custom_call", output_to_operand_aliasing={{}: (4, {})} | custom-call | flops 1 | bytes 1 | tf_op jit(solution)/shard_map/pallas_call | solution.py:142
  59.5 0.0 collective-permute-done.6.refs_5_
  59.5 0.0 collective-permute-done.4.refs_3_
  59.5 0.4 collective-permute-done.5.refs_4_
  59.9 6.0 %shard_map.44 = (f32[512,1152]{1,0:T(8,128)}, f32[512,1152]{1,0:T(8,128)}) custom-call(bf16[512,1152]{1,0:T(8,128)(2,1)S(1)} %copy-done, bf16[512,1152]{1,0:T(8,128)(2,1)S(1)} %copy-done.1, bf16[512,1152]{1,0:T(8,128)(2,1)S(1)} %get-tuple-element.7.refs_2_, bf16[512,1152]{1,0:T(8,128)(2,1)S(1)} %collective-permute-done.4.refs_3_, ...), custom_call_target="tpu_custom_call" | custom-call | flops 1 | bytes 1 | tf_op jit(solution)/shard_map/pallas_call | solution.py:152
Async XLA Ops:
  0.6 54.5 %collective-permute-start.1 = (bf16[512,1152]{1,0:T(8,128)(2,1)}, bf16[512,1152]{1,0:T(8,128)(2,1)S(1)}, u32[]{:S(2)}, u32[]{:S(2)}) collective-permute-start(bf16[512,1152]{1,0:T(8,128)(2,1)} %refs_0_.1), channel_id=1, source_target_pairs={{0,28},{2,30},{4,0},{6,2},{8,4},{10,6},{12,8},{14,10},{16,12},{18,... | collective-permute-start | bytes 3538952 | tf_op jit(solution)/shard_map/ppermute | solution.py:21
  6.7 48.7 %collective-permute-start = (bf16[512,1152]{1,0:T(8,128)(2,1)}, bf16[512,1152]{1,0:T(8,128)(2,1)S(1)}, u32[]{:S(2)}, u32[]{:S(2)}) collective-permute-start(bf16[512,1152]{1,0:T(8,128)(2,1)} %refs_1_.1), channel_id=1, source_target_pairs={{0,4},{2,6},{4,8},{6,10},{8,12},{10,14},{12,16},{14,18},{16,20},{1... | collective-permute-start | bytes 3538952 | tf_op jit(solution)/shard_map/ppermute | solution.py:21
  8.3 3.0 %copy-start = (bf16[512,1152]{1,0:T(8,128)(2,1)S(1)}, bf16[512,1152]{1,0:T(8,128)(2,1)}, u32[]{:S(2)}) copy-start(bf16[512,1152]{1,0:T(8,128)(2,1)} %refs_0_.1) | copy-start | bytes 3538948
  8.4 3.0 %copy-start.1 = (bf16[512,1152]{1,0:T(8,128)(2,1)S(1)}, bf16[512,1152]{1,0:T(8,128)(2,1)}, u32[]{:S(2)}) copy-start(bf16[512,1152]{1,0:T(8,128)(2,1)} %refs_1_.1) | copy-start | bytes 3538948
  8.5 2.1 %collective-permute-start.3 = (bf16[256,1152]{1,0:T(8,128)(2,1)S(1)}, bf16[256,1152]{1,0:T(8,128)(2,1)S(1)}, u32[]{:S(2)}, u32[]{:S(2)}) collective-permute-start(bf16[256,1152]{1,0:T(8,128)(2,1)S(1)} %get-tuple-element.12), channel_id=1, source_target_pairs={{0,2},{2,0},{4,6},{6,4},{8,10},{10,8},{12,14},{14,12},{16,18},{18,... | collective-permute-start | bytes 1769480 | tf_op jit(solution)/shard_map/ppermute | solution.py:21
  8.5 2.8 %collective-permute-start.2 = (bf16[256,1152]{1,0:T(8,128)(2,1)S(1)}, bf16[256,1152]{1,0:T(8,128)(2,1)S(1)}, u32[]{:S(2)}, u32[]{:S(2)}) collective-permute-start(bf16[256,1152]{1,0:T(8,128)(2,1)S(1)} %get-tuple-element.13), channel_id=1, source_target_pairs={{0,2},{2,0},{4,6},{6,4},{8,10},{10,8},{12,14},{14,12},{16,18},{18,... | collective-permute-start | bytes 1769480 | tf_op jit(solution)/shard_map/ppermute | solution.py:21
  9.0 50.4 %collective-permute-start.6 = (bf16[512,1152]{1,0:T(8,128)(2,1)S(1)}, bf16[512,1152]{1,0:T(8,128)(2,1)S(1)}, u32[]{:S(2)}, u32[]{:S(2)}) collective-permute-start(bf16[512,1152]{1,0:T(8,128)(2,1)S(1)} %get-tuple-element.7.refs_2_), channel_id=1, source_target_pairs={{0,26},{2,8},{4,30},{6,12},{8,2},{10,16},{12,6},{14,20},{16,10},{1... | collective-permute-start | bytes 3538952 | tf_op jit(solution)/shard_map/ppermute | solution.py:21
  55.4 4.1 %collective-permute-start.4 = (bf16[512,1152]{1,0:T(8,128)(2,1)S(1)}, bf16[512,1152]{1,0:T(8,128)(2,1)S(1)}, u32[]{:S(2)}, u32[]{:S(2)}) collective-permute-start(bf16[512,1152]{1,0:T(8,128)(2,1)S(1)} %collective-permute-done.texts), channel_id=1, source_target_pairs={{0,2},{2,0},{4,6},{6,4},{8,10},{10,8},{12,14},{14,12},{16,18},{18,... | collective-permute-start | bytes 3538952 | tf_op jit(solution)/shard_map/ppermute | solution.py:21
  55.4 4.5 %collective-permute-start.5 = (bf16[512,1152]{1,0:T(8,128)(2,1)S(1)}, bf16[512,1152]{1,0:T(8,128)(2,1)S(1)}, u32[]{:S(2)}, u32[]{:S(2)}) collective-permute-start(bf16[512,1152]{1,0:T(8,128)(2,1)S(1)} %collective-permute-done.1.images), channel_id=1, source_target_pairs={{0,2},{2,0},{4,6},{6,4},{8,10},{10,8},{12,14},{14,12},{16,18},{18,... | collective-permute-start | bytes 3538952 | tf_op jit(solution)/shard_map/ppermute | solution.py:21

commit v5 on v1

v5 whole, which is shorter than its diff:
```python
import functools
import math

import jax
import jax.numpy as jnp
from jax import lax
from jax.experimental import pallas as pl
from jax.experimental.pallas import tpu as pltpu
from jax.sharding import PartitionSpec as P

AXIS = "blk"
TILE = 256
NEAR_PARTS = 2
SWAP_PARTS = 2
VMEM_MIB = 32
VMEM = pl.BlockSpec(memory_space=pltpu.VMEM)
ANY = pl.BlockSpec(memory_space=pl.ANY)
LOG2_E = math.log2(math.e)


def send(block, target):
    count = lax.axis_size(AXIS)
    return lax.ppermute(block, AXIS, [(i, target(i) % count) for i in range(count)])


def swap(block):
    return [send(part, lambda i: i ^ 1) for part in jnp.split(block, SWAP_PARTS)]


def core():
    return lax.rem(lax.axis_index(AXIS), 2)


def tiles(rows):
    return [pl.ds(start, TILE) for start in range(0, rows, TILE)]


def logits(own, span, others):
    return lax.dot_general(
        own[span], others[...], (((1,), (1,)), ((), ())), preferred_element_type=jnp.float32
    )


def grow(factor, inner_prod):
    return jnp.exp2(LOG2_E - (factor * LOG2_E) * inner_prod)


def product(weight, others):
    return jnp.dot(weight.astype(jnp.bfloat16), others[...], preferred_element_type=jnp.float32)


def add_all(factor, units):
    following = logits(*units[0][:3])
    for k, (_, span, others, use) in enumerate(units):
        inner_prod = following
        if k + 1 < len(units):
            following = logits(*units[k + 1][:3])
        weight = pl.reciprocal(1.0 + grow(factor, inner_prod), approx=True)
        use(span, product(weight, others))


def join(visitors, joined):
    start = 0
    for visitor in visitors:
        joined[pl.ds(start, visitor.shape[0])] = visitor[...]
        start += visitor.shape[0]
    return joined


def pick_kernel(image_ref, text_ref, *refs):
    sides, sems = refs[:2], refs[2]

    def copy(*sources):
        copies = [
            pltpu.make_async_copy(source, side, sems.at[k])
            for k, (source, side) in enumerate(zip(sources, sides))
        ]
        for one in copies:
            one.start()
        for one in copies:
            one.wait()

    @pl.when(core() == 0)
    def _():
        copy(image_ref, text_ref)

    @pl.when(core() == 1)
    def _():
        copy(text_ref, image_ref)


def own_kernel(factor, side_0, side_1, *refs):
    near, (sum_0, sum_1, joined) = refs[:NEAR_PARTS], refs[NEAR_PARTS:]
    rows = side_0.shape[0]
    for own, others, total in ((side_0, side_1, sum_0), (side_1, side_0, sum_1)):
        for span in tiles(rows):
            shape = (TILE, rows)
            row = lax.broadcasted_iota(jnp.int32, shape, 0) + span.start
            matched = (row == lax.broadcasted_iota(jnp.int32, shape, 1)).astype(jnp.float32)
            weight = 1.0 / (1.0 + grow(factor, logits(own, span, others))) - matched
            total[span] = product(weight, others)

    def use(span, value):
        sum_1[span] += value

    others = join(near, joined)
    add_all(factor, [(side_1, span, others, use) for span in tiles(rows)])


def both_kernel(factor, side_0, side_1, visitor_0, *refs):
    visitors_1, (total_0, total_1, sum_0, sum_1, joined) = refs[:SWAP_PARTS], refs[SWAP_PARTS:]

    def use_0(span, value):
        sum_0[span] = total_0[span] + value

    def use_1(span, value):
        sum_1[span] = total_1[span] + value

    spans = tiles(side_0.shape[0])
    units = [(side_0, span, visitor_0, use_0) for span in spans]
    visitor_1 = join(visitors_1, joined)
    units += [(side_1, span, visitor_1, use_1) for span in spans]
    add_all(factor, units)


def one_kernel(factor, scale, own, visitor, total, out):
    def use(span, value):
        out[span] = (total[span] + value) * scale

    add_all(factor, [(own, span, visitor, use) for span in tiles(own.shape[0])])


def last_kernel(factor, side_0, *refs):
    visitors, refs = refs[:SWAP_PARTS], refs[SWAP_PARTS:]
    total, grad_1, image_out, text_out, held, joined, sems = refs
    spans = tiles(side_0.shape[0])

    def move(k, is_core):
        outs = (text_out, image_out) if is_core else (image_out, text_out)
        if k == len(spans):
            return pltpu.make_async_copy(grad_1, outs[1], sems.at[k])
        return pltpu.make_async_copy(held.at[spans[k]], outs[0].at[spans[k]], sems.at[k])

    def each(which, act):
        for is_core in (0, 1):

            @pl.when(core() == is_core)
            def _():
                for k in which:
                    act(move(k, is_core))

    def use(span, value):
        held[span] = (total[span] + value) * factor
        each((span.start // TILE,), lambda copy: copy.start())

    each((len(spans),), lambda copy: copy.start())
    visitor = join(visitors, joined)
    add_all(factor, [(side_0, span, visitor, use) for span in spans])
    each(range(len(spans) + 1), lambda copy: copy.wait())


def local(image_embed, text_embed):
    rows, width = image_embed.shape
    factor = 2.0 / math.sqrt(width)
    kept = pltpu.VMEM((rows, width), jnp.float32)
    block = pltpu.VMEM((rows, width), image_embed.dtype)
    grad = jax.ShapeDtypeStruct((rows, width), jnp.float32)

    def call(kernel, outs, operands, scratch=(), aliases=None, in_spec=VMEM, flops=1):
        spec = ANY if outs[0] is grad else VMEM
        return pl.pallas_call(
            kernel,
            out_shape=tuple(outs),
            in_specs=[in_spec] * len(operands),
            out_specs=(spec,) * len(outs),
            scratch_shapes=list(scratch),
            input_output_aliases=aliases or {},
            cost_estimate=pl.CostEstimate(flops=flops, bytes_accessed=1, transcendentals=0),
            compiler_params=pltpu.CompilerParams(vmem_limit_bytes=VMEM_MIB << 20),
        )(*operands)

    side_0, side_1 = call(
        pick_kernel,
        (block, block),
        [pltpu.with_memory_space_constraint(x, pltpu.HBM) for x in (image_embed, text_embed)],
        [pltpu.SemaphoreType.DMA((2,))],
        in_spec=ANY,
    )
    near = swap(side_1)
    ahead = send(side_1, lambda i: i - 2 if i % 2 else i + 2)
    far = send(side_0, lambda i: i + 3 if i % 2 else i - 3)
    sum_0, sum_1 = call(
        functools.partial(own_kernel, factor), (kept, kept), (side_0, side_1, *near), [block]
    )
    later, sum_0, sum_1 = lax.optimization_barrier((side_0, sum_0, sum_1))
    behind = send(later, lambda i: i + 2 if i % 2 else i - 2)

    ahead, sum_0, sum_1 = lax.optimization_barrier((ahead, sum_0, sum_1))
    sum_0, sum_1 = call(
        functools.partial(both_kernel, factor),
        (kept, kept),
        (side_0, side_1, ahead, *swap(ahead), sum_0, sum_1),
        [block],
        {3 + SWAP_PARTS: 0, 4 + SWAP_PARTS: 1},
    )
    far, sum_0 = lax.optimization_barrier((far, sum_0))
    (sum_0,) = call(
        functools.partial(one_kernel, factor, 1.0),
        (kept,),
        (side_0, far, sum_0),
        aliases={2: 0},
        flops=1 << 30,
    )
    behind, sum_0 = lax.optimization_barrier((behind, sum_0))
    (grad_1,) = call(
        functools.partial(one_kernel, factor, factor),
        (kept,),
        (side_1, behind, sum_1),
        aliases={2: 0},
    )
    return call(
        functools.partial(last_kernel, factor),
        (grad, grad),
        (side_0, *swap(behind), sum_0, grad_1),
        [kept, block, pltpu.SemaphoreType.DMA((rows // TILE + 1,))],
    )


def solution(mesh):
    spec = P(("rep", "blk"), None)
    return jax.shard_map(
        local, mesh=mesh, in_specs=(spec, spec), out_specs=(spec, spec), check_vma=False
    )
```

time: 90.9 us -> 66.1 us (0.73)
  matrix products: 38.4 us -> 0 us
  Pallas kernels: 0 us -> 16.6 us
  waiting for transfers between devices: 44.2 us -> 39 us
  starting transfers between devices: 6.94 us -> 9.37 us
    dot_general x9 -> x0, matrix products: 38.4 us -> none  [the longest x4 18.3 us: text_term(): lax.dot_general(weight, images, (((0,), (0,)), ((), ())), preferred_eleme...]
    pallas_call x0 -> x6, Pallas kernels: none -> 16.6 us  [call(): pl.pallas_call(kernel, out_shape=tuple(outs), in_specs=[in_spec] * len(op...]
    ppermute x6 -> x9, waiting for transfers between devices: 44.2 us -> 39 us  [send(): lax.ppermute(block, AXIS, [(i, target(i) % count) for i in range(count)])]
    ppermute x6 -> x9, starting transfers between devices: 6.94 us -> 9.37 us  [send(): lax.ppermute(block, AXIS, [(i, target(i) % count) for i in range(count)])]
  transfers between devices with their start and end apart: 6 -> 9, of which waited for: 3 -> 7; matrix products, arithmetic and copies ran while one was open for 36% -> 0% of each run, Pallas kernels for 0% -> 18%
where the time goes in v5:
time: 66.1 us; the launch traced here: 65.9 us
  waiting for transfers between devices  39 us (59%)
  Pallas kernels  16.6 us (25%)
  starting transfers between devices  9.37 us (14%)
  between operations  0.7 us (1%)
    ppermute x9, waiting for transfers between devices, send(): lax.ppermute(block, AXIS, [(i, target(i) % count) for i in range(count)])  39 us
    pallas_call x6, Pallas kernels, call(): pl.pallas_call(kernel, out_shape=tuple(outs), in_specs=[in_spec] * len(op...  16.6 us
    ppermute x9, starting transfers between devices, send(): lax.ppermute(block, AXIS, [(i, target(i) % count) for i in range(count)])  9.37 us
  transfers between devices with their start and end apart: 9, of which 7 were waited for; matrix products, arithmetic and copies ran while one was open for 0% of the time, Pallas kernels for 18%

profile of v5, /device:TPU:0, one launch (start us, length us, event | category | flops | bytes accessed | tf_op | source)
XLA Modules:
  0.0 65.9 jit_solution(1919943837805129150)
XLA Ops:
  0.6 1.7 %shard_map.41 = (bf16[512,1152]{1,0:T(8,128)(2,1)S(1)}, bf16[512,1152]{1,0:T(8,128)(2,1)S(1)}) custom-call(bf16[512,1152]{1,0:T(8,128)(2,1)} %image_ref.1, bf16[512,1152]{1,0:T(8,128)(2,1)} %text_ref.1), custom_call_target="tpu_custom_call" | custom-call | flops 1 | bytes 1 | tf_op jit(solution)/shard_map/pallas_call | solution.py:171
  2.3 3.0 %collective-permute-start.4 = (bf16[512,1152]{1,0:T(8,128)(2,1)S(1)}, bf16[512,1152]{1,0:T(8,128)(2,1)S(1)}, u32[]{:S(2)}, u32[]{:S(2)}) collective-permute-start(bf16[512,1152]{1,0:T(8,128)(2,1)S(1)} %get-tuple-element.19.side_1.own), channel_id=1, source_target_pairs={{0,4},{2,30},{4,8},{6,2},{8,12},{10,6},{12,16},{14,10},{16,20},{18... | collective-permute-start | bytes 3538952 | tf_op jit(solution)/shard_map/ppermute | solution.py:23
  5.3 0.1 fusion.2
  5.4 2.7 %collective-permute-start = (bf16[256,1152]{1,0:T(8,128)(2,1)S(1)}, bf16[256,1152]{1,0:T(8,128)(2,1)S(1)}, u32[]{:S(2)}, u32[]{:S(2)}) collective-permute-start(bf16[256,1152]{1,0:T(8,128)(2,1)S(1)} %get-tuple-element.39), channel_id=1, source_target_pairs={{0,2},{2,0},{4,6},{6,4},{8,10},{10,8},{12,14},{14,12},{16,18},{18,... | collective-permute-start | bytes 1769480 | tf_op jit(solution)/shard_map/ppermute | solution.py:23
  8.1 0.1 collective-permute-start.1
  8.1 1.1 %collective-permute-start.3 = (bf16[512,1152]{1,0:T(8,128)(2,1)S(1)}, bf16[512,1152]{1,0:T(8,128)(2,1)S(1)}, u32[]{:S(2)}, u32[]{:S(2)}) collective-permute-start(bf16[512,1152]{1,0:T(8,128)(2,1)S(1)} %get-tuple-element.22.side_0.own), channel_id=1, source_target_pairs={{0,26},{2,8},{4,30},{6,12},{8,2},{10,16},{12,6},{14,20},{16,10},{1... | collective-permute-start | bytes 3538952 | tf_op jit(solution)/shard_map/ppermute | solution.py:23
  9.3 0.4 collective-permute-done.refs_0_
  9.7 0.8 %collective-permute-done.1.refs_1_ = bf16[256,1152]{1,0:T(8,128)(2,1)S(1)} collective-permute-done((bf16[256,1152]{1,0:T(8,128)(2,1)S(1)}, bf16[256,1152]{1,0:T(8,128)(2,1)S(1)}, u32[]{:S(2)}, u32[]{:S(2)}) %collective-permute-start.1) | collective-permute-done | bytes 589856 | tf_op jit(solution)/shard_map/ppermute | solution.py:23
  10.5 4.9 %shard_map.42 = (f32[512,1152]{1,0:T(8,128)S(1)}, f32[512,1152]{1,0:T(8,128)S(1)}) custom-call(bf16[512,1152]{1,0:T(8,128)(2,1)S(1)} %get-tuple-element.22.side_0.own, bf16[512,1152]{1,0:T(8,128)(2,1)S(1)} %get-tuple-element.19.side_1.own, bf16[256,1152]{1,0:T(8,128)(2,1)S(1)} %collective-permute-done.refs_0_, ...), custom_call_target="tpu_custom_call" | custom-call | flops 1 | bytes 1 | tf_op jit(solution)/shard_map/pallas_call | solution.py:171
  15.5 0.9 %collective-permute-start.2 = (bf16[512,1152]{1,0:T(8,128)(2,1)S(1)}, bf16[512,1152]{1,0:T(8,128)(2,1)S(1)}, u32[]{:S(2)}, u32[]{:S(2)}) collective-permute-start(bf16[512,1152]{1,0:T(8,128)(2,1)S(1)} %get-tuple-element.22.side_0.own), channel_id=1, source_target_pairs={{0,28},{2,6},{4,0},{6,10},{8,4},{10,14},{12,8},{14,18},{16,12},{18... | collective-permute-start | bytes 3538952 | tf_op jit(solution)/shard_map/ppermute | solution.py:23
  16.3 34.1 %collective-permute-done.4.visitor_0 = bf16[512,1152]{1,0:T(8,128)(2,1)S(1)} collective-permute-done((bf16[512,1152]{1,0:T(8,128)(2,1)S(1)}, bf16[512,1152]{1,0:T(8,128)(2,1)S(1)}, u32[]{:S(2)}, u32[]{:S(2)}) %collective-permute-start.4) | collective-permute-done | bytes 1179680 | tf_op jit(solution)/shard_map/ppermute | solution.py:23
  50.4 0.1 fusion.1
  50.5 0.1 collective-permute-start.5
  50.6 0.5 collective-permute-start.6
  51.1 1.5 %collective-permute-done.5.refs_0_ = bf16[256,1152]{1,0:T(8,128)(2,1)S(1)} collective-permute-done((bf16[256,1152]{1,0:T(8,128)(2,1)S(1)}, bf16[256,1152]{1,0:T(8,128)(2,1)S(1)}, u32[]{:S(2)}, u32[]{:S(2)}) %collective-permute-start.5) | collective-permute-done | bytes 589856 | tf_op jit(solution)/shard_map/ppermute | solution.py:23
  52.6 0.8 %collective-permute-done.6.refs_1_ = bf16[256,1152]{1,0:T(8,128)(2,1)S(1)} collective-permute-done((bf16[256,1152]{1,0:T(8,128)(2,1)S(1)}, bf16[256,1152]{1,0:T(8,128)(2,1)S(1)}, u32[]{:S(2)}, u32[]{:S(2)}) %collective-permute-start.6) | collective-permute-done | bytes 589856 | tf_op jit(solution)/shard_map/ppermute | solution.py:23
  53.4 3.4 %shard_map.43 = (f32[512,1152]{1,0:T(8,128)S(1)}, f32[512,1152]{1,0:T(8,128)S(1)}) custom-call(bf16[512,1152]{1,0:T(8,128)(2,1)S(1)} %get-tuple-element.22.side_0.own, bf16[512,1152]{1,0:T(8,128)(2,1)S(1)} %get-tuple-element.19.side_1.own, bf16[512,1152]{1,0:T(8,128)(2,1)S(1)} %collective-permute-done.4.visitor_0, ...), custom_call_target="tpu_custom_call", output_to_operand_aliasing={{0}: (5, {}), {1}: (6, {})} | custom-call | flops 1 | bytes 1 | tf_op jit(solution)/shard_map/pallas_call | solution.py:171
  56.8 0.9 %collective-permute-done.3.visitor = bf16[512,1152]{1,0:T(8,128)(2,1)S(1)} collective-permute-done((bf16[512,1152]{1,0:T(8,128)(2,1)S(1)}, bf16[512,1152]{1,0:T(8,128)(2,1)S(1)}, u32[]{:S(2)}, u32[]{:S(2)}) %collective-permute-start.3) | collective-permute-done | bytes 1179680 | tf_op jit(solution)/shard_map/ppermute | solution.py:23
  57.7 1.7 %shard_map.44.refs_2_ = f32[512,1152]{1,0:T(8,128)S(1)} custom-call(bf16[512,1152]{1,0:T(8,128)(2,1)S(1)} %get-tuple-element.22.side_0.own, bf16[512,1152]{1,0:T(8,128)(2,1)S(1)} %collective-permute-done.3.visitor, f32[512,1152]{1,0:T(8,128)S(1)} %get-tuple-element.30.total), custom_call_target="tpu_custom_call", output_to_operand_aliasing={{}: (2, {})} | custom-call | flops 1073741824 | bytes 1 | tf_op jit(solution)/shard_map/pallas_call | solution.py:171
  59.4 0.0 collective-permute-done.2.visitor
  59.4 0.1 fusion
  59.5 1.0 %collective-permute-start.7 = (bf16[256,1152]{1,0:T(8,128)(2,1)S(1)}, bf16[256,1152]{1,0:T(8,128)(2,1)S(1)}, u32[]{:S(2)}, u32[]{:S(2)}) collective-permute-start(bf16[256,1152]{1,0:T(8,128)(2,1)S(1)} %get-tuple-element.35), channel_id=1, source_target_pairs={{0,2},{2,0},{4,6},{6,4},{8,10},{10,8},{12,14},{14,12},{16,18},{18,... | collective-permute-start | bytes 1769480 | tf_op jit(solution)/shard_map/ppermute | solution.py:23
  60.5 0.1 collective-permute-start.8
  60.6 1.9 %shard_map.45.refs_3_ = f32[512,1152]{1,0:T(8,128)S(1)} custom-call(bf16[512,1152]{1,0:T(8,128)(2,1)S(1)} %get-tuple-element.19.side_1.own, bf16[512,1152]{1,0:T(8,128)(2,1)S(1)} %collective-permute-done.2.visitor, f32[512,1152]{1,0:T(8,128)S(1)} %get-tuple-element.33.total), custom_call_target="tpu_custom_call", output_to_operand_aliasing={{}: (2, {})} | custom-call | flops 1 | bytes 1 | tf_op jit(solution)/shard_map/pallas_call | solution.py:171
  62.5 0.0 collective-permute-done.7.refs_0_
  62.5 0.4 collective-permute-done.8.refs_1_
  63.0 3.0 %shard_map.46 = (f32[512,1152]{1,0:T(8,128)}, f32[512,1152]{1,0:T(8,128)}) custom-call(bf16[512,1152]{1,0:T(8,128)(2,1)S(1)} %get-tuple-element.22.side_0.own, bf16[256,1152]{1,0:T(8,128)(2,1)S(1)} %collective-permute-done.7.refs_0_, bf16[256,1152]{1,0:T(8,128)(2,1)S(1)} %collective-permute-done.8.refs_1_, f32[512,1152]{1,0:T(8,128)S(1)} %shard_map.44.refs_2_, ...), custom_call_target="tpu_custom_call" | custom-call | flops 1 | bytes 1 | tf_op jit(solution)/shard_map/pallas_call | solution.py:171
Async XLA Ops:
  2.3 48.1 %collective-permute-start.4 = (bf16[512,1152]{1,0:T(8,128)(2,1)S(1)}, bf16[512,1152]{1,0:T(8,128)(2,1)S(1)}, u32[]{:S(2)}, u32[]{:S(2)}) collective-permute-start(bf16[512,1152]{1,0:T(8,128)(2,1)S(1)} %get-tuple-element.19.side_1.own), channel_id=1, source_target_pairs={{0,4},{2,30},{4,8},{6,2},{8,12},{10,6},{12,16},{14,10},{16,20},{18... | collective-permute-start | bytes 3538952 | tf_op jit(solution)/shard_map/ppermute | solution.py:23
  5.4 4.3 %collective-permute-start = (bf16[256,1152]{1,0:T(8,128)(2,1)S(1)}, bf16[256,1152]{1,0:T(8,128)(2,1)S(1)}, u32[]{:S(2)}, u32[]{:S(2)}) collective-permute-start(bf16[256,1152]{1,0:T(8,128)(2,1)S(1)} %get-tuple-element.39), channel_id=1, source_target_pairs={{0,2},{2,0},{4,6},{6,4},{8,10},{10,8},{12,14},{14,12},{16,18},{18,... | collective-permute-start | bytes 1769480 | tf_op jit(solution)/shard_map/ppermute | solution.py:23
  8.1 2.5 %collective-permute-start.1 = (bf16[256,1152]{1,0:T(8,128)(2,1)S(1)}, bf16[256,1152]{1,0:T(8,128)(2,1)S(1)}, u32[]{:S(2)}, u32[]{:S(2)}) collective-permute-start(bf16[256,1152]{1,0:T(8,128)(2,1)S(1)} %get-tuple-element.38), channel_id=1, source_target_pairs={{0,2},{2,0},{4,6},{6,4},{8,10},{10,8},{12,14},{14,12},{16,18},{18,... | collective-permute-start | bytes 1769480 | tf_op jit(solution)/shard_map/ppermute | solution.py:23
  8.1 49.6 %collective-permute-start.3 = (bf16[512,1152]{1,0:T(8,128)(2,1)S(1)}, bf16[512,1152]{1,0:T(8,128)(2,1)S(1)}, u32[]{:S(2)}, u32[]{:S(2)}) collective-permute-start(bf16[512,1152]{1,0:T(8,128)(2,1)S(1)} %get-tuple-element.22.side_0.own), channel_id=1, source_target_pairs={{0,26},{2,8},{4,30},{6,12},{8,2},{10,16},{12,6},{14,20},{16,10},{1... | collective-permute-start | bytes 3538952 | tf_op jit(solution)/shard_map/ppermute | solution.py:23
  15.5 44.0 %collective-permute-start.2 = (bf16[512,1152]{1,0:T(8,128)(2,1)S(1)}, bf16[512,1152]{1,0:T(8,128)(2,1)S(1)}, u32[]{:S(2)}, u32[]{:S(2)}) collective-permute-start(bf16[512,1152]{1,0:T(8,128)(2,1)S(1)} %get-tuple-element.22.side_0.own), channel_id=1, source_target_pairs={{0,28},{2,6},{4,0},{6,10},{8,4},{10,14},{12,8},{14,18},{16,12},{18... | collective-permute-start | bytes 3538952 | tf_op jit(solution)/shard_map/ppermute | solution.py:23
  50.5 2.1 %collective-permute-start.5 = (bf16[256,1152]{1,0:T(8,128)(2,1)S(1)}, bf16[256,1152]{1,0:T(8,128)(2,1)S(1)}, u32[]{:S(2)}, u32[]{:S(2)}) collective-permute-start(bf16[256,1152]{1,0:T(8,128)(2,1)S(1)} %get-tuple-element.37), channel_id=1, source_target_pairs={{0,2},{2,0},{4,6},{6,4},{8,10},{10,8},{12,14},{14,12},{16,18},{18,... | collective-permute-start | bytes 1769480 | tf_op jit(solution)/shard_map/ppermute | solution.py:23
  50.6 2.8 %collective-permute-start.6 = (bf16[256,1152]{1,0:T(8,128)(2,1)S(1)}, bf16[256,1152]{1,0:T(8,128)(2,1)S(1)}, u32[]{:S(2)}, u32[]{:S(2)}) collective-permute-start(bf16[256,1152]{1,0:T(8,128)(2,1)S(1)} %get-tuple-element.36), channel_id=1, source_target_pairs={{0,2},{2,0},{4,6},{6,4},{8,10},{10,8},{12,14},{14,12},{16,18},{18,... | collective-permute-start | bytes 1769480 | tf_op jit(solution)/shard_map/ppermute | solution.py:23
  59.5 3.0 %collective-permute-start.7 = (bf16[256,1152]{1,0:T(8,128)(2,1)S(1)}, bf16[256,1152]{1,0:T(8,128)(2,1)S(1)}, u32[]{:S(2)}, u32[]{:S(2)}) collective-permute-start(bf16[256,1152]{1,0:T(8,128)(2,1)S(1)} %get-tuple-element.35), channel_id=1, source_target_pairs={{0,2},{2,0},{4,6},{6,4},{8,10},{10,8},{12,14},{14,12},{16,18},{18,... | collective-permute-start | bytes 1769480 | tf_op jit(solution)/shard_map/ppermute | solution.py:23
  60.5 2.5 %collective-permute-start.8 = (bf16[256,1152]{1,0:T(8,128)(2,1)S(1)}, bf16[256,1152]{1,0:T(8,128)(2,1)S(1)}, u32[]{:S(2)}, u32[]{:S(2)}) collective-permute-start(bf16[256,1152]{1,0:T(8,128)(2,1)S(1)} %get-tuple-element.34), channel_id=1, source_target_pairs={{0,2},{2,0},{4,6},{6,4},{8,10},{10,8},{12,14},{14,12},{16,18},{18,... | collective-permute-start | bytes 1769480 | tf_op jit(solution)/shard_map/ppermute | solution.py:23

commit v6 on v1

v6 whole, which is shorter than its diff:
```python
import functools
import math

import jax
import jax.numpy as jnp
from jax import lax
from jax.experimental import pallas as pl
from jax.experimental.pallas import tpu as pltpu
from jax.sharding import PartitionSpec as P

AXIS = "blk"
TEXT_PARTS = 2
SWAP_PARTS = 4
NEAR_PARTS = 1
LAST_TILE = 256
COPY_ROWS = 128
VMEM_MIB = 32
VMEM = pl.BlockSpec(memory_space=pltpu.VMEM)
ANY = pl.BlockSpec(memory_space=pl.ANY)
LOG2_E = math.log2(math.e)


def send(block, target):
    count = lax.axis_size(AXIS)
    return lax.ppermute(block, AXIS, [(i, target(i) % count) for i in range(count)])


def swap(block, parts):
    return [send(part, lambda i: i ^ 1) for part in jnp.split(block, parts)]


def core():
    return lax.rem(lax.axis_index(AXIS), 2)


def logits(own, others):
    return lax.dot_general(
        own[...], others[...], (((1,), (1,)), ((), ())), preferred_element_type=jnp.float32
    )


def decay(factor, inner_prod):
    return jnp.exp2(LOG2_E - (factor * LOG2_E) * inner_prod)


def product(weight, others):
    return jnp.dot(weight.astype(jnp.bfloat16), others[...], preferred_element_type=jnp.float32)


def add_all(factor, units):
    following = logits(*units[0][:2])
    for k, (_, others, use) in enumerate(units):
        inner_prod = following
        if k + 1 < len(units):
            following = logits(*units[k + 1][:2])
        weight = pl.reciprocal(1.0 + decay(factor, inner_prod), approx=True)
        use(product(weight, others))


def join(visitors, joined):
    start = 0
    for visitor in visitors:
        joined[pl.ds(start, visitor.shape[0])] = visitor[...]
        start += visitor.shape[0]
    return joined


def pick_kernel(image_ref, text_ref, *refs):
    parts, (far_own, near_own, sems) = refs[:TEXT_PARTS], refs[TEXT_PARTS:]
    rows = parts[0].shape[0]
    for is_core, (far, near) in enumerate(((image_ref, text_ref), (text_ref, image_ref))):

        @pl.when(core() == is_core)
        def _():
            moves = [(text_ref.at[pl.ds(k * rows, rows)], part) for k, part in enumerate(parts)]
            moves += [(far, far_own), (near, near_own)]
            copies = [pltpu.make_async_copy(*move, sems.at[k]) for k, move in enumerate(moves)]
            for copy in copies:
                copy.start()
            for copy in copies:
                copy.wait()


def own_kernel(factor, image_ref, text_ref, image_sum, text_sum):
    rows = image_ref.shape[0]
    shape = (rows, rows)
    matched = lax.broadcasted_iota(jnp.int32, shape, 0) == lax.broadcasted_iota(
        jnp.int32, shape, 1
    )
    for own, others, total in ((image_ref, text_ref, image_sum), (text_ref, image_ref, text_sum)):
        chance = 1.0 / (1.0 + decay(factor, logits(own, others)))
        total[...] = product(chance - matched.astype(jnp.float32), others)


def text_kernel(factor, image_ref, near_own, *refs):
    near, refs = refs[:NEAR_PARTS], refs[NEAR_PARTS:]
    texts, refs = refs[:TEXT_PARTS], refs[TEXT_PARTS:]
    swapped, refs = refs[:SWAP_PARTS], refs[SWAP_PARTS:]
    image_total, text_total, image_sum, text_sum, *joined = refs
    is_1 = core().astype(jnp.float32)

    def use_near(value):
        image_sum[...] = image_total[...] + value * is_1
        text_sum[...] = text_total[...] + value * (1.0 - is_1)

    def use(value):
        image_sum[...] += value

    units = [(near_own, join(near, joined[0]), use_near)]
    units.append((image_ref, join(texts, joined[1]), use))
    units.append((image_ref, join(swapped, joined[2]), use))
    add_all(factor, units)


def image_kernel(factor, text_ref, images, text_total, text_sum):
    def use(value):
        text_sum[...] = text_total[...] + value

    add_all(factor, [(text_ref, images, use)])


def last_kernel(factor, text_ref, far_own, far, *refs):
    swapped, refs = refs[:SWAP_PARTS], refs[SWAP_PARTS:]
    image_total, text_total, image_out, text_out, image_held, text_held, joined, sems = refs
    rows = text_ref.shape[0]
    is_1 = core().astype(jnp.float32)
    copies = []

    def leave(held, out, start):
        for first in range(start, start + LAST_TILE, COPY_ROWS):
            span = pl.ds(first, COPY_ROWS)
            copies.append(pltpu.make_async_copy(held.at[span], out.at[span], sems.at[len(copies)]))
            copies[-1].start()

    def use_far(start):
        span = pl.ds(start, LAST_TILE)

        def use(value):
            image_held[span] = (image_total[span] + value * (1.0 - is_1)) * factor
            leave(image_held, image_out, start)
            text_held[span] = text_total[span] + value * is_1

        return (far_own.at[span], far, use)

    def use_swapped(start):
        span = pl.ds(start, LAST_TILE)

        def use(value):
            text_held[span] = (text_held[span] + value) * factor
            leave(text_held, text_out, start)

        return (text_ref.at[span], joined, use)

    join(swapped, joined)
    starts = range(0, rows, LAST_TILE)
    add_all(factor, [use_far(start) for start in starts] + [use_swapped(start) for start in starts])
    for copy in copies:
        copy.wait()


def local(image_embed, text_embed):
    rows, width = image_embed.shape
    factor = 2.0 / math.sqrt(width)
    kept = pltpu.VMEM((rows, width), jnp.float32)
    block = pltpu.VMEM((rows, width), image_embed.dtype)
    part = pltpu.VMEM((rows // TEXT_PARTS, width), image_embed.dtype)
    grad = jax.ShapeDtypeStruct((rows, width), jnp.float32)

    def call(kernel, outs, operands, scratch=(), aliases=None, in_spec=VMEM):
        return pl.pallas_call(
            kernel,
            out_shape=tuple(outs),
            in_specs=[in_spec] * len(operands),
            out_specs=(ANY if outs[0] is grad else VMEM,) * len(outs),
            scratch_shapes=list(scratch),
            input_output_aliases=aliases or {},
            cost_estimate=pl.CostEstimate(flops=1, bytes_accessed=1, transcendentals=0),
            compiler_params=pltpu.CompilerParams(vmem_limit_bytes=VMEM_MIB << 20),
        )(*operands)

    def after(values, earlier):
        out = lax.optimization_barrier((*values, *earlier))
        return out[: len(values)], out[len(values) :]

    *text_parts, far_own, near_own = call(
        pick_kernel,
        [part] * TEXT_PARTS + [block, block],
        [pltpu.with_memory_space_constraint(x, pltpu.HBM) for x in (image_embed, text_embed)],
        [pltpu.SemaphoreType.DMA((TEXT_PARTS + 2,))],
        in_spec=ANY,
    )
    texts = [send(piece, lambda i: i + 2) for piece in text_parts]
    images = send(image_embed, lambda i: i - 2)
    far = send(far_own, lambda i: i + 3 if i % 2 else i - 3)
    sums = call(functools.partial(own_kernel, factor), (kept, kept), (image_embed, text_embed))

    texts, sums = after(texts, sums)
    swapped = [part for text in texts for part in swap(text, SWAP_PARTS // TEXT_PARTS)]
    near = swap(near_own, NEAR_PARTS)
    count = 2 + NEAR_PARTS + TEXT_PARTS + SWAP_PARTS
    sums = call(
        functools.partial(text_kernel, factor),
        (kept, kept),
        (image_embed, near_own, *near, *texts, *swapped, *sums),
        [block] * 3,
        {count: 0, count + 1: 1},
    )
    (images,), (image_sum, text_sum) = after((images,), sums)
    swapped = swap(images, SWAP_PARTS)
    (text_sum,) = call(
        functools.partial(image_kernel, factor), (kept,), (text_embed, images, text_sum), (), {2: 0}
    )
    return call(
        functools.partial(last_kernel, factor),
        (grad, grad),
        (text_embed, far_own, far, *swapped, image_sum, text_sum),
        [kept, kept, block, pltpu.SemaphoreType.DMA((2 * rows // COPY_ROWS,))],
    )


def solution(mesh):
    spec = P(("rep", "blk"), None)
    return jax.shard_map(
        local, mesh=mesh, in_specs=(spec, spec), out_specs=(spec, spec), check_vma=False
    )
```

time: 90.9 us -> 72.8 us (0.80)
  matrix products: 38.4 us -> 0 us
  Pallas kernels: 0 us -> 16.5 us
  starting transfers between devices: 6.94 us -> 11.6 us
    dot_general x9 -> x0, matrix products: 38.4 us -> none  [the longest x4 18.3 us: text_term(): lax.dot_general(weight, images, (((0,), (0,)), ((), ())), preferred_eleme...]
    pallas_call x0 -> x5, Pallas kernels: none -> 16.5 us  [call(): pl.pallas_call(kernel, out_shape=tuple(outs), in_specs=[in_spec] * len(op...]
    ppermute x6 -> x13, starting transfers between devices: 6.94 us -> 11.6 us  [send(): lax.ppermute(block, AXIS, [(i, target(i) % count) for i in range(count)])]
    ppermute x6 -> x13, waiting for transfers between devices: 44.2 us -> 43.5 us  [send(): lax.ppermute(block, AXIS, [(i, target(i) % count) for i in range(count)])]
  transfers between devices with their start and end apart: 6 -> 13, of which waited for: 3 -> 6; matrix products, arithmetic and copies ran while one was open for 36% -> 0% of each run, Pallas kernels for 0% -> 14%
where the time goes in v6:
time: 72.8 us; the launch traced here: 72.6 us
  waiting for transfers between devices  43.5 us (60%)
  Pallas kernels  16.5 us (23%)
  starting transfers between devices  11.6 us (16%)
  between operations  0.75 us (1%)
    ppermute x13, waiting for transfers between devices, send(): lax.ppermute(block, AXIS, [(i, target(i) % count) for i in range(count)])  43.5 us
    pallas_call x5, Pallas kernels, call(): pl.pallas_call(kernel, out_shape=tuple(outs), in_specs=[in_spec] * len(op...  16.5 us
    ppermute x13, starting transfers between devices, send(): lax.ppermute(block, AXIS, [(i, target(i) % count) for i in range(count)])  11.6 us
  transfers between devices with their start and end apart: 13, of which 6 were waited for; matrix products, arithmetic and copies ran while one was open for 0% of the time, Pallas kernels for 14%

profile of v6, /device:TPU:0, one launch (start us, length us, event | category | flops | bytes accessed | tf_op | source)
XLA Modules:
  0.0 72.6 jit_solution(12217774805826919619)
XLA Ops:
  0.6 2.2 %shard_map.41 = (bf16[256,1152]{1,0:T(8,128)(2,1)S(1)}, bf16[256,1152]{1,0:T(8,128)(2,1)S(1)}, bf16[512,1152]{1,0:T(8,128)(2,1)S(1)}, bf16[512,1152]{1,0:T(8,128)(2,1)S(1)}) custom-call(bf16[512,1152]{1,0:T(8,128)(2,1)} %image_ref.5, bf16[512,1152]{1,0:T(8,128)(2,1)} %text_ref.7), custom_call_target="tpu_custom_call" | custom-call | flops 1 | bytes 1 | tf_op jit(solution)/shard_map/pallas_call | solution.py:170
  2.8 3.0 %collective-permute-start.3 = (bf16[256,1152]{1,0:T(8,128)(2,1)S(1)}, bf16[256,1152]{1,0:T(8,128)(2,1)S(1)}, u32[]{:S(2)}, u32[]{:S(2)}) collective-permute-start(bf16[256,1152]{1,0:T(8,128)(2,1)S(1)} %get-tuple-element.19), channel_id=1, source_target_pairs={{0,4},{2,6},{4,8},{6,10},{8,12},{10,14},{12,16},{14,18},{16,20},{1... | collective-permute-start | bytes 1769480 | tf_op jit(solution)/shard_map/ppermute | solution.py:25
  5.9 1.5 %collective-permute-start.4 = (bf16[256,1152]{1,0:T(8,128)(2,1)S(1)}, bf16[256,1152]{1,0:T(8,128)(2,1)S(1)}, u32[]{:S(2)}, u32[]{:S(2)}) collective-permute-start(bf16[256,1152]{1,0:T(8,128)(2,1)S(1)} %get-tuple-element.20), channel_id=1, source_target_pairs={{0,4},{2,6},{4,8},{6,10},{8,12},{10,14},{12,16},{14,18},{16,20},{1... | collective-permute-start | bytes 1769480 | tf_op jit(solution)/shard_map/ppermute | solution.py:25
  7.4 3.2 %collective-permute-start.1 = (bf16[512,1152]{1,0:T(8,128)(2,1)S(1)}, bf16[512,1152]{1,0:T(8,128)(2,1)S(1)}, u32[]{:S(2)}, u32[]{:S(2)}) collective-permute-start(bf16[512,1152]{1,0:T(8,128)(2,1)S(1)} %copy-done.1), channel_id=1, source_target_pairs={{0,28},{2,30},{4,0},{6,2},{8,4},{10,6},{12,8},{14,10},{16,12},{18,... | collective-permute-start | bytes 3538952 | tf_op jit(solution)/shard_map/ppermute | solution.py:25
  10.6 0.0 collective-permute-start.2
  10.6 1.9 %collective-permute-start = (bf16[512,1152]{1,0:T(8,128)(2,1)S(1)}, bf16[512,1152]{1,0:T(8,128)(2,1)S(1)}, u32[]{:S(2)}, u32[]{:S(2)}) collective-permute-start(bf16[512,1152]{1,0:T(8,128)(2,1)S(1)} %get-tuple-element.17.far_own), channel_id=1, source_target_pairs={{0,26},{2,8},{4,30},{6,12},{8,2},{10,16},{12,6},{14,20},{16,10},{1... | collective-permute-start | bytes 3538952 | tf_op jit(solution)/shard_map/ppermute | solution.py:25
  12.5 3.2 %shard_map.42 = (f32[512,1152]{1,0:T(8,128)S(1)}, f32[512,1152]{1,0:T(8,128)S(1)}) custom-call(bf16[512,1152]{1,0:T(8,128)(2,1)S(1)} %copy-done.1, bf16[512,1152]{1,0:T(8,128)(2,1)S(1)} %copy-done), custom_call_target="tpu_custom_call" | custom-call | flops 1 | bytes 1 | tf_op jit(solution)/shard_map/pallas_call | solution.py:170
  15.7 29.1 %collective-permute-done.3.refs_1_ = bf16[256,1152]{1,0:T(8,128)(2,1)S(1)} collective-permute-done((bf16[256,1152]{1,0:T(8,128)(2,1)S(1)}, bf16[256,1152]{1,0:T(8,128)(2,1)S(1)}, u32[]{:S(2)}, u32[]{:S(2)}) %collective-permute-start.3) | collective-permute-done | bytes 589856 | tf_op jit(solution)/shard_map/ppermute | solution.py:25
  44.9 11.6 %collective-permute-done.4.refs_2_ = bf16[256,1152]{1,0:T(8,128)(2,1)S(1)} collective-permute-done((bf16[256,1152]{1,0:T(8,128)(2,1)S(1)}, bf16[256,1152]{1,0:T(8,128)(2,1)S(1)}, u32[]{:S(2)}, u32[]{:S(2)}) %collective-permute-start.4) | collective-permute-done | bytes 589856 | tf_op jit(solution)/shard_map/ppermute | solution.py:25
  56.5 0.1 collective-permute-start.5
  56.6 0.5 collective-permute-start.6
  57.1 1.0 %collective-permute-done.5.refs_3_ = bf16[128,1152]{1,0:T(8,128)(2,1)S(1)} collective-permute-done((bf16[128,1152]{1,0:T(8,128)(2,1)S(1)}, bf16[128,1152]{1,0:T(8,128)(2,1)S(1)}, u32[]{:S(2)}, u32[]{:S(2)}) %collective-permute-start.5) | collective-permute-done | bytes 294944 | tf_op jit(solution)/shard_map/ppermute | solution.py:25
  58.2 0.1 collective-permute-start.7
  58.3 0.3 collective-permute-done.6.refs_4_
  58.6 0.1 collective-permute-start.8
  58.7 1.0 %collective-permute-done.7.refs_5_ = bf16[128,1152]{1,0:T(8,128)(2,1)S(1)} collective-permute-done((bf16[128,1152]{1,0:T(8,128)(2,1)S(1)}, bf16[128,1152]{1,0:T(8,128)(2,1)S(1)}, u32[]{:S(2)}, u32[]{:S(2)}) %collective-permute-start.7) | collective-permute-done | bytes 294944 | tf_op jit(solution)/shard_map/ppermute | solution.py:25
  59.7 0.4 collective-permute-done.8.refs_6_
  60.2 0.0 collective-permute-done.2.refs_0_
  60.2 5.2 %shard_map.43 = (f32[512,1152]{1,0:T(8,128)S(1)}, f32[512,1152]{1,0:T(8,128)S(1)}) custom-call(bf16[512,1152]{1,0:T(8,128)(2,1)S(1)} %copy-done.1, bf16[512,1152]{1,0:T(8,128)(2,1)S(1)} %get-tuple-element.18.near_own, bf16[512,1152]{1,0:T(8,128)(2,1)S(1)} %collective-permute-done.2.refs_0_, ...), custom_call_target="tpu_custom_call", output_to_operand_aliasing={{0}: (9, {}), {1}: (10, {})} | custom-call | flops 1 | bytes 1 | tf_op jit(solution)/shard_map/pallas_call | solution.py:170
  65.4 0.0 collective-permute-done.1.images
  65.4 0.1 fusion
  65.5 0.2 collective-permute-start.10
  65.7 0.4 collective-permute-start.11
  66.1 0.1 collective-permute-start.12
  66.2 0.4 collective-permute-start.9
  66.6 1.8 %shard_map.44.refs_5_ = f32[512,1152]{1,0:T(8,128)S(1)} custom-call(bf16[512,1152]{1,0:T(8,128)(2,1)S(1)} %copy-done, bf16[512,1152]{1,0:T(8,128)(2,1)S(1)} %collective-permute-done.1.images, f32[512,1152]{1,0:T(8,128)S(1)} %get-tuple-element.31.text_total), custom_call_target="tpu_custom_call", output_to_operand_aliasing={{}: (2, {})} | custom-call | flops 1 | bytes 1 | tf_op jit(solution)/shard_map/pallas_call | solution.py:170
  68.4 0.0 collective-permute-done.far
  68.4 0.0 collective-permute-done.10.refs_1_
  68.4 0.0 collective-permute-done.11.refs_2_
  68.4 0.0 collective-permute-done.12.refs_3_
  68.4 0.0 collective-permute-done.9.refs_0_
  68.4 4.2 %shard_map.45 = (f32[512,1152]{1,0:T(8,128)}, f32[512,1152]{1,0:T(8,128)}) custom-call(bf16[512,1152]{1,0:T(8,128)(2,1)S(1)} %copy-done, bf16[512,1152]{1,0:T(8,128)(2,1)S(1)} %get-tuple-element.17.far_own, bf16[512,1152]{1,0:T(8,128)(2,1)S(1)} %collective-permute-done.far, bf16[128,1152]{1,0:T(8,128)(2,1)S(1)} %collective-permute-done.9.refs_0_, ...), custom_call_target="tpu_custom_call" | custom-call | flops 1 | bytes 1 | tf_op jit(solution)/shard_map/pallas_call | solution.py:170
  (6 shorter events, 0.1 us)
Async XLA Ops:
  0.6 6.7 %copy-start.1 = (bf16[512,1152]{1,0:T(8,128)(2,1)S(1)}, bf16[512,1152]{1,0:T(8,128)(2,1)}, u32[]{:S(2)}) copy-start(bf16[512,1152]{1,0:T(8,128)(2,1)} %image_ref.5) | copy-start | bytes 3538948
  0.6 11.9 %copy-start = (bf16[512,1152]{1,0:T(8,128)(2,1)S(1)}, bf16[512,1152]{1,0:T(8,128)(2,1)}, u32[]{:S(2)}) copy-start(bf16[512,1152]{1,0:T(8,128)(2,1)} %text_ref.7) | copy-start | bytes 3538948
  2.8 42.0 %collective-permute-start.3 = (bf16[256,1152]{1,0:T(8,128)(2,1)S(1)}, bf16[256,1152]{1,0:T(8,128)(2,1)S(1)}, u32[]{:S(2)}, u32[]{:S(2)}) collective-permute-start(bf16[256,1152]{1,0:T(8,128)(2,1)S(1)} %get-tuple-element.19), channel_id=1, source_target_pairs={{0,4},{2,6},{4,8},{6,10},{8,12},{10,14},{12,16},{14,18},{16,20},{1... | collective-permute-start | bytes 1769480 | tf_op jit(solution)/shard_map/ppermute | solution.py:25
  5.9 50.6 %collective-permute-start.4 = (bf16[256,1152]{1,0:T(8,128)(2,1)S(1)}, bf16[256,1152]{1,0:T(8,128)(2,1)S(1)}, u32[]{:S(2)}, u32[]{:S(2)}) collective-permute-start(bf16[256,1152]{1,0:T(8,128)(2,1)S(1)} %get-tuple-element.20), channel_id=1, source_target_pairs={{0,4},{2,6},{4,8},{6,10},{8,12},{10,14},{12,16},{14,18},{16,20},{1... | collective-permute-start | bytes 1769480 | tf_op jit(solution)/shard_map/ppermute | solution.py:25
  7.4 58.0 %collective-permute-start.1 = (bf16[512,1152]{1,0:T(8,128)(2,1)S(1)}, bf16[512,1152]{1,0:T(8,128)(2,1)S(1)}, u32[]{:S(2)}, u32[]{:S(2)}) collective-permute-start(bf16[512,1152]{1,0:T(8,128)(2,1)S(1)} %copy-done.1), channel_id=1, source_target_pairs={{0,28},{2,30},{4,0},{6,2},{8,4},{10,6},{12,8},{14,10},{16,12},{18,... | collective-permute-start | bytes 3538952 | tf_op jit(solution)/shard_map/ppermute | solution.py:25
  10.6 49.6 %collective-permute-start.2 = (bf16[512,1152]{1,0:T(8,128)(2,1)S(1)}, bf16[512,1152]{1,0:T(8,128)(2,1)S(1)}, u32[]{:S(2)}, u32[]{:S(2)}) collective-permute-start(bf16[512,1152]{1,0:T(8,128)(2,1)S(1)} %get-tuple-element.18.near_own), channel_id=1, source_target_pairs={{0,2},{2,0},{4,6},{6,4},{8,10},{10,8},{12,14},{14,12},{16,18},{18,... | collective-permute-start | bytes 3538952 | tf_op jit(solution)/shard_map/ppermute | solution.py:25
  10.6 57.8 %collective-permute-start = (bf16[512,1152]{1,0:T(8,128)(2,1)S(1)}, bf16[512,1152]{1,0:T(8,128)(2,1)S(1)}, u32[]{:S(2)}, u32[]{:S(2)}) collective-permute-start(bf16[512,1152]{1,0:T(8,128)(2,1)S(1)} %get-tuple-element.17.far_own), channel_id=1, source_target_pairs={{0,26},{2,8},{4,30},{6,12},{8,2},{10,16},{12,6},{14,20},{16,10},{1... | collective-permute-start | bytes 3538952 | tf_op jit(solution)/shard_map/ppermute | solution.py:25
  56.5 1.6 %collective-permute-start.5 = (bf16[128,1152]{1,0:T(8,128)(2,1)S(1)}, bf16[128,1152]{1,0:T(8,128)(2,1)S(1)}, u32[]{:S(2)}, u32[]{:S(2)}) collective-permute-start(bf16[128,1152]{1,0:T(8,128)(2,1)S(1)} %get-tuple-element.39), channel_id=1, source_target_pairs={{0,2},{2,0},{4,6},{6,4},{8,10},{10,8},{12,14},{14,12},{16,18},{18,... | collective-permute-start | bytes 884744 | tf_op jit(solution)/shard_map/ppermute | solution.py:25
  56.6 2.0 %collective-permute-start.6 = (bf16[128,1152]{1,0:T(8,128)(2,1)S(1)}, bf16[128,1152]{1,0:T(8,128)(2,1)S(1)}, u32[]{:S(2)}, u32[]{:S(2)}) collective-permute-start(bf16[128,1152]{1,0:T(8,128)(2,1)S(1)} %get-tuple-element.38), channel_id=1, source_target_pairs={{0,2},{2,0},{4,6},{6,4},{8,10},{10,8},{12,14},{14,12},{16,18},{18,... | collective-permute-start | bytes 884744 | tf_op jit(solution)/shard_map/ppermute | solution.py:25
  58.2 1.6 %collective-permute-start.7 = (bf16[128,1152]{1,0:T(8,128)(2,1)S(1)}, bf16[128,1152]{1,0:T(8,128)(2,1)S(1)}, u32[]{:S(2)}, u32[]{:S(2)}) collective-permute-start(bf16[128,1152]{1,0:T(8,128)(2,1)S(1)} %get-tuple-element.37), channel_id=1, source_target_pairs={{0,2},{2,0},{4,6},{6,4},{8,10},{10,8},{12,14},{14,12},{16,18},{18,... | collective-permute-start | bytes 884744 | tf_op jit(solution)/shard_map/ppermute | solution.py:25
  58.6 1.6 %collective-permute-start.8 = (bf16[128,1152]{1,0:T(8,128)(2,1)S(1)}, bf16[128,1152]{1,0:T(8,128)(2,1)S(1)}, u32[]{:S(2)}, u32[]{:S(2)}) collective-permute-start(bf16[128,1152]{1,0:T(8,128)(2,1)S(1)} %get-tuple-element.36), channel_id=1, source_target_pairs={{0,2},{2,0},{4,6},{6,4},{8,10},{10,8},{12,14},{14,12},{16,18},{18,... | collective-permute-start | bytes 884744 | tf_op jit(solution)/shard_map/ppermute | solution.py:25
  65.5 2.9 %collective-permute-start.10 = (bf16[128,1152]{1,0:T(8,128)(2,1)S(1)}, bf16[128,1152]{1,0:T(8,128)(2,1)S(1)}, u32[]{:S(2)}, u32[]{:S(2)}) collective-permute-start(bf16[128,1152]{1,0:T(8,128)(2,1)S(1)} %get-tuple-element.34), channel_id=1, source_target_pairs={{0,2},{2,0},{4,6},{6,4},{8,10},{10,8},{12,14},{14,12},{16,18},{18,... | collective-permute-start | bytes 884744 | tf_op jit(solution)/shard_map/ppermute | solution.py:25
  65.7 2.7 %collective-permute-start.11 = (bf16[128,1152]{1,0:T(8,128)(2,1)S(1)}, bf16[128,1152]{1,0:T(8,128)(2,1)S(1)}, u32[]{:S(2)}, u32[]{:S(2)}) collective-permute-start(bf16[128,1152]{1,0:T(8,128)(2,1)S(1)} %get-tuple-element.33), channel_id=1, source_target_pairs={{0,2},{2,0},{4,6},{6,4},{8,10},{10,8},{12,14},{14,12},{16,18},{18,... | collective-permute-start | bytes 884744 | tf_op jit(solution)/shard_map/ppermute | solution.py:25
  66.1 2.3 %collective-permute-start.12 = (bf16[128,1152]{1,0:T(8,128)(2,1)S(1)}, bf16[128,1152]{1,0:T(8,128)(2,1)S(1)}, u32[]{:S(2)}, u32[]{:S(2)}) collective-permute-start(bf16[128,1152]{1,0:T(8,128)(2,1)S(1)} %get-tuple-element.32), channel_id=1, source_target_pairs={{0,2},{2,0},{4,6},{6,4},{8,10},{10,8},{12,14},{14,12},{16,18},{18,... | collective-permute-start | bytes 884744 | tf_op jit(solution)/shard_map/ppermute | solution.py:25
  66.2 2.2 %collective-permute-start.9 = (bf16[128,1152]{1,0:T(8,128)(2,1)S(1)}, bf16[128,1152]{1,0:T(8,128)(2,1)S(1)}, u32[]{:S(2)}, u32[]{:S(2)}) collective-permute-start(bf16[128,1152]{1,0:T(8,128)(2,1)S(1)} %get-tuple-element.35), channel_id=1, source_target_pairs={{0,2},{2,0},{4,6},{6,4},{8,10},{10,8},{12,14},{14,12},{16,18},{18,... | collective-permute-start | bytes 884744 | tf_op jit(solution)/shard_map/ppermute | solution.py:25

commit v7 on v6

v7 whole, which is shorter than its diff:
```python
import functools
import math

import jax
import jax.numpy as jnp
from jax import lax
from jax.experimental import pallas as pl
from jax.experimental.pallas import tpu as pltpu
from jax.sharding import PartitionSpec as P

AXIS = "blk"
FIRST_IMAGES = 8
FIRST_TEXTS = 10
LAST_TILE = 256
COPY_ROWS = 128
VMEM_MIB = 32
VMEM = pl.BlockSpec(memory_space=pltpu.VMEM)
ANY = pl.BlockSpec(memory_space=pl.ANY)
LOG2_E = math.log2(math.e)


def send(block, target, senders=(0, 1)):
    count = lax.axis_size(AXIS)
    route = [(i, target(i) % count) for i in range(count) if i % 2 in senders]
    return lax.ppermute(block, AXIS, route)


def swap(block, parts):
    return [send(part, lambda i: i ^ 1) for part in jnp.split(block, parts)]


def core():
    return lax.rem(lax.axis_index(AXIS), 2)


def logits(own, others):
    return lax.dot_general(
        own[...], others[...], (((1,), (1,)), ((), ())), preferred_element_type=jnp.float32
    )


def decay(factor, inner_prod):
    return jnp.exp2(LOG2_E - (factor * LOG2_E) * inner_prod)


def product(weight, others):
    return jnp.dot(weight.astype(jnp.bfloat16), others[...], preferred_element_type=jnp.float32)


def add_all(factor, units):
    following = logits(*units[0][:2])
    for k, (_, others, use) in enumerate(units):
        inner_prod = following
        if k + 1 < len(units):
            following = logits(*units[k + 1][:2])
        weight = pl.reciprocal(1.0 + decay(factor, inner_prod), approx=True)
        use(product(weight, others))


def join(visitors, joined):
    if len(visitors) == 1:
        return visitors[0]
    start = 0
    for visitor in visitors:
        joined[pl.ds(start, visitor.shape[0])] = visitor[...]
        start += visitor.shape[0]
    return joined.at[pl.ds(0, start)]


def pick_kernel(image_ref, text_ref, *refs):
    outs, sems = refs[:2], refs[2]
    copies = []
    for k, (source, out) in enumerate(zip((image_ref, text_ref), outs)):
        rows = pl.ds(0, out.shape[0])
        copies.append(pltpu.make_async_copy(source.at[rows], out, sems.at[k]))
        copies[-1].start()
    for copy in copies:
        copy.wait()


def core_pick_kernel(image_ref, text_ref, far_own, sem):
    for is_core, far in enumerate((image_ref, text_ref)):

        @pl.when(core() == is_core)
        def _():
            copy = pltpu.make_async_copy(far, far_own, sem)
            copy.start()
            copy.wait()


def own_kernel(factor, image_ref, text_ref, image_sum, text_sum):
    rows = image_ref.shape[0]
    shape = (rows, rows)
    matched = lax.broadcasted_iota(jnp.int32, shape, 0) == lax.broadcasted_iota(
        jnp.int32, shape, 1
    )
    for own, others, total in ((image_ref, text_ref, image_sum), (text_ref, image_ref, text_sum)):
        chance = 1.0 / (1.0 + decay(factor, logits(own, others)))
        total[...] = product(chance - matched.astype(jnp.float32), others)


def step_kernel(factor, units, sides, *refs):
    is_1 = core().astype(jnp.float32)
    parts = []
    for _, count in units:
        parts.append((refs[0], refs[1 : 1 + count]))
        refs = refs[1 + count :]
    totals = dict(zip(sides, refs))
    sums = dict(zip(sides, refs[len(sides) :]))
    joined = refs[2 * len(sides) :]
    touched = set()

    def add(side, value):
        sums[side][...] = (sums if side in touched else totals)[side][...] + value
        touched.add(side)

    def use(side, value):
        if side < 2:
            add(side, value)
        else:
            add(side - 2, value * (1.0 - is_1))
            add(3 - side, value * is_1)

    add_all(
        factor,
        [
            (own, join(visitors, scratch), functools.partial(use, side))
            for (side, _), (own, visitors), scratch in zip(units, parts, joined)
        ],
    )


def last_kernel(factor, counts, *refs):
    parts = []
    for count in counts:
        parts.append((refs[0], refs[1 : 1 + count], refs[1 + count]))
        refs = refs[2 + count :]
    outs, helds, joined, sems = refs[:2], refs[2:4], refs[4:6], refs[6]
    copies = []

    def use(total, held, out, start, value):
        rows = pl.ds(start, LAST_TILE)
        held[rows] = (total[rows] + value) * factor
        for first in range(start, start + LAST_TILE, COPY_ROWS):
            span = pl.ds(first, COPY_ROWS)
            copies.append(pltpu.make_async_copy(held.at[span], out.at[span], sems.at[len(copies)]))
            copies[-1].start()

    units = []
    for (own, visitors, total), held, out, scratch in zip(parts, helds, outs, joined):
        others = join(visitors, scratch)
        for start in range(0, own.shape[0], LAST_TILE):
            act = functools.partial(use, total, held, out, start)
            units.append((own.at[pl.ds(start, LAST_TILE)], others, act))
    add_all(factor, units)
    for copy in copies:
        copy.wait()


def local(image_embed, text_embed):
    rows, width = image_embed.shape
    dtype = image_embed.dtype
    factor = 2.0 / math.sqrt(width)
    kept = pltpu.VMEM((rows, width), jnp.float32)
    block = pltpu.VMEM((rows, width), dtype)
    grad = jax.ShapeDtypeStruct((rows, width), jnp.float32)

    def call(kernel, outs, operands, scratch=(), aliases=None, in_spec=VMEM):
        return pl.pallas_call(
            kernel,
            out_shape=tuple(outs),
            in_specs=[in_spec] * len(operands),
            out_specs=(ANY if outs[0] is grad else VMEM,) * len(outs),
            scratch_shapes=list(scratch),
            input_output_aliases=aliases or {},
            cost_estimate=pl.CostEstimate(flops=1, bytes_accessed=1, transcendentals=0),
            compiler_params=pltpu.CompilerParams(vmem_limit_bytes=VMEM_MIB << 20),
        )(*operands)

    def depth(visitors):
        return pltpu.VMEM((sum(visitor.shape[0] for visitor in visitors), width), dtype)

    def step(units, sums):
        sides = tuple(sums)
        operands = [ref for _, own, visitors in units for ref in (own, *visitors)]
        counts = [(side, len(visitors)) for side, _, visitors in units]
        return dict(
            zip(
                sides,
                call(
                    functools.partial(step_kernel, factor, counts, sides),
                    [kept] * len(sides),
                    (*operands, *sums.values()),
                    [depth(visitors) for _, _, visitors in units],
                    {len(operands) + k: k for k in range(len(sides))},
                ),
            )
        )

    def after(value, *earlier):
        return lax.optimization_barrier((value, *earlier))[0]

    def next_images(piece):
        return send(piece, lambda i: i - 2)

    def next_texts(piece):
        return send(piece, lambda i: i + 2)

    in_hbm = [pltpu.with_memory_space_constraint(x, pltpu.HBM) for x in (image_embed, text_embed)]
    cut_images, cut_texts = rows * FIRST_IMAGES // 16, rows * FIRST_TEXTS // 16
    heads = (cut_images, cut_texts)
    image_head, text_head = call(
        pick_kernel,
        [pltpu.VMEM((head, width), dtype) for head in heads],
        in_hbm,
        [pltpu.SemaphoreType.DMA((2,))],
        in_spec=ANY,
    )
    images, texts = next_images(image_head), next_texts(text_head)
    (far_own,) = call(
        core_pick_kernel, [block], in_hbm, [pltpu.SemaphoreType.DMA], in_spec=ANY
    )
    far = send(far_own, lambda i: i + 3 if i % 2 else i - 3)
    near_text = send(text_embed, lambda i: i + 1, (0,))
    near_image = send(image_embed, lambda i: i - 1, (1,))
    sums = call(functools.partial(own_kernel, factor), (kept, kept), (image_embed, text_embed))
    sums = step(
        [(0, image_embed, (near_text,)), (1, text_embed, (near_image,))],
        dict(enumerate(sums)),
    )

    images = after(images, *sums.values())
    later_images = next_images(after(image_embed[cut_images:], images))
    sums |= step([(1, text_embed, (images, *swap(images, 2)))], {1: sums[1]})
    texts = after(texts, *sums.values())
    later_texts = next_texts(after(text_embed[cut_texts:], texts))
    sums |= step([(0, image_embed, (texts, *swap(texts, 2)))], {0: sums[0]})
    sums = step([(2, far_own, (after(far, sums[0]),))], sums)

    images, texts = after(later_images, sums[0]), after(later_texts, sums[0])
    swapped_images, swapped_texts = swap(images, 2), swap(texts, 1)
    sums = step([(1, text_embed, (images,)), (0, image_embed, (texts,))], sums)
    operands = (image_embed, *swapped_texts, sums[0], text_embed, *swapped_images, sums[1])
    return call(
        functools.partial(last_kernel, factor, (1, 2)),
        (grad, grad),
        operands,
        [kept, kept, depth((texts,)), depth((images,))]
        + [pltpu.SemaphoreType.DMA((2 * rows // COPY_ROWS,))],
    )


def solution(mesh):
    spec = P(("rep", "blk"), None)
    return jax.shard_map(
        local, mesh=mesh, in_specs=(spec, spec), out_specs=(spec, spec), check_vma=False
    )
```

time: 72.8 us -> 74.3 us (1.021)
  waiting for transfers between devices: 43.5 us -> 36.3 us
  starting transfers between devices: 11.6 us -> 15.9 us
  Pallas kernels: 16.5 us -> 20.6 us
    ppermute x13 -> x14, waiting for transfers between devices: 43.5 us -> 36.3 us  [send(): return lax.ppermute(block, AXIS, route)]
    ppermute x13 -> x14, starting transfers between devices: 11.6 us -> 15.9 us  [send(): return lax.ppermute(block, AXIS, route)]
    pallas_call x5 -> x9, Pallas kernels: 16.5 us -> 20.6 us  [call(): pl.pallas_call(kernel, out_shape=tuple(outs), in_specs=[in_spec] * len(op...]
  transfers between devices with their start and end apart: 13 -> 14, of which waited for: 6 -> 6; matrix products, arithmetic and copies ran while one was open for 0% -> 0% of each run, Pallas kernels for 14% -> 24%
where the time goes in v7:
time: 74.3 us; the launch traced here: 74.1 us
  waiting for transfers between devices  36.3 us (49%)
  Pallas kernels  20.6 us (28%)
  starting transfers between devices  15.9 us (21%)
  between operations  0.97 us (1%)
    ppermute x14, waiting for transfers between devices, send(): return lax.ppermute(block, AXIS, route)  36.3 us
    pallas_call x9, Pallas kernels, call(): pl.pallas_call(kernel, out_shape=tuple(outs), in_specs=[in_spec] * len(op...  20.6 us
    ppermute x14, starting transfers between devices, send(): return lax.ppermute(block, AXIS, route)  15.9 us
  transfers between devices with their start and end apart: 14, of which 6 were waited for; matrix products, arithmetic and copies ran while one was open for 0% of the time, Pallas kernels for 24%

profile of v7, /device:TPU:0, one launch (start us, length us, event | category | flops | bytes accessed | tf_op | source)
XLA Modules:
  0.0 74.1 jit_solution(5607656891021216739)
XLA Ops:
  0.6 2.4 %collective-permute-start.1 = (bf16[512,1152]{1,0:T(8,128)(2,1)}, bf16[512,1152]{1,0:T(8,128)(2,1)S(1)}, u32[]{:S(2)}, u32[]{:S(2)}) collective-permute-start(bf16[512,1152]{1,0:T(8,128)(2,1)} %refs_3_.1), channel_id=1, source_target_pairs={{0,2},{4,6},{8,10},{12,14},{16,18},{20,22},{24,26},{28,30},{1,3},{... | collective-permute-start | bytes 3538952 | tf_op jit(solution)/shard_map/ppermute | solution.py:25
  3.1 1.3 %collective-permute-start.2 = (bf16[512,1152]{1,0:T(8,128)(2,1)}, bf16[512,1152]{1,0:T(8,128)(2,1)S(1)}, u32[]{:S(2)}, u32[]{:S(2)}) collective-permute-start(bf16[512,1152]{1,0:T(8,128)(2,1)} %refs_0_.9), channel_id=1, source_target_pairs={{2,0},{6,4},{10,8},{14,12},{18,16},{22,20},{26,24},{30,28},{3,1},{... | collective-permute-start | bytes 3538952 | tf_op jit(solution)/shard_map/ppermute | solution.py:25
  4.4 1.3 %shard_map.41 = (bf16[256,1152]{1,0:T(8,128)(2,1)S(1)}, bf16[320,1152]{1,0:T(8,128)(2,1)S(1)}) custom-call(bf16[512,1152]{1,0:T(8,128)(2,1)} %refs_0_.9, bf16[512,1152]{1,0:T(8,128)(2,1)} %refs_3_.1), custom_call_target="tpu_custom_call" | custom-call | flops 1 | bytes 1 | tf_op jit(solution)/shard_map/pallas_call | solution.py:169
  5.7 0.0 copy-start
  5.7 0.0 copy-start.1
  5.7 5.4 %collective-permute-start.3 = (bf16[256,1152]{1,0:T(8,128)(2,1)S(1)}, bf16[256,1152]{1,0:T(8,128)(2,1)S(1)}, u32[]{:S(2)}, u32[]{:S(2)}) collective-permute-start(bf16[256,1152]{1,0:T(8,128)(2,1)S(1)} %get-tuple-element.23), channel_id=1, source_target_pairs={{0,28},{2,30},{4,0},{6,2},{8,4},{10,6},{12,8},{14,10},{16,12},{18,... | collective-permute-start | bytes 1769480 | tf_op jit(solution)/shard_map/ppermute | solution.py:25
  11.2 1.3 %shard_map.45.refs_0_ = bf16[512,1152]{1,0:T(8,128)(2,1)S(1)} custom-call(bf16[512,1152]{1,0:T(8,128)(2,1)} %refs_0_.9, bf16[512,1152]{1,0:T(8,128)(2,1)} %refs_3_.1), custom_call_target="tpu_custom_call" | custom-call | flops 1 | bytes 1 | tf_op jit(solution)/shard_map/pallas_call | solution.py:169
  12.4 1.4 %collective-permute-start.7 = (bf16[512,1152]{1,0:T(8,128)(2,1)S(1)}, bf16[512,1152]{1,0:T(8,128)(2,1)S(1)}, u32[]{:S(2)}, u32[]{:S(2)}) collective-permute-start(bf16[512,1152]{1,0:T(8,128)(2,1)S(1)} %shard_map.45.refs_0_), channel_id=1, source_target_pairs={{0,26},{2,8},{4,30},{6,12},{8,2},{10,16},{12,6},{14,20},{16,10},{1... | collective-permute-start | bytes 3538952 | tf_op jit(solution)/shard_map/ppermute | solution.py:25
  13.8 3.2 %shard_map.42 = (f32[512,1152]{1,0:T(8,128)S(1)}, f32[512,1152]{1,0:T(8,128)S(1)}) custom-call(bf16[512,1152]{1,0:T(8,128)(2,1)S(1)} %copy-done, bf16[512,1152]{1,0:T(8,128)(2,1)S(1)} %copy-done.1), custom_call_target="tpu_custom_call" | custom-call | flops 1 | bytes 1 | tf_op jit(solution)/shard_map/pallas_call | solution.py:169
  17.0 0.0 collective-permute-done.1.refs_1_
  17.0 3.4 %shard_map.43 = (f32[512,1152]{1,0:T(8,128)S(1)}, f32[512,1152]{1,0:T(8,128)S(1)}) custom-call(bf16[512,1152]{1,0:T(8,128)(2,1)S(1)} %copy-done, bf16[512,1152]{1,0:T(8,128)(2,1)S(1)} %collective-permute-done.1.refs_1_, bf16[512,1152]{1,0:T(8,128)(2,1)S(1)} %copy-done.1, ...), custom_call_target="tpu_custom_call", output_to_operand_aliasing={{0}: (4, {}), {1}: (5, {})} | custom-call | flops 1 | bytes 1 | tf_op jit(solution)/shard_map/pallas_call | solution.py:169
  20.4 17.2 %collective-permute-done.3.refs_1_ = bf16[256,1152]{1,0:T(8,128)(2,1)S(1)} collective-permute-done((bf16[256,1152]{1,0:T(8,128)(2,1)S(1)}, bf16[256,1152]{1,0:T(8,128)(2,1)S(1)}, u32[]{:S(2)}, u32[]{:S(2)}) %collective-permute-start.3) | collective-permute-done | bytes 589856 | tf_op jit(solution)/shard_map/ppermute | solution.py:25
  37.7 0.6 collective-permute-start.4
  38.3 0.1 collective-permute-start.5
  38.5 3.2 %collective-permute-start.11 = (bf16[256,1152]{1,0:T(8,128)(2,1)S(1)}, bf16[256,1152]{1,0:T(8,128)(2,1)S(1)}, u32[]{:S(2)}, u32[]{:S(2)}) collective-permute-start(bf16[256,1152]{1,0:T(8,128)(2,1)S(1)} %slice.7), channel_id=1, source_target_pairs={{0,28},{2,30},{4,0},{6,2},{8,4},{10,6},{12,8},{14,10},{16,12},{18,... | collective-permute-start | bytes 1769480 | tf_op jit(solution)/shard_map/ppermute | solution.py:25
  41.7 1.8 %shard_map.44.refs_3_ = f32[512,1152]{1,0:T(8,128)S(1)} custom-call(bf16[512,1152]{1,0:T(8,128)(2,1)S(1)} %copy-done.1, bf16[256,1152]{1,0:T(8,128)(2,1)S(1)} %collective-permute-done.3.refs_1_, bf16[128,1152]{1,0:T(8,128)(2,1)S(1)} %collective-permute-done.4.refs_2_, ...), custom_call_target="tpu_custom_call", output_to_operand_aliasing={{}: (4, {})} | custom-call | flops 1 | bytes 1 | tf_op jit(solution)/shard_map/pallas_call | solution.py:169
  43.5 0.2 collective-permute-start.6
  43.8 0.1 fusion
  43.9 0.1 collective-permute-start.8
  44.0 0.4 collective-permute-start.9
  44.4 1.2 %collective-permute-done.8.refs_2_ = bf16[160,1152]{1,0:T(8,128)(2,1)S(1)} collective-permute-done((bf16[160,1152]{1,0:T(8,128)(2,1)S(1)}, bf16[160,1152]{1,0:T(8,128)(2,1)S(1)}, u32[]{:S(2)}, u32[]{:S(2)}) %collective-permute-start.8) | collective-permute-done | bytes 368672 | tf_op jit(solution)/shard_map/ppermute | solution.py:25
  45.6 0.5 collective-permute-done.9.refs_3_
  46.1 2.6 %shard_map.46.refs_2_ = f32[512,1152]{1,0:T(8,128)S(1)} custom-call(bf16[512,1152]{1,0:T(8,128)(2,1)S(1)} %copy-done, bf16[320,1152]{1,0:T(8,128)(2,1)S(1)} %collective-permute-done.refs_1_, bf16[160,1152]{1,0:T(8,128)(2,1)S(1)} %collective-permute-done.8.refs_2_, ...), custom_call_target="tpu_custom_call", output_to_operand_aliasing={{}: (4, {})} | custom-call | flops 1 | bytes 1 | tf_op jit(solution)/shard_map/pallas_call | solution.py:169
  48.7 2.6 %collective-permute-done.7.refs_1_ = bf16[512,1152]{1,0:T(8,128)(2,1)S(1)} collective-permute-done((bf16[512,1152]{1,0:T(8,128)(2,1)S(1)}, bf16[512,1152]{1,0:T(8,128)(2,1)S(1)}, u32[]{:S(2)}, u32[]{:S(2)}) %collective-permute-start.7) | collective-permute-done | bytes 1179680 | tf_op jit(solution)/shard_map/ppermute | solution.py:25
  51.3 1.9 %shard_map.47 = (f32[512,1152]{1,0:T(8,128)S(1)}, f32[512,1152]{1,0:T(8,128)S(1)}) custom-call(bf16[512,1152]{1,0:T(8,128)(2,1)S(1)} %shard_map.45.refs_0_, bf16[512,1152]{1,0:T(8,128)(2,1)S(1)} %collective-permute-done.7.refs_1_, f32[512,1152]{1,0:T(8,128)S(1)} %shard_map.46.refs_2_, ...), custom_call_target="tpu_custom_call", output_to_operand_aliasing={{0}: (2, {}), {1}: (3, {})} | custom-call | flops 1 | bytes 1 | tf_op jit(solution)/shard_map/pallas_call | solution.py:169
  53.2 9.5 %collective-permute-done.11.refs_1_ = bf16[256,1152]{1,0:T(8,128)(2,1)S(1)} collective-permute-done((bf16[256,1152]{1,0:T(8,128)(2,1)S(1)}, bf16[256,1152]{1,0:T(8,128)(2,1)S(1)}, u32[]{:S(2)}, u32[]{:S(2)}) %collective-permute-start.11) | collective-permute-done | bytes 589856 | tf_op jit(solution)/shard_map/ppermute | solution.py:25
  62.7 5.3 %collective-permute-done.6.refs_3_ = bf16[192,1152]{1,0:T(8,128)(2,1)S(1)} collective-permute-done((bf16[192,1152]{1,0:T(8,128)(2,1)S(1)}, bf16[192,1152]{1,0:T(8,128)(2,1)S(1)}, u32[]{:S(2)}, u32[]{:S(2)}) %collective-permute-start.6) | collective-permute-done | bytes 442400 | tf_op jit(solution)/shard_map/ppermute | solution.py:25
  68.0 0.1 collective-permute-start.10
  68.1 0.5 collective-permute-start.12
  68.6 0.1 collective-permute-start.13
  68.7 2.1 %shard_map.48 = (f32[512,1152]{1,0:T(8,128)S(1)}, f32[512,1152]{1,0:T(8,128)S(1)}) custom-call(bf16[512,1152]{1,0:T(8,128)(2,1)S(1)} %copy-done.1, bf16[256,1152]{1,0:T(8,128)(2,1)S(1)} %collective-permute-done.11.refs_1_, bf16[512,1152]{1,0:T(8,128)(2,1)S(1)} %copy-done, ...), custom_call_target="tpu_custom_call", output_to_operand_aliasing={{0}: (4, {}), {1}: (5, {})} | custom-call | flops 1 | bytes 1 | tf_op jit(solution)/shard_map/pallas_call | solution.py:169
  70.8 3.1 %shard_map.49 = (f32[512,1152]{1,0:T(8,128)}, f32[512,1152]{1,0:T(8,128)}) custom-call(bf16[512,1152]{1,0:T(8,128)(2,1)S(1)} %copy-done, bf16[192,1152]{1,0:T(8,128)(2,1)S(1)} %collective-permute-done.10.refs_1_, f32[512,1152]{1,0:T(8,128)S(1)} %get-tuple-element.34.refs_2_, bf16[512,1152]{1,0:T(8,128)(2,1)S(1)} %copy-done.1, ...), custom_call_target="tpu_custom_call" | custom-call | flops 1 | bytes 1 | tf_op jit(solution)/shard_map/pallas_call | solution.py:169
  (14 shorter events, 0.2 us)
Async XLA Ops:
  0.6 16.4 %collective-permute-start.1 = (bf16[512,1152]{1,0:T(8,128)(2,1)}, bf16[512,1152]{1,0:T(8,128)(2,1)S(1)}, u32[]{:S(2)}, u32[]{:S(2)}) collective-permute-start(bf16[512,1152]{1,0:T(8,128)(2,1)} %refs_3_.1), channel_id=1, source_target_pairs={{0,2},{4,6},{8,10},{12,14},{16,18},{20,22},{24,26},{28,30},{1,3},{... | collective-permute-start | bytes 3538952 | tf_op jit(solution)/shard_map/ppermute | solution.py:25
  3.1 14.0 %collective-permute-start.2 = (bf16[512,1152]{1,0:T(8,128)(2,1)}, bf16[512,1152]{1,0:T(8,128)(2,1)S(1)}, u32[]{:S(2)}, u32[]{:S(2)}) collective-permute-start(bf16[512,1152]{1,0:T(8,128)(2,1)} %refs_0_.9), channel_id=1, source_target_pairs={{2,0},{6,4},{10,8},{14,12},{18,16},{22,20},{26,24},{30,28},{3,1},{... | collective-permute-start | bytes 3538952 | tf_op jit(solution)/shard_map/ppermute | solution.py:25
  5.7 8.1 %copy-start = (bf16[512,1152]{1,0:T(8,128)(2,1)S(1)}, bf16[512,1152]{1,0:T(8,128)(2,1)}, u32[]{:S(2)}) copy-start(bf16[512,1152]{1,0:T(8,128)(2,1)} %refs_0_.9) | copy-start | bytes 3538948
  5.7 8.1 %copy-start.1 = (bf16[512,1152]{1,0:T(8,128)(2,1)S(1)}, bf16[512,1152]{1,0:T(8,128)(2,1)}, u32[]{:S(2)}) copy-start(bf16[512,1152]{1,0:T(8,128)(2,1)} %refs_3_.1) | copy-start | bytes 3538948
  5.7 31.9 %collective-permute-start.3 = (bf16[256,1152]{1,0:T(8,128)(2,1)S(1)}, bf16[256,1152]{1,0:T(8,128)(2,1)S(1)}, u32[]{:S(2)}, u32[]{:S(2)}) collective-permute-start(bf16[256,1152]{1,0:T(8,128)(2,1)S(1)} %get-tuple-element.23), channel_id=1, source_target_pairs={{0,28},{2,30},{4,0},{6,2},{8,4},{10,6},{12,8},{14,10},{16,12},{18,... | collective-permute-start | bytes 1769480 | tf_op jit(solution)/shard_map/ppermute | solution.py:25
  11.2 32.4 %collective-permute-start = (bf16[320,1152]{1,0:T(8,128)(2,1)S(1)}, bf16[320,1152]{1,0:T(8,128)(2,1)S(1)}, u32[]{:S(2)}, u32[]{:S(2)}) collective-permute-start(bf16[320,1152]{1,0:T(8,128)(2,1)S(1)} %get-tuple-element.19), channel_id=1, source_target_pairs={{0,4},{2,6},{4,8},{6,10},{8,12},{10,14},{12,16},{14,18},{16,20},{1... | collective-permute-start | bytes 2211848 | tf_op jit(solution)/shard_map/ppermute | solution.py:25
  12.4 38.9 %collective-permute-start.7 = (bf16[512,1152]{1,0:T(8,128)(2,1)S(1)}, bf16[512,1152]{1,0:T(8,128)(2,1)S(1)}, u32[]{:S(2)}, u32[]{:S(2)}) collective-permute-start(bf16[512,1152]{1,0:T(8,128)(2,1)S(1)} %shard_map.45.refs_0_), channel_id=1, source_target_pairs={{0,26},{2,8},{4,30},{6,12},{8,2},{10,16},{12,6},{14,20},{16,10},{1... | collective-permute-start | bytes 3538952 | tf_op jit(solution)/shard_map/ppermute | solution.py:25
  37.7 4.0 %collective-permute-start.4 = (bf16[128,1152]{1,0:T(8,128)(2,1)S(1)}, bf16[128,1152]{1,0:T(8,128)(2,1)S(1)}, u32[]{:S(2)}, u32[]{:S(2)}) collective-permute-start(bf16[128,1152]{1,0:T(8,128)(2,1)S(1)} %get-tuple-element.41), channel_id=1, source_target_pairs={{0,2},{2,0},{4,6},{6,4},{8,10},{10,8},{12,14},{14,12},{16,18},{18,... | collective-permute-start | bytes 884744 | tf_op jit(solution)/shard_map/ppermute | solution.py:25
  38.3 3.4 %collective-permute-start.5 = (bf16[128,1152]{1,0:T(8,128)(2,1)S(1)}, bf16[128,1152]{1,0:T(8,128)(2,1)S(1)}, u32[]{:S(2)}, u32[]{:S(2)}) collective-permute-start(bf16[128,1152]{1,0:T(8,128)(2,1)S(1)} %get-tuple-element.40), channel_id=1, source_target_pairs={{0,2},{2,0},{4,6},{6,4},{8,10},{10,8},{12,14},{14,12},{16,18},{18,... | collective-permute-start | bytes 884744 | tf_op jit(solution)/shard_map/ppermute | solution.py:25
  38.5 24.2 %collective-permute-start.11 = (bf16[256,1152]{1,0:T(8,128)(2,1)S(1)}, bf16[256,1152]{1,0:T(8,128)(2,1)S(1)}, u32[]{:S(2)}, u32[]{:S(2)}) collective-permute-start(bf16[256,1152]{1,0:T(8,128)(2,1)S(1)} %slice.7), channel_id=1, source_target_pairs={{0,28},{2,30},{4,0},{6,2},{8,4},{10,6},{12,8},{14,10},{16,12},{18,... | collective-permute-start | bytes 1769480 | tf_op jit(solution)/shard_map/ppermute | solution.py:25
  43.5 24.4 %collective-permute-start.6 = (bf16[192,1152]{1,0:T(8,128)(2,1)S(1)}, bf16[192,1152]{1,0:T(8,128)(2,1)S(1)}, u32[]{:S(2)}, u32[]{:S(2)}) collective-permute-start(bf16[192,1152]{1,0:T(8,128)(2,1)S(1)} %slice.6), channel_id=1, source_target_pairs={{0,4},{2,6},{4,8},{6,10},{8,12},{10,14},{12,16},{14,18},{16,20},{1... | collective-permute-start | bytes 1327112 | tf_op jit(solution)/shard_map/ppermute | solution.py:25
  43.9 1.8 %collective-permute-start.8 = (bf16[160,1152]{1,0:T(8,128)(2,1)S(1)}, bf16[160,1152]{1,0:T(8,128)(2,1)S(1)}, u32[]{:S(2)}, u32[]{:S(2)}) collective-permute-start(bf16[160,1152]{1,0:T(8,128)(2,1)S(1)} %get-tuple-element.37), channel_id=1, source_target_pairs={{0,2},{2,0},{4,6},{6,4},{8,10},{10,8},{12,14},{14,12},{16,18},{18,... | collective-permute-start | bytes 1105928 | tf_op jit(solution)/shard_map/ppermute | solution.py:25
  44.0 2.1 %collective-permute-start.9 = (bf16[160,1152]{1,0:T(8,128)(2,1)S(1)}, bf16[160,1152]{1,0:T(8,128)(2,1)S(1)}, u32[]{:S(2)}, u32[]{:S(2)}) collective-permute-start(bf16[160,1152]{1,0:T(8,128)(2,1)S(1)} %get-tuple-element.36), channel_id=1, source_target_pairs={{0,2},{2,0},{4,6},{6,4},{8,10},{10,8},{12,14},{14,12},{16,18},{18,... | collective-permute-start | bytes 1105928 | tf_op jit(solution)/shard_map/ppermute | solution.py:25
  68.0 2.8 %collective-permute-start.10 = (bf16[192,1152]{1,0:T(8,128)(2,1)S(1)}, bf16[192,1152]{1,0:T(8,128)(2,1)S(1)}, u32[]{:S(2)}, u32[]{:S(2)}) collective-permute-start(bf16[192,1152]{1,0:T(8,128)(2,1)S(1)} %collective-permute-done.6.refs_3_), channel_id=1, source_target_pairs={{0,2},{2,0},{4,6},{6,4},{8,10},{10,8},{12,14},{14,12},{16,18},{18,... | collective-permute-start | bytes 1327112 | tf_op jit(solution)/shard_map/ppermute | solution.py:25
  68.1 2.7 %collective-permute-start.12 = (bf16[128,1152]{1,0:T(8,128)(2,1)S(1)}, bf16[128,1152]{1,0:T(8,128)(2,1)S(1)}, u32[]{:S(2)}, u32[]{:S(2)}) collective-permute-start(bf16[128,1152]{1,0:T(8,128)(2,1)S(1)} %get-tuple-element.39), channel_id=1, source_target_pairs={{0,2},{2,0},{4,6},{6,4},{8,10},{10,8},{12,14},{14,12},{16,18},{18,... | collective-permute-start | bytes 884744 | tf_op jit(solution)/shard_map/ppermute | solution.py:25
  68.6 2.2 %collective-permute-start.13 = (bf16[128,1152]{1,0:T(8,128)(2,1)S(1)}, bf16[128,1152]{1,0:T(8,128)(2,1)S(1)}, u32[]{:S(2)}, u32[]{:S(2)}) collective-permute-start(bf16[128,1152]{1,0:T(8,128)(2,1)S(1)} %get-tuple-element.38), channel_id=1, source_target_pairs={{0,2},{2,0},{4,6},{6,4},{8,10},{10,8},{12,14},{14,12},{16,18},{18,... | collective-permute-start | bytes 884744 | tf_op jit(solution)/shard_map/ppermute | solution.py:25

commit v8 on v7

--- a/solution.py
+++ b/solution.py
@@ -10,7 +10,7 @@
 
 AXIS = "blk"
 FIRST_IMAGES = 8
-FIRST_TEXTS = 10
+FIRST_TEXTS = 8
 LAST_TILE = 256
 COPY_ROWS = 128
 VMEM_MIB = 32
@@ -19,10 +19,9 @@
 LOG2_E = math.log2(math.e)
 
 
-def send(block, target, senders=(0, 1)):
+def send(block, target):
     count = lax.axis_size(AXIS)
-    route = [(i, target(i) % count) for i in range(count) if i % 2 in senders]
-    return lax.ppermute(block, AXIS, route)
+    return lax.ppermute(block, AXIS, [(i, target(i) % count) for i in range(count)])
 
 
 def swap(block, parts):
@@ -67,25 +66,25 @@
     return joined.at[pl.ds(0, start)]
 
 
-def pick_kernel(image_ref, text_ref, *refs):
-    outs, sems = refs[:2], refs[2]
-    copies = []
-    for k, (source, out) in enumerate(zip((image_ref, text_ref), outs)):
-        rows = pl.ds(0, out.shape[0])
-        copies.append(pltpu.make_async_copy(source.at[rows], out, sems.at[k]))
-        copies[-1].start()
-    for copy in copies:
-        copy.wait()
-
-
-def core_pick_kernel(image_ref, text_ref, far_own, sem):
-    for is_core, far in enumerate((image_ref, text_ref)):
+def pick_kernel(image_ref, text_ref, image_head, text_head, far_own, near_own, sems):
+    def move(k, source, out):
+        return pltpu.make_async_copy(source.at[pl.ds(0, out.shape[0])], out, sems.at[k])
+
+    heads = [move(0, image_ref, image_head), move(1, text_ref, text_head)]
+    for head in heads:
+        head.start()
+    for is_core, (far, near) in enumerate(((image_ref, text_ref), (text_ref, image_ref))):
 
         @pl.when(core() == is_core)
         def _():
-            copy = pltpu.make_async_copy(far, far_own, sem)
-            copy.start()
-            copy.wait()
+            blocks = [move(2, far, far_own), move(3, near, near_own)]
+            for block in blocks:
+                block.start()
+            for block in blocks:
+                block.wait()
+
+    for head in heads:
+        head.wait()
 
 
 def own_kernel(factor, image_ref, text_ref, image_sum, text_sum):
@@ -209,40 +208,45 @@
     in_hbm = [pltpu.with_memory_space_constraint(x, pltpu.HBM) for x in (image_embed, text_embed)]
     cut_images, cut_texts = rows * FIRST_IMAGES // 16, rows * FIRST_TEXTS // 16
     heads = (cut_images, cut_texts)
-    image_head, text_head = call(
+    image_head, text_head, far_own, near_own = call(
         pick_kernel,
-        [pltpu.VMEM((head, width), dtype) for head in heads],
+        [pltpu.VMEM((head, width), dtype) for head in heads] + [block, block],
         in_hbm,
-        [pltpu.SemaphoreType.DMA((2,))],
+        [pltpu.SemaphoreType.DMA((4,))],
         in_spec=ANY,
     )
     images, texts = next_images(image_head), next_texts(text_head)
-    (far_own,) = call(
-        core_pick_kernel, [block], in_hbm, [pltpu.SemaphoreType.DMA], in_spec=ANY
-    )
     far = send(far_own, lambda i: i + 3 if i % 2 else i - 3)
-    near_text = send(text_embed, lambda i: i + 1, (0,))
-    near_image = send(image_embed, lambda i: i - 1, (1,))
+    near = swap(near_own, 1)
+    later_images = next_images(image_embed[cut_images:])
+    later_texts = next_texts(text_embed[cut_texts:])
     sums = call(functools.partial(own_kernel, factor), (kept, kept), (image_embed, text_embed))
+    sums = dict(enumerate(sums))
+    sums = step([(3, near_own, near)], sums)
+
+    images, texts = after(images, *sums.values()), after(texts, *sums.values())
+    swapped_images, swapped_texts = swap(images, 2), swap(texts, 2)
     sums = step(
-        [(0, image_embed, (near_text,)), (1, text_embed, (near_image,))],
-        dict(enumerate(sums)),
-    )
-
-    images = after(images, *sums.values())
-    later_images = next_images(after(image_embed[cut_images:], images))
-    sums |= step([(1, text_embed, (images, *swap(images, 2)))], {1: sums[1]})
-    texts = after(texts, *sums.values())
-    later_texts = next_texts(after(text_embed[cut_texts:], texts))
-    sums |= step([(0, image_embed, (texts, *swap(texts, 2)))], {0: sums[0]})
+        [
+            (0, image_embed, (texts, *swapped_texts)),
+            (1, text_embed, (images, *swapped_images)),
+        ],
+        sums,
+    )
     sums = step([(2, far_own, (after(far, sums[0]),))], sums)
 
     images, texts = after(later_images, sums[0]), after(later_texts, sums[0])
-    swapped_images, swapped_texts = swap(images, 2), swap(texts, 1)
-    sums = step([(1, text_embed, (images,)), (0, image_embed, (texts,))], sums)
+    swapped_images, swapped_texts = swap(images, 1), swap(texts, 1)
+    sums = step(
+        [
+            (0, image_embed, (texts,)),
+            (1, text_embed, (images,)),
+        ],
+        sums,
+    )
     operands = (image_embed, *swapped_texts, sums[0], text_embed, *swapped_images, sums[1])
     return call(
-        functools.partial(last_kernel, factor, (1, 2)),
+        functools.partial(last_kernel, factor, (1, 1)),
         (grad, grad),
         operands,
         [kept, kept, depth((texts,)), depth((images,))]

time: 74.3 us -> 71.3 us (0.960)
  waiting for transfers between devices: 36.3 us -> 40 us
  starting transfers between devices: 15.9 us -> 12.5 us
  Pallas kernels: 20.6 us -> 17.6 us
    ppermute x14 -> x12, waiting for transfers between devices: 36.3 us -> 40 us  [send(): lax.ppermute(block, AXIS, [(i, target(i) % count) for i in range(count)])]
    ppermute x14 -> x12, starting transfers between devices: 15.9 us -> 12.5 us  [send(): lax.ppermute(block, AXIS, [(i, target(i) % count) for i in range(count)])]
    pallas_call x9 -> x7, Pallas kernels: 20.6 us -> 17.6 us  [call(): pl.pallas_call(kernel, out_shape=tuple(outs), in_specs=[in_spec] * len(op...]
  transfers between devices with their start and end apart: 14 -> 12, of which waited for: 6 -> 9; matrix products, arithmetic and copies ran while one was open for 0% -> 0% of each run, Pallas kernels for 24% -> 17%
where the time goes in v8:
time: 71.3 us; the launch traced here: 71.2 us
  waiting for transfers between devices  40 us (56%)
  Pallas kernels  17.6 us (25%)
  starting transfers between devices  12.5 us (18%)
  between operations  0.91 us (1%)
    ppermute x12, waiting for transfers between devices, send(): lax.ppermute(block, AXIS, [(i, target(i) % count) for i in range(count)])  40 us
    pallas_call x7, Pallas kernels, call(): pl.pallas_call(kernel, out_shape=tuple(outs), in_specs=[in_spec] * len(op...  17.6 us
    ppermute x12, starting transfers between devices, send(): lax.ppermute(block, AXIS, [(i, target(i) % count) for i in range(count)])  12.5 us
  transfers between devices with their start and end apart: 12, of which 9 were waited for; matrix products, arithmetic and copies ran while one was open for 0% of the time, Pallas kernels for 17%

profile of v8, /device:TPU:0, one launch (start us, length us, event | category | flops | bytes accessed | tf_op | source)
XLA Modules:
  0.0 71.2 jit_solution(7706322982912268216)
XLA Ops:
  0.6 0.0 copy-start
  0.6 2.2 %shard_map.41 = (bf16[256,1152]{1,0:T(8,128)(2,1)S(1)}, bf16[256,1152]{1,0:T(8,128)(2,1)S(1)}, bf16[512,1152]{1,0:T(8,128)(2,1)S(1)}, bf16[512,1152]{1,0:T(8,128)(2,1)S(1)}) custom-call(bf16[512,1152]{1,0:T(8,128)(2,1)} %refs_0_.5, bf16[512,1152]{1,0:T(8,128)(2,1)} %refs_3_.1), custom_call_target="tpu_custom_call" | custom-call | flops 1 | bytes 1 | tf_op jit(solution)/shard_map/pallas_call | solution.py:168
  2.8 0.5 collective-permute-start.3
  3.3 5.6 %collective-permute-start.6 = (bf16[256,1152]{1,0:T(8,128)(2,1)S(1)}, bf16[256,1152]{1,0:T(8,128)(2,1)S(1)}, u32[]{:S(2)}, u32[]{:S(2)}) collective-permute-start(bf16[256,1152]{1,0:T(8,128)(2,1)S(1)} %get-tuple-element.29), channel_id=1, source_target_pairs={{0,28},{2,30},{4,0},{6,2},{8,4},{10,6},{12,8},{14,10},{16,12},{18,... | collective-permute-start | bytes 1769480 | tf_op jit(solution)/shard_map/ppermute | solution.py:24
  9.0 0.0 collective-permute-start.2
  9.0 0.6 collective-permute-start.1
  9.6 4.2 %collective-permute-start.10 = (bf16[256,1152]{1,0:T(8,128)(2,1)S(1)}, bf16[256,1152]{1,0:T(8,128)(2,1)S(1)}, u32[]{:S(2)}, u32[]{:S(2)}) collective-permute-start(bf16[256,1152]{1,0:T(8,128)(2,1)S(1)} %slice.7), channel_id=1, source_target_pairs={{0,28},{2,30},{4,0},{6,2},{8,4},{10,6},{12,8},{14,10},{16,12},{18,... | collective-permute-start | bytes 1769480 | tf_op jit(solution)/shard_map/ppermute | solution.py:24
  13.8 3.2 %shard_map.42 = (f32[512,1152]{1,0:T(8,128)S(1)}, f32[512,1152]{1,0:T(8,128)S(1)}) custom-call(bf16[512,1152]{1,0:T(8,128)(2,1)S(1)} %copy-done, bf16[512,1152]{1,0:T(8,128)(2,1)S(1)} %copy-done.1), custom_call_target="tpu_custom_call" | custom-call | flops 1 | bytes 1 | tf_op jit(solution)/shard_map/pallas_call | solution.py:168
  17.1 0.0 collective-permute-done.3.refs_1_
  17.1 0.3 collective-permute-start
  17.4 1.9 %shard_map.43 = (f32[512,1152]{1,0:T(8,128)S(1)}, f32[512,1152]{1,0:T(8,128)S(1)}) custom-call(bf16[512,1152]{1,0:T(8,128)(2,1)S(1)} %get-tuple-element.23.refs_0_, bf16[512,1152]{1,0:T(8,128)(2,1)S(1)} %collective-permute-done.3.refs_1_, f32[512,1152]{1,0:T(8,128)S(1)} %get-tuple-element.24.refs_2_, ...), custom_call_target="tpu_custom_call", output_to_operand_aliasing={{0}: (2, {}), {1}: (3, {})} | custom-call | flops 1 | bytes 1 | tf_op jit(solution)/shard_map/pallas_call | solution.py:168
  19.2 13.5 %collective-permute-done.6.refs_5_ = bf16[256,1152]{1,0:T(8,128)(2,1)S(1)} collective-permute-done((bf16[256,1152]{1,0:T(8,128)(2,1)S(1)}, bf16[256,1152]{1,0:T(8,128)(2,1)S(1)}, u32[]{:S(2)}, u32[]{:S(2)}) %collective-permute-start.6) | collective-permute-done | bytes 589856 | tf_op jit(solution)/shard_map/ppermute | solution.py:24
  32.8 0.1 collective-permute-start.7
  32.9 4.8 %collective-permute-done.2.refs_1_ = bf16[256,1152]{1,0:T(8,128)(2,1)S(1)} collective-permute-done((bf16[256,1152]{1,0:T(8,128)(2,1)S(1)}, bf16[256,1152]{1,0:T(8,128)(2,1)S(1)}, u32[]{:S(2)}, u32[]{:S(2)}) %collective-permute-start.2) | collective-permute-done | bytes 589856 | tf_op jit(solution)/shard_map/ppermute | solution.py:24
  37.7 0.0 collective-permute-start.8
  37.7 0.0 collective-permute-done.7.refs_6_
  37.7 0.6 collective-permute-start.4
  38.3 0.9 %collective-permute-done.8.refs_7_ = bf16[128,1152]{1,0:T(8,128)(2,1)S(1)} collective-permute-done((bf16[128,1152]{1,0:T(8,128)(2,1)S(1)}, bf16[128,1152]{1,0:T(8,128)(2,1)S(1)}, u32[]{:S(2)}, u32[]{:S(2)}) %collective-permute-start.8) | collective-permute-done | bytes 294944 | tf_op jit(solution)/shard_map/ppermute | solution.py:24
  39.2 0.1 collective-permute-start.5
  39.4 0.3 collective-permute-done.4.refs_2_
  39.7 1.2 %collective-permute-done.5.refs_3_ = bf16[128,1152]{1,0:T(8,128)(2,1)S(1)} collective-permute-done((bf16[128,1152]{1,0:T(8,128)(2,1)S(1)}, bf16[128,1152]{1,0:T(8,128)(2,1)S(1)}, u32[]{:S(2)}, u32[]{:S(2)}) %collective-permute-start.5) | collective-permute-done | bytes 294944 | tf_op jit(solution)/shard_map/ppermute | solution.py:24
  40.8 3.4 %shard_map.44 = (f32[512,1152]{1,0:T(8,128)S(1)}, f32[512,1152]{1,0:T(8,128)S(1)}) custom-call(bf16[512,1152]{1,0:T(8,128)(2,1)S(1)} %copy-done, bf16[256,1152]{1,0:T(8,128)(2,1)S(1)} %collective-permute-done.2.refs_1_, bf16[128,1152]{1,0:T(8,128)(2,1)S(1)} %collective-permute-done.4.refs_2_, ...), custom_call_target="tpu_custom_call", output_to_operand_aliasing={{0}: (8, {}), {1}: (9, {})} | custom-call | flops 1 | bytes 1 | tf_op jit(solution)/shard_map/pallas_call | solution.py:168
  44.3 3.7 %collective-permute-done.1.refs_1_ = bf16[512,1152]{1,0:T(8,128)(2,1)S(1)} collective-permute-done((bf16[512,1152]{1,0:T(8,128)(2,1)S(1)}, bf16[512,1152]{1,0:T(8,128)(2,1)S(1)}, u32[]{:S(2)}, u32[]{:S(2)}) %collective-permute-start.1) | collective-permute-done | bytes 1179680 | tf_op jit(solution)/shard_map/ppermute | solution.py:24
  47.9 1.9 %shard_map.45 = (f32[512,1152]{1,0:T(8,128)S(1)}, f32[512,1152]{1,0:T(8,128)S(1)}) custom-call(bf16[512,1152]{1,0:T(8,128)(2,1)S(1)} %get-tuple-element.21.refs_0_, bf16[512,1152]{1,0:T(8,128)(2,1)S(1)} %collective-permute-done.1.refs_1_, f32[512,1152]{1,0:T(8,128)S(1)} %get-tuple-element.31.refs_2_, ...), custom_call_target="tpu_custom_call", output_to_operand_aliasing={{0}: (2, {}), {1}: (3, {})} | custom-call | flops 1 | bytes 1 | tf_op jit(solution)/shard_map/pallas_call | solution.py:168
  49.8 10.3 %collective-permute-done.10.refs_3_ = bf16[256,1152]{1,0:T(8,128)(2,1)S(1)} collective-permute-done((bf16[256,1152]{1,0:T(8,128)(2,1)S(1)}, bf16[256,1152]{1,0:T(8,128)(2,1)S(1)}, u32[]{:S(2)}, u32[]{:S(2)}) %collective-permute-start.10) | collective-permute-done | bytes 589856 | tf_op jit(solution)/shard_map/ppermute | solution.py:24
  60.1 4.9 %collective-permute-done.refs_1_ = bf16[256,1152]{1,0:T(8,128)(2,1)S(1)} collective-permute-done((bf16[256,1152]{1,0:T(8,128)(2,1)S(1)}, bf16[256,1152]{1,0:T(8,128)(2,1)S(1)}, u32[]{:S(2)}, u32[]{:S(2)}) %collective-permute-start) | collective-permute-done | bytes 589856 | tf_op jit(solution)/shard_map/ppermute | solution.py:24
  65.0 0.0 collective-permute-start.11
  65.0 0.5 collective-permute-start.9
  65.5 2.0 %shard_map.46 = (f32[512,1152]{1,0:T(8,128)S(1)}, f32[512,1152]{1,0:T(8,128)S(1)}) custom-call(bf16[512,1152]{1,0:T(8,128)(2,1)S(1)} %copy-done, bf16[256,1152]{1,0:T(8,128)(2,1)S(1)} %collective-permute-done.refs_1_, bf16[512,1152]{1,0:T(8,128)(2,1)S(1)} %copy-done.1, ...), custom_call_target="tpu_custom_call", output_to_operand_aliasing={{0}: (4, {}), {1}: (5, {})} | custom-call | flops 1 | bytes 1 | tf_op jit(solution)/shard_map/pallas_call | solution.py:168
  67.5 0.0 collective-permute-done.11.refs_4_
  67.5 0.4 collective-permute-done.9.refs_1_
  67.9 3.1 %shard_map.47 = (f32[512,1152]{1,0:T(8,128)}, f32[512,1152]{1,0:T(8,128)}) custom-call(bf16[512,1152]{1,0:T(8,128)(2,1)S(1)} %copy-done, bf16[256,1152]{1,0:T(8,128)(2,1)S(1)} %collective-permute-done.9.refs_1_, f32[512,1152]{1,0:T(8,128)S(1)} %get-tuple-element.38.refs_2_, bf16[512,1152]{1,0:T(8,128)(2,1)S(1)} %copy-done.1, ...), custom_call_target="tpu_custom_call" | custom-call | flops 1 | bytes 1 | tf_op jit(solution)/shard_map/pallas_call | solution.py:168
  (7 shorter events, 0.2 us)
Async XLA Ops:
  0.6 8.9 %copy-start = (bf16[512,1152]{1,0:T(8,128)(2,1)S(1)}, bf16[512,1152]{1,0:T(8,128)(2,1)}, u32[]{:S(2)}) copy-start(bf16[512,1152]{1,0:T(8,128)(2,1)} %refs_0_.5) | copy-start | bytes 3538948
  0.6 13.2 %copy-start.1 = (bf16[512,1152]{1,0:T(8,128)(2,1)S(1)}, bf16[512,1152]{1,0:T(8,128)(2,1)}, u32[]{:S(2)}) copy-start(bf16[512,1152]{1,0:T(8,128)(2,1)} %refs_3_.1) | copy-start | bytes 3538948
  2.8 14.2 %collective-permute-start.3 = (bf16[512,1152]{1,0:T(8,128)(2,1)S(1)}, bf16[512,1152]{1,0:T(8,128)(2,1)S(1)}, u32[]{:S(2)}, u32[]{:S(2)}) collective-permute-start(bf16[512,1152]{1,0:T(8,128)(2,1)S(1)} %get-tuple-element.23.refs_0_), channel_id=1, source_target_pairs={{0,2},{2,0},{4,6},{6,4},{8,10},{10,8},{12,14},{14,12},{16,18},{18,... | collective-permute-start | bytes 3538952 | tf_op jit(solution)/shard_map/ppermute | solution.py:24
  3.3 29.4 %collective-permute-start.6 = (bf16[256,1152]{1,0:T(8,128)(2,1)S(1)}, bf16[256,1152]{1,0:T(8,128)(2,1)S(1)}, u32[]{:S(2)}, u32[]{:S(2)}) collective-permute-start(bf16[256,1152]{1,0:T(8,128)(2,1)S(1)} %get-tuple-element.29), channel_id=1, source_target_pairs={{0,28},{2,30},{4,0},{6,2},{8,4},{10,6},{12,8},{14,10},{16,12},{18,... | collective-permute-start | bytes 1769480 | tf_op jit(solution)/shard_map/ppermute | solution.py:24
  9.0 28.7 %collective-permute-start.2 = (bf16[256,1152]{1,0:T(8,128)(2,1)S(1)}, bf16[256,1152]{1,0:T(8,128)(2,1)S(1)}, u32[]{:S(2)}, u32[]{:S(2)}) collective-permute-start(bf16[256,1152]{1,0:T(8,128)(2,1)S(1)} %get-tuple-element.22), channel_id=1, source_target_pairs={{0,4},{2,6},{4,8},{6,10},{8,12},{10,14},{12,16},{14,18},{16,20},{1... | collective-permute-start | bytes 1769480 | tf_op jit(solution)/shard_map/ppermute | solution.py:24
  9.0 39.0 %collective-permute-start.1 = (bf16[512,1152]{1,0:T(8,128)(2,1)S(1)}, bf16[512,1152]{1,0:T(8,128)(2,1)S(1)}, u32[]{:S(2)}, u32[]{:S(2)}) collective-permute-start(bf16[512,1152]{1,0:T(8,128)(2,1)S(1)} %get-tuple-element.21.refs_0_), channel_id=1, source_target_pairs={{0,26},{2,8},{4,30},{6,12},{8,2},{10,16},{12,6},{14,20},{16,10},{1... | collective-permute-start | bytes 3538952 | tf_op jit(solution)/shard_map/ppermute | solution.py:24
  9.6 50.6 %collective-permute-start.10 = (bf16[256,1152]{1,0:T(8,128)(2,1)S(1)}, bf16[256,1152]{1,0:T(8,128)(2,1)S(1)}, u32[]{:S(2)}, u32[]{:S(2)}) collective-permute-start(bf16[256,1152]{1,0:T(8,128)(2,1)S(1)} %slice.7), channel_id=1, source_target_pairs={{0,28},{2,30},{4,0},{6,2},{8,4},{10,6},{12,8},{14,10},{16,12},{18,... | collective-permute-start | bytes 1769480 | tf_op jit(solution)/shard_map/ppermute | solution.py:24
  17.1 48.0 %collective-permute-start = (bf16[256,1152]{1,0:T(8,128)(2,1)S(1)}, bf16[256,1152]{1,0:T(8,128)(2,1)S(1)}, u32[]{:S(2)}, u32[]{:S(2)}) collective-permute-start(bf16[256,1152]{1,0:T(8,128)(2,1)S(1)} %slice.6), channel_id=1, source_target_pairs={{0,4},{2,6},{4,8},{6,10},{8,12},{10,14},{12,16},{14,18},{16,20},{1... | collective-permute-start | bytes 1769480 | tf_op jit(solution)/shard_map/ppermute | solution.py:24
  32.8 4.9 %collective-permute-start.7 = (bf16[128,1152]{1,0:T(8,128)(2,1)S(1)}, bf16[128,1152]{1,0:T(8,128)(2,1)S(1)}, u32[]{:S(2)}, u32[]{:S(2)}) collective-permute-start(bf16[128,1152]{1,0:T(8,128)(2,1)S(1)} %get-tuple-element.41), channel_id=1, source_target_pairs={{0,2},{2,0},{4,6},{6,4},{8,10},{10,8},{12,14},{14,12},{16,18},{18,... | collective-permute-start | bytes 884744 | tf_op jit(solution)/shard_map/ppermute | solution.py:24
  37.7 1.6 %collective-permute-start.8 = (bf16[128,1152]{1,0:T(8,128)(2,1)S(1)}, bf16[128,1152]{1,0:T(8,128)(2,1)S(1)}, u32[]{:S(2)}, u32[]{:S(2)}) collective-permute-start(bf16[128,1152]{1,0:T(8,128)(2,1)S(1)} %get-tuple-element.40), channel_id=1, source_target_pairs={{0,2},{2,0},{4,6},{6,4},{8,10},{10,8},{12,14},{14,12},{16,18},{18,... | collective-permute-start | bytes 884744 | tf_op jit(solution)/shard_map/ppermute | solution.py:24
  37.7 1.9 %collective-permute-start.4 = (bf16[128,1152]{1,0:T(8,128)(2,1)S(1)}, bf16[128,1152]{1,0:T(8,128)(2,1)S(1)}, u32[]{:S(2)}, u32[]{:S(2)}) collective-permute-start(bf16[128,1152]{1,0:T(8,128)(2,1)S(1)} %get-tuple-element.43), channel_id=1, source_target_pairs={{0,2},{2,0},{4,6},{6,4},{8,10},{10,8},{12,14},{14,12},{16,18},{18,... | collective-permute-start | bytes 884744 | tf_op jit(solution)/shard_map/ppermute | solution.py:24
  39.2 1.6 %collective-permute-start.5 = (bf16[128,1152]{1,0:T(8,128)(2,1)S(1)}, bf16[128,1152]{1,0:T(8,128)(2,1)S(1)}, u32[]{:S(2)}, u32[]{:S(2)}) collective-permute-start(bf16[128,1152]{1,0:T(8,128)(2,1)S(1)} %get-tuple-element.42), channel_id=1, source_target_pairs={{0,2},{2,0},{4,6},{6,4},{8,10},{10,8},{12,14},{14,12},{16,18},{18,... | collective-permute-start | bytes 884744 | tf_op jit(solution)/shard_map/ppermute | solution.py:24
  65.0 2.5 %collective-permute-start.11 = (bf16[256,1152]{1,0:T(8,128)(2,1)S(1)}, bf16[256,1152]{1,0:T(8,128)(2,1)S(1)}, u32[]{:S(2)}, u32[]{:S(2)}) collective-permute-start(bf16[256,1152]{1,0:T(8,128)(2,1)S(1)} %collective-permute-done.10.refs_3_), channel_id=1, source_target_pairs={{0,2},{2,0},{4,6},{6,4},{8,10},{10,8},{12,14},{14,12},{16,18},{18,... | collective-permute-start | bytes 1769480 | tf_op jit(solution)/shard_map/ppermute | solution.py:24
  65.0 2.8 %collective-permute-start.9 = (bf16[256,1152]{1,0:T(8,128)(2,1)S(1)}, bf16[256,1152]{1,0:T(8,128)(2,1)S(1)}, u32[]{:S(2)}, u32[]{:S(2)}) collective-permute-start(bf16[256,1152]{1,0:T(8,128)(2,1)S(1)} %collective-permute-done.refs_1_), channel_id=1, source_target_pairs={{0,2},{2,0},{4,6},{6,4},{8,10},{10,8},{12,14},{14,12},{16,18},{18,... | collective-permute-start | bytes 1769480 | tf_op jit(solution)/shard_map/ppermute | solution.py:24

commit v9 on v8

--- a/solution.py
+++ b/solution.py
@@ -66,25 +66,30 @@
     return joined.at[pl.ds(0, start)]
 
 
-def pick_kernel(image_ref, text_ref, image_head, text_head, far_own, near_own, sems):
-    def move(k, source, out):
-        return pltpu.make_async_copy(source.at[pl.ds(0, out.shape[0])], out, sems.at[k])
-
-    heads = [move(0, image_ref, image_head), move(1, text_ref, text_head)]
-    for head in heads:
-        head.start()
+def pick_kernel(image_ref, text_ref, *refs):
+    outs, sems = refs[:2], refs[2]
+    copies = []
+    for k, (source, out) in enumerate(zip((image_ref, text_ref), outs)):
+        rows = pl.ds(0, out.shape[0])
+        copies.append(pltpu.make_async_copy(source.at[rows], out, sems.at[k]))
+        copies[-1].start()
+    for copy in copies:
+        copy.wait()
+
+
+def core_pick_kernel(image_ref, text_ref, far_own, near_own, sems):
     for is_core, (far, near) in enumerate(((image_ref, text_ref), (text_ref, image_ref))):
 
         @pl.when(core() == is_core)
         def _():
-            blocks = [move(2, far, far_own), move(3, near, near_own)]
-            for block in blocks:
-                block.start()
-            for block in blocks:
-                block.wait()
-
-    for head in heads:
-        head.wait()
+            copies = [
+                pltpu.make_async_copy(far, far_own, sems.at[0]),
+                pltpu.make_async_copy(near, near_own, sems.at[1]),
+            ]
+            for copy in copies:
+                copy.start()
+            for copy in copies:
+                copy.wait()
 
 
 def own_kernel(factor, image_ref, text_ref, image_sum, text_sum):
@@ -120,10 +125,16 @@
             add(side - 2, value * (1.0 - is_1))
             add(3 - side, value * is_1)
 
+    def meet(side, own, visitors, scratch):
+        others = join(visitors, scratch)
+        if side == 3:
+            others = others.at[pl.ds((1 - core()) * own.shape[0], own.shape[0])]
+        return own, others, functools.partial(use, side)
+
     add_all(
         factor,
         [
-            (own, join(visitors, scratch), functools.partial(use, side))
+            meet(side, own, visitors, scratch)
             for (side, _), (own, visitors), scratch in zip(units, parts, joined)
         ],
     )
@@ -208,26 +219,30 @@
     in_hbm = [pltpu.with_memory_space_constraint(x, pltpu.HBM) for x in (image_embed, text_embed)]
     cut_images, cut_texts = rows * FIRST_IMAGES // 16, rows * FIRST_TEXTS // 16
     heads = (cut_images, cut_texts)
-    image_head, text_head, far_own, near_own = call(
+    image_head, text_head = call(
         pick_kernel,
-        [pltpu.VMEM((head, width), dtype) for head in heads] + [block, block],
+        [pltpu.VMEM((head, width), dtype) for head in heads],
         in_hbm,
-        [pltpu.SemaphoreType.DMA((4,))],
+        [pltpu.SemaphoreType.DMA((2,))],
         in_spec=ANY,
     )
     images, texts = next_images(image_head), next_texts(text_head)
+    far_own, near_own = call(
+        core_pick_kernel, [block, block], in_hbm, [pltpu.SemaphoreType.DMA((2,))], in_spec=ANY
+    )
     far = send(far_own, lambda i: i + 3 if i % 2 else i - 3)
-    near = swap(near_own, 1)
+    pairs = [[i, i + 1] for i in range(0, lax.axis_size(AXIS), 2)]
+    near = [lax.all_gather(near_own, AXIS, axis_index_groups=pairs, tiled=True)]
     later_images = next_images(image_embed[cut_images:])
     later_texts = next_texts(text_embed[cut_texts:])
     sums = call(functools.partial(own_kernel, factor), (kept, kept), (image_embed, text_embed))
     sums = dict(enumerate(sums))
-    sums = step([(3, near_own, near)], sums)
 
     images, texts = after(images, *sums.values()), after(texts, *sums.values())
     swapped_images, swapped_texts = swap(images, 2), swap(texts, 2)
     sums = step(
         [
+            (3, near_own, near),
             (0, image_embed, (texts, *swapped_texts)),
             (1, text_embed, (images, *swapped_images)),
         ],

time: 71.3 us -> 88 us (1.23)
  waiting for transfers between devices: 40 us -> 18.9 us
  local copies, waits for them, and re-layouts: 0.19 us -> 19.5 us
  between operations: 0.91 us -> 14.2 us
  Pallas kernels: 17.6 us -> 23.9 us
  starting transfers between devices: 12.5 us -> 10.6 us
    ppermute x12 -> x11, waiting for transfers between devices: 40 us -> 18.9 us  [send(): lax.ppermute(block, AXIS, [(i, target(i) % count) for i in range(count)])]
    unnamed x4 -> x34, local copies, waits for them, and re-layouts: 0.01 us -> 17.6 us
    pallas_call x7, Pallas kernels: 17.6 us -> 23.9 us  [call(): pl.pallas_call(kernel, out_shape=tuple(outs), in_specs=[in_spec] * len(op...]
    ppermute x12 -> x11, starting transfers between devices: 12.5 us -> 10.6 us  [send(): lax.ppermute(block, AXIS, [(i, target(i) % count) for i in range(count)])]
    slice x1, local copies, waits for them, and re-layouts: 0.05 us -> 0.93 us  [local(): later_texts = next_texts(text_embed[cut_texts:])]
  transfers between devices with their start and end apart: 12 -> 12, of which waited for: 9 -> 4; matrix products, arithmetic and copies ran while one was open for 0% -> 2% of each run, Pallas kernels for 17% -> 20%
where the time goes in v9:
time: 88 us; the launch traced here: 87.2 us
  Pallas kernels  23.9 us (27%)
  local copies, waits for them, and re-layouts  19.5 us (22%)
  waiting for transfers between devices  18.9 us (21%)
  between operations  14.2 us (16%)
  starting transfers between devices  10.6 us (12%)
    pallas_call x7, Pallas kernels, call(): pl.pallas_call(kernel, out_shape=tuple(outs), in_specs=[in_spec] * len(op...  23.9 us
    ppermute x11, waiting for transfers between devices, send(): lax.ppermute(block, AXIS, [(i, target(i) % count) for i in range(count)])  18.9 us
    unnamed x34, local copies, waits for them, and re-layouts  17.6 us
    ppermute x11, starting transfers between devices, send(): lax.ppermute(block, AXIS, [(i, target(i) % count) for i in range(count)])  10.6 us
  transfers between devices with their start and end apart: 12, of which 4 were waited for; matrix products, arithmetic and copies ran while one was open for 2% of the time, Pallas kernels for 20%

profile of v9, /device:TPU:0, one launch (start us, length us, event | category | flops | bytes accessed | tf_op | source)
XLA Modules:
  0.0 87.2 jit_solution(3576980870539617753)
XLA Ops:
  7.2 3.1 %shard_map.41 = (bf16[512,1152]{1,0:T(8,128)(2,1)}, bf16[512,1152]{1,0:T(8,128)(2,1)}) custom-call(bf16[512,1152]{1,0:T(8,128)(2,1)} %refs_0_.3, bf16[512,1152]{1,0:T(8,128)(2,1)} %refs_3_.1), custom_call_target="tpu_custom_call" | custom-call | flops 1 | bytes 1 | tf_op jit(solution)/shard_map/pallas_call | solution.py:179
  10.4 1.4 %shard_map.42 = (bf16[256,1152]{1,0:T(8,128)(2,1)S(1)}, bf16[256,1152]{1,0:T(8,128)(2,1)S(1)}) custom-call(bf16[512,1152]{1,0:T(8,128)(2,1)} %refs_0_.3, bf16[512,1152]{1,0:T(8,128)(2,1)} %refs_3_.1), custom_call_target="tpu_custom_call" | custom-call | flops 1 | bytes 1 | tf_op jit(solution)/shard_map/pallas_call | solution.py:179
  11.8 3.0 %collective-permute-start.2 = (bf16[256,1152]{1,0:T(8,128)(2,1)S(1)}, bf16[256,1152]{1,0:T(8,128)(2,1)S(1)}, u32[]{:S(2)}, u32[]{:S(2)}) collective-permute-start(bf16[256,1152]{1,0:T(8,128)(2,1)S(1)} %get-tuple-element.21), channel_id=1, source_target_pairs={{0,4},{2,6},{4,8},{6,10},{8,12},{10,14},{12,16},{14,18},{16,20},{1... | collective-permute-start | bytes 1769480 | tf_op jit(solution)/shard_map/ppermute | solution.py:24
  14.8 3.1 %collective-permute-start.5 = (bf16[256,1152]{1,0:T(8,128)(2,1)S(1)}, bf16[256,1152]{1,0:T(8,128)(2,1)S(1)}, u32[]{:S(2)}, u32[]{:S(2)}) collective-permute-start(bf16[256,1152]{1,0:T(8,128)(2,1)S(1)} %get-tuple-element.25), channel_id=1, source_target_pairs={{0,28},{2,30},{4,0},{6,2},{8,4},{10,6},{12,8},{14,10},{16,12},{18,... | collective-permute-start | bytes 1769480 | tf_op jit(solution)/shard_map/ppermute | solution.py:24
  17.9 0.8 collective-permute-start.1
  18.7 0.9 slice.7
  19.6 1.2 %collective-permute-start.9 = (bf16[256,1152]{1,0:T(8,128)(2,1)}, bf16[256,1152]{1,0:T(8,128)(2,1)}, u32[]{:S(2)}, u32[]{:S(2)}) collective-permute-start(bf16[256,1152]{1,0:T(8,128)(2,1)} %slice.7), channel_id=1, source_target_pairs={{0,28},{2,30},{4,0},{6,2},{8,4},{10,6},{12,8},{14,10},{16,12},{18,... | collective-permute-start | bytes 1769480 | tf_op jit(solution)/shard_map/ppermute | solution.py:24
  20.7 0.9 %slice.6 = bf16[256,1152]{1,0:T(8,128)(2,1)} slice(bf16[512,1152]{1,0:T(8,128)(2,1)S(1)} %copy-done.1), slice={[256:512], [0:1152]} | slice | bytes 1179648 | tf_op jit(solution)/shard_map/slice | solution.py:237
  21.7 0.8 collective-permute-start
  22.5 3.2 %shard_map.43 = (f32[512,1152]{1,0:T(8,128)S(1)}, f32[512,1152]{1,0:T(8,128)S(1)}) custom-call(bf16[512,1152]{1,0:T(8,128)(2,1)S(1)} %copy-done, bf16[512,1152]{1,0:T(8,128)(2,1)S(1)} %copy-done.1), custom_call_target="tpu_custom_call" | custom-call | flops 1 | bytes 1 | tf_op jit(solution)/shard_map/pallas_call | solution.py:179
  25.7 1.4 %copy-done.2 = f32[512,1152]{1,0:T(8,128)} copy-done((f32[512,1152]{1,0:T(8,128)}, f32[512,1152]{1,0:T(8,128)S(1)}, u32[]{:S(2)}) %copy-start.2) | copy-done | bytes 2359320
  27.1 1.4 %copy-done.6 = f32[512,1152]{1,0:T(8,128)} copy-done((f32[512,1152]{1,0:T(8,128)}, f32[512,1152]{1,0:T(8,128)S(1)}, u32[]{:S(2)}) %copy-start.6) | copy-done | bytes 2359320
  28.5 17.4 %collective-permute-done.2.refs_3_ = bf16[256,1152]{1,0:T(8,128)(2,1)S(1)} collective-permute-done((bf16[256,1152]{1,0:T(8,128)(2,1)S(1)}, bf16[256,1152]{1,0:T(8,128)(2,1)S(1)}, u32[]{:S(2)}, u32[]{:S(2)}) %collective-permute-start.2) | collective-permute-done | bytes 589856 | tf_op jit(solution)/shard_map/ppermute | solution.py:24
  46.1 0.5 collective-permute-start.4
  46.6 1.0 %collective-permute-done.3.refs_4_ = bf16[128,1152]{1,0:T(8,128)(2,1)S(1)} collective-permute-done((bf16[128,1152]{1,0:T(8,128)(2,1)S(1)}, bf16[128,1152]{1,0:T(8,128)(2,1)S(1)}, u32[]{:S(2)}, u32[]{:S(2)}) %collective-permute-start.3) | collective-permute-done | bytes 294944 | tf_op jit(solution)/shard_map/ppermute | solution.py:24
  47.6 0.7 copy-done.9
  48.5 0.7 copy-done.11
  49.9 0.7 copy-done.13
  50.8 0.7 copy-done.15
  51.5 1.7 %copy-done.3 = f32[512,1152]{1,0:T(8,128)S(1)} copy-done((f32[512,1152]{1,0:T(8,128)S(1)}, f32[512,1152]{1,0:T(8,128)}, u32[]{:S(2)}) %copy-start.3) | copy-done | bytes 2359320
  53.2 1.7 %copy-done.7 = f32[512,1152]{1,0:T(8,128)S(1)} copy-done((f32[512,1152]{1,0:T(8,128)S(1)}, f32[512,1152]{1,0:T(8,128)}, u32[]{:S(2)}) %copy-start.7) | copy-done | bytes 2359320
  54.9 1.7 %copy-done.8 = bf16[1024,1152]{1,0:T(8,128)(2,1)S(1)} copy-done((bf16[1024,1152]{1,0:T(8,128)(2,1)S(1)}, bf16[1024,1152]{1,0:T(8,128)(2,1)}, u32[]{:S(2)}) %copy-start.8) | copy-done | bytes 2359320
  56.5 1.0 %copy-done.10 = bf16[128,1152]{1,0:T(8,128)(2,1)S(1)} copy-done((bf16[128,1152]{1,0:T(8,128)(2,1)S(1)}, bf16[128,1152]{1,0:T(8,128)(2,1)}, u32[]{:S(2)}) %copy-start.10) | copy-done | bytes 294936
  57.5 1.0 %copy-done.12 = bf16[128,1152]{1,0:T(8,128)(2,1)S(1)} copy-done((bf16[128,1152]{1,0:T(8,128)(2,1)S(1)}, bf16[128,1152]{1,0:T(8,128)(2,1)}, u32[]{:S(2)}) %copy-start.12) | copy-done | bytes 294936
  58.5 1.0 %copy-done.14 = bf16[128,1152]{1,0:T(8,128)(2,1)S(1)} copy-done((bf16[128,1152]{1,0:T(8,128)(2,1)S(1)}, bf16[128,1152]{1,0:T(8,128)(2,1)}, u32[]{:S(2)}) %copy-start.14) | copy-done | bytes 294936
  59.4 1.0 %copy-done.16 = bf16[128,1152]{1,0:T(8,128)(2,1)S(1)} copy-done((bf16[128,1152]{1,0:T(8,128)(2,1)S(1)}, bf16[128,1152]{1,0:T(8,128)(2,1)}, u32[]{:S(2)}) %copy-start.16) | copy-done | bytes 294936
  60.4 6.4 %shard_map.44 = (f32[512,1152]{1,0:T(8,128)S(1)}, f32[512,1152]{1,0:T(8,128)S(1)}) custom-call(bf16[512,1152]{1,0:T(8,128)(2,1)} %get-tuple-element.20.refs_0_, bf16[1024,1152]{1,0:T(8,128)(2,1)S(1)} %copy-done.8, bf16[512,1152]{1,0:T(8,128)(2,1)S(1)} %copy-done, ...), custom_call_target="tpu_custom_call", output_to_operand_aliasing={{0}: (10, {}), {1}: (11, {})} | custom-call | flops 1 | bytes 1 | tf_op jit(solution)/shard_map/pallas_call | solution.py:179
  66.8 1.4 %copy-done.4 = f32[512,1152]{1,0:T(8,128)} copy-done((f32[512,1152]{1,0:T(8,128)}, f32[512,1152]{1,0:T(8,128)S(1)}, u32[]{:S(2)}) %copy-start.4) | copy-done | bytes 2359320
  68.2 1.7 %copy-done.5 = f32[512,1152]{1,0:T(8,128)S(1)} copy-done((f32[512,1152]{1,0:T(8,128)S(1)}, f32[512,1152]{1,0:T(8,128)}, u32[]{:S(2)}) %copy-start.5) | copy-done | bytes 2359320
  69.9 3.5 %shard_map.45 = (f32[512,1152]{1,0:T(8,128)S(1)}, f32[512,1152]{1,0:T(8,128)S(1)}) custom-call(bf16[512,1152]{1,0:T(8,128)(2,1)} %get-tuple-element.19.refs_0_, bf16[512,1152]{1,0:T(8,128)(2,1)} %collective-permute-done.1.refs_1_, f32[512,1152]{1,0:T(8,128)S(1)} %copy-done.5, ...), custom_call_target="tpu_custom_call", output_to_operand_aliasing={{0}: (2, {}), {1}: (3, {})} | custom-call | flops 1 | bytes 1 | tf_op jit(solution)/shard_map/pallas_call | solution.py:179
  74.0 3.2 %shard_map.46 = (f32[512,1152]{1,0:T(8,128)S(1)}, f32[512,1152]{1,0:T(8,128)S(1)}) custom-call(bf16[512,1152]{1,0:T(8,128)(2,1)S(1)} %copy-done, bf16[256,1152]{1,0:T(8,128)(2,1)} %collective-permute-done.refs_1_, bf16[512,1152]{1,0:T(8,128)(2,1)S(1)} %copy-done.1, ...), custom_call_target="tpu_custom_call", output_to_operand_aliasing={{0}: (4, {}), {1}: (5, {})} | custom-call | flops 1 | bytes 1 | tf_op jit(solution)/shard_map/pallas_call | solution.py:179
  77.2 3.1 %shard_map.47 = (f32[512,1152]{1,0:T(8,128)}, f32[512,1152]{1,0:T(8,128)}) custom-call(bf16[512,1152]{1,0:T(8,128)(2,1)S(1)} %copy-done, bf16[256,1152]{1,0:T(8,128)(2,1)S(1)} %collective-permute-done.8.refs_1_, f32[512,1152]{1,0:T(8,128)S(1)} %get-tuple-element.34.refs_2_, bf16[512,1152]{1,0:T(8,128)(2,1)S(1)} %copy-done.1, ...), custom_call_target="tpu_custom_call" | custom-call | flops 1 | bytes 1 | tf_op jit(solution)/shard_map/pallas_call | solution.py:179
  (38 shorter events, 1.9 us)
Async XLA Ops:
  7.2 44.4 %all-gather.2.cloned.1.call-start = ((), (), s32[]{:S(2)}) async-start(), calls=%async_computation | async-start | bytes 3538944 | tf_op jit(solution)/shard_map/all_gather | solution.py:235
  10.3 8.4 %copy-start = (bf16[512,1152]{1,0:T(8,128)(2,1)S(1)}, bf16[512,1152]{1,0:T(8,128)(2,1)}, u32[]{:S(2)}) copy-start(bf16[512,1152]{1,0:T(8,128)(2,1)} %refs_0_.3) | copy-start | bytes 3538948
  10.3 10.4 %copy-start.1 = (bf16[512,1152]{1,0:T(8,128)(2,1)S(1)}, bf16[512,1152]{1,0:T(8,128)(2,1)}, u32[]{:S(2)}) copy-start(bf16[512,1152]{1,0:T(8,128)(2,1)} %refs_3_.1) | copy-start | bytes 3538948
  11.8 34.2 %collective-permute-start.2 = (bf16[256,1152]{1,0:T(8,128)(2,1)S(1)}, bf16[256,1152]{1,0:T(8,128)(2,1)S(1)}, u32[]{:S(2)}, u32[]{:S(2)}) collective-permute-start(bf16[256,1152]{1,0:T(8,128)(2,1)S(1)} %get-tuple-element.21), channel_id=1, source_target_pairs={{0,4},{2,6},{4,8},{6,10},{8,12},{10,14},{12,16},{14,18},{16,20},{1... | collective-permute-start | bytes 1769480 | tf_op jit(solution)/shard_map/ppermute | solution.py:24
  14.8 31.3 %collective-permute-start.5 = (bf16[256,1152]{1,0:T(8,128)(2,1)S(1)}, bf16[256,1152]{1,0:T(8,128)(2,1)S(1)}, u32[]{:S(2)}, u32[]{:S(2)}) collective-permute-start(bf16[256,1152]{1,0:T(8,128)(2,1)S(1)} %get-tuple-element.25), channel_id=1, source_target_pairs={{0,28},{2,30},{4,0},{6,2},{8,4},{10,6},{12,8},{14,10},{16,12},{18,... | collective-permute-start | bytes 1769480 | tf_op jit(solution)/shard_map/ppermute | solution.py:24
  17.9 50.3 %collective-permute-start.1 = (bf16[512,1152]{1,0:T(8,128)(2,1)}, bf16[512,1152]{1,0:T(8,128)(2,1)}, u32[]{:S(2)}, u32[]{:S(2)}) collective-permute-start(bf16[512,1152]{1,0:T(8,128)(2,1)} %get-tuple-element.19.refs_0_), channel_id=1, source_target_pairs={{0,26},{2,8},{4,30},{6,12},{8,2},{10,16},{12,6},{14,20},{16,10},{1... | collective-permute-start | bytes 3538952 | tf_op jit(solution)/shard_map/ppermute | solution.py:24
  19.6 53.8 %collective-permute-start.9 = (bf16[256,1152]{1,0:T(8,128)(2,1)}, bf16[256,1152]{1,0:T(8,128)(2,1)}, u32[]{:S(2)}, u32[]{:S(2)}) collective-permute-start(bf16[256,1152]{1,0:T(8,128)(2,1)} %slice.7), channel_id=1, source_target_pairs={{0,28},{2,30},{4,0},{6,2},{8,4},{10,6},{12,8},{14,10},{16,12},{18,... | collective-permute-start | bytes 1769480 | tf_op jit(solution)/shard_map/ppermute | solution.py:24
  21.7 51.7 %collective-permute-start = (bf16[256,1152]{1,0:T(8,128)(2,1)}, bf16[256,1152]{1,0:T(8,128)(2,1)}, u32[]{:S(2)}, u32[]{:S(2)}) collective-permute-start(bf16[256,1152]{1,0:T(8,128)(2,1)} %slice.6), channel_id=1, source_target_pairs={{0,4},{2,6},{4,8},{6,10},{8,12},{10,14},{12,16},{14,18},{16,20},{1... | collective-permute-start | bytes 1769480 | tf_op jit(solution)/shard_map/ppermute | solution.py:24
  25.7 1.4 %copy-start.2 = (f32[512,1152]{1,0:T(8,128)}, f32[512,1152]{1,0:T(8,128)S(1)}, u32[]{:S(2)}) copy-start(f32[512,1152]{1,0:T(8,128)S(1)} %get-tuple-element.22.refs_10_) | copy-start | bytes 7077892
  27.1 1.4 %copy-start.6 = (f32[512,1152]{1,0:T(8,128)}, f32[512,1152]{1,0:T(8,128)S(1)}, u32[]{:S(2)}) copy-start(f32[512,1152]{1,0:T(8,128)S(1)} %get-tuple-element.23.refs_11_) | copy-start | bytes 7077892
  46.0 1.6 %collective-permute-start.3 = (bf16[128,1152]{1,0:T(8,128)(2,1)S(1)}, bf16[128,1152]{1,0:T(8,128)(2,1)S(1)}, u32[]{:S(2)}, u32[]{:S(2)}) collective-permute-start(bf16[128,1152]{1,0:T(8,128)(2,1)S(1)} %get-tuple-element.39), channel_id=1, source_target_pairs={{0,2},{2,0},{4,6},{6,4},{8,10},{10,8},{12,14},{14,12},{16,18},{18,... | collective-permute-start | bytes 884744 | tf_op jit(solution)/shard_map/ppermute | solution.py:24
  46.1 2.4 %collective-permute-start.4 = (bf16[128,1152]{1,0:T(8,128)(2,1)S(1)}, bf16[128,1152]{1,0:T(8,128)(2,1)S(1)}, u32[]{:S(2)}, u32[]{:S(2)}) collective-permute-start(bf16[128,1152]{1,0:T(8,128)(2,1)S(1)} %get-tuple-element.38), channel_id=1, source_target_pairs={{0,2},{2,0},{4,6},{6,4},{8,10},{10,8},{12,14},{14,12},{16,18},{18,... | collective-permute-start | bytes 884744 | tf_op jit(solution)/shard_map/ppermute | solution.py:24
  47.6 0.7 copy-start.9
  48.4 1.6 %collective-permute-start.6 = (bf16[128,1152]{1,0:T(8,128)(2,1)S(1)}, bf16[128,1152]{1,0:T(8,128)(2,1)S(1)}, u32[]{:S(2)}, u32[]{:S(2)}) collective-permute-start(bf16[128,1152]{1,0:T(8,128)(2,1)S(1)} %get-tuple-element.37), channel_id=1, source_target_pairs={{0,2},{2,0},{4,6},{6,4},{8,10},{10,8},{12,14},{14,12},{16,18},{18,... | collective-permute-start | bytes 884744 | tf_op jit(solution)/shard_map/ppermute | solution.py:24
  48.5 0.7 copy-start.11
  49.2 1.6 %collective-permute-start.7 = (bf16[128,1152]{1,0:T(8,128)(2,1)S(1)}, bf16[128,1152]{1,0:T(8,128)(2,1)S(1)}, u32[]{:S(2)}, u32[]{:S(2)}) collective-permute-start(bf16[128,1152]{1,0:T(8,128)(2,1)S(1)} %get-tuple-element.36), channel_id=1, source_target_pairs={{0,2},{2,0},{4,6},{6,4},{8,10},{10,8},{12,14},{14,12},{16,18},{18,... | collective-permute-start | bytes 884744 | tf_op jit(solution)/shard_map/ppermute | solution.py:24
  49.9 0.7 copy-start.13
  50.8 0.7 copy-start.15
  51.5 1.7 %copy-start.3 = (f32[512,1152]{1,0:T(8,128)S(1)}, f32[512,1152]{1,0:T(8,128)}, u32[]{:S(2)}) copy-start(f32[512,1152]{1,0:T(8,128)} %copy-done.2) | copy-start | bytes 7077892
  53.2 1.7 %copy-start.7 = (f32[512,1152]{1,0:T(8,128)S(1)}, f32[512,1152]{1,0:T(8,128)}, u32[]{:S(2)}) copy-start(f32[512,1152]{1,0:T(8,128)} %copy-done.6) | copy-start | bytes 7077892
  54.9 1.7 %copy-start.8 = (bf16[1024,1152]{1,0:T(8,128)(2,1)S(1)}, bf16[1024,1152]{1,0:T(8,128)(2,1)}, u32[]{:S(2)}) copy-start(bf16[1024,1152]{1,0:T(8,128)(2,1)} %all-gather.2.cloned.1.call-done.refs_1_) | copy-start | bytes 7077892
  56.5 1.0 %copy-start.10 = (bf16[128,1152]{1,0:T(8,128)(2,1)S(1)}, bf16[128,1152]{1,0:T(8,128)(2,1)}, u32[]{:S(2)}) copy-start(bf16[128,1152]{1,0:T(8,128)(2,1)} %copy-done.9) | copy-start | bytes 884740
  57.5 1.0 %copy-start.12 = (bf16[128,1152]{1,0:T(8,128)(2,1)S(1)}, bf16[128,1152]{1,0:T(8,128)(2,1)}, u32[]{:S(2)}) copy-start(bf16[128,1152]{1,0:T(8,128)(2,1)} %copy-done.11) | copy-start | bytes 884740
  58.5 1.0 %copy-start.14 = (bf16[128,1152]{1,0:T(8,128)(2,1)S(1)}, bf16[128,1152]{1,0:T(8,128)(2,1)}, u32[]{:S(2)}) copy-start(bf16[128,1152]{1,0:T(8,128)(2,1)} %copy-done.13) | copy-start | bytes 884740
  59.4 1.0 %copy-start.16 = (bf16[128,1152]{1,0:T(8,128)(2,1)S(1)}, bf16[128,1152]{1,0:T(8,128)(2,1)}, u32[]{:S(2)}) copy-start(bf16[128,1152]{1,0:T(8,128)(2,1)} %copy-done.15) | copy-start | bytes 884740
  66.8 1.4 %copy-start.4 = (f32[512,1152]{1,0:T(8,128)}, f32[512,1152]{1,0:T(8,128)S(1)}, u32[]{:S(2)}) copy-start(f32[512,1152]{1,0:T(8,128)S(1)} %get-tuple-element.27.refs_2_) | copy-start | bytes 7077892
  68.2 1.7 %copy-start.5 = (f32[512,1152]{1,0:T(8,128)S(1)}, f32[512,1152]{1,0:T(8,128)}, u32[]{:S(2)}) copy-start(f32[512,1152]{1,0:T(8,128)} %copy-done.4) | copy-start | bytes 7077892
  73.4 3.8 %collective-permute-start.10 = (bf16[256,1152]{1,0:T(8,128)(2,1)}, bf16[256,1152]{1,0:T(8,128)(2,1)S(1)}, u32[]{:S(2)}, u32[]{:S(2)}) collective-permute-start(bf16[256,1152]{1,0:T(8,128)(2,1)} %collective-permute-done.9.refs_3_), channel_id=1, source_target_pairs={{0,2},{2,0},{4,6},{6,4},{8,10},{10,8},{12,14},{14,12},{16,18},{18,... | collective-permute-start | bytes 1769480 | tf_op jit(solution)/shard_map/ppermute | solution.py:24
  73.8 3.4 %collective-permute-start.8 = (bf16[256,1152]{1,0:T(8,128)(2,1)}, bf16[256,1152]{1,0:T(8,128)(2,1)S(1)}, u32[]{:S(2)}, u32[]{:S(2)}) collective-permute-start(bf16[256,1152]{1,0:T(8,128)(2,1)} %collective-permute-done.refs_1_), channel_id=1, source_target_pairs={{0,2},{2,0},{4,6},{6,4},{8,10},{10,8},{12,14},{14,12},{16,18},{18,... | collective-permute-start | bytes 1769480 | tf_op jit(solution)/shard_map/ppermute | solution.py:24
Sparse Core Ops, SparseCore 0:
  10.5 13.6 all-gather.1

commit v10 on v8

--- a/solution.py
+++ b/solution.py
@@ -11,6 +11,7 @@
 AXIS = "blk"
 FIRST_IMAGES = 8
 FIRST_TEXTS = 8
+NEAR_PARTS = 1
 LAST_TILE = 256
 COPY_ROWS = 128
 VMEM_MIB = 32
@@ -87,7 +88,8 @@
         head.wait()
 
 
-def own_kernel(factor, image_ref, text_ref, image_sum, text_sum):
+def own_kernel(factor, image_ref, text_ref, near_own, *refs):
+    near, (image_sum, text_sum, joined) = refs[:NEAR_PARTS], refs[NEAR_PARTS:]
     rows = image_ref.shape[0]
     shape = (rows, rows)
     matched = lax.broadcasted_iota(jnp.int32, shape, 0) == lax.broadcasted_iota(
@@ -96,6 +98,13 @@
     for own, others, total in ((image_ref, text_ref, image_sum), (text_ref, image_ref, text_sum)):
         chance = 1.0 / (1.0 + decay(factor, logits(own, others)))
         total[...] = product(chance - matched.astype(jnp.float32), others)
+    is_1 = core().astype(jnp.float32)
+
+    def use(value):
+        image_sum[...] += value * is_1
+        text_sum[...] += value * (1.0 - is_1)
+
+    add_all(factor, [(near_own, join(near, joined), use)])
 
 
 def step_kernel(factor, units, sides, *refs):
@@ -220,9 +229,13 @@
     near = swap(near_own, 1)
     later_images = next_images(image_embed[cut_images:])
     later_texts = next_texts(text_embed[cut_texts:])
-    sums = call(functools.partial(own_kernel, factor), (kept, kept), (image_embed, text_embed))
+    sums = call(
+        functools.partial(own_kernel, factor),
+        (kept, kept),
+        (image_embed, text_embed, near_own, *near),
+        [block],
+    )
     sums = dict(enumerate(sums))
-    sums = step([(3, near_own, near)], sums)
 
     images, texts = after(images, *sums.values()), after(texts, *sums.values())
     swapped_images, swapped_texts = swap(images, 2), swap(texts, 2)

time: 71.3 us -> 71.2 us (level)
  waiting for transfers between devices: 40 us -> 40.8 us
    ppermute x12, waiting for transfers between devices: 40 us -> 40.8 us  [send(): lax.ppermute(block, AXIS, [(i, target(i) % count) for i in range(count)])]
    pallas_call x7 -> x6, Pallas kernels: 17.6 us -> 17 us  [call(): pl.pallas_call(kernel, out_shape=tuple(outs), in_specs=[in_spec] * len(op...]
  transfers between devices with their start and end apart: 12 -> 12, of which waited for: 9 -> 9; matrix products, arithmetic and copies ran while one was open for 0% -> 0% of each run, Pallas kernels for 17% -> 16%
where the time goes in v10:
time: 71.2 us; the launch traced here: 71 us
  waiting for transfers between devices  40.8 us (57%)
  Pallas kernels  17 us (24%)
  starting transfers between devices  12.3 us (17%)
  between operations  0.74 us (1%)
    ppermute x12, waiting for transfers between devices, send(): lax.ppermute(block, AXIS, [(i, target(i) % count) for i in range(count)])  40.8 us
    pallas_call x6, Pallas kernels, call(): pl.pallas_call(kernel, out_shape=tuple(outs), in_specs=[in_spec] * len(op...  17 us
    ppermute x12, starting transfers between devices, send(): lax.ppermute(block, AXIS, [(i, target(i) % count) for i in range(count)])  12.3 us
  transfers between devices with their start and end apart: 12, of which 9 were waited for; matrix products, arithmetic and copies ran while one was open for 0% of the time, Pallas kernels for 16%

profile of v10, /device:TPU:0, one launch (start us, length us, event | category | flops | bytes accessed | tf_op | source)
XLA Modules:
  0.0 71.0 jit_solution(17249663410237733245)
XLA Ops:
  0.6 0.0 copy-start.1
  0.6 2.2 %shard_map.41 = (bf16[256,1152]{1,0:T(8,128)(2,1)S(1)}, bf16[256,1152]{1,0:T(8,128)(2,1)S(1)}, bf16[512,1152]{1,0:T(8,128)(2,1)S(1)}, bf16[512,1152]{1,0:T(8,128)(2,1)S(1)}) custom-call(bf16[512,1152]{1,0:T(8,128)(2,1)} %refs_0_.5, bf16[512,1152]{1,0:T(8,128)(2,1)} %refs_3_.1), custom_call_target="tpu_custom_call" | custom-call | flops 1 | bytes 1 | tf_op jit(solution)/shard_map/pallas_call | solution.py:177
  2.8 0.5 collective-permute-start.3
  3.3 5.6 %collective-permute-start.6 = (bf16[256,1152]{1,0:T(8,128)(2,1)S(1)}, bf16[256,1152]{1,0:T(8,128)(2,1)S(1)}, u32[]{:S(2)}, u32[]{:S(2)}) collective-permute-start(bf16[256,1152]{1,0:T(8,128)(2,1)S(1)} %get-tuple-element.25), channel_id=1, source_target_pairs={{0,28},{2,30},{4,0},{6,2},{8,4},{10,6},{12,8},{14,10},{16,12},{18,... | collective-permute-start | bytes 1769480 | tf_op jit(solution)/shard_map/ppermute | solution.py:25
  9.0 0.0 collective-permute-start.2
  9.0 0.6 collective-permute-start.1
  9.5 0.0 copy-done.1
  9.6 4.2 %collective-permute-start.10 = (bf16[256,1152]{1,0:T(8,128)(2,1)S(1)}, bf16[256,1152]{1,0:T(8,128)(2,1)S(1)}, u32[]{:S(2)}, u32[]{:S(2)}) collective-permute-start(bf16[256,1152]{1,0:T(8,128)(2,1)S(1)} %slice.7), channel_id=1, source_target_pairs={{0,28},{2,30},{4,0},{6,2},{8,4},{10,6},{12,8},{14,10},{16,12},{18,... | collective-permute-start | bytes 1769480 | tf_op jit(solution)/shard_map/ppermute | solution.py:25
  13.8 0.0 collective-permute-done.3.refs_0_
  13.9 0.1 collective-permute-start
  14.0 4.4 %shard_map.42 = (f32[512,1152]{1,0:T(8,128)S(1)}, f32[512,1152]{1,0:T(8,128)S(1)}) custom-call(bf16[512,1152]{1,0:T(8,128)(2,1)S(1)} %copy-done.1, bf16[512,1152]{1,0:T(8,128)(2,1)S(1)} %copy-done, bf16[512,1152]{1,0:T(8,128)(2,1)S(1)} %get-tuple-element.21.near_own, bf16[512,1152]{1,0:T(8,128)(2,1)S(1)} %collective-permute-done.3.refs_0_), custom_call_target="tpu_custom_call" | custom-call | flops 1 | bytes 1 | tf_op jit(solution)/shard_map/pallas_call | solution.py:177
  18.4 14.3 %collective-permute-done.6.refs_5_ = bf16[256,1152]{1,0:T(8,128)(2,1)S(1)} collective-permute-done((bf16[256,1152]{1,0:T(8,128)(2,1)S(1)}, bf16[256,1152]{1,0:T(8,128)(2,1)S(1)}, u32[]{:S(2)}, u32[]{:S(2)}) %collective-permute-start.6) | collective-permute-done | bytes 589856 | tf_op jit(solution)/shard_map/ppermute | solution.py:25
  32.8 0.1 collective-permute-start.7
  32.9 4.8 %collective-permute-done.2.refs_1_ = bf16[256,1152]{1,0:T(8,128)(2,1)S(1)} collective-permute-done((bf16[256,1152]{1,0:T(8,128)(2,1)S(1)}, bf16[256,1152]{1,0:T(8,128)(2,1)S(1)}, u32[]{:S(2)}, u32[]{:S(2)}) %collective-permute-start.2) | collective-permute-done | bytes 589856 | tf_op jit(solution)/shard_map/ppermute | solution.py:25
  37.7 0.0 collective-permute-start.8
  37.7 0.0 collective-permute-done.7.refs_6_
  37.7 0.6 collective-permute-start.4
  38.3 0.9 %collective-permute-done.8.refs_7_ = bf16[128,1152]{1,0:T(8,128)(2,1)S(1)} collective-permute-done((bf16[128,1152]{1,0:T(8,128)(2,1)S(1)}, bf16[128,1152]{1,0:T(8,128)(2,1)S(1)}, u32[]{:S(2)}, u32[]{:S(2)}) %collective-permute-start.8) | collective-permute-done | bytes 294944 | tf_op jit(solution)/shard_map/ppermute | solution.py:25
  39.2 0.1 collective-permute-start.5
  39.4 0.3 collective-permute-done.4.refs_2_
  39.7 1.2 %collective-permute-done.5.refs_3_ = bf16[128,1152]{1,0:T(8,128)(2,1)S(1)} collective-permute-done((bf16[128,1152]{1,0:T(8,128)(2,1)S(1)}, bf16[128,1152]{1,0:T(8,128)(2,1)S(1)}, u32[]{:S(2)}, u32[]{:S(2)}) %collective-permute-start.5) | collective-permute-done | bytes 294944 | tf_op jit(solution)/shard_map/ppermute | solution.py:25
  40.8 3.4 %shard_map.43 = (f32[512,1152]{1,0:T(8,128)S(1)}, f32[512,1152]{1,0:T(8,128)S(1)}) custom-call(bf16[512,1152]{1,0:T(8,128)(2,1)S(1)} %copy-done.1, bf16[256,1152]{1,0:T(8,128)(2,1)S(1)} %collective-permute-done.2.refs_1_, bf16[128,1152]{1,0:T(8,128)(2,1)S(1)} %collective-permute-done.4.refs_2_, ...), custom_call_target="tpu_custom_call", output_to_operand_aliasing={{0}: (8, {}), {1}: (9, {})} | custom-call | flops 1 | bytes 1 | tf_op jit(solution)/shard_map/pallas_call | solution.py:177
  44.3 3.7 %collective-permute-done.1.refs_1_ = bf16[512,1152]{1,0:T(8,128)(2,1)S(1)} collective-permute-done((bf16[512,1152]{1,0:T(8,128)(2,1)S(1)}, bf16[512,1152]{1,0:T(8,128)(2,1)S(1)}, u32[]{:S(2)}, u32[]{:S(2)}) %collective-permute-start.1) | collective-permute-done | bytes 1179680 | tf_op jit(solution)/shard_map/ppermute | solution.py:25
  47.9 1.9 %shard_map.44 = (f32[512,1152]{1,0:T(8,128)S(1)}, f32[512,1152]{1,0:T(8,128)S(1)}) custom-call(bf16[512,1152]{1,0:T(8,128)(2,1)S(1)} %get-tuple-element.19.refs_0_, bf16[512,1152]{1,0:T(8,128)(2,1)S(1)} %collective-permute-done.1.refs_1_, f32[512,1152]{1,0:T(8,128)S(1)} %get-tuple-element.27.refs_2_, ...), custom_call_target="tpu_custom_call", output_to_operand_aliasing={{0}: (2, {}), {1}: (3, {})} | custom-call | flops 1 | bytes 1 | tf_op jit(solution)/shard_map/pallas_call | solution.py:177
  49.8 10.3 %collective-permute-done.10.refs_3_ = bf16[256,1152]{1,0:T(8,128)(2,1)S(1)} collective-permute-done((bf16[256,1152]{1,0:T(8,128)(2,1)S(1)}, bf16[256,1152]{1,0:T(8,128)(2,1)S(1)}, u32[]{:S(2)}, u32[]{:S(2)}) %collective-permute-start.10) | collective-permute-done | bytes 589856 | tf_op jit(solution)/shard_map/ppermute | solution.py:25
  60.1 4.9 %collective-permute-done.refs_1_ = bf16[256,1152]{1,0:T(8,128)(2,1)S(1)} collective-permute-done((bf16[256,1152]{1,0:T(8,128)(2,1)S(1)}, bf16[256,1152]{1,0:T(8,128)(2,1)S(1)}, u32[]{:S(2)}, u32[]{:S(2)}) %collective-permute-start) | collective-permute-done | bytes 589856 | tf_op jit(solution)/shard_map/ppermute | solution.py:25
  65.0 0.0 collective-permute-start.11
  65.0 0.5 collective-permute-start.9
  65.5 1.9 %shard_map.45 = (f32[512,1152]{1,0:T(8,128)S(1)}, f32[512,1152]{1,0:T(8,128)S(1)}) custom-call(bf16[512,1152]{1,0:T(8,128)(2,1)S(1)} %copy-done.1, bf16[256,1152]{1,0:T(8,128)(2,1)S(1)} %collective-permute-done.refs_1_, bf16[512,1152]{1,0:T(8,128)(2,1)S(1)} %copy-done, ...), custom_call_target="tpu_custom_call", output_to_operand_aliasing={{0}: (4, {}), {1}: (5, {})} | custom-call | flops 1 | bytes 1 | tf_op jit(solution)/shard_map/pallas_call | solution.py:177
  67.5 0.0 collective-permute-done.11.refs_4_
  67.5 0.4 collective-permute-done.9.refs_1_
  67.9 3.1 %shard_map.46 = (f32[512,1152]{1,0:T(8,128)}, f32[512,1152]{1,0:T(8,128)}) custom-call(bf16[512,1152]{1,0:T(8,128)(2,1)S(1)} %copy-done.1, bf16[256,1152]{1,0:T(8,128)(2,1)S(1)} %collective-permute-done.9.refs_1_, f32[512,1152]{1,0:T(8,128)S(1)} %get-tuple-element.34.refs_2_, bf16[512,1152]{1,0:T(8,128)(2,1)S(1)} %copy-done, ...), custom_call_target="tpu_custom_call" | custom-call | flops 1 | bytes 1 | tf_op jit(solution)/shard_map/pallas_call | solution.py:177
  (6 shorter events, 0.2 us)
Async XLA Ops:
  0.6 8.9 %copy-start.1 = (bf16[512,1152]{1,0:T(8,128)(2,1)S(1)}, bf16[512,1152]{1,0:T(8,128)(2,1)}, u32[]{:S(2)}) copy-start(bf16[512,1152]{1,0:T(8,128)(2,1)} %refs_0_.5) | copy-start | bytes 3538948
  0.6 13.2 %copy-start = (bf16[512,1152]{1,0:T(8,128)(2,1)S(1)}, bf16[512,1152]{1,0:T(8,128)(2,1)}, u32[]{:S(2)}) copy-start(bf16[512,1152]{1,0:T(8,128)(2,1)} %refs_3_.1) | copy-start | bytes 3538948
  2.8 11.0 %collective-permute-start.3 = (bf16[512,1152]{1,0:T(8,128)(2,1)S(1)}, bf16[512,1152]{1,0:T(8,128)(2,1)S(1)}, u32[]{:S(2)}, u32[]{:S(2)}) collective-permute-start(bf16[512,1152]{1,0:T(8,128)(2,1)S(1)} %get-tuple-element.21.near_own), channel_id=1, source_target_pairs={{0,2},{2,0},{4,6},{6,4},{8,10},{10,8},{12,14},{14,12},{16,18},{18,... | collective-permute-start | bytes 3538952 | tf_op jit(solution)/shard_map/ppermute | solution.py:25
  3.3 29.4 %collective-permute-start.6 = (bf16[256,1152]{1,0:T(8,128)(2,1)S(1)}, bf16[256,1152]{1,0:T(8,128)(2,1)S(1)}, u32[]{:S(2)}, u32[]{:S(2)}) collective-permute-start(bf16[256,1152]{1,0:T(8,128)(2,1)S(1)} %get-tuple-element.25), channel_id=1, source_target_pairs={{0,28},{2,30},{4,0},{6,2},{8,4},{10,6},{12,8},{14,10},{16,12},{18,... | collective-permute-start | bytes 1769480 | tf_op jit(solution)/shard_map/ppermute | solution.py:25
  9.0 28.7 %collective-permute-start.2 = (bf16[256,1152]{1,0:T(8,128)(2,1)S(1)}, bf16[256,1152]{1,0:T(8,128)(2,1)S(1)}, u32[]{:S(2)}, u32[]{:S(2)}) collective-permute-start(bf16[256,1152]{1,0:T(8,128)(2,1)S(1)} %get-tuple-element.20), channel_id=1, source_target_pairs={{0,4},{2,6},{4,8},{6,10},{8,12},{10,14},{12,16},{14,18},{16,20},{1... | collective-permute-start | bytes 1769480 | tf_op jit(solution)/shard_map/ppermute | solution.py:25
  9.0 39.0 %collective-permute-start.1 = (bf16[512,1152]{1,0:T(8,128)(2,1)S(1)}, bf16[512,1152]{1,0:T(8,128)(2,1)S(1)}, u32[]{:S(2)}, u32[]{:S(2)}) collective-permute-start(bf16[512,1152]{1,0:T(8,128)(2,1)S(1)} %get-tuple-element.19.refs_0_), channel_id=1, source_target_pairs={{0,26},{2,8},{4,30},{6,12},{8,2},{10,16},{12,6},{14,20},{16,10},{1... | collective-permute-start | bytes 3538952 | tf_op jit(solution)/shard_map/ppermute | solution.py:25
  9.6 50.6 %collective-permute-start.10 = (bf16[256,1152]{1,0:T(8,128)(2,1)S(1)}, bf16[256,1152]{1,0:T(8,128)(2,1)S(1)}, u32[]{:S(2)}, u32[]{:S(2)}) collective-permute-start(bf16[256,1152]{1,0:T(8,128)(2,1)S(1)} %slice.7), channel_id=1, source_target_pairs={{0,28},{2,30},{4,0},{6,2},{8,4},{10,6},{12,8},{14,10},{16,12},{18,... | collective-permute-start | bytes 1769480 | tf_op jit(solution)/shard_map/ppermute | solution.py:25
  13.9 51.2 %collective-permute-start = (bf16[256,1152]{1,0:T(8,128)(2,1)S(1)}, bf16[256,1152]{1,0:T(8,128)(2,1)S(1)}, u32[]{:S(2)}, u32[]{:S(2)}) collective-permute-start(bf16[256,1152]{1,0:T(8,128)(2,1)S(1)} %slice.6), channel_id=1, source_target_pairs={{0,4},{2,6},{4,8},{6,10},{8,12},{10,14},{12,16},{14,18},{16,20},{1... | collective-permute-start | bytes 1769480 | tf_op jit(solution)/shard_map/ppermute | solution.py:25
  32.8 4.9 %collective-permute-start.7 = (bf16[128,1152]{1,0:T(8,128)(2,1)S(1)}, bf16[128,1152]{1,0:T(8,128)(2,1)S(1)}, u32[]{:S(2)}, u32[]{:S(2)}) collective-permute-start(bf16[128,1152]{1,0:T(8,128)(2,1)S(1)} %get-tuple-element.37), channel_id=1, source_target_pairs={{0,2},{2,0},{4,6},{6,4},{8,10},{10,8},{12,14},{14,12},{16,18},{18,... | collective-permute-start | bytes 884744 | tf_op jit(solution)/shard_map/ppermute | solution.py:25
  37.7 1.6 %collective-permute-start.8 = (bf16[128,1152]{1,0:T(8,128)(2,1)S(1)}, bf16[128,1152]{1,0:T(8,128)(2,1)S(1)}, u32[]{:S(2)}, u32[]{:S(2)}) collective-permute-start(bf16[128,1152]{1,0:T(8,128)(2,1)S(1)} %get-tuple-element.36), channel_id=1, source_target_pairs={{0,2},{2,0},{4,6},{6,4},{8,10},{10,8},{12,14},{14,12},{16,18},{18,... | collective-permute-start | bytes 884744 | tf_op jit(solution)/shard_map/ppermute | solution.py:25
  37.7 1.9 %collective-permute-start.4 = (bf16[128,1152]{1,0:T(8,128)(2,1)S(1)}, bf16[128,1152]{1,0:T(8,128)(2,1)S(1)}, u32[]{:S(2)}, u32[]{:S(2)}) collective-permute-start(bf16[128,1152]{1,0:T(8,128)(2,1)S(1)} %get-tuple-element.39), channel_id=1, source_target_pairs={{0,2},{2,0},{4,6},{6,4},{8,10},{10,8},{12,14},{14,12},{16,18},{18,... | collective-permute-start | bytes 884744 | tf_op jit(solution)/shard_map/ppermute | solution.py:25
  39.2 1.6 %collective-permute-start.5 = (bf16[128,1152]{1,0:T(8,128)(2,1)S(1)}, bf16[128,1152]{1,0:T(8,128)(2,1)S(1)}, u32[]{:S(2)}, u32[]{:S(2)}) collective-permute-start(bf16[128,1152]{1,0:T(8,128)(2,1)S(1)} %get-tuple-element.38), channel_id=1, source_target_pairs={{0,2},{2,0},{4,6},{6,4},{8,10},{10,8},{12,14},{14,12},{16,18},{18,... | collective-permute-start | bytes 884744 | tf_op jit(solution)/shard_map/ppermute | solution.py:25
  65.0 2.5 %collective-permute-start.11 = (bf16[256,1152]{1,0:T(8,128)(2,1)S(1)}, bf16[256,1152]{1,0:T(8,128)(2,1)S(1)}, u32[]{:S(2)}, u32[]{:S(2)}) collective-permute-start(bf16[256,1152]{1,0:T(8,128)(2,1)S(1)} %collective-permute-done.10.refs_3_), channel_id=1, source_target_pairs={{0,2},{2,0},{4,6},{6,4},{8,10},{10,8},{12,14},{14,12},{16,18},{18,... | collective-permute-start | bytes 1769480 | tf_op jit(solution)/shard_map/ppermute | solution.py:25
  65.0 2.8 %collective-permute-start.9 = (bf16[256,1152]{1,0:T(8,128)(2,1)S(1)}, bf16[256,1152]{1,0:T(8,128)(2,1)S(1)}, u32[]{:S(2)}, u32[]{:S(2)}) collective-permute-start(bf16[256,1152]{1,0:T(8,128)(2,1)S(1)} %collective-permute-done.refs_1_), channel_id=1, source_target_pairs={{0,2},{2,0},{4,6},{6,4},{8,10},{10,8},{12,14},{14,12},{16,18},{18,... | collective-permute-start | bytes 1769480 | tf_op jit(solution)/shard_map/ppermute | solution.py:25

commit v11 on v10

--- a/solution.py
+++ b/solution.py
@@ -67,25 +67,34 @@
     return joined.at[pl.ds(0, start)]
 
 
-def pick_kernel(image_ref, text_ref, image_head, text_head, far_own, near_own, sems):
+def pick_kernel(image_ref, text_ref, image_head, text_head, near_own, sems):
     def move(k, source, out):
         return pltpu.make_async_copy(source.at[pl.ds(0, out.shape[0])], out, sems.at[k])
 
     heads = [move(0, image_ref, image_head), move(1, text_ref, text_head)]
     for head in heads:
         head.start()
-    for is_core, (far, near) in enumerate(((image_ref, text_ref), (text_ref, image_ref))):
+    for is_core, near in enumerate((text_ref, image_ref)):
 
         @pl.when(core() == is_core)
         def _():
-            blocks = [move(2, far, far_own), move(3, near, near_own)]
-            for block in blocks:
-                block.start()
-            for block in blocks:
-                block.wait()
+            block = move(2, near, near_own)
+            block.start()
+            block.wait()
 
     for head in heads:
         head.wait()
+
+
+def far_pick_kernel(image_ref, text_ref, *refs):
+    far_own, sem = refs[-2:]
+    for is_core, far in enumerate((image_ref, text_ref)):
+
+        @pl.when(core() == is_core)
+        def _():
+            copy = pltpu.make_async_copy(far, far_own, sem)
+            copy.start()
+            copy.wait()
 
 
 def own_kernel(factor, image_ref, text_ref, near_own, *refs):
@@ -138,28 +147,36 @@
     )
 
 
-def last_kernel(factor, counts, *refs):
+def last_kernel(factor, counts, far_own, far, *refs):
     parts = []
     for count in counts:
         parts.append((refs[0], refs[1 : 1 + count], refs[1 + count]))
         refs = refs[2 + count :]
     outs, helds, joined, sems = refs[:2], refs[2:4], refs[4:6], refs[6]
+    starts = range(0, far_own.shape[0], LAST_TILE)
+    is_1 = core().astype(jnp.float32)
     copies = []
 
-    def use(total, held, out, start, value):
+    def use_far(start, value):
         rows = pl.ds(start, LAST_TILE)
-        held[rows] = (total[rows] + value) * factor
+        helds[0][rows] = parts[0][2][rows] + value * (1.0 - is_1)
+        helds[1][rows] = parts[1][2][rows] + value * is_1
+
+    def use(held, out, start, value):
+        rows = pl.ds(start, LAST_TILE)
+        held[rows] = (held[rows] + value) * factor
         for first in range(start, start + LAST_TILE, COPY_ROWS):
             span = pl.ds(first, COPY_ROWS)
             copies.append(pltpu.make_async_copy(held.at[span], out.at[span], sems.at[len(copies)]))
             copies[-1].start()
 
-    units = []
-    for (own, visitors, total), held, out, scratch in zip(parts, helds, outs, joined):
+    def unit(own, others, start, act, *args):
+        return (own.at[pl.ds(start, LAST_TILE)], others, functools.partial(act, *args, start))
+
+    units = [unit(far_own, far, start, use_far) for start in starts]
+    for (own, visitors, _), held, out, scratch in zip(parts, helds, outs, joined):
         others = join(visitors, scratch)
-        for start in range(0, own.shape[0], LAST_TILE):
-            act = functools.partial(use, total, held, out, start)
-            units.append((own.at[pl.ds(start, LAST_TILE)], others, act))
+        units += [unit(own, others, start, use, held, out) for start in starts]
     add_all(factor, units)
     for copy in copies:
         copy.wait()
@@ -217,16 +234,19 @@
     in_hbm = [pltpu.with_memory_space_constraint(x, pltpu.HBM) for x in (image_embed, text_embed)]
     cut_images, cut_texts = rows * FIRST_IMAGES // 16, rows * FIRST_TEXTS // 16
     heads = (cut_images, cut_texts)
-    image_head, text_head, far_own, near_own = call(
+    image_head, text_head, near_own = call(
         pick_kernel,
-        [pltpu.VMEM((head, width), dtype) for head in heads] + [block, block],
+        [pltpu.VMEM((head, width), dtype) for head in heads] + [block],
         in_hbm,
-        [pltpu.SemaphoreType.DMA((4,))],
+        [pltpu.SemaphoreType.DMA((3,))],
         in_spec=ANY,
     )
     images, texts = next_images(image_head), next_texts(text_head)
+    near = swap(near_own, 1)
+    (far_own,) = call(
+        far_pick_kernel, [block], in_hbm, [pltpu.SemaphoreType.DMA], in_spec=ANY
+    )
     far = send(far_own, lambda i: i + 3 if i % 2 else i - 3)
-    near = swap(near_own, 1)
     later_images = next_images(image_embed[cut_images:])
     later_texts = next_texts(text_embed[cut_texts:])
     sums = call(
@@ -246,7 +266,6 @@
         ],
         sums,
     )
-    sums = step([(2, far_own, (after(far, sums[0]),))], sums)
 
     images, texts = after(later_images, sums[0]), after(later_texts, sums[0])
     swapped_images, swapped_texts = swap(images, 1), swap(texts, 1)
@@ -258,6 +277,7 @@
         sums,
     )
     operands = (image_embed, *swapped_texts, sums[0], text_embed, *swapped_images, sums[1])
+    operands = (far_own, far, *operands)
     return call(
         functools.partial(last_kernel, factor, (1, 1)),
         (grad, grad),

time: 71.2 us -> 66.8 us (0.938)
  the two profiles are of different devices: /device:TPU:0 before, /device:TPU:5 now
where the time goes in v11:
time: 66.8 us; the launch traced here: 66.6 us
  waiting for transfers between devices  38 us (57%)
  Pallas kernels  17.2 us (26%)
  starting transfers between devices  10.4 us (16%)
  between operations  0.74 us (1%)
    ppermute x12, waiting for transfers between devices, send(): lax.ppermute(block, AXIS, [(i, target(i) % count) for i in range(count)])  38 us
    pallas_call x6, Pallas kernels, call(): pl.pallas_call(kernel, out_shape=tuple(outs), in_specs=[in_spec] * len(op...  17.2 us
    ppermute x12, starting transfers between devices, send(): lax.ppermute(block, AXIS, [(i, target(i) % count) for i in range(count)])  10.4 us
  transfers between devices with their start and end apart: 12, of which 8 were waited for; matrix products, arithmetic and copies ran while one was open for 0% of the time, Pallas kernels for 17%

profile of v11, /device:TPU:5, one launch (start us, length us, event | category | flops | bytes accessed | tf_op | source)
XLA Modules:
  0.0 66.6 jit_solution(10274516517957166017)
XLA Ops:
  0.6 0.0 copy-start
  0.6 0.0 copy-start.2
  0.7 1.8 %shard_map.42 = (bf16[256,1152]{1,0:T(8,128)(2,1)S(1)}, bf16[256,1152]{1,0:T(8,128)(2,1)S(1)}, bf16[512,1152]{1,0:T(8,128)(2,1)S(1)}) custom-call(bf16[512,1152]{1,0:T(8,128)(2,1)} %refs_0_.5, bf16[512,1152]{1,0:T(8,128)(2,1)} %refs_3_.1), custom_call_target="tpu_custom_call" | custom-call | flops 1 | bytes 1 | tf_op jit(solution)/shard_map/pallas_call | solution.py:194
  2.5 0.7 %collective-permute-start.3 = (bf16[512,1152]{1,0:T(8,128)(2,1)S(1)}, bf16[512,1152]{1,0:T(8,128)(2,1)S(1)}, u32[]{:S(2)}, u32[]{:S(2)}) collective-permute-start(bf16[512,1152]{1,0:T(8,128)(2,1)S(1)} %get-tuple-element.16.near_own), channel_id=1, source_target_pairs={{0,2},{2,0},{4,6},{6,4},{8,10},{10,8},{12,14},{14,12},{16,18},{18,... | collective-permute-start | bytes 3538952 | tf_op jit(solution)/shard_map/ppermute | solution.py:25
  3.2 0.0 collective-permute-start.6
  3.2 2.4 %collective-permute-start.2 = (bf16[256,1152]{1,0:T(8,128)(2,1)S(1)}, bf16[256,1152]{1,0:T(8,128)(2,1)S(1)}, u32[]{:S(2)}, u32[]{:S(2)}) collective-permute-start(bf16[256,1152]{1,0:T(8,128)(2,1)S(1)} %get-tuple-element.15), channel_id=1, source_target_pairs={{0,4},{2,6},{4,8},{6,10},{8,12},{10,14},{12,16},{14,18},{16,20},{1... | collective-permute-start | bytes 1769480 | tf_op jit(solution)/shard_map/ppermute | solution.py:25
  5.6 0.0 copy-start.1
  5.6 0.0 copy-start.3
  5.7 2.2 %collective-permute-start.10 = (bf16[256,1152]{1,0:T(8,128)(2,1)S(1)}, bf16[256,1152]{1,0:T(8,128)(2,1)S(1)}, u32[]{:S(2)}, u32[]{:S(2)}) collective-permute-start(bf16[256,1152]{1,0:T(8,128)(2,1)S(1)} %slice.7), channel_id=1, source_target_pairs={{0,28},{2,30},{4,0},{6,2},{8,4},{10,6},{12,8},{14,10},{16,12},{18,... | collective-permute-start | bytes 1769480 | tf_op jit(solution)/shard_map/ppermute | solution.py:25
  7.9 0.3 collective-permute-start.1
  8.2 1.3 %shard_map.41.far_own = bf16[512,1152]{1,0:T(8,128)(2,1)S(1)} custom-call(bf16[512,1152]{1,0:T(8,128)(2,1)} %refs_0_.5, bf16[512,1152]{1,0:T(8,128)(2,1)} %refs_3_.1), custom_call_target="tpu_custom_call" | custom-call | flops 1 | bytes 1 | tf_op jit(solution)/shard_map/pallas_call | solution.py:194
  9.5 2.4 %collective-permute-start = (bf16[512,1152]{1,0:T(8,128)(2,1)S(1)}, bf16[512,1152]{1,0:T(8,128)(2,1)S(1)}, u32[]{:S(2)}, u32[]{:S(2)}) collective-permute-start(bf16[512,1152]{1,0:T(8,128)(2,1)S(1)} %shard_map.41.far_own), channel_id=1, source_target_pairs={{0,26},{2,8},{4,30},{6,12},{8,2},{10,16},{12,6},{14,20},{16,10},{1... | collective-permute-start | bytes 3538952 | tf_op jit(solution)/shard_map/ppermute | solution.py:25
  11.9 4.4 %shard_map.43 = (f32[512,1152]{1,0:T(8,128)S(1)}, f32[512,1152]{1,0:T(8,128)S(1)}) custom-call(bf16[512,1152]{1,0:T(8,128)(2,1)S(1)} %copy-done.1, bf16[512,1152]{1,0:T(8,128)(2,1)S(1)} %copy-done.3, bf16[512,1152]{1,0:T(8,128)(2,1)S(1)} %get-tuple-element.16.near_own, bf16[512,1152]{1,0:T(8,128)(2,1)S(1)} %collective-permute-done.3.refs_0_), custom_call_target="tpu_custom_call" | custom-call | flops 1 | bytes 1 | tf_op jit(solution)/shard_map/pallas_call | solution.py:194
  16.3 25.0 %collective-permute-done.6.refs_5_ = bf16[256,1152]{1,0:T(8,128)(2,1)S(1)} collective-permute-done((bf16[256,1152]{1,0:T(8,128)(2,1)S(1)}, bf16[256,1152]{1,0:T(8,128)(2,1)S(1)}, u32[]{:S(2)}, u32[]{:S(2)}) %collective-permute-start.6) | collective-permute-done | bytes 589856 | tf_op jit(solution)/shard_map/ppermute | solution.py:25
  41.4 1.0 %collective-permute-start.7 = (bf16[128,1152]{1,0:T(8,128)(2,1)S(1)}, bf16[128,1152]{1,0:T(8,128)(2,1)S(1)}, u32[]{:S(2)}, u32[]{:S(2)}) collective-permute-start(bf16[128,1152]{1,0:T(8,128)(2,1)S(1)} %get-tuple-element.29), channel_id=1, source_target_pairs={{0,2},{2,0},{4,6},{6,4},{8,10},{10,8},{12,14},{14,12},{16,18},{18,... | collective-permute-start | bytes 884744 | tf_op jit(solution)/shard_map/ppermute | solution.py:25
  42.4 2.3 %collective-permute-done.2.refs_1_ = bf16[256,1152]{1,0:T(8,128)(2,1)S(1)} collective-permute-done((bf16[256,1152]{1,0:T(8,128)(2,1)S(1)}, bf16[256,1152]{1,0:T(8,128)(2,1)S(1)}, u32[]{:S(2)}, u32[]{:S(2)}) %collective-permute-start.2) | collective-permute-done | bytes 589856 | tf_op jit(solution)/shard_map/ppermute | solution.py:25
  44.7 0.5 collective-permute-start.8
  45.2 0.0 collective-permute-done.7.refs_6_
  45.2 0.1 collective-permute-start.4
  45.3 1.1 %collective-permute-done.8.refs_7_ = bf16[128,1152]{1,0:T(8,128)(2,1)S(1)} collective-permute-done((bf16[128,1152]{1,0:T(8,128)(2,1)S(1)}, bf16[128,1152]{1,0:T(8,128)(2,1)S(1)}, u32[]{:S(2)}, u32[]{:S(2)}) %collective-permute-start.8) | collective-permute-done | bytes 294944 | tf_op jit(solution)/shard_map/ppermute | solution.py:25
  46.4 0.4 collective-permute-start.5
  46.8 0.1 collective-permute-done.4.refs_2_
  46.9 1.1 %collective-permute-done.5.refs_3_ = bf16[128,1152]{1,0:T(8,128)(2,1)S(1)} collective-permute-done((bf16[128,1152]{1,0:T(8,128)(2,1)S(1)}, bf16[128,1152]{1,0:T(8,128)(2,1)S(1)}, u32[]{:S(2)}, u32[]{:S(2)}) %collective-permute-start.5) | collective-permute-done | bytes 294944 | tf_op jit(solution)/shard_map/ppermute | solution.py:25
  48.0 3.4 %shard_map.44 = (f32[512,1152]{1,0:T(8,128)S(1)}, f32[512,1152]{1,0:T(8,128)S(1)}) custom-call(bf16[512,1152]{1,0:T(8,128)(2,1)S(1)} %copy-done.1, bf16[256,1152]{1,0:T(8,128)(2,1)S(1)} %collective-permute-done.2.refs_1_, bf16[128,1152]{1,0:T(8,128)(2,1)S(1)} %collective-permute-done.4.refs_2_, ...), custom_call_target="tpu_custom_call", output_to_operand_aliasing={{0}: (8, {}), {1}: (9, {})} | custom-call | flops 1 | bytes 1 | tf_op jit(solution)/shard_map/pallas_call | solution.py:194
  51.4 2.6 %collective-permute-done.10.refs_3_ = bf16[256,1152]{1,0:T(8,128)(2,1)S(1)} collective-permute-done((bf16[256,1152]{1,0:T(8,128)(2,1)S(1)}, bf16[256,1152]{1,0:T(8,128)(2,1)S(1)}, u32[]{:S(2)}, u32[]{:S(2)}) %collective-permute-start.10) | collective-permute-done | bytes 589856 | tf_op jit(solution)/shard_map/ppermute | solution.py:25
  54.0 3.3 %collective-permute-done.1.refs_1_ = bf16[256,1152]{1,0:T(8,128)(2,1)S(1)} collective-permute-done((bf16[256,1152]{1,0:T(8,128)(2,1)S(1)}, bf16[256,1152]{1,0:T(8,128)(2,1)S(1)}, u32[]{:S(2)}, u32[]{:S(2)}) %collective-permute-start.1) | collective-permute-done | bytes 589856 | tf_op jit(solution)/shard_map/ppermute | solution.py:25
  57.3 0.4 collective-permute-start.11
  57.8 0.1 collective-permute-start.9
  57.8 1.9 %shard_map.45 = (f32[512,1152]{1,0:T(8,128)S(1)}, f32[512,1152]{1,0:T(8,128)S(1)}) custom-call(bf16[512,1152]{1,0:T(8,128)(2,1)S(1)} %copy-done.1, bf16[256,1152]{1,0:T(8,128)(2,1)S(1)} %collective-permute-done.1.refs_1_, bf16[512,1152]{1,0:T(8,128)(2,1)S(1)} %copy-done.3, ...), custom_call_target="tpu_custom_call", output_to_operand_aliasing={{0}: (4, {}), {1}: (5, {})} | custom-call | flops 1 | bytes 1 | tf_op jit(solution)/shard_map/pallas_call | solution.py:194
  59.8 2.5 %collective-permute-done.far = bf16[512,1152]{1,0:T(8,128)(2,1)S(1)} collective-permute-done((bf16[512,1152]{1,0:T(8,128)(2,1)S(1)}, bf16[512,1152]{1,0:T(8,128)(2,1)S(1)}, u32[]{:S(2)}, u32[]{:S(2)}) %collective-permute-start) | collective-permute-done | bytes 1179680 | tf_op jit(solution)/shard_map/ppermute | solution.py:25
  62.2 0.0 collective-permute-done.11.refs_4_
  62.3 4.4 %shard_map.46 = (f32[512,1152]{1,0:T(8,128)}, f32[512,1152]{1,0:T(8,128)}) custom-call(bf16[512,1152]{1,0:T(8,128)(2,1)S(1)} %shard_map.41.far_own, bf16[512,1152]{1,0:T(8,128)(2,1)S(1)} %collective-permute-done.far, bf16[512,1152]{1,0:T(8,128)(2,1)S(1)} %copy-done.1, bf16[256,1152]{1,0:T(8,128)(2,1)S(1)} %collective-permute-done.9.refs_1_, ...), custom_call_target="tpu_custom_call" | custom-call | flops 1 | bytes 1 | tf_op jit(solution)/shard_map/pallas_call | solution.py:194
  (10 shorter events, 0.2 us)
Async XLA Ops:
  0.6 4.9 %copy-start = (bf16[512,1152]{1,0:T(8,128)(2,1)S(1)}, bf16[512,1152]{1,0:T(8,128)(2,1)}, u32[]{:S(2)}) copy-start(bf16[512,1152]{1,0:T(8,128)(2,1)} %refs_0_.5) | copy-start | bytes 3538948
  0.6 7.2 %copy-start.2 = (bf16[512,1152]{1,0:T(8,128)(2,1)S(1)}, bf16[512,1152]{1,0:T(8,128)(2,1)}, u32[]{:S(2)}) copy-start(bf16[512,1152]{1,0:T(8,128)(2,1)} %refs_3_.1) | copy-start | bytes 3538948
  2.5 7.0 %collective-permute-start.3 = (bf16[512,1152]{1,0:T(8,128)(2,1)S(1)}, bf16[512,1152]{1,0:T(8,128)(2,1)S(1)}, u32[]{:S(2)}, u32[]{:S(2)}) collective-permute-start(bf16[512,1152]{1,0:T(8,128)(2,1)S(1)} %get-tuple-element.16.near_own), channel_id=1, source_target_pairs={{0,2},{2,0},{4,6},{6,4},{8,10},{10,8},{12,14},{14,12},{16,18},{18,... | collective-permute-start | bytes 3538952 | tf_op jit(solution)/shard_map/ppermute | solution.py:25
  3.2 38.2 %collective-permute-start.6 = (bf16[256,1152]{1,0:T(8,128)(2,1)S(1)}, bf16[256,1152]{1,0:T(8,128)(2,1)S(1)}, u32[]{:S(2)}, u32[]{:S(2)}) collective-permute-start(bf16[256,1152]{1,0:T(8,128)(2,1)S(1)} %get-tuple-element.20), channel_id=1, source_target_pairs={{0,28},{2,30},{4,0},{6,2},{8,4},{10,6},{12,8},{14,10},{16,12},{18,... | collective-permute-start | bytes 1769480 | tf_op jit(solution)/shard_map/ppermute | solution.py:25
  3.2 41.5 %collective-permute-start.2 = (bf16[256,1152]{1,0:T(8,128)(2,1)S(1)}, bf16[256,1152]{1,0:T(8,128)(2,1)S(1)}, u32[]{:S(2)}, u32[]{:S(2)}) collective-permute-start(bf16[256,1152]{1,0:T(8,128)(2,1)S(1)} %get-tuple-element.15), channel_id=1, source_target_pairs={{0,4},{2,6},{4,8},{6,10},{8,12},{10,14},{12,16},{14,18},{16,20},{1... | collective-permute-start | bytes 1769480 | tf_op jit(solution)/shard_map/ppermute | solution.py:25
  5.6 6.3 %copy-start.1 = (bf16[512,1152]{1,0:T(8,128)(2,1)S(1)}, bf16[512,1152]{1,0:T(8,128)(2,1)}, u32[]{:S(2)}) copy-start(bf16[512,1152]{1,0:T(8,128)(2,1)} %refs_0_.5) | copy-start | bytes 3538948
  5.6 6.3 %copy-start.3 = (bf16[512,1152]{1,0:T(8,128)(2,1)S(1)}, bf16[512,1152]{1,0:T(8,128)(2,1)}, u32[]{:S(2)}) copy-start(bf16[512,1152]{1,0:T(8,128)(2,1)} %refs_3_.1) | copy-start | bytes 3538948
  5.7 48.4 %collective-permute-start.10 = (bf16[256,1152]{1,0:T(8,128)(2,1)S(1)}, bf16[256,1152]{1,0:T(8,128)(2,1)S(1)}, u32[]{:S(2)}, u32[]{:S(2)}) collective-permute-start(bf16[256,1152]{1,0:T(8,128)(2,1)S(1)} %slice.7), channel_id=1, source_target_pairs={{0,28},{2,30},{4,0},{6,2},{8,4},{10,6},{12,8},{14,10},{16,12},{18,... | collective-permute-start | bytes 1769480 | tf_op jit(solution)/shard_map/ppermute | solution.py:25
  7.9 49.4 %collective-permute-start.1 = (bf16[256,1152]{1,0:T(8,128)(2,1)S(1)}, bf16[256,1152]{1,0:T(8,128)(2,1)S(1)}, u32[]{:S(2)}, u32[]{:S(2)}) collective-permute-start(bf16[256,1152]{1,0:T(8,128)(2,1)S(1)} %slice.6), channel_id=1, source_target_pairs={{0,4},{2,6},{4,8},{6,10},{8,12},{10,14},{12,16},{14,18},{16,20},{1... | collective-permute-start | bytes 1769480 | tf_op jit(solution)/shard_map/ppermute | solution.py:25
  9.5 52.8 %collective-permute-start = (bf16[512,1152]{1,0:T(8,128)(2,1)S(1)}, bf16[512,1152]{1,0:T(8,128)(2,1)S(1)}, u32[]{:S(2)}, u32[]{:S(2)}) collective-permute-start(bf16[512,1152]{1,0:T(8,128)(2,1)S(1)} %shard_map.41.far_own), channel_id=1, source_target_pairs={{0,26},{2,8},{4,30},{6,12},{8,2},{10,16},{12,6},{14,20},{16,10},{1... | collective-permute-start | bytes 3538952 | tf_op jit(solution)/shard_map/ppermute | solution.py:25
  41.4 3.8 %collective-permute-start.7 = (bf16[128,1152]{1,0:T(8,128)(2,1)S(1)}, bf16[128,1152]{1,0:T(8,128)(2,1)S(1)}, u32[]{:S(2)}, u32[]{:S(2)}) collective-permute-start(bf16[128,1152]{1,0:T(8,128)(2,1)S(1)} %get-tuple-element.29), channel_id=1, source_target_pairs={{0,2},{2,0},{4,6},{6,4},{8,10},{10,8},{12,14},{14,12},{16,18},{18,... | collective-permute-start | bytes 884744 | tf_op jit(solution)/shard_map/ppermute | solution.py:25
  44.7 1.7 %collective-permute-start.8 = (bf16[128,1152]{1,0:T(8,128)(2,1)S(1)}, bf16[128,1152]{1,0:T(8,128)(2,1)S(1)}, u32[]{:S(2)}, u32[]{:S(2)}) collective-permute-start(bf16[128,1152]{1,0:T(8,128)(2,1)S(1)} %get-tuple-element.28), channel_id=1, source_target_pairs={{0,2},{2,0},{4,6},{6,4},{8,10},{10,8},{12,14},{14,12},{16,18},{18,... | collective-permute-start | bytes 884744 | tf_op jit(solution)/shard_map/ppermute | solution.py:25
  45.2 1.6 %collective-permute-start.4 = (bf16[128,1152]{1,0:T(8,128)(2,1)S(1)}, bf16[128,1152]{1,0:T(8,128)(2,1)S(1)}, u32[]{:S(2)}, u32[]{:S(2)}) collective-permute-start(bf16[128,1152]{1,0:T(8,128)(2,1)S(1)} %get-tuple-element.31), channel_id=1, source_target_pairs={{0,2},{2,0},{4,6},{6,4},{8,10},{10,8},{12,14},{14,12},{16,18},{18,... | collective-permute-start | bytes 884744 | tf_op jit(solution)/shard_map/ppermute | solution.py:25
  46.4 1.6 %collective-permute-start.5 = (bf16[128,1152]{1,0:T(8,128)(2,1)S(1)}, bf16[128,1152]{1,0:T(8,128)(2,1)S(1)}, u32[]{:S(2)}, u32[]{:S(2)}) collective-permute-start(bf16[128,1152]{1,0:T(8,128)(2,1)S(1)} %get-tuple-element.30), channel_id=1, source_target_pairs={{0,2},{2,0},{4,6},{6,4},{8,10},{10,8},{12,14},{14,12},{16,18},{18,... | collective-permute-start | bytes 884744 | tf_op jit(solution)/shard_map/ppermute | solution.py:25
  57.3 4.9 %collective-permute-start.11 = (bf16[256,1152]{1,0:T(8,128)(2,1)S(1)}, bf16[256,1152]{1,0:T(8,128)(2,1)S(1)}, u32[]{:S(2)}, u32[]{:S(2)}) collective-permute-start(bf16[256,1152]{1,0:T(8,128)(2,1)S(1)} %collective-permute-done.10.refs_3_), channel_id=1, source_target_pairs={{0,2},{2,0},{4,6},{6,4},{8,10},{10,8},{12,14},{14,12},{16,18},{18,... | collective-permute-start | bytes 1769480 | tf_op jit(solution)/shard_map/ppermute | solution.py:25
  57.8 4.5 %collective-permute-start.9 = (bf16[256,1152]{1,0:T(8,128)(2,1)S(1)}, bf16[256,1152]{1,0:T(8,128)(2,1)S(1)}, u32[]{:S(2)}, u32[]{:S(2)}) collective-permute-start(bf16[256,1152]{1,0:T(8,128)(2,1)S(1)} %collective-permute-done.1.refs_1_), channel_id=1, source_target_pairs={{0,2},{2,0},{4,6},{6,4},{8,10},{10,8},{12,14},{14,12},{16,18},{18,... | collective-permute-start | bytes 1769480 | tf_op jit(solution)/shard_map/ppermute | solution.py:25

commit v12 on v10

--- a/solution.py
+++ b/solution.py
@@ -107,7 +107,7 @@
     add_all(factor, [(near_own, join(near, joined), use)])
 
 
-def step_kernel(factor, units, sides, *refs):
+def step_kernel(factor, scale, units, sides, *refs):
     is_1 = core().astype(jnp.float32)
     parts = []
     for _, count in units:
@@ -119,7 +119,8 @@
     touched = set()
 
     def add(side, value):
-        sums[side][...] = (sums if side in touched else totals)[side][...] + value
+        total = (sums if side in touched else totals)[side][...]
+        sums[side][...] = (total + value) * scale
         touched.add(side)
 
     def use(side, value):
@@ -138,31 +139,41 @@
     )
 
 
-def last_kernel(factor, counts, *refs):
-    parts = []
-    for count in counts:
-        parts.append((refs[0], refs[1 : 1 + count], refs[1 + count]))
-        refs = refs[2 + count :]
-    outs, helds, joined, sems = refs[:2], refs[2:4], refs[4:6], refs[6]
-    copies = []
-
-    def use(total, held, out, start, value):
-        rows = pl.ds(start, LAST_TILE)
-        held[rows] = (total[rows] + value) * factor
-        for first in range(start, start + LAST_TILE, COPY_ROWS):
-            span = pl.ds(first, COPY_ROWS)
-            copies.append(pltpu.make_async_copy(held.at[span], out.at[span], sems.at[len(copies)]))
-            copies[-1].start()
-
+def last_kernel(factor, far_own, far, *refs):
+    sums, outs, held, sems = refs[:2], refs[2:4], refs[4], refs[5]
+    firsts = range(0, far_own.shape[0], COPY_ROWS)
+
+    def whole(side):
+        return pltpu.make_async_copy(sums[side], outs[side], sems.at[len(firsts)])
+
+    def part(side, first):
+        span = pl.ds(first, COPY_ROWS)
+        return pltpu.make_async_copy(held.at[span], outs[side].at[span], sems.at[first // COPY_ROWS])
+
+    def on_each_core(act):
+        for is_core in (0, 1):
+            pl.when(core() == is_core)(functools.partial(act, is_core))
+
+    def use(start, value):
+        def add(side):
+            rows = pl.ds(start, LAST_TILE)
+            held[rows] = sums[side][rows] + value * factor
+            for first in range(start, start + LAST_TILE, COPY_ROWS):
+                part(side, first).start()
+
+        on_each_core(add)
+
+    def finish(side):
+        whole(1 - side).wait()
+        for first in firsts:
+            part(side, first).wait()
+
+    on_each_core(lambda side: whole(1 - side).start())
     units = []
-    for (own, visitors, total), held, out, scratch in zip(parts, helds, outs, joined):
-        others = join(visitors, scratch)
-        for start in range(0, own.shape[0], LAST_TILE):
-            act = functools.partial(use, total, held, out, start)
-            units.append((own.at[pl.ds(start, LAST_TILE)], others, act))
+    for start in range(0, far_own.shape[0], LAST_TILE):
+        units.append((far_own.at[pl.ds(start, LAST_TILE)], far, functools.partial(use, start)))
     add_all(factor, units)
-    for copy in copies:
-        copy.wait()
+    on_each_core(finish)
 
 
 def local(image_embed, text_embed):
@@ -188,7 +199,7 @@
     def depth(visitors):
         return pltpu.VMEM((sum(visitor.shape[0] for visitor in visitors), width), dtype)
 
-    def step(units, sums):
+    def step(units, sums, scale=1.0):
         sides = tuple(sums)
         operands = [ref for _, own, visitors in units for ref in (own, *visitors)]
         counts = [(side, len(visitors)) for side, _, visitors in units]
@@ -196,7 +207,7 @@
             zip(
                 sides,
                 call(
-                    functools.partial(step_kernel, factor, counts, sides),
+                    functools.partial(step_kernel, factor, scale, counts, sides),
                     [kept] * len(sides),
                     (*operands, *sums.values()),
                     [depth(visitors) for _, _, visitors in units],
@@ -246,7 +257,6 @@
         ],
         sums,
     )
-    sums = step([(2, far_own, (after(far, sums[0]),))], sums)
 
     images, texts = after(later_images, sums[0]), after(later_texts, sums[0])
     swapped_images, swapped_texts = swap(images, 1), swap(texts, 1)
@@ -257,13 +267,14 @@
         ],
         sums,
     )
-    operands = (image_embed, *swapped_texts, sums[0], text_embed, *swapped_images, sums[1])
+    sums = step(
+        [(0, image_embed, swapped_texts), (1, text_embed, swapped_images)], sums, scale=factor
+    )
     return call(
-        functools.partial(last_kernel, factor, (1, 1)),
+        functools.partial(last_kernel, factor),
         (grad, grad),
-        operands,
-        [kept, kept, depth((texts,)), depth((images,))]
-        + [pltpu.SemaphoreType.DMA((2 * rows // COPY_ROWS,))],
+        (far_own, after(far, sums[0]), sums[0], sums[1]),
+        [kept, pltpu.SemaphoreType.DMA((rows // COPY_ROWS + 1,))],
     )
 
 

time: 71.2 us -> 66.6 us (0.935)
  waiting for transfers between devices: 40.8 us -> 35.5 us
    ppermute x12, waiting for transfers between devices: 40.8 us -> 35.5 us  [send(): lax.ppermute(block, AXIS, [(i, target(i) % count) for i in range(count)])]
  transfers between devices with their start and end apart: 12 -> 12, of which waited for: 9 -> 8; matrix products, arithmetic and copies ran while one was open for 0% -> 0% of each run, Pallas kernels for 16% -> 19%
where the time goes in v12:
time: 66.6 us; the launch traced here: 66.4 us
  waiting for transfers between devices  35.5 us (53%)
  Pallas kernels  17.6 us (26%)
  starting transfers between devices  12.4 us (19%)
  between operations  0.76 us (1%)
    ppermute x12, waiting for transfers between devices, send(): lax.ppermute(block, AXIS, [(i, target(i) % count) for i in range(count)])  35.5 us
    pallas_call x6, Pallas kernels, call(): pl.pallas_call(kernel, out_shape=tuple(outs), in_specs=[in_spec] * len(op...  17.6 us
    ppermute x12, starting transfers between devices, send(): lax.ppermute(block, AXIS, [(i, target(i) % count) for i in range(count)])  12.4 us
  transfers between devices with their start and end apart: 12, of which 8 were waited for; matrix products, arithmetic and copies ran while one was open for 0% of the time, Pallas kernels for 19%

profile of v12, /device:TPU:0, one launch (start us, length us, event | category | flops | bytes accessed | tf_op | source)
XLA Modules:
  0.0 66.4 jit_solution(11885374675834933299)
XLA Ops:
  0.6 0.0 copy-start.1
  0.6 0.0 copy-start
  0.6 2.2 %shard_map.41 = (bf16[256,1152]{1,0:T(8,128)(2,1)S(1)}, bf16[256,1152]{1,0:T(8,128)(2,1)S(1)}, bf16[512,1152]{1,0:T(8,128)(2,1)S(1)}, bf16[512,1152]{1,0:T(8,128)(2,1)S(1)}) custom-call(bf16[512,1152]{1,0:T(8,128)(2,1)} %refs_0_.5, bf16[512,1152]{1,0:T(8,128)(2,1)} %refs_2_.3), custom_call_target="tpu_custom_call" | custom-call | flops 1 | bytes 1 | tf_op jit(solution)/shard_map/pallas_call | solution.py:188
  2.8 0.5 collective-permute-start.3
  3.3 5.6 %collective-permute-start.6 = (bf16[256,1152]{1,0:T(8,128)(2,1)S(1)}, bf16[256,1152]{1,0:T(8,128)(2,1)S(1)}, u32[]{:S(2)}, u32[]{:S(2)}) collective-permute-start(bf16[256,1152]{1,0:T(8,128)(2,1)S(1)} %get-tuple-element.25), channel_id=1, source_target_pairs={{0,28},{2,30},{4,0},{6,2},{8,4},{10,6},{12,8},{14,10},{16,12},{18,... | collective-permute-start | bytes 1769480 | tf_op jit(solution)/shard_map/ppermute | solution.py:25
  9.0 0.0 collective-permute-start.2
  9.0 4.8 %collective-permute-start.10 = (bf16[256,1152]{1,0:T(8,128)(2,1)S(1)}, bf16[256,1152]{1,0:T(8,128)(2,1)S(1)}, u32[]{:S(2)}, u32[]{:S(2)}) collective-permute-start(bf16[256,1152]{1,0:T(8,128)(2,1)S(1)} %slice.7), channel_id=1, source_target_pairs={{0,28},{2,30},{4,0},{6,2},{8,4},{10,6},{12,8},{14,10},{16,12},{18,... | collective-permute-start | bytes 1769480 | tf_op jit(solution)/shard_map/ppermute | solution.py:25
  13.8 0.1 collective-permute-start.1
  13.9 0.0 collective-permute-done.3.refs_0_
  13.9 0.1 collective-permute-start
  14.0 4.4 %shard_map.42 = (f32[512,1152]{1,0:T(8,128)S(1)}, f32[512,1152]{1,0:T(8,128)S(1)}) custom-call(bf16[512,1152]{1,0:T(8,128)(2,1)S(1)} %copy-done.1, bf16[512,1152]{1,0:T(8,128)(2,1)S(1)} %copy-done, bf16[512,1152]{1,0:T(8,128)(2,1)S(1)} %get-tuple-element.21.near_own, bf16[512,1152]{1,0:T(8,128)(2,1)S(1)} %collective-permute-done.3.refs_0_), custom_call_target="tpu_custom_call" | custom-call | flops 1 | bytes 1 | tf_op jit(solution)/shard_map/pallas_call | solution.py:188
  18.4 27.0 %collective-permute-done.6.refs_5_ = bf16[256,1152]{1,0:T(8,128)(2,1)S(1)} collective-permute-done((bf16[256,1152]{1,0:T(8,128)(2,1)S(1)}, bf16[256,1152]{1,0:T(8,128)(2,1)S(1)}, u32[]{:S(2)}, u32[]{:S(2)}) %collective-permute-start.6) | collective-permute-done | bytes 589856 | tf_op jit(solution)/shard_map/ppermute | solution.py:25
  45.4 0.1 collective-permute-start.7
  45.5 0.0 collective-permute-done.2.refs_1_
  45.5 0.5 collective-permute-start.8
  46.1 1.0 %collective-permute-done.7.refs_6_ = bf16[128,1152]{1,0:T(8,128)(2,1)S(1)} collective-permute-done((bf16[128,1152]{1,0:T(8,128)(2,1)S(1)}, bf16[128,1152]{1,0:T(8,128)(2,1)S(1)}, u32[]{:S(2)}, u32[]{:S(2)}) %collective-permute-start.7) | collective-permute-done | bytes 294944 | tf_op jit(solution)/shard_map/ppermute | solution.py:25
  47.1 0.1 collective-permute-start.4
  47.2 0.3 collective-permute-done.8.refs_7_
  47.5 0.1 collective-permute-start.5
  47.6 1.0 %collective-permute-done.4.refs_2_ = bf16[128,1152]{1,0:T(8,128)(2,1)S(1)} collective-permute-done((bf16[128,1152]{1,0:T(8,128)(2,1)S(1)}, bf16[128,1152]{1,0:T(8,128)(2,1)S(1)}, u32[]{:S(2)}, u32[]{:S(2)}) %collective-permute-start.4) | collective-permute-done | bytes 294944 | tf_op jit(solution)/shard_map/ppermute | solution.py:25
  48.7 0.4 collective-permute-done.5.refs_3_
  49.1 3.4 %shard_map.43 = (f32[512,1152]{1,0:T(8,128)S(1)}, f32[512,1152]{1,0:T(8,128)S(1)}) custom-call(bf16[512,1152]{1,0:T(8,128)(2,1)S(1)} %copy-done.1, bf16[256,1152]{1,0:T(8,128)(2,1)S(1)} %collective-permute-done.2.refs_1_, bf16[128,1152]{1,0:T(8,128)(2,1)S(1)} %collective-permute-done.4.refs_2_, ...), custom_call_target="tpu_custom_call", output_to_operand_aliasing={{0}: (8, {}), {1}: (9, {})} | custom-call | flops 1 | bytes 1 | tf_op jit(solution)/shard_map/pallas_call | solution.py:188
  52.5 5.3 %collective-permute-done.10.refs_3_ = bf16[256,1152]{1,0:T(8,128)(2,1)S(1)} collective-permute-done((bf16[256,1152]{1,0:T(8,128)(2,1)S(1)}, bf16[256,1152]{1,0:T(8,128)(2,1)S(1)}, u32[]{:S(2)}, u32[]{:S(2)}) %collective-permute-start.10) | collective-permute-done | bytes 589856 | tf_op jit(solution)/shard_map/ppermute | solution.py:25
  57.8 0.2 collective-permute-done.1.refs_1_
  58.0 0.1 collective-permute-start.11
  58.0 0.5 collective-permute-start.9
  58.5 1.9 %shard_map.44 = (f32[512,1152]{1,0:T(8,128)S(1)}, f32[512,1152]{1,0:T(8,128)S(1)}) custom-call(bf16[512,1152]{1,0:T(8,128)(2,1)S(1)} %copy-done.1, bf16[256,1152]{1,0:T(8,128)(2,1)S(1)} %collective-permute-done.1.refs_1_, bf16[512,1152]{1,0:T(8,128)(2,1)S(1)} %copy-done, ...), custom_call_target="tpu_custom_call", output_to_operand_aliasing={{0}: (4, {}), {1}: (5, {})} | custom-call | flops 1 | bytes 1 | tf_op jit(solution)/shard_map/pallas_call | solution.py:188
  60.4 0.0 collective-permute-done.11.refs_3_
  60.4 0.4 collective-permute-done.9.refs_1_
  60.8 2.6 %shard_map.45 = (f32[512,1152]{1,0:T(8,128)S(1)}, f32[512,1152]{1,0:T(8,128)S(1)}) custom-call(bf16[512,1152]{1,0:T(8,128)(2,1)S(1)} %copy-done.1, bf16[256,1152]{1,0:T(8,128)(2,1)S(1)} %collective-permute-done.9.refs_1_, bf16[512,1152]{1,0:T(8,128)(2,1)S(1)} %copy-done, ...), custom_call_target="tpu_custom_call", output_to_operand_aliasing={{0}: (4, {}), {1}: (5, {})} | custom-call | flops 1 | bytes 1 | tf_op jit(solution)/shard_map/pallas_call | solution.py:188
  63.4 0.0 collective-permute-done.far
  63.4 3.1 %shard_map.46 = (f32[512,1152]{1,0:T(8,128)}, f32[512,1152]{1,0:T(8,128)}) custom-call(bf16[512,1152]{1,0:T(8,128)(2,1)S(1)} %get-tuple-element.19.far_own, bf16[512,1152]{1,0:T(8,128)(2,1)S(1)} %collective-permute-done.far, f32[512,1152]{1,0:T(8,128)S(1)} %get-tuple-element.33.refs_0_, f32[512,1152]{1,0:T(8,128)S(1)} %get-tuple-element.35.refs_1_), custom_call_target="tpu_custom_call" | custom-call | flops 1 | bytes 1 | tf_op jit(solution)/shard_map/pallas_call | solution.py:188
  (6 shorter events, 0.2 us)
Async XLA Ops:
  0.6 8.3 %copy-start.1 = (bf16[512,1152]{1,0:T(8,128)(2,1)S(1)}, bf16[512,1152]{1,0:T(8,128)(2,1)}, u32[]{:S(2)}) copy-start(bf16[512,1152]{1,0:T(8,128)(2,1)} %refs_0_.5) | copy-start | bytes 3538948
  0.6 13.2 %copy-start = (bf16[512,1152]{1,0:T(8,128)(2,1)S(1)}, bf16[512,1152]{1,0:T(8,128)(2,1)}, u32[]{:S(2)}) copy-start(bf16[512,1152]{1,0:T(8,128)(2,1)} %refs_2_.3) | copy-start | bytes 3538948
  2.8 11.1 %collective-permute-start.3 = (bf16[512,1152]{1,0:T(8,128)(2,1)S(1)}, bf16[512,1152]{1,0:T(8,128)(2,1)S(1)}, u32[]{:S(2)}, u32[]{:S(2)}) collective-permute-start(bf16[512,1152]{1,0:T(8,128)(2,1)S(1)} %get-tuple-element.21.near_own), channel_id=1, source_target_pairs={{0,2},{2,0},{4,6},{6,4},{8,10},{10,8},{12,14},{14,12},{16,18},{18,... | collective-permute-start | bytes 3538952 | tf_op jit(solution)/shard_map/ppermute | solution.py:25
  3.3 42.0 %collective-permute-start.6 = (bf16[256,1152]{1,0:T(8,128)(2,1)S(1)}, bf16[256,1152]{1,0:T(8,128)(2,1)S(1)}, u32[]{:S(2)}, u32[]{:S(2)}) collective-permute-start(bf16[256,1152]{1,0:T(8,128)(2,1)S(1)} %get-tuple-element.25), channel_id=1, source_target_pairs={{0,28},{2,30},{4,0},{6,2},{8,4},{10,6},{12,8},{14,10},{16,12},{18,... | collective-permute-start | bytes 1769480 | tf_op jit(solution)/shard_map/ppermute | solution.py:25
  9.0 36.6 %collective-permute-start.2 = (bf16[256,1152]{1,0:T(8,128)(2,1)S(1)}, bf16[256,1152]{1,0:T(8,128)(2,1)S(1)}, u32[]{:S(2)}, u32[]{:S(2)}) collective-permute-start(bf16[256,1152]{1,0:T(8,128)(2,1)S(1)} %get-tuple-element.20), channel_id=1, source_target_pairs={{0,4},{2,6},{4,8},{6,10},{8,12},{10,14},{12,16},{14,18},{16,20},{1... | collective-permute-start | bytes 1769480 | tf_op jit(solution)/shard_map/ppermute | solution.py:25
  9.0 48.8 %collective-permute-start.10 = (bf16[256,1152]{1,0:T(8,128)(2,1)S(1)}, bf16[256,1152]{1,0:T(8,128)(2,1)S(1)}, u32[]{:S(2)}, u32[]{:S(2)}) collective-permute-start(bf16[256,1152]{1,0:T(8,128)(2,1)S(1)} %slice.7), channel_id=1, source_target_pairs={{0,28},{2,30},{4,0},{6,2},{8,4},{10,6},{12,8},{14,10},{16,12},{18,... | collective-permute-start | bytes 1769480 | tf_op jit(solution)/shard_map/ppermute | solution.py:25
  13.8 44.1 %collective-permute-start.1 = (bf16[256,1152]{1,0:T(8,128)(2,1)S(1)}, bf16[256,1152]{1,0:T(8,128)(2,1)S(1)}, u32[]{:S(2)}, u32[]{:S(2)}) collective-permute-start(bf16[256,1152]{1,0:T(8,128)(2,1)S(1)} %slice.6), channel_id=1, source_target_pairs={{0,4},{2,6},{4,8},{6,10},{8,12},{10,14},{12,16},{14,18},{16,20},{1... | collective-permute-start | bytes 1769480 | tf_op jit(solution)/shard_map/ppermute | solution.py:25
  13.9 49.4 %collective-permute-start = (bf16[512,1152]{1,0:T(8,128)(2,1)S(1)}, bf16[512,1152]{1,0:T(8,128)(2,1)S(1)}, u32[]{:S(2)}, u32[]{:S(2)}) collective-permute-start(bf16[512,1152]{1,0:T(8,128)(2,1)S(1)} %get-tuple-element.19.far_own), channel_id=1, source_target_pairs={{0,26},{2,8},{4,30},{6,12},{8,2},{10,16},{12,6},{14,20},{16,10},{1... | collective-permute-start | bytes 3538952 | tf_op jit(solution)/shard_map/ppermute | solution.py:25
  45.4 1.6 %collective-permute-start.7 = (bf16[128,1152]{1,0:T(8,128)(2,1)S(1)}, bf16[128,1152]{1,0:T(8,128)(2,1)S(1)}, u32[]{:S(2)}, u32[]{:S(2)}) collective-permute-start(bf16[128,1152]{1,0:T(8,128)(2,1)S(1)} %get-tuple-element.37), channel_id=1, source_target_pairs={{0,2},{2,0},{4,6},{6,4},{8,10},{10,8},{12,14},{14,12},{16,18},{18,... | collective-permute-start | bytes 884744 | tf_op jit(solution)/shard_map/ppermute | solution.py:25
  45.5 2.0 %collective-permute-start.8 = (bf16[128,1152]{1,0:T(8,128)(2,1)S(1)}, bf16[128,1152]{1,0:T(8,128)(2,1)S(1)}, u32[]{:S(2)}, u32[]{:S(2)}) collective-permute-start(bf16[128,1152]{1,0:T(8,128)(2,1)S(1)} %get-tuple-element.36), channel_id=1, source_target_pairs={{0,2},{2,0},{4,6},{6,4},{8,10},{10,8},{12,14},{14,12},{16,18},{18,... | collective-permute-start | bytes 884744 | tf_op jit(solution)/shard_map/ppermute | solution.py:25
  47.1 1.6 %collective-permute-start.4 = (bf16[128,1152]{1,0:T(8,128)(2,1)S(1)}, bf16[128,1152]{1,0:T(8,128)(2,1)S(1)}, u32[]{:S(2)}, u32[]{:S(2)}) collective-permute-start(bf16[128,1152]{1,0:T(8,128)(2,1)S(1)} %get-tuple-element.39), channel_id=1, source_target_pairs={{0,2},{2,0},{4,6},{6,4},{8,10},{10,8},{12,14},{14,12},{16,18},{18,... | collective-permute-start | bytes 884744 | tf_op jit(solution)/shard_map/ppermute | solution.py:25
  47.5 1.6 %collective-permute-start.5 = (bf16[128,1152]{1,0:T(8,128)(2,1)S(1)}, bf16[128,1152]{1,0:T(8,128)(2,1)S(1)}, u32[]{:S(2)}, u32[]{:S(2)}) collective-permute-start(bf16[128,1152]{1,0:T(8,128)(2,1)S(1)} %get-tuple-element.38), channel_id=1, source_target_pairs={{0,2},{2,0},{4,6},{6,4},{8,10},{10,8},{12,14},{14,12},{16,18},{18,... | collective-permute-start | bytes 884744 | tf_op jit(solution)/shard_map/ppermute | solution.py:25
  58.0 2.5 %collective-permute-start.11 = (bf16[256,1152]{1,0:T(8,128)(2,1)S(1)}, bf16[256,1152]{1,0:T(8,128)(2,1)S(1)}, u32[]{:S(2)}, u32[]{:S(2)}) collective-permute-start(bf16[256,1152]{1,0:T(8,128)(2,1)S(1)} %collective-permute-done.10.refs_3_), channel_id=1, source_target_pairs={{0,2},{2,0},{4,6},{6,4},{8,10},{10,8},{12,14},{14,12},{16,18},{18,... | collective-permute-start | bytes 1769480 | tf_op jit(solution)/shard_map/ppermute | solution.py:25
  58.0 2.8 %collective-permute-start.9 = (bf16[256,1152]{1,0:T(8,128)(2,1)S(1)}, bf16[256,1152]{1,0:T(8,128)(2,1)S(1)}, u32[]{:S(2)}, u32[]{:S(2)}) collective-permute-start(bf16[256,1152]{1,0:T(8,128)(2,1)S(1)} %collective-permute-done.1.refs_1_), channel_id=1, source_target_pairs={{0,2},{2,0},{4,6},{6,4},{8,10},{10,8},{12,14},{14,12},{16,18},{18,... | collective-permute-start | bytes 1769480 | tf_op jit(solution)/shard_map/ppermute | solution.py:25

commit v13 on v12

--- a/solution.py
+++ b/solution.py
@@ -107,7 +107,7 @@
     add_all(factor, [(near_own, join(near, joined), use)])
 
 
-def step_kernel(factor, scale, units, sides, *refs):
+def step_kernel(factor, units, sides, *refs):
     is_1 = core().astype(jnp.float32)
     parts = []
     for _, count in units:
@@ -119,8 +119,7 @@
     touched = set()
 
     def add(side, value):
-        total = (sums if side in touched else totals)[side][...]
-        sums[side][...] = (total + value) * scale
+        sums[side][...] = (sums if side in touched else totals)[side][...] + value
         touched.add(side)
 
     def use(side, value):
@@ -139,39 +138,46 @@
     )
 
 
-def last_kernel(factor, far_own, far, *refs):
-    sums, outs, held, sems = refs[:2], refs[2:4], refs[4], refs[5]
-    firsts = range(0, far_own.shape[0], COPY_ROWS)
-
-    def whole(side):
-        return pltpu.make_async_copy(sums[side], outs[side], sems.at[len(firsts)])
-
-    def part(side, first):
-        span = pl.ds(first, COPY_ROWS)
-        return pltpu.make_async_copy(held.at[span], outs[side].at[span], sems.at[first // COPY_ROWS])
+def last_kernel(factor, far_own, near_own, far, texts, images, *refs):
+    sums, outs, (helds, joined, others, sems) = refs[:2], refs[2:4], refs[4:]
+    rows = far_own.shape[0]
+    visitors = (texts, images)
 
     def on_each_core(act):
         for is_core in (0, 1):
             pl.when(core() == is_core)(functools.partial(act, is_core))
 
-    def use(start, value):
-        def add(side):
-            rows = pl.ds(start, LAST_TILE)
-            held[rows] = sums[side][rows] + value * factor
+    def move(is_far, side, first):
+        span = pl.ds(first, COPY_ROWS)
+        sem = sems.at[is_far, first // COPY_ROWS]
+        return pltpu.make_async_copy(helds.at[is_far, span], outs[side].at[span], sem)
+
+    def place(side):
+        joined[pl.ds(rows, texts.shape[0])] = visitors[side][...]
+        others[...] = visitors[1 - side][...]
+
+    def use(is_far, start, value):
+        def add(far_side):
+            side = far_side if is_far else 1 - far_side
+            span = pl.ds(start, LAST_TILE)
+            helds[is_far, span] = (sums[side][span] + value) * factor
             for first in range(start, start + LAST_TILE, COPY_ROWS):
-                part(side, first).start()
+                move(is_far, side, first).start()
 
         on_each_core(add)
 
-    def finish(side):
-        whole(1 - side).wait()
-        for first in firsts:
-            part(side, first).wait()
-
-    on_each_core(lambda side: whole(1 - side).start())
+    def finish(far_side):
+        for is_far in (0, 1):
+            for first in range(0, rows, COPY_ROWS):
+                move(is_far, far_side if is_far else 1 - far_side, first).wait()
+
+    joined[pl.ds(0, rows)] = far[...]
+    on_each_core(place)
     units = []
-    for start in range(0, far_own.shape[0], LAST_TILE):
-        units.append((far_own.at[pl.ds(start, LAST_TILE)], far, functools.partial(use, start)))
+    for is_far, (own, met) in enumerate(((near_own, others), (far_own, joined))):
+        for start in range(0, rows, LAST_TILE):
+            act = functools.partial(use, is_far, start)
+            units.append((own.at[pl.ds(start, LAST_TILE)], met, act))
     add_all(factor, units)
     on_each_core(finish)
 
@@ -199,7 +205,7 @@
     def depth(visitors):
         return pltpu.VMEM((sum(visitor.shape[0] for visitor in visitors), width), dtype)
 
-    def step(units, sums, scale=1.0):
+    def step(units, sums):
         sides = tuple(sums)
         operands = [ref for _, own, visitors in units for ref in (own, *visitors)]
         counts = [(side, len(visitors)) for side, _, visitors in units]
@@ -207,7 +213,7 @@
             zip(
                 sides,
                 call(
-                    functools.partial(step_kernel, factor, scale, counts, sides),
+                    functools.partial(step_kernel, factor, counts, sides),
                     [kept] * len(sides),
                     (*operands, *sums.values()),
                     [depth(visitors) for _, _, visitors in units],
@@ -267,14 +273,16 @@
         ],
         sums,
     )
-    sums = step(
-        [(0, image_embed, swapped_texts), (1, text_embed, swapped_images)], sums, scale=factor
-    )
     return call(
         functools.partial(last_kernel, factor),
         (grad, grad),
-        (far_own, after(far, sums[0]), sums[0], sums[1]),
-        [kept, pltpu.SemaphoreType.DMA((rows // COPY_ROWS + 1,))],
+        (far_own, near_own, far, *swapped_texts, *swapped_images, sums[0], sums[1]),
+        [
+            pltpu.VMEM((2, rows, width), jnp.float32),
+            pltpu.VMEM((2 * rows - cut_texts, width), dtype),
+            pltpu.VMEM((rows - cut_texts, width), dtype),
+            pltpu.SemaphoreType.DMA((2, rows // COPY_ROWS)),
+        ],
     )
 
 

time: 66.6 us -> 68.2 us (1.024)
  the two profiles are of different devices: /device:TPU:0 before, /device:TPU:5 now
where the time goes in v13:
time: 68.2 us; the launch traced here: 68 us
  waiting for transfers between devices  39.3 us (58%)
  Pallas kernels  17.4 us (26%)
  starting transfers between devices  10.4 us (15%)
  between operations  0.71 us (1%)
    ppermute x12, waiting for transfers between devices, send(): lax.ppermute(block, AXIS, [(i, target(i) % count) for i in range(count)])  39.3 us
    pallas_call x5, Pallas kernels, call(): pl.pallas_call(kernel, out_shape=tuple(outs), in_specs=[in_spec] * len(op...  17.4 us
    ppermute x12, starting transfers between devices, send(): lax.ppermute(block, AXIS, [(i, target(i) % count) for i in range(count)])  10.4 us
  transfers between devices with their start and end apart: 12, of which 8 were waited for; matrix products, arithmetic and copies ran while one was open for 0% of the time, Pallas kernels for 14%

profile of v13, /device:TPU:5, one launch (start us, length us, event | category | flops | bytes accessed | tf_op | source)
XLA Modules:
  0.0 68.0 jit_solution(421248410266212098)
XLA Ops:
  0.6 0.0 copy-start
  0.6 0.0 copy-start.1
  0.6 2.2 %shard_map.41 = (bf16[256,1152]{1,0:T(8,128)(2,1)S(1)}, bf16[256,1152]{1,0:T(8,128)(2,1)S(1)}, bf16[512,1152]{1,0:T(8,128)(2,1)S(1)}, bf16[512,1152]{1,0:T(8,128)(2,1)S(1)}) custom-call(bf16[512,1152]{1,0:T(8,128)(2,1)} %refs_0_.3, bf16[512,1152]{1,0:T(8,128)(2,1)} %refs_2_.1), custom_call_target="tpu_custom_call" | custom-call | flops 1 | bytes 1 | tf_op jit(solution)/shard_map/pallas_call | solution.py:194
  2.8 0.7 %collective-permute-start.3 = (bf16[512,1152]{1,0:T(8,128)(2,1)S(1)}, bf16[512,1152]{1,0:T(8,128)(2,1)S(1)}, u32[]{:S(2)}, u32[]{:S(2)}) collective-permute-start(bf16[512,1152]{1,0:T(8,128)(2,1)S(1)} %get-tuple-element.17.near_own), channel_id=1, source_target_pairs={{0,2},{2,0},{4,6},{6,4},{8,10},{10,8},{12,14},{14,12},{16,18},{18,... | collective-permute-start | bytes 3538952 | tf_op jit(solution)/shard_map/ppermute | solution.py:25
  3.6 0.0 collective-permute-start.6
  3.6 2.4 %collective-permute-start.2 = (bf16[256,1152]{1,0:T(8,128)(2,1)S(1)}, bf16[256,1152]{1,0:T(8,128)(2,1)S(1)}, u32[]{:S(2)}, u32[]{:S(2)}) collective-permute-start(bf16[256,1152]{1,0:T(8,128)(2,1)S(1)} %get-tuple-element.18), channel_id=1, source_target_pairs={{0,4},{2,6},{4,8},{6,10},{8,12},{10,14},{12,16},{14,18},{16,20},{1... | collective-permute-start | bytes 1769480 | tf_op jit(solution)/shard_map/ppermute | solution.py:25
  5.9 0.0 copy-done
  6.0 2.2 %collective-permute-start.10 = (bf16[256,1152]{1,0:T(8,128)(2,1)S(1)}, bf16[256,1152]{1,0:T(8,128)(2,1)S(1)}, u32[]{:S(2)}, u32[]{:S(2)}) collective-permute-start(bf16[256,1152]{1,0:T(8,128)(2,1)S(1)} %slice.7), channel_id=1, source_target_pairs={{0,28},{2,30},{4,0},{6,2},{8,4},{10,6},{12,8},{14,10},{16,12},{18,... | collective-permute-start | bytes 1769480 | tf_op jit(solution)/shard_map/ppermute | solution.py:25
  8.2 0.3 collective-permute-start.1
  8.5 0.0 collective-permute-done.3.refs_0_
  8.5 2.4 %collective-permute-start = (bf16[512,1152]{1,0:T(8,128)(2,1)S(1)}, bf16[512,1152]{1,0:T(8,128)(2,1)S(1)}, u32[]{:S(2)}, u32[]{:S(2)}) collective-permute-start(bf16[512,1152]{1,0:T(8,128)(2,1)S(1)} %get-tuple-element.16.far_own), channel_id=1, source_target_pairs={{0,26},{2,8},{4,30},{6,12},{8,2},{10,16},{12,6},{14,20},{16,10},{1... | collective-permute-start | bytes 3538952 | tf_op jit(solution)/shard_map/ppermute | solution.py:25
  10.9 4.4 %shard_map.42 = (f32[512,1152]{1,0:T(8,128)S(1)}, f32[512,1152]{1,0:T(8,128)S(1)}) custom-call(bf16[512,1152]{1,0:T(8,128)(2,1)S(1)} %copy-done, bf16[512,1152]{1,0:T(8,128)(2,1)S(1)} %copy-done.1, bf16[512,1152]{1,0:T(8,128)(2,1)S(1)} %get-tuple-element.17.near_own, bf16[512,1152]{1,0:T(8,128)(2,1)S(1)} %collective-permute-done.3.refs_0_), custom_call_target="tpu_custom_call" | custom-call | flops 1 | bytes 1 | tf_op jit(solution)/shard_map/pallas_call | solution.py:194
  15.3 26.4 %collective-permute-done.6.refs_5_ = bf16[256,1152]{1,0:T(8,128)(2,1)S(1)} collective-permute-done((bf16[256,1152]{1,0:T(8,128)(2,1)S(1)}, bf16[256,1152]{1,0:T(8,128)(2,1)S(1)}, u32[]{:S(2)}, u32[]{:S(2)}) %collective-permute-start.6) | collective-permute-done | bytes 589856 | tf_op jit(solution)/shard_map/ppermute | solution.py:25
  41.8 1.0 %collective-permute-start.7 = (bf16[128,1152]{1,0:T(8,128)(2,1)S(1)}, bf16[128,1152]{1,0:T(8,128)(2,1)S(1)}, u32[]{:S(2)}, u32[]{:S(2)}) collective-permute-start(bf16[128,1152]{1,0:T(8,128)(2,1)S(1)} %get-tuple-element.31), channel_id=1, source_target_pairs={{0,2},{2,0},{4,6},{6,4},{8,10},{10,8},{12,14},{14,12},{16,18},{18,... | collective-permute-start | bytes 884744 | tf_op jit(solution)/shard_map/ppermute | solution.py:25
  42.8 2.3 %collective-permute-done.2.refs_1_ = bf16[256,1152]{1,0:T(8,128)(2,1)S(1)} collective-permute-done((bf16[256,1152]{1,0:T(8,128)(2,1)S(1)}, bf16[256,1152]{1,0:T(8,128)(2,1)S(1)}, u32[]{:S(2)}, u32[]{:S(2)}) %collective-permute-start.2) | collective-permute-done | bytes 589856 | tf_op jit(solution)/shard_map/ppermute | solution.py:25
  45.0 0.5 collective-permute-start.8
  45.6 0.0 collective-permute-done.7.refs_6_
  45.6 0.1 collective-permute-start.4
  45.7 1.1 %collective-permute-done.8.refs_7_ = bf16[128,1152]{1,0:T(8,128)(2,1)S(1)} collective-permute-done((bf16[128,1152]{1,0:T(8,128)(2,1)S(1)}, bf16[128,1152]{1,0:T(8,128)(2,1)S(1)}, u32[]{:S(2)}, u32[]{:S(2)}) %collective-permute-start.8) | collective-permute-done | bytes 294944 | tf_op jit(solution)/shard_map/ppermute | solution.py:25
  46.7 0.4 collective-permute-start.5
  47.1 0.1 collective-permute-done.4.refs_2_
  47.2 1.1 %collective-permute-done.5.refs_3_ = bf16[128,1152]{1,0:T(8,128)(2,1)S(1)} collective-permute-done((bf16[128,1152]{1,0:T(8,128)(2,1)S(1)}, bf16[128,1152]{1,0:T(8,128)(2,1)S(1)}, u32[]{:S(2)}, u32[]{:S(2)}) %collective-permute-start.5) | collective-permute-done | bytes 294944 | tf_op jit(solution)/shard_map/ppermute | solution.py:25
  48.3 3.4 %shard_map.43 = (f32[512,1152]{1,0:T(8,128)S(1)}, f32[512,1152]{1,0:T(8,128)S(1)}) custom-call(bf16[512,1152]{1,0:T(8,128)(2,1)S(1)} %copy-done, bf16[256,1152]{1,0:T(8,128)(2,1)S(1)} %collective-permute-done.2.refs_1_, bf16[128,1152]{1,0:T(8,128)(2,1)S(1)} %collective-permute-done.4.refs_2_, ...), custom_call_target="tpu_custom_call", output_to_operand_aliasing={{0}: (8, {}), {1}: (9, {})} | custom-call | flops 1 | bytes 1 | tf_op jit(solution)/shard_map/pallas_call | solution.py:194
  51.8 2.6 %collective-permute-done.10.refs_3_ = bf16[256,1152]{1,0:T(8,128)(2,1)S(1)} collective-permute-done((bf16[256,1152]{1,0:T(8,128)(2,1)S(1)}, bf16[256,1152]{1,0:T(8,128)(2,1)S(1)}, u32[]{:S(2)}, u32[]{:S(2)}) %collective-permute-start.10) | collective-permute-done | bytes 589856 | tf_op jit(solution)/shard_map/ppermute | solution.py:25
  54.4 3.3 %collective-permute-done.1.refs_1_ = bf16[256,1152]{1,0:T(8,128)(2,1)S(1)} collective-permute-done((bf16[256,1152]{1,0:T(8,128)(2,1)S(1)}, bf16[256,1152]{1,0:T(8,128)(2,1)S(1)}, u32[]{:S(2)}, u32[]{:S(2)}) %collective-permute-start.1) | collective-permute-done | bytes 589856 | tf_op jit(solution)/shard_map/ppermute | solution.py:25
  57.7 0.4 collective-permute-start.11
  58.1 0.1 collective-permute-start.9
  58.2 1.9 %shard_map.44 = (f32[512,1152]{1,0:T(8,128)S(1)}, f32[512,1152]{1,0:T(8,128)S(1)}) custom-call(bf16[512,1152]{1,0:T(8,128)(2,1)S(1)} %copy-done, bf16[256,1152]{1,0:T(8,128)(2,1)S(1)} %collective-permute-done.1.refs_1_, bf16[512,1152]{1,0:T(8,128)(2,1)S(1)} %copy-done.1, ...), custom_call_target="tpu_custom_call", output_to_operand_aliasing={{0}: (4, {}), {1}: (5, {})} | custom-call | flops 1 | bytes 1 | tf_op jit(solution)/shard_map/pallas_call | solution.py:194
  60.2 2.4 %collective-permute-done.far = bf16[512,1152]{1,0:T(8,128)(2,1)S(1)} collective-permute-done((bf16[512,1152]{1,0:T(8,128)(2,1)S(1)}, bf16[512,1152]{1,0:T(8,128)(2,1)S(1)}, u32[]{:S(2)}, u32[]{:S(2)}) %collective-permute-start) | collective-permute-done | bytes 1179680 | tf_op jit(solution)/shard_map/ppermute | solution.py:25
  62.6 0.0 collective-permute-done.11.images
  62.6 0.0 collective-permute-done.9.texts
  62.6 5.4 %shard_map.45 = (f32[512,1152]{1,0:T(8,128)}, f32[512,1152]{1,0:T(8,128)}) custom-call(bf16[512,1152]{1,0:T(8,128)(2,1)S(1)} %get-tuple-element.16.far_own, bf16[512,1152]{1,0:T(8,128)(2,1)S(1)} %get-tuple-element.17.near_own, bf16[512,1152]{1,0:T(8,128)(2,1)S(1)} %collective-permute-done.far, bf16[256,1152]{1,0:T(8,128)(2,1)S(1)} %collective-permute-done.9.texts, ...), custom_call_target="tpu_custom_call" | custom-call | flops 1 | bytes 1 | tf_op jit(solution)/shard_map/pallas_call | solution.py:194
  (5 shorter events, 0.2 us)
Async XLA Ops:
  0.6 5.3 %copy-start = (bf16[512,1152]{1,0:T(8,128)(2,1)S(1)}, bf16[512,1152]{1,0:T(8,128)(2,1)}, u32[]{:S(2)}) copy-start(bf16[512,1152]{1,0:T(8,128)(2,1)} %refs_0_.3) | copy-start | bytes 3538948
  0.6 7.5 %copy-start.1 = (bf16[512,1152]{1,0:T(8,128)(2,1)S(1)}, bf16[512,1152]{1,0:T(8,128)(2,1)}, u32[]{:S(2)}) copy-start(bf16[512,1152]{1,0:T(8,128)(2,1)} %refs_2_.1) | copy-start | bytes 3538948
  2.8 5.7 %collective-permute-start.3 = (bf16[512,1152]{1,0:T(8,128)(2,1)S(1)}, bf16[512,1152]{1,0:T(8,128)(2,1)S(1)}, u32[]{:S(2)}, u32[]{:S(2)}) collective-permute-start(bf16[512,1152]{1,0:T(8,128)(2,1)S(1)} %get-tuple-element.17.near_own), channel_id=1, source_target_pairs={{0,2},{2,0},{4,6},{6,4},{8,10},{10,8},{12,14},{14,12},{16,18},{18,... | collective-permute-start | bytes 3538952 | tf_op jit(solution)/shard_map/ppermute | solution.py:25
  3.6 38.2 %collective-permute-start.6 = (bf16[256,1152]{1,0:T(8,128)(2,1)S(1)}, bf16[256,1152]{1,0:T(8,128)(2,1)S(1)}, u32[]{:S(2)}, u32[]{:S(2)}) collective-permute-start(bf16[256,1152]{1,0:T(8,128)(2,1)S(1)} %get-tuple-element.22), channel_id=1, source_target_pairs={{0,28},{2,30},{4,0},{6,2},{8,4},{10,6},{12,8},{14,10},{16,12},{18,... | collective-permute-start | bytes 1769480 | tf_op jit(solution)/shard_map/ppermute | solution.py:25
  3.6 41.5 %collective-permute-start.2 = (bf16[256,1152]{1,0:T(8,128)(2,1)S(1)}, bf16[256,1152]{1,0:T(8,128)(2,1)S(1)}, u32[]{:S(2)}, u32[]{:S(2)}) collective-permute-start(bf16[256,1152]{1,0:T(8,128)(2,1)S(1)} %get-tuple-element.18), channel_id=1, source_target_pairs={{0,4},{2,6},{4,8},{6,10},{8,12},{10,14},{12,16},{14,18},{16,20},{1... | collective-permute-start | bytes 1769480 | tf_op jit(solution)/shard_map/ppermute | solution.py:25
  6.0 48.4 %collective-permute-start.10 = (bf16[256,1152]{1,0:T(8,128)(2,1)S(1)}, bf16[256,1152]{1,0:T(8,128)(2,1)S(1)}, u32[]{:S(2)}, u32[]{:S(2)}) collective-permute-start(bf16[256,1152]{1,0:T(8,128)(2,1)S(1)} %slice.7), channel_id=1, source_target_pairs={{0,28},{2,30},{4,0},{6,2},{8,4},{10,6},{12,8},{14,10},{16,12},{18,... | collective-permute-start | bytes 1769480 | tf_op jit(solution)/shard_map/ppermute | solution.py:25
  8.2 49.5 %collective-permute-start.1 = (bf16[256,1152]{1,0:T(8,128)(2,1)S(1)}, bf16[256,1152]{1,0:T(8,128)(2,1)S(1)}, u32[]{:S(2)}, u32[]{:S(2)}) collective-permute-start(bf16[256,1152]{1,0:T(8,128)(2,1)S(1)} %slice.6), channel_id=1, source_target_pairs={{0,4},{2,6},{4,8},{6,10},{8,12},{10,14},{12,16},{14,18},{16,20},{1... | collective-permute-start | bytes 1769480 | tf_op jit(solution)/shard_map/ppermute | solution.py:25
  8.5 54.0 %collective-permute-start = (bf16[512,1152]{1,0:T(8,128)(2,1)S(1)}, bf16[512,1152]{1,0:T(8,128)(2,1)S(1)}, u32[]{:S(2)}, u32[]{:S(2)}) collective-permute-start(bf16[512,1152]{1,0:T(8,128)(2,1)S(1)} %get-tuple-element.16.far_own), channel_id=1, source_target_pairs={{0,26},{2,8},{4,30},{6,12},{8,2},{10,16},{12,6},{14,20},{16,10},{1... | collective-permute-start | bytes 3538952 | tf_op jit(solution)/shard_map/ppermute | solution.py:25
  41.8 3.8 %collective-permute-start.7 = (bf16[128,1152]{1,0:T(8,128)(2,1)S(1)}, bf16[128,1152]{1,0:T(8,128)(2,1)S(1)}, u32[]{:S(2)}, u32[]{:S(2)}) collective-permute-start(bf16[128,1152]{1,0:T(8,128)(2,1)S(1)} %get-tuple-element.31), channel_id=1, source_target_pairs={{0,2},{2,0},{4,6},{6,4},{8,10},{10,8},{12,14},{14,12},{16,18},{18,... | collective-permute-start | bytes 884744 | tf_op jit(solution)/shard_map/ppermute | solution.py:25
  45.0 1.7 %collective-permute-start.8 = (bf16[128,1152]{1,0:T(8,128)(2,1)S(1)}, bf16[128,1152]{1,0:T(8,128)(2,1)S(1)}, u32[]{:S(2)}, u32[]{:S(2)}) collective-permute-start(bf16[128,1152]{1,0:T(8,128)(2,1)S(1)} %get-tuple-element.30), channel_id=1, source_target_pairs={{0,2},{2,0},{4,6},{6,4},{8,10},{10,8},{12,14},{14,12},{16,18},{18,... | collective-permute-start | bytes 884744 | tf_op jit(solution)/shard_map/ppermute | solution.py:25
  45.6 1.6 %collective-permute-start.4 = (bf16[128,1152]{1,0:T(8,128)(2,1)S(1)}, bf16[128,1152]{1,0:T(8,128)(2,1)S(1)}, u32[]{:S(2)}, u32[]{:S(2)}) collective-permute-start(bf16[128,1152]{1,0:T(8,128)(2,1)S(1)} %get-tuple-element.33), channel_id=1, source_target_pairs={{0,2},{2,0},{4,6},{6,4},{8,10},{10,8},{12,14},{14,12},{16,18},{18,... | collective-permute-start | bytes 884744 | tf_op jit(solution)/shard_map/ppermute | solution.py:25
  46.7 1.6 %collective-permute-start.5 = (bf16[128,1152]{1,0:T(8,128)(2,1)S(1)}, bf16[128,1152]{1,0:T(8,128)(2,1)S(1)}, u32[]{:S(2)}, u32[]{:S(2)}) collective-permute-start(bf16[128,1152]{1,0:T(8,128)(2,1)S(1)} %get-tuple-element.32), channel_id=1, source_target_pairs={{0,2},{2,0},{4,6},{6,4},{8,10},{10,8},{12,14},{14,12},{16,18},{18,... | collective-permute-start | bytes 884744 | tf_op jit(solution)/shard_map/ppermute | solution.py:25
  57.7 4.9 %collective-permute-start.11 = (bf16[256,1152]{1,0:T(8,128)(2,1)S(1)}, bf16[256,1152]{1,0:T(8,128)(2,1)S(1)}, u32[]{:S(2)}, u32[]{:S(2)}) collective-permute-start(bf16[256,1152]{1,0:T(8,128)(2,1)S(1)} %collective-permute-done.10.refs_3_), channel_id=1, source_target_pairs={{0,2},{2,0},{4,6},{6,4},{8,10},{10,8},{12,14},{14,12},{16,18},{18,... | collective-permute-start | bytes 1769480 | tf_op jit(solution)/shard_map/ppermute | solution.py:25
  58.1 4.4 %collective-permute-start.9 = (bf16[256,1152]{1,0:T(8,128)(2,1)S(1)}, bf16[256,1152]{1,0:T(8,128)(2,1)S(1)}, u32[]{:S(2)}, u32[]{:S(2)}) collective-permute-start(bf16[256,1152]{1,0:T(8,128)(2,1)S(1)} %collective-permute-done.1.refs_1_), channel_id=1, source_target_pairs={{0,2},{2,0},{4,6},{6,4},{8,10},{10,8},{12,14},{14,12},{16,18},{18,... | collective-permute-start | bytes 1769480 | tf_op jit(solution)/shard_map/ppermute | solution.py:25

commit v14 on v10

--- a/solution.py
+++ b/solution.py
@@ -138,28 +138,36 @@
     )
 
 
-def last_kernel(factor, counts, *refs):
+def last_kernel(factor, counts, far_own, far, *refs):
     parts = []
     for count in counts:
         parts.append((refs[0], refs[1 : 1 + count], refs[1 + count]))
         refs = refs[2 + count :]
     outs, helds, joined, sems = refs[:2], refs[2:4], refs[4:6], refs[6]
+    starts = range(0, far_own.shape[0], LAST_TILE)
+    is_1 = core().astype(jnp.float32)
     copies = []
 
-    def use(total, held, out, start, value):
+    def use_far(start, value):
         rows = pl.ds(start, LAST_TILE)
-        held[rows] = (total[rows] + value) * factor
+        helds[0][rows] = parts[0][2][rows] + value * (1.0 - is_1)
+        helds[1][rows] = parts[1][2][rows] + value * is_1
+
+    def use(held, out, start, value):
+        rows = pl.ds(start, LAST_TILE)
+        held[rows] = (held[rows] + value) * factor
         for first in range(start, start + LAST_TILE, COPY_ROWS):
             span = pl.ds(first, COPY_ROWS)
             copies.append(pltpu.make_async_copy(held.at[span], out.at[span], sems.at[len(copies)]))
             copies[-1].start()
 
-    units = []
-    for (own, visitors, total), held, out, scratch in zip(parts, helds, outs, joined):
+    def unit(own, others, start, act, *args):
+        return (own.at[pl.ds(start, LAST_TILE)], others, functools.partial(act, *args, start))
+
+    units = [unit(far_own, far, start, use_far) for start in starts]
+    for (own, visitors, _), held, out, scratch in zip(parts, helds, outs, joined):
         others = join(visitors, scratch)
-        for start in range(0, own.shape[0], LAST_TILE):
-            act = functools.partial(use, total, held, out, start)
-            units.append((own.at[pl.ds(start, LAST_TILE)], others, act))
+        units += [unit(own, others, start, use, held, out) for start in starts]
     add_all(factor, units)
     for copy in copies:
         copy.wait()
@@ -241,12 +249,11 @@
     swapped_images, swapped_texts = swap(images, 2), swap(texts, 2)
     sums = step(
         [
+            (1, text_embed, (images, *swapped_images)),
             (0, image_embed, (texts, *swapped_texts)),
-            (1, text_embed, (images, *swapped_images)),
         ],
         sums,
     )
-    sums = step([(2, far_own, (after(far, sums[0]),))], sums)
 
     images, texts = after(later_images, sums[0]), after(later_texts, sums[0])
     swapped_images, swapped_texts = swap(images, 1), swap(texts, 1)
@@ -258,6 +265,7 @@
         sums,
     )
     operands = (image_embed, *swapped_texts, sums[0], text_embed, *swapped_images, sums[1])
+    operands = (far_own, far, *operands)
     return call(
         functools.partial(last_kernel, factor, (1, 1)),
         (grad, grad),

time: 71.2 us -> 66.6 us (0.935)
  waiting for transfers between devices: 40.8 us -> 38.8 us
  starting transfers between devices: 12.3 us -> 10.5 us
    ppermute x12, waiting for transfers between devices: 40.8 us -> 38.8 us  [send(): lax.ppermute(block, AXIS, [(i, target(i) % count) for i in range(count)])]
    ppermute x12, starting transfers between devices: 12.3 us -> 10.5 us  [send(): lax.ppermute(block, AXIS, [(i, target(i) % count) for i in range(count)])]
    pallas_call x6 -> x5, Pallas kernels: 17 us -> 16.3 us  [call(): pl.pallas_call(kernel, out_shape=tuple(outs), in_specs=[in_spec] * len(op...]
  transfers between devices with their start and end apart: 12 -> 12, of which waited for: 9 -> 7; matrix products, arithmetic and copies ran while one was open for 0% -> 0% of each run, Pallas kernels for 16% -> 15%
where the time goes in v14:
time: 66.6 us; the launch traced here: 66.5 us
  waiting for transfers between devices  38.8 us (58%)
  Pallas kernels  16.3 us (24%)
  starting transfers between devices  10.5 us (16%)
  between operations  0.73 us (1%)
    ppermute x12, waiting for transfers between devices, send(): lax.ppermute(block, AXIS, [(i, target(i) % count) for i in range(count)])  38.8 us
    pallas_call x5, Pallas kernels, call(): pl.pallas_call(kernel, out_shape=tuple(outs), in_specs=[in_spec] * len(op...  16.3 us
    ppermute x12, starting transfers between devices, send(): lax.ppermute(block, AXIS, [(i, target(i) % count) for i in range(count)])  10.5 us
  transfers between devices with their start and end apart: 12, of which 7 were waited for; matrix products, arithmetic and copies ran while one was open for 0% of the time, Pallas kernels for 15%

profile of v14, /device:TPU:0, one launch (start us, length us, event | category | flops | bytes accessed | tf_op | source)
XLA Modules:
  0.0 66.5 jit_solution(8239688458404692695)
XLA Ops:
  0.6 0.0 copy-start.1
  0.6 0.0 copy-start
  0.6 2.2 %shard_map.41 = (bf16[256,1152]{1,0:T(8,128)(2,1)S(1)}, bf16[256,1152]{1,0:T(8,128)(2,1)S(1)}, bf16[512,1152]{1,0:T(8,128)(2,1)S(1)}, bf16[512,1152]{1,0:T(8,128)(2,1)S(1)}) custom-call(bf16[512,1152]{1,0:T(8,128)(2,1)} %refs_0_.5, bf16[512,1152]{1,0:T(8,128)(2,1)} %refs_3_.1), custom_call_target="tpu_custom_call" | custom-call | flops 1 | bytes 1 | tf_op jit(solution)/shard_map/pallas_call | solution.py:185
  2.8 0.5 collective-permute-start.3
  3.3 2.6 %collective-permute-start.6 = (bf16[256,1152]{1,0:T(8,128)(2,1)S(1)}, bf16[256,1152]{1,0:T(8,128)(2,1)S(1)}, u32[]{:S(2)}, u32[]{:S(2)}) collective-permute-start(bf16[256,1152]{1,0:T(8,128)(2,1)S(1)} %get-tuple-element.22), channel_id=1, source_target_pairs={{0,4},{2,6},{4,8},{6,10},{8,12},{10,14},{12,16},{14,18},{16,20},{1... | collective-permute-start | bytes 1769480 | tf_op jit(solution)/shard_map/ppermute | solution.py:25
  5.9 3.1 %collective-permute-start.2 = (bf16[256,1152]{1,0:T(8,128)(2,1)S(1)}, bf16[256,1152]{1,0:T(8,128)(2,1)S(1)}, u32[]{:S(2)}, u32[]{:S(2)}) collective-permute-start(bf16[256,1152]{1,0:T(8,128)(2,1)S(1)} %get-tuple-element.17), channel_id=1, source_target_pairs={{0,28},{2,30},{4,0},{6,2},{8,4},{10,6},{12,8},{14,10},{16,12},{18,... | collective-permute-start | bytes 1769480 | tf_op jit(solution)/shard_map/ppermute | solution.py:25
  9.0 0.0 copy-done.1
  9.1 2.0 %collective-permute-start.10 = (bf16[256,1152]{1,0:T(8,128)(2,1)S(1)}, bf16[256,1152]{1,0:T(8,128)(2,1)S(1)}, u32[]{:S(2)}, u32[]{:S(2)}) collective-permute-start(bf16[256,1152]{1,0:T(8,128)(2,1)S(1)} %slice.7), channel_id=1, source_target_pairs={{0,28},{2,30},{4,0},{6,2},{8,4},{10,6},{12,8},{14,10},{16,12},{18,... | collective-permute-start | bytes 1769480 | tf_op jit(solution)/shard_map/ppermute | solution.py:25
  11.1 0.1 collective-permute-start.1
  11.3 0.0 collective-permute-done.3.refs_0_
  11.3 0.8 %collective-permute-start = (bf16[512,1152]{1,0:T(8,128)(2,1)S(1)}, bf16[512,1152]{1,0:T(8,128)(2,1)S(1)}, u32[]{:S(2)}, u32[]{:S(2)}) collective-permute-start(bf16[512,1152]{1,0:T(8,128)(2,1)S(1)} %get-tuple-element.16.far_own), channel_id=1, source_target_pairs={{0,26},{2,8},{4,30},{6,12},{8,2},{10,16},{12,6},{14,20},{16,10},{1... | collective-permute-start | bytes 3538952 | tf_op jit(solution)/shard_map/ppermute | solution.py:25
  12.1 4.4 %shard_map.42 = (f32[512,1152]{1,0:T(8,128)S(1)}, f32[512,1152]{1,0:T(8,128)S(1)}) custom-call(bf16[512,1152]{1,0:T(8,128)(2,1)S(1)} %copy-done.1, bf16[512,1152]{1,0:T(8,128)(2,1)S(1)} %copy-done, bf16[512,1152]{1,0:T(8,128)(2,1)S(1)} %get-tuple-element.18.near_own, bf16[512,1152]{1,0:T(8,128)(2,1)S(1)} %collective-permute-done.3.refs_0_), custom_call_target="tpu_custom_call" | custom-call | flops 1 | bytes 1 | tf_op jit(solution)/shard_map/pallas_call | solution.py:185
  16.5 28.3 %collective-permute-done.6.refs_5_ = bf16[256,1152]{1,0:T(8,128)(2,1)S(1)} collective-permute-done((bf16[256,1152]{1,0:T(8,128)(2,1)S(1)}, bf16[256,1152]{1,0:T(8,128)(2,1)S(1)}, u32[]{:S(2)}, u32[]{:S(2)}) %collective-permute-start.6) | collective-permute-done | bytes 589856 | tf_op jit(solution)/shard_map/ppermute | solution.py:25
  44.9 0.1 collective-permute-start.7
  45.0 2.4 %collective-permute-done.2.refs_1_ = bf16[256,1152]{1,0:T(8,128)(2,1)S(1)} collective-permute-done((bf16[256,1152]{1,0:T(8,128)(2,1)S(1)}, bf16[256,1152]{1,0:T(8,128)(2,1)S(1)}, u32[]{:S(2)}, u32[]{:S(2)}) %collective-permute-start.2) | collective-permute-done | bytes 589856 | tf_op jit(solution)/shard_map/ppermute | solution.py:25
  47.4 0.0 collective-permute-start.8
  47.4 0.0 collective-permute-done.7.refs_6_
  47.4 0.6 collective-permute-start.4
  48.0 0.9 %collective-permute-done.8.refs_7_ = bf16[128,1152]{1,0:T(8,128)(2,1)S(1)} collective-permute-done((bf16[128,1152]{1,0:T(8,128)(2,1)S(1)}, bf16[128,1152]{1,0:T(8,128)(2,1)S(1)}, u32[]{:S(2)}, u32[]{:S(2)}) %collective-permute-start.8) | collective-permute-done | bytes 294944 | tf_op jit(solution)/shard_map/ppermute | solution.py:25
  49.0 0.1 collective-permute-start.5
  49.1 0.3 collective-permute-done.4.refs_2_
  49.4 1.2 %collective-permute-done.5.refs_3_ = bf16[128,1152]{1,0:T(8,128)(2,1)S(1)} collective-permute-done((bf16[128,1152]{1,0:T(8,128)(2,1)S(1)}, bf16[128,1152]{1,0:T(8,128)(2,1)S(1)}, u32[]{:S(2)}, u32[]{:S(2)}) %collective-permute-start.5) | collective-permute-done | bytes 294944 | tf_op jit(solution)/shard_map/ppermute | solution.py:25
  50.5 3.4 %shard_map.43 = (f32[512,1152]{1,0:T(8,128)S(1)}, f32[512,1152]{1,0:T(8,128)S(1)}) custom-call(bf16[512,1152]{1,0:T(8,128)(2,1)S(1)} %copy-done, bf16[256,1152]{1,0:T(8,128)(2,1)S(1)} %collective-permute-done.2.refs_1_, bf16[128,1152]{1,0:T(8,128)(2,1)S(1)} %collective-permute-done.4.refs_2_, ...), custom_call_target="tpu_custom_call", output_to_operand_aliasing={{0}: (8, {}), {1}: (9, {})} | custom-call | flops 1 | bytes 1 | tf_op jit(solution)/shard_map/pallas_call | solution.py:185
  54.0 5.3 %collective-permute-done.10.refs_3_ = bf16[256,1152]{1,0:T(8,128)(2,1)S(1)} collective-permute-done((bf16[256,1152]{1,0:T(8,128)(2,1)S(1)}, bf16[256,1152]{1,0:T(8,128)(2,1)S(1)}, u32[]{:S(2)}, u32[]{:S(2)}) %collective-permute-start.10) | collective-permute-done | bytes 589856 | tf_op jit(solution)/shard_map/ppermute | solution.py:25
  59.2 0.0 collective-permute-done.1.refs_1_
  59.2 0.0 collective-permute-start.11
  59.2 0.5 collective-permute-start.9
  59.8 2.0 %shard_map.44 = (f32[512,1152]{1,0:T(8,128)S(1)}, f32[512,1152]{1,0:T(8,128)S(1)}) custom-call(bf16[512,1152]{1,0:T(8,128)(2,1)S(1)} %copy-done.1, bf16[256,1152]{1,0:T(8,128)(2,1)S(1)} %collective-permute-done.1.refs_1_, bf16[512,1152]{1,0:T(8,128)(2,1)S(1)} %copy-done, ...), custom_call_target="tpu_custom_call", output_to_operand_aliasing={{0}: (4, {}), {1}: (5, {})} | custom-call | flops 1 | bytes 1 | tf_op jit(solution)/shard_map/pallas_call | solution.py:185
  61.7 0.0 collective-permute-done.far
  61.7 0.0 collective-permute-done.11.refs_4_
  61.7 0.4 collective-permute-done.9.refs_1_
  62.1 4.4 %shard_map.45 = (f32[512,1152]{1,0:T(8,128)}, f32[512,1152]{1,0:T(8,128)}) custom-call(bf16[512,1152]{1,0:T(8,128)(2,1)S(1)} %get-tuple-element.16.far_own, bf16[512,1152]{1,0:T(8,128)(2,1)S(1)} %collective-permute-done.far, bf16[512,1152]{1,0:T(8,128)(2,1)S(1)} %copy-done.1, bf16[256,1152]{1,0:T(8,128)(2,1)S(1)} %collective-permute-done.9.refs_1_, ...), custom_call_target="tpu_custom_call" | custom-call | flops 1 | bytes 1 | tf_op jit(solution)/shard_map/pallas_call | solution.py:185
  (5 shorter events, 0.2 us)
Async XLA Ops:
  0.6 8.4 %copy-start.1 = (bf16[512,1152]{1,0:T(8,128)(2,1)S(1)}, bf16[512,1152]{1,0:T(8,128)(2,1)}, u32[]{:S(2)}) copy-start(bf16[512,1152]{1,0:T(8,128)(2,1)} %refs_0_.5) | copy-start | bytes 3538948
  0.6 10.5 %copy-start = (bf16[512,1152]{1,0:T(8,128)(2,1)S(1)}, bf16[512,1152]{1,0:T(8,128)(2,1)}, u32[]{:S(2)}) copy-start(bf16[512,1152]{1,0:T(8,128)(2,1)} %refs_3_.1) | copy-start | bytes 3538948
  2.8 8.5 %collective-permute-start.3 = (bf16[512,1152]{1,0:T(8,128)(2,1)S(1)}, bf16[512,1152]{1,0:T(8,128)(2,1)S(1)}, u32[]{:S(2)}, u32[]{:S(2)}) collective-permute-start(bf16[512,1152]{1,0:T(8,128)(2,1)S(1)} %get-tuple-element.18.near_own), channel_id=1, source_target_pairs={{0,2},{2,0},{4,6},{6,4},{8,10},{10,8},{12,14},{14,12},{16,18},{18,... | collective-permute-start | bytes 3538952 | tf_op jit(solution)/shard_map/ppermute | solution.py:25
  3.3 41.5 %collective-permute-start.6 = (bf16[256,1152]{1,0:T(8,128)(2,1)S(1)}, bf16[256,1152]{1,0:T(8,128)(2,1)S(1)}, u32[]{:S(2)}, u32[]{:S(2)}) collective-permute-start(bf16[256,1152]{1,0:T(8,128)(2,1)S(1)} %get-tuple-element.22), channel_id=1, source_target_pairs={{0,4},{2,6},{4,8},{6,10},{8,12},{10,14},{12,16},{14,18},{16,20},{1... | collective-permute-start | bytes 1769480 | tf_op jit(solution)/shard_map/ppermute | solution.py:25
  5.9 41.5 %collective-permute-start.2 = (bf16[256,1152]{1,0:T(8,128)(2,1)S(1)}, bf16[256,1152]{1,0:T(8,128)(2,1)S(1)}, u32[]{:S(2)}, u32[]{:S(2)}) collective-permute-start(bf16[256,1152]{1,0:T(8,128)(2,1)S(1)} %get-tuple-element.17), channel_id=1, source_target_pairs={{0,28},{2,30},{4,0},{6,2},{8,4},{10,6},{12,8},{14,10},{16,12},{18,... | collective-permute-start | bytes 1769480 | tf_op jit(solution)/shard_map/ppermute | solution.py:25
  9.1 50.1 %collective-permute-start.10 = (bf16[256,1152]{1,0:T(8,128)(2,1)S(1)}, bf16[256,1152]{1,0:T(8,128)(2,1)S(1)}, u32[]{:S(2)}, u32[]{:S(2)}) collective-permute-start(bf16[256,1152]{1,0:T(8,128)(2,1)S(1)} %slice.7), channel_id=1, source_target_pairs={{0,28},{2,30},{4,0},{6,2},{8,4},{10,6},{12,8},{14,10},{16,12},{18,... | collective-permute-start | bytes 1769480 | tf_op jit(solution)/shard_map/ppermute | solution.py:25
  11.1 48.1 %collective-permute-start.1 = (bf16[256,1152]{1,0:T(8,128)(2,1)S(1)}, bf16[256,1152]{1,0:T(8,128)(2,1)S(1)}, u32[]{:S(2)}, u32[]{:S(2)}) collective-permute-start(bf16[256,1152]{1,0:T(8,128)(2,1)S(1)} %slice.6), channel_id=1, source_target_pairs={{0,4},{2,6},{4,8},{6,10},{8,12},{10,14},{12,16},{14,18},{16,20},{1... | collective-permute-start | bytes 1769480 | tf_op jit(solution)/shard_map/ppermute | solution.py:25
  11.3 50.4 %collective-permute-start = (bf16[512,1152]{1,0:T(8,128)(2,1)S(1)}, bf16[512,1152]{1,0:T(8,128)(2,1)S(1)}, u32[]{:S(2)}, u32[]{:S(2)}) collective-permute-start(bf16[512,1152]{1,0:T(8,128)(2,1)S(1)} %get-tuple-element.16.far_own), channel_id=1, source_target_pairs={{0,26},{2,8},{4,30},{6,12},{8,2},{10,16},{12,6},{14,20},{16,10},{1... | collective-permute-start | bytes 3538952 | tf_op jit(solution)/shard_map/ppermute | solution.py:25
  44.9 2.5 %collective-permute-start.7 = (bf16[128,1152]{1,0:T(8,128)(2,1)S(1)}, bf16[128,1152]{1,0:T(8,128)(2,1)S(1)}, u32[]{:S(2)}, u32[]{:S(2)}) collective-permute-start(bf16[128,1152]{1,0:T(8,128)(2,1)S(1)} %get-tuple-element.31), channel_id=1, source_target_pairs={{0,2},{2,0},{4,6},{6,4},{8,10},{10,8},{12,14},{14,12},{16,18},{18,... | collective-permute-start | bytes 884744 | tf_op jit(solution)/shard_map/ppermute | solution.py:25
  47.4 1.6 %collective-permute-start.8 = (bf16[128,1152]{1,0:T(8,128)(2,1)S(1)}, bf16[128,1152]{1,0:T(8,128)(2,1)S(1)}, u32[]{:S(2)}, u32[]{:S(2)}) collective-permute-start(bf16[128,1152]{1,0:T(8,128)(2,1)S(1)} %get-tuple-element.30), channel_id=1, source_target_pairs={{0,2},{2,0},{4,6},{6,4},{8,10},{10,8},{12,14},{14,12},{16,18},{18,... | collective-permute-start | bytes 884744 | tf_op jit(solution)/shard_map/ppermute | solution.py:25
  47.4 1.9 %collective-permute-start.4 = (bf16[128,1152]{1,0:T(8,128)(2,1)S(1)}, bf16[128,1152]{1,0:T(8,128)(2,1)S(1)}, u32[]{:S(2)}, u32[]{:S(2)}) collective-permute-start(bf16[128,1152]{1,0:T(8,128)(2,1)S(1)} %get-tuple-element.33), channel_id=1, source_target_pairs={{0,2},{2,0},{4,6},{6,4},{8,10},{10,8},{12,14},{14,12},{16,18},{18,... | collective-permute-start | bytes 884744 | tf_op jit(solution)/shard_map/ppermute | solution.py:25
  49.0 1.6 %collective-permute-start.5 = (bf16[128,1152]{1,0:T(8,128)(2,1)S(1)}, bf16[128,1152]{1,0:T(8,128)(2,1)S(1)}, u32[]{:S(2)}, u32[]{:S(2)}) collective-permute-start(bf16[128,1152]{1,0:T(8,128)(2,1)S(1)} %get-tuple-element.32), channel_id=1, source_target_pairs={{0,2},{2,0},{4,6},{6,4},{8,10},{10,8},{12,14},{14,12},{16,18},{18,... | collective-permute-start | bytes 884744 | tf_op jit(solution)/shard_map/ppermute | solution.py:25
  59.2 2.5 %collective-permute-start.11 = (bf16[256,1152]{1,0:T(8,128)(2,1)S(1)}, bf16[256,1152]{1,0:T(8,128)(2,1)S(1)}, u32[]{:S(2)}, u32[]{:S(2)}) collective-permute-start(bf16[256,1152]{1,0:T(8,128)(2,1)S(1)} %collective-permute-done.10.refs_3_), channel_id=1, source_target_pairs={{0,2},{2,0},{4,6},{6,4},{8,10},{10,8},{12,14},{14,12},{16,18},{18,... | collective-permute-start | bytes 1769480 | tf_op jit(solution)/shard_map/ppermute | solution.py:25
  59.2 2.8 %collective-permute-start.9 = (bf16[256,1152]{1,0:T(8,128)(2,1)S(1)}, bf16[256,1152]{1,0:T(8,128)(2,1)S(1)}, u32[]{:S(2)}, u32[]{:S(2)}) collective-permute-start(bf16[256,1152]{1,0:T(8,128)(2,1)S(1)} %collective-permute-done.1.refs_1_), channel_id=1, source_target_pairs={{0,2},{2,0},{4,6},{6,4},{8,10},{10,8},{12,14},{14,12},{16,18},{18,... | collective-permute-start | bytes 1769480 | tf_op jit(solution)/shard_map/ppermute | solution.py:25

commit v15 on v9

--- a/solution.py
+++ b/solution.py
@@ -11,6 +11,8 @@
 AXIS = "blk"
 FIRST_IMAGES = 8
 FIRST_TEXTS = 8
+NEAR_ENDS = (11, 22)
+NEAR_PARTS = len(NEAR_ENDS) + 1
 LAST_TILE = 256
 COPY_ROWS = 128
 VMEM_MIB = 32
@@ -92,7 +94,8 @@
                 copy.wait()
 
 
-def own_kernel(factor, image_ref, text_ref, image_sum, text_sum):
+def own_kernel(factor, image_ref, text_ref, near_own, *refs):
+    near, (image_sum, text_sum, joined) = refs[:NEAR_PARTS], refs[NEAR_PARTS:]
     rows = image_ref.shape[0]
     shape = (rows, rows)
     matched = lax.broadcasted_iota(jnp.int32, shape, 0) == lax.broadcasted_iota(
@@ -101,6 +104,13 @@
     for own, others, total in ((image_ref, text_ref, image_sum), (text_ref, image_ref, text_sum)):
         chance = 1.0 / (1.0 + decay(factor, logits(own, others)))
         total[...] = product(chance - matched.astype(jnp.float32), others)
+    is_1 = core().astype(jnp.float32)
+
+    def use(value):
+        image_sum[...] += value * is_1
+        text_sum[...] += value * (1.0 - is_1)
+
+    add_all(factor, [(near_own, join(near, joined), use)])
 
 
 def step_kernel(factor, units, sides, *refs):
@@ -125,43 +135,41 @@
             add(side - 2, value * (1.0 - is_1))
             add(3 - side, value * is_1)
 
-    def meet(side, own, visitors, scratch):
-        others = join(visitors, scratch)
-        if side == 3:
-            others = others.at[pl.ds((1 - core()) * own.shape[0], own.shape[0])]
-        return own, others, functools.partial(use, side)
-
     add_all(
         factor,
         [
-            meet(side, own, visitors, scratch)
+            (own, join(visitors, scratch), functools.partial(use, side))
             for (side, _), (own, visitors), scratch in zip(units, parts, joined)
         ],
     )
 
 
-def last_kernel(factor, counts, *refs):
-    parts = []
-    for count in counts:
-        parts.append((refs[0], refs[1 : 1 + count], refs[1 + count]))
-        refs = refs[2 + count :]
-    outs, helds, joined, sems = refs[:2], refs[2:4], refs[4:6], refs[6]
+def last_kernel(factor, far_own, far, image_ref, texts, image_sum, text_ref, images, *refs):
+    text_sum, outs, helds, far_held, sems = refs[0], refs[1:3], refs[3:5], refs[5], refs[6]
+    sides = ((image_ref, texts, image_sum), (text_ref, images, text_sum))
+    is_1 = core().astype(jnp.float32)
+    masks = ((1.0 - is_1) * factor, is_1 * factor)
     copies = []
 
-    def use(total, held, out, start, value):
+    def use_far(start, value):
+        far_held[pl.ds(start, LAST_TILE)] = value
+
+    def use(side, start, value):
         rows = pl.ds(start, LAST_TILE)
-        held[rows] = (total[rows] + value) * factor
+        held, out = helds[side], outs[side]
+        total = (sides[side][2][rows] + value) * factor
+        held[rows] = total + far_held[rows] * masks[side]
         for first in range(start, start + LAST_TILE, COPY_ROWS):
             span = pl.ds(first, COPY_ROWS)
             copies.append(pltpu.make_async_copy(held.at[span], out.at[span], sems.at[len(copies)]))
             copies[-1].start()
 
     units = []
-    for (own, visitors, total), held, out, scratch in zip(parts, helds, outs, joined):
-        others = join(visitors, scratch)
-        for start in range(0, own.shape[0], LAST_TILE):
-            act = functools.partial(use, total, held, out, start)
-            units.append((own.at[pl.ds(start, LAST_TILE)], others, act))
+    for start in range(0, far_own.shape[0], LAST_TILE):
+        rows = pl.ds(start, LAST_TILE)
+        units.append((far_own.at[rows], far, functools.partial(use_far, start)))
+        for side, (own, others, _) in enumerate(sides):
+            units.append((own.at[rows], others, functools.partial(use, side, start)))
     add_all(factor, units)
     for copy in copies:
         copy.wait()
@@ -231,24 +239,29 @@
         core_pick_kernel, [block, block], in_hbm, [pltpu.SemaphoreType.DMA((2,))], in_spec=ANY
     )
     far = send(far_own, lambda i: i + 3 if i % 2 else i - 3)
-    pairs = [[i, i + 1] for i in range(0, lax.axis_size(AXIS), 2)]
-    near = [lax.all_gather(near_own, AXIS, axis_index_groups=pairs, tiled=True)]
+    near = [
+        send(part, lambda i: i ^ 1)
+        for part in jnp.split(near_own, [rows * end // 32 for end in NEAR_ENDS])
+    ]
     later_images = next_images(image_embed[cut_images:])
     later_texts = next_texts(text_embed[cut_texts:])
-    sums = call(functools.partial(own_kernel, factor), (kept, kept), (image_embed, text_embed))
+    sums = call(
+        functools.partial(own_kernel, factor),
+        (kept, kept),
+        (image_embed, text_embed, near_own, *near),
+        [block],
+    )
     sums = dict(enumerate(sums))
 
     images, texts = after(images, *sums.values()), after(texts, *sums.values())
     swapped_images, swapped_texts = swap(images, 2), swap(texts, 2)
     sums = step(
         [
-            (3, near_own, near),
+            (1, text_embed, (images, *swapped_images)),
             (0, image_embed, (texts, *swapped_texts)),
-            (1, text_embed, (images, *swapped_images)),
         ],
         sums,
     )
-    sums = step([(2, far_own, (after(far, sums[0]),))], sums)
 
     images, texts = after(later_images, sums[0]), after(later_texts, sums[0])
     swapped_images, swapped_texts = swap(images, 1), swap(texts, 1)
@@ -259,13 +272,11 @@
         ],
         sums,
     )
-    operands = (image_embed, *swapped_texts, sums[0], text_embed, *swapped_images, sums[1])
     return call(
-        functools.partial(last_kernel, factor, (1, 1)),
+        functools.partial(last_kernel, factor),
         (grad, grad),
-        operands,
-        [kept, kept, depth((texts,)), depth((images,))]
-        + [pltpu.SemaphoreType.DMA((2 * rows // COPY_ROWS,))],
+        (far_own, far, image_embed, *swapped_texts, sums[0], text_embed, *swapped_images, sums[1]),
+        [kept] * 3 + [pltpu.SemaphoreType.DMA((2 * rows // COPY_ROWS,))],
     )
 
 

time: 88 us -> 68.2 us (0.78)
  local copies, waits for them, and re-layouts: 19.5 us -> 0.29 us
  waiting for transfers between devices: 18.9 us -> 38 us
  between operations: 14.2 us -> 0.76 us
  Pallas kernels: 23.9 us -> 17.1 us
  starting transfers between devices: 10.6 us -> 11.9 us
    ppermute x11 -> x14, waiting for transfers between devices: 18.9 us -> 38 us  [send(): lax.ppermute(block, AXIS, [(i, target(i) % count) for i in range(count)])]
    unnamed x34 -> x4, local copies, waits for them, and re-layouts: 17.6 us -> 0.01 us
    pallas_call x7 -> x6, Pallas kernels: 23.9 us -> 17.1 us  [call(): pl.pallas_call(kernel, out_shape=tuple(outs), in_specs=[in_spec] * len(op...]
    ppermute x11 -> x14, starting transfers between devices: 10.6 us -> 11.9 us  [send(): lax.ppermute(block, AXIS, [(i, target(i) % count) for i in range(count)])]
    slice x1, local copies, waits for them, and re-layouts: 0.93 us -> 0.05 us  [local(): later_texts = next_texts(text_embed[cut_texts:])]
  transfers between devices with their start and end apart: 12 -> 14, of which waited for: 4 -> 7; matrix products, arithmetic and copies ran while one was open for 2% -> 0% of each run, Pallas kernels for 20% -> 17%
where the time goes in v15:
time: 68.2 us; the launch traced here: 68 us
  waiting for transfers between devices  38 us (56%)
  Pallas kernels  17.1 us (25%)
  starting transfers between devices  11.9 us (17%)
  between operations  0.76 us (1%)
    ppermute x14, waiting for transfers between devices, send(): lax.ppermute(block, AXIS, [(i, target(i) % count) for i in range(count)])  38 us
    pallas_call x6, Pallas kernels, call(): pl.pallas_call(kernel, out_shape=tuple(outs), in_specs=[in_spec] * len(op...  17.1 us
    ppermute x14, starting transfers between devices, send(): lax.ppermute(block, AXIS, [(i, target(i) % count) for i in range(count)])  11.9 us
  transfers between devices with their start and end apart: 14, of which 7 were waited for; matrix products, arithmetic and copies ran while one was open for 0% of the time, Pallas kernels for 17%

profile of v15, /device:TPU:0, one launch (start us, length us, event | category | flops | bytes accessed | tf_op | source)
XLA Modules:
  0.0 68.0 jit_solution(16133476766718472370)
XLA Ops:
  0.6 1.3 %shard_map.42 = (bf16[256,1152]{1,0:T(8,128)(2,1)S(1)}, bf16[256,1152]{1,0:T(8,128)(2,1)S(1)}) custom-call(bf16[512,1152]{1,0:T(8,128)(2,1)} %image_ref.7, bf16[512,1152]{1,0:T(8,128)(2,1)} %text_ref.7), custom_call_target="tpu_custom_call" | custom-call | flops 1 | bytes 1 | tf_op jit(solution)/shard_map/pallas_call | solution.py:187
  1.9 0.0 copy-start
  1.9 3.0 %collective-permute-start.8 = (bf16[256,1152]{1,0:T(8,128)(2,1)S(1)}, bf16[256,1152]{1,0:T(8,128)(2,1)S(1)}, u32[]{:S(2)}, u32[]{:S(2)}) collective-permute-start(bf16[256,1152]{1,0:T(8,128)(2,1)S(1)} %get-tuple-element.22), channel_id=1, source_target_pairs={{0,4},{2,6},{4,8},{6,10},{8,12},{10,14},{12,16},{14,18},{16,20},{1... | collective-permute-start | bytes 1769480 | tf_op jit(solution)/shard_map/ppermute | solution.py:26
  4.9 1.6 %shard_map.41 = (bf16[512,1152]{1,0:T(8,128)(2,1)S(1)}, bf16[512,1152]{1,0:T(8,128)(2,1)S(1)}) custom-call(bf16[512,1152]{1,0:T(8,128)(2,1)} %image_ref.7, bf16[512,1152]{1,0:T(8,128)(2,1)} %text_ref.7), custom_call_target="tpu_custom_call" | custom-call | flops 1 | bytes 1 | tf_op jit(solution)/shard_map/pallas_call | solution.py:187
  6.6 0.0 copy-start.1
  6.6 0.1 fusion
  6.7 0.1 collective-permute-start.3
  6.7 0.5 collective-permute-start.4
  7.3 0.1 collective-permute-start.5
  7.4 3.1 %collective-permute-start.2 = (bf16[256,1152]{1,0:T(8,128)(2,1)S(1)}, bf16[256,1152]{1,0:T(8,128)(2,1)S(1)}, u32[]{:S(2)}, u32[]{:S(2)}) collective-permute-start(bf16[256,1152]{1,0:T(8,128)(2,1)S(1)} %get-tuple-element.17), channel_id=1, source_target_pairs={{0,28},{2,30},{4,0},{6,2},{8,4},{10,6},{12,8},{14,10},{16,12},{18,... | collective-permute-start | bytes 1769480 | tf_op jit(solution)/shard_map/ppermute | solution.py:26
  10.7 2.0 %collective-permute-start.12 = (bf16[256,1152]{1,0:T(8,128)(2,1)S(1)}, bf16[256,1152]{1,0:T(8,128)(2,1)S(1)}, u32[]{:S(2)}, u32[]{:S(2)}) collective-permute-start(bf16[256,1152]{1,0:T(8,128)(2,1)S(1)} %slice.7), channel_id=1, source_target_pairs={{0,28},{2,30},{4,0},{6,2},{8,4},{10,6},{12,8},{14,10},{16,12},{18,... | collective-permute-start | bytes 1769480 | tf_op jit(solution)/shard_map/ppermute | solution.py:26
  12.7 0.0 collective-permute-done.3.refs_0_
  12.7 0.0 collective-permute-start.1
  12.8 0.0 collective-permute-done.4.refs_1_
  12.8 1.6 %collective-permute-start = (bf16[512,1152]{1,0:T(8,128)(2,1)S(1)}, bf16[512,1152]{1,0:T(8,128)(2,1)S(1)}, u32[]{:S(2)}, u32[]{:S(2)}) collective-permute-start(bf16[512,1152]{1,0:T(8,128)(2,1)S(1)} %get-tuple-element.16.far_own), channel_id=1, source_target_pairs={{0,26},{2,8},{4,30},{6,12},{8,2},{10,16},{12,6},{14,20},{16,10},{1... | collective-permute-start | bytes 3538952 | tf_op jit(solution)/shard_map/ppermute | solution.py:26
  14.4 4.4 %shard_map.43 = (f32[512,1152]{1,0:T(8,128)S(1)}, f32[512,1152]{1,0:T(8,128)S(1)}) custom-call(bf16[512,1152]{1,0:T(8,128)(2,1)S(1)} %copy-done, bf16[512,1152]{1,0:T(8,128)(2,1)S(1)} %copy-done.1, bf16[512,1152]{1,0:T(8,128)(2,1)S(1)} %get-tuple-element.18.near_own, bf16[176,1152]{1,0:T(8,128)(2,1)S(1)} %collective-permute-done.3.refs_0_, ...), custom_call_target="tpu_custom_call" | custom-call | flops 1 | bytes 1 | tf_op jit(solution)/shard_map/pallas_call | solution.py:187
  18.8 25.1 %collective-permute-done.8.refs_5_ = bf16[256,1152]{1,0:T(8,128)(2,1)S(1)} collective-permute-done((bf16[256,1152]{1,0:T(8,128)(2,1)S(1)}, bf16[256,1152]{1,0:T(8,128)(2,1)S(1)}, u32[]{:S(2)}, u32[]{:S(2)}) %collective-permute-start.8) | collective-permute-done | bytes 589856 | tf_op jit(solution)/shard_map/ppermute | solution.py:26
  44.0 0.1 collective-permute-start.10
  44.1 2.5 %collective-permute-done.2.refs_1_ = bf16[256,1152]{1,0:T(8,128)(2,1)S(1)} collective-permute-done((bf16[256,1152]{1,0:T(8,128)(2,1)S(1)}, bf16[256,1152]{1,0:T(8,128)(2,1)S(1)}, u32[]{:S(2)}, u32[]{:S(2)}) %collective-permute-start.2) | collective-permute-done | bytes 589856 | tf_op jit(solution)/shard_map/ppermute | solution.py:26
  46.6 0.0 collective-permute-start.9
  46.7 0.6 collective-permute-start.6
  47.3 0.9 %collective-permute-done.9.refs_6_ = bf16[128,1152]{1,0:T(8,128)(2,1)S(1)} collective-permute-done((bf16[128,1152]{1,0:T(8,128)(2,1)S(1)}, bf16[128,1152]{1,0:T(8,128)(2,1)S(1)}, u32[]{:S(2)}, u32[]{:S(2)}) %collective-permute-start.9) | collective-permute-done | bytes 294944 | tf_op jit(solution)/shard_map/ppermute | solution.py:26
  48.2 0.1 collective-permute-start.7
  48.3 0.3 collective-permute-done.6.refs_2_
  48.6 1.2 %collective-permute-done.7.refs_3_ = bf16[128,1152]{1,0:T(8,128)(2,1)S(1)} collective-permute-done((bf16[128,1152]{1,0:T(8,128)(2,1)S(1)}, bf16[128,1152]{1,0:T(8,128)(2,1)S(1)}, u32[]{:S(2)}, u32[]{:S(2)}) %collective-permute-start.7) | collective-permute-done | bytes 294944 | tf_op jit(solution)/shard_map/ppermute | solution.py:26
  49.8 3.4 %shard_map.44 = (f32[512,1152]{1,0:T(8,128)S(1)}, f32[512,1152]{1,0:T(8,128)S(1)}) custom-call(bf16[512,1152]{1,0:T(8,128)(2,1)S(1)} %copy-done.1, bf16[256,1152]{1,0:T(8,128)(2,1)S(1)} %collective-permute-done.2.refs_1_, bf16[128,1152]{1,0:T(8,128)(2,1)S(1)} %collective-permute-done.6.refs_2_, ...), custom_call_target="tpu_custom_call", output_to_operand_aliasing={{0}: (8, {}), {1}: (9, {})} | custom-call | flops 1 | bytes 1 | tf_op jit(solution)/shard_map/pallas_call | solution.py:187
  53.2 6.0 %collective-permute-done.12.refs_3_ = bf16[256,1152]{1,0:T(8,128)(2,1)S(1)} collective-permute-done((bf16[256,1152]{1,0:T(8,128)(2,1)S(1)}, bf16[256,1152]{1,0:T(8,128)(2,1)S(1)}, u32[]{:S(2)}, u32[]{:S(2)}) %collective-permute-start.12) | collective-permute-done | bytes 589856 | tf_op jit(solution)/shard_map/ppermute | solution.py:26
  59.2 0.1 collective-permute-start.13
  59.3 0.4 collective-permute-start.11
  59.7 1.9 %shard_map.45 = (f32[512,1152]{1,0:T(8,128)S(1)}, f32[512,1152]{1,0:T(8,128)S(1)}) custom-call(bf16[512,1152]{1,0:T(8,128)(2,1)S(1)} %copy-done, bf16[256,1152]{1,0:T(8,128)(2,1)S(1)} %collective-permute-done.1.refs_1_, bf16[512,1152]{1,0:T(8,128)(2,1)S(1)} %copy-done.1, ...), custom_call_target="tpu_custom_call", output_to_operand_aliasing={{0}: (4, {}), {1}: (5, {})} | custom-call | flops 1 | bytes 1 | tf_op jit(solution)/shard_map/pallas_call | solution.py:187
  61.7 1.9 %collective-permute-done.far = bf16[512,1152]{1,0:T(8,128)(2,1)S(1)} collective-permute-done((bf16[512,1152]{1,0:T(8,128)(2,1)S(1)}, bf16[512,1152]{1,0:T(8,128)(2,1)S(1)}, u32[]{:S(2)}, u32[]{:S(2)}) %collective-permute-start) | collective-permute-done | bytes 1179680 | tf_op jit(solution)/shard_map/ppermute | solution.py:26
  63.6 4.4 %shard_map.46 = (f32[512,1152]{1,0:T(8,128)}, f32[512,1152]{1,0:T(8,128)}) custom-call(bf16[512,1152]{1,0:T(8,128)(2,1)S(1)} %get-tuple-element.16.far_own, bf16[512,1152]{1,0:T(8,128)(2,1)S(1)} %collective-permute-done.far, bf16[512,1152]{1,0:T(8,128)(2,1)S(1)} %copy-done, bf16[256,1152]{1,0:T(8,128)(2,1)S(1)} %collective-permute-done.11.texts, ...), custom_call_target="tpu_custom_call" | custom-call | flops 1 | bytes 1 | tf_op jit(solution)/shard_map/pallas_call | solution.py:187
  (12 shorter events, 0.2 us)
Async XLA Ops:
  1.9 8.7 %copy-start = (bf16[512,1152]{1,0:T(8,128)(2,1)S(1)}, bf16[512,1152]{1,0:T(8,128)(2,1)}, u32[]{:S(2)}) copy-start(bf16[512,1152]{1,0:T(8,128)(2,1)} %image_ref.7) | copy-start | bytes 3538948
  1.9 42.0 %collective-permute-start.8 = (bf16[256,1152]{1,0:T(8,128)(2,1)S(1)}, bf16[256,1152]{1,0:T(8,128)(2,1)S(1)}, u32[]{:S(2)}, u32[]{:S(2)}) collective-permute-start(bf16[256,1152]{1,0:T(8,128)(2,1)S(1)} %get-tuple-element.22), channel_id=1, source_target_pairs={{0,4},{2,6},{4,8},{6,10},{8,12},{10,14},{12,16},{14,18},{16,20},{1... | collective-permute-start | bytes 1769480 | tf_op jit(solution)/shard_map/ppermute | solution.py:26
  6.6 4.0 %copy-start.1 = (bf16[512,1152]{1,0:T(8,128)(2,1)S(1)}, bf16[512,1152]{1,0:T(8,128)(2,1)}, u32[]{:S(2)}) copy-start(bf16[512,1152]{1,0:T(8,128)(2,1)} %text_ref.7) | copy-start | bytes 3538948
  6.7 6.1 %collective-permute-start.3 = (bf16[176,1152]{1,0:T(8,128)(2,1)S(1)}, bf16[176,1152]{1,0:T(8,128)(2,1)S(1)}, u32[]{:S(2)}, u32[]{:S(2)}) collective-permute-start(bf16[176,1152]{1,0:T(8,128)(2,1)S(1)} %get-tuple-element.31), channel_id=1, source_target_pairs={{0,2},{2,0},{4,6},{6,4},{8,10},{10,8},{12,14},{14,12},{16,18},{18,... | collective-permute-start | bytes 1216520 | tf_op jit(solution)/shard_map/ppermute | solution.py:26
  6.7 6.0 %collective-permute-start.4 = (bf16[176,1152]{1,0:T(8,128)(2,1)S(1)}, bf16[176,1152]{1,0:T(8,128)(2,1)S(1)}, u32[]{:S(2)}, u32[]{:S(2)}) collective-permute-start(bf16[176,1152]{1,0:T(8,128)(2,1)S(1)} %get-tuple-element.30), channel_id=1, source_target_pairs={{0,2},{2,0},{4,6},{6,4},{8,10},{10,8},{12,14},{14,12},{16,18},{18,... | collective-permute-start | bytes 1216520 | tf_op jit(solution)/shard_map/ppermute | solution.py:26
  7.3 3.4 %collective-permute-start.5 = (bf16[160,1152]{1,0:T(8,128)(2,1)S(1)}, bf16[160,1152]{1,0:T(8,128)(2,1)S(1)}, u32[]{:S(2)}, u32[]{:S(2)}) collective-permute-start(bf16[160,1152]{1,0:T(8,128)(2,1)S(1)} %split.23), channel_id=1, source_target_pairs={{0,2},{2,0},{4,6},{6,4},{8,10},{10,8},{12,14},{14,12},{16,18},{18,... | collective-permute-start | bytes 1105928 | tf_op jit(solution)/shard_map/ppermute | solution.py:26
  7.4 39.2 %collective-permute-start.2 = (bf16[256,1152]{1,0:T(8,128)(2,1)S(1)}, bf16[256,1152]{1,0:T(8,128)(2,1)S(1)}, u32[]{:S(2)}, u32[]{:S(2)}) collective-permute-start(bf16[256,1152]{1,0:T(8,128)(2,1)S(1)} %get-tuple-element.17), channel_id=1, source_target_pairs={{0,28},{2,30},{4,0},{6,2},{8,4},{10,6},{12,8},{14,10},{16,12},{18,... | collective-permute-start | bytes 1769480 | tf_op jit(solution)/shard_map/ppermute | solution.py:26
  10.7 48.5 %collective-permute-start.12 = (bf16[256,1152]{1,0:T(8,128)(2,1)S(1)}, bf16[256,1152]{1,0:T(8,128)(2,1)S(1)}, u32[]{:S(2)}, u32[]{:S(2)}) collective-permute-start(bf16[256,1152]{1,0:T(8,128)(2,1)S(1)} %slice.7), channel_id=1, source_target_pairs={{0,28},{2,30},{4,0},{6,2},{8,4},{10,6},{12,8},{14,10},{16,12},{18,... | collective-permute-start | bytes 1769480 | tf_op jit(solution)/shard_map/ppermute | solution.py:26
  12.7 46.5 %collective-permute-start.1 = (bf16[256,1152]{1,0:T(8,128)(2,1)S(1)}, bf16[256,1152]{1,0:T(8,128)(2,1)S(1)}, u32[]{:S(2)}, u32[]{:S(2)}) collective-permute-start(bf16[256,1152]{1,0:T(8,128)(2,1)S(1)} %slice.6), channel_id=1, source_target_pairs={{0,4},{2,6},{4,8},{6,10},{8,12},{10,14},{12,16},{14,18},{16,20},{1... | collective-permute-start | bytes 1769480 | tf_op jit(solution)/shard_map/ppermute | solution.py:26
  12.8 50.8 %collective-permute-start = (bf16[512,1152]{1,0:T(8,128)(2,1)S(1)}, bf16[512,1152]{1,0:T(8,128)(2,1)S(1)}, u32[]{:S(2)}, u32[]{:S(2)}) collective-permute-start(bf16[512,1152]{1,0:T(8,128)(2,1)S(1)} %get-tuple-element.16.far_own), channel_id=1, source_target_pairs={{0,26},{2,8},{4,30},{6,12},{8,2},{10,16},{12,6},{14,20},{16,10},{1... | collective-permute-start | bytes 3538952 | tf_op jit(solution)/shard_map/ppermute | solution.py:26
  44.0 2.7 %collective-permute-start.10 = (bf16[128,1152]{1,0:T(8,128)(2,1)S(1)}, bf16[128,1152]{1,0:T(8,128)(2,1)S(1)}, u32[]{:S(2)}, u32[]{:S(2)}) collective-permute-start(bf16[128,1152]{1,0:T(8,128)(2,1)S(1)} %get-tuple-element.32), channel_id=1, source_target_pairs={{0,2},{2,0},{4,6},{6,4},{8,10},{10,8},{12,14},{14,12},{16,18},{18,... | collective-permute-start | bytes 884744 | tf_op jit(solution)/shard_map/ppermute | solution.py:26
  46.6 1.6 %collective-permute-start.9 = (bf16[128,1152]{1,0:T(8,128)(2,1)S(1)}, bf16[128,1152]{1,0:T(8,128)(2,1)S(1)}, u32[]{:S(2)}, u32[]{:S(2)}) collective-permute-start(bf16[128,1152]{1,0:T(8,128)(2,1)S(1)} %get-tuple-element.33), channel_id=1, source_target_pairs={{0,2},{2,0},{4,6},{6,4},{8,10},{10,8},{12,14},{14,12},{16,18},{18,... | collective-permute-start | bytes 884744 | tf_op jit(solution)/shard_map/ppermute | solution.py:26
  46.7 1.9 %collective-permute-start.6 = (bf16[128,1152]{1,0:T(8,128)(2,1)S(1)}, bf16[128,1152]{1,0:T(8,128)(2,1)S(1)}, u32[]{:S(2)}, u32[]{:S(2)}) collective-permute-start(bf16[128,1152]{1,0:T(8,128)(2,1)S(1)} %get-tuple-element.35), channel_id=1, source_target_pairs={{0,2},{2,0},{4,6},{6,4},{8,10},{10,8},{12,14},{14,12},{16,18},{18,... | collective-permute-start | bytes 884744 | tf_op jit(solution)/shard_map/ppermute | solution.py:26
  48.2 1.6 %collective-permute-start.7 = (bf16[128,1152]{1,0:T(8,128)(2,1)S(1)}, bf16[128,1152]{1,0:T(8,128)(2,1)S(1)}, u32[]{:S(2)}, u32[]{:S(2)}) collective-permute-start(bf16[128,1152]{1,0:T(8,128)(2,1)S(1)} %get-tuple-element.34), channel_id=1, source_target_pairs={{0,2},{2,0},{4,6},{6,4},{8,10},{10,8},{12,14},{14,12},{16,18},{18,... | collective-permute-start | bytes 884744 | tf_op jit(solution)/shard_map/ppermute | solution.py:26
  59.2 4.4 %collective-permute-start.13 = (bf16[256,1152]{1,0:T(8,128)(2,1)S(1)}, bf16[256,1152]{1,0:T(8,128)(2,1)S(1)}, u32[]{:S(2)}, u32[]{:S(2)}) collective-permute-start(bf16[256,1152]{1,0:T(8,128)(2,1)S(1)} %collective-permute-done.12.refs_3_), channel_id=1, source_target_pairs={{0,2},{2,0},{4,6},{6,4},{8,10},{10,8},{12,14},{14,12},{16,18},{18,... | collective-permute-start | bytes 1769480 | tf_op jit(solution)/shard_map/ppermute | solution.py:26
  59.3 4.3 %collective-permute-start.11 = (bf16[256,1152]{1,0:T(8,128)(2,1)S(1)}, bf16[256,1152]{1,0:T(8,128)(2,1)S(1)}, u32[]{:S(2)}, u32[]{:S(2)}) collective-permute-start(bf16[256,1152]{1,0:T(8,128)(2,1)S(1)} %collective-permute-done.1.refs_1_), channel_id=1, source_target_pairs={{0,2},{2,0},{4,6},{6,4},{8,10},{10,8},{12,14},{14,12},{16,18},{18,... | collective-permute-start | bytes 1769480 | tf_op jit(solution)/shard_map/ppermute | solution.py:26

commit v16 on v14

--- a/solution.py
+++ b/solution.py
@@ -9,9 +9,7 @@
 from jax.sharding import PartitionSpec as P
 
 AXIS = "blk"
-FIRST_IMAGES = 8
-FIRST_TEXTS = 8
-NEAR_PARTS = 1
+NEAR_PARTS = 2
 LAST_TILE = 256
 COPY_ROWS = 128
 VMEM_MIB = 32
@@ -67,25 +65,19 @@
     return joined.at[pl.ds(0, start)]
 
 
-def pick_kernel(image_ref, text_ref, image_head, text_head, far_own, near_own, sems):
-    def move(k, source, out):
-        return pltpu.make_async_copy(source.at[pl.ds(0, out.shape[0])], out, sems.at[k])
-
-    heads = [move(0, image_ref, image_head), move(1, text_ref, text_head)]
-    for head in heads:
-        head.start()
+def core_pick_kernel(image_ref, text_ref, far_own, near_own, sems):
     for is_core, (far, near) in enumerate(((image_ref, text_ref), (text_ref, image_ref))):
 
         @pl.when(core() == is_core)
         def _():
-            blocks = [move(2, far, far_own), move(3, near, near_own)]
-            for block in blocks:
-                block.start()
-            for block in blocks:
-                block.wait()
-
-    for head in heads:
-        head.wait()
+            copies = [
+                pltpu.make_async_copy(far, far_own, sems.at[0]),
+                pltpu.make_async_copy(near, near_own, sems.at[1]),
+            ]
+            for copy in copies:
+                copy.start()
+            for copy in copies:
+                copy.wait()
 
 
 def own_kernel(factor, image_ref, text_ref, near_own, *refs):
@@ -223,20 +215,12 @@
         return send(piece, lambda i: i + 2)
 
     in_hbm = [pltpu.with_memory_space_constraint(x, pltpu.HBM) for x in (image_embed, text_embed)]
-    cut_images, cut_texts = rows * FIRST_IMAGES // 16, rows * FIRST_TEXTS // 16
-    heads = (cut_images, cut_texts)
-    image_head, text_head, far_own, near_own = call(
-        pick_kernel,
-        [pltpu.VMEM((head, width), dtype) for head in heads] + [block, block],
-        in_hbm,
-        [pltpu.SemaphoreType.DMA((4,))],
-        in_spec=ANY,
-    )
-    images, texts = next_images(image_head), next_texts(text_head)
+    images, texts = next_images(image_embed), next_texts(text_embed)
+    far_own, near_own = call(
+        core_pick_kernel, [block, block], in_hbm, [pltpu.SemaphoreType.DMA((2,))], in_spec=ANY
+    )
     far = send(far_own, lambda i: i + 3 if i % 2 else i - 3)
-    near = swap(near_own, 1)
-    later_images = next_images(image_embed[cut_images:])
-    later_texts = next_texts(text_embed[cut_texts:])
+    near = swap(near_own, 2)
     sums = call(
         functools.partial(own_kernel, factor),
         (kept, kept),
@@ -246,28 +230,12 @@
     sums = dict(enumerate(sums))
 
     images, texts = after(images, *sums.values()), after(texts, *sums.values())
-    swapped_images, swapped_texts = swap(images, 2), swap(texts, 2)
-    sums = step(
-        [
-            (1, text_embed, (images, *swapped_images)),
-            (0, image_embed, (texts, *swapped_texts)),
-        ],
-        sums,
-    )
-
-    images, texts = after(later_images, sums[0]), after(later_texts, sums[0])
-    swapped_images, swapped_texts = swap(images, 1), swap(texts, 1)
-    sums = step(
-        [
-            (0, image_embed, (texts,)),
-            (1, text_embed, (images,)),
-        ],
-        sums,
-    )
+    swapped_images, swapped_texts = swap(images, 2), swap(texts, 1)
+    sums = step([(1, text_embed, (images,)), (0, image_embed, (texts,))], sums)
     operands = (image_embed, *swapped_texts, sums[0], text_embed, *swapped_images, sums[1])
     operands = (far_own, far, *operands)
     return call(
-        functools.partial(last_kernel, factor, (1, 1)),
+        functools.partial(last_kernel, factor, (1, 2)),
         (grad, grad),
         operands,
         [kept, kept, depth((texts,)), depth((images,))]

time: 66.6 us -> 66.4 us (level)
  waiting for transfers between devices: 38.8 us -> 41.4 us
  starting transfers between devices: 10.5 us -> 8.85 us
  Pallas kernels: 16.3 us -> 15.1 us
    ppermute x12 -> x8, waiting for transfers between devices: 38.8 us -> 41.4 us  [send(): lax.ppermute(block, AXIS, [(i, target(i) % count) for i in range(count)])]
    ppermute x12 -> x8, starting transfers between devices: 10.5 us -> 8.85 us  [send(): lax.ppermute(block, AXIS, [(i, target(i) % count) for i in range(count)])]
    pallas_call x5 -> x4, Pallas kernels: 16.3 us -> 15.1 us  [call(): pl.pallas_call(kernel, out_shape=tuple(outs), in_specs=[in_spec] * len(op...]
  transfers between devices with their start and end apart: 12 -> 8, of which waited for: 7 -> 3; matrix products, arithmetic and copies ran while one was open for 0% -> 0% of each run, Pallas kernels for 15% -> 14%
where the time goes in v16:
time: 66.4 us; the launch traced here: 66.3 us
  waiting for transfers between devices  41.4 us (62%)
  Pallas kernels  15.1 us (23%)
  starting transfers between devices  8.85 us (13%)
  between operations  0.73 us (1%)
    ppermute x8, waiting for transfers between devices, send(): lax.ppermute(block, AXIS, [(i, target(i) % count) for i in range(count)])  41.4 us
    pallas_call x4, Pallas kernels, call(): pl.pallas_call(kernel, out_shape=tuple(outs), in_specs=[in_spec] * len(op...  15.1 us
    ppermute x8, starting transfers between devices, send(): lax.ppermute(block, AXIS, [(i, target(i) % count) for i in range(count)])  8.85 us
  transfers between devices with their start and end apart: 8, of which 3 were waited for; matrix products, arithmetic and copies ran while one was open for 0% of the time, Pallas kernels for 14%

profile of v16, /device:TPU:0, one launch (start us, length us, event | category | flops | bytes accessed | tf_op | source)
XLA Modules:
  0.0 66.3 jit_solution(8099365122031379764)
XLA Ops:
  0.6 3.0 %collective-permute-start.1 = (bf16[512,1152]{1,0:T(8,128)(2,1)}, bf16[512,1152]{1,0:T(8,128)(2,1)S(1)}, u32[]{:S(2)}, u32[]{:S(2)}) collective-permute-start(bf16[512,1152]{1,0:T(8,128)(2,1)} %refs_3_.1), channel_id=1, source_target_pairs={{0,4},{2,6},{4,8},{6,10},{8,12},{10,14},{12,16},{14,18},{16,20},{1... | collective-permute-start | bytes 3538952 | tf_op jit(solution)/shard_map/ppermute | solution.py:23
  3.6 3.1 %collective-permute-start.5 = (bf16[512,1152]{1,0:T(8,128)(2,1)}, bf16[512,1152]{1,0:T(8,128)(2,1)S(1)}, u32[]{:S(2)}, u32[]{:S(2)}) collective-permute-start(bf16[512,1152]{1,0:T(8,128)(2,1)} %refs_0_.3), channel_id=1, source_target_pairs={{0,28},{2,30},{4,0},{6,2},{8,4},{10,6},{12,8},{14,10},{16,12},{18,... | collective-permute-start | bytes 3538952 | tf_op jit(solution)/shard_map/ppermute | solution.py:23
  6.8 1.6 %shard_map.41 = (bf16[512,1152]{1,0:T(8,128)(2,1)S(1)}, bf16[512,1152]{1,0:T(8,128)(2,1)S(1)}) custom-call(bf16[512,1152]{1,0:T(8,128)(2,1)} %refs_0_.3, bf16[512,1152]{1,0:T(8,128)(2,1)} %refs_3_.1), custom_call_target="tpu_custom_call" | custom-call | flops 1 | bytes 1 | tf_op jit(solution)/shard_map/pallas_call | solution.py:177
  8.4 0.0 copy-start
  8.4 0.0 copy-start.1
  8.4 0.1 fusion.1
  8.5 0.1 collective-permute-start.3
  8.6 0.5 collective-permute-start.2
  9.1 1.6 %collective-permute-start = (bf16[512,1152]{1,0:T(8,128)(2,1)S(1)}, bf16[512,1152]{1,0:T(8,128)(2,1)S(1)}, u32[]{:S(2)}, u32[]{:S(2)}) collective-permute-start(bf16[512,1152]{1,0:T(8,128)(2,1)S(1)} %get-tuple-element.10.far_own), channel_id=1, source_target_pairs={{0,26},{2,8},{4,30},{6,12},{8,2},{10,16},{12,6},{14,20},{16,10},{1... | collective-permute-start | bytes 3538952 | tf_op jit(solution)/shard_map/ppermute | solution.py:23
  10.7 0.0 collective-permute-done.3.refs_1_
  10.7 0.7 %collective-permute-done.2.refs_0_ = bf16[256,1152]{1,0:T(8,128)(2,1)S(1)} collective-permute-done((bf16[256,1152]{1,0:T(8,128)(2,1)S(1)}, bf16[256,1152]{1,0:T(8,128)(2,1)S(1)}, u32[]{:S(2)}, u32[]{:S(2)}) %collective-permute-start.2) | collective-permute-done | bytes 589856 | tf_op jit(solution)/shard_map/ppermute | solution.py:23
  11.4 0.0 copy-done
  11.4 0.0 copy-done.1
  11.4 4.4 %shard_map.42 = (f32[512,1152]{1,0:T(8,128)S(1)}, f32[512,1152]{1,0:T(8,128)S(1)}) custom-call(bf16[512,1152]{1,0:T(8,128)(2,1)S(1)} %copy-done, bf16[512,1152]{1,0:T(8,128)(2,1)S(1)} %copy-done.1, bf16[512,1152]{1,0:T(8,128)(2,1)S(1)} %get-tuple-element.11.near_own, bf16[256,1152]{1,0:T(8,128)(2,1)S(1)} %collective-permute-done.2.refs_0_, ...), custom_call_target="tpu_custom_call" | custom-call | flops 1 | bytes 1 | tf_op jit(solution)/shard_map/pallas_call | solution.py:177
  15.9 38.6 %collective-permute-done.1.refs_3_ = bf16[512,1152]{1,0:T(8,128)(2,1)S(1)} collective-permute-done((bf16[512,1152]{1,0:T(8,128)(2,1)}, bf16[512,1152]{1,0:T(8,128)(2,1)S(1)}, u32[]{:S(2)}, u32[]{:S(2)}) %collective-permute-start.1) | collective-permute-done | bytes 1179680 | tf_op jit(solution)/shard_map/ppermute | solution.py:23
  54.5 0.0 collective-permute-start.4
  54.5 2.1 %collective-permute-done.5.refs_1_ = bf16[512,1152]{1,0:T(8,128)(2,1)S(1)} collective-permute-done((bf16[512,1152]{1,0:T(8,128)(2,1)}, bf16[512,1152]{1,0:T(8,128)(2,1)S(1)}, u32[]{:S(2)}, u32[]{:S(2)}) %collective-permute-start.5) | collective-permute-done | bytes 1179680 | tf_op jit(solution)/shard_map/ppermute | solution.py:23
  56.6 0.1 fusion
  56.7 0.1 collective-permute-start.7
  56.7 0.5 collective-permute-start.6
  57.2 3.4 %shard_map.43 = (f32[512,1152]{1,0:T(8,128)S(1)}, f32[512,1152]{1,0:T(8,128)S(1)}) custom-call(bf16[512,1152]{1,0:T(8,128)(2,1)S(1)} %copy-done.1, bf16[512,1152]{1,0:T(8,128)(2,1)S(1)} %collective-permute-done.5.refs_1_, bf16[512,1152]{1,0:T(8,128)(2,1)S(1)} %copy-done, ...), custom_call_target="tpu_custom_call", output_to_operand_aliasing={{0}: (4, {}), {1}: (5, {})} | custom-call | flops 1 | bytes 1 | tf_op jit(solution)/shard_map/pallas_call | solution.py:177
  60.6 0.0 collective-permute-done.far
  60.6 0.0 collective-permute-done.7.refs_5_
  60.7 0.0 collective-permute-done.6.refs_4_
  60.7 0.0 collective-permute-done.4.refs_1_
  60.7 5.6 %shard_map.44 = (f32[512,1152]{1,0:T(8,128)}, f32[512,1152]{1,0:T(8,128)}) custom-call(bf16[512,1152]{1,0:T(8,128)(2,1)S(1)} %get-tuple-element.10.far_own, bf16[512,1152]{1,0:T(8,128)(2,1)S(1)} %collective-permute-done.far, bf16[512,1152]{1,0:T(8,128)(2,1)S(1)} %copy-done, bf16[512,1152]{1,0:T(8,128)(2,1)S(1)} %collective-permute-done.4.refs_1_, ...), custom_call_target="tpu_custom_call" | custom-call | flops 1 | bytes 1 | tf_op jit(solution)/shard_map/pallas_call | solution.py:177
Async XLA Ops:
  0.6 53.8 %collective-permute-start.1 = (bf16[512,1152]{1,0:T(8,128)(2,1)}, bf16[512,1152]{1,0:T(8,128)(2,1)S(1)}, u32[]{:S(2)}, u32[]{:S(2)}) collective-permute-start(bf16[512,1152]{1,0:T(8,128)(2,1)} %refs_3_.1), channel_id=1, source_target_pairs={{0,4},{2,6},{4,8},{6,10},{8,12},{10,14},{12,16},{14,18},{16,20},{1... | collective-permute-start | bytes 3538952 | tf_op jit(solution)/shard_map/ppermute | solution.py:23
  3.6 52.9 %collective-permute-start.5 = (bf16[512,1152]{1,0:T(8,128)(2,1)}, bf16[512,1152]{1,0:T(8,128)(2,1)S(1)}, u32[]{:S(2)}, u32[]{:S(2)}) collective-permute-start(bf16[512,1152]{1,0:T(8,128)(2,1)} %refs_0_.3), channel_id=1, source_target_pairs={{0,28},{2,30},{4,0},{6,2},{8,4},{10,6},{12,8},{14,10},{16,12},{18,... | collective-permute-start | bytes 3538952 | tf_op jit(solution)/shard_map/ppermute | solution.py:23
  8.4 3.0 %copy-start = (bf16[512,1152]{1,0:T(8,128)(2,1)S(1)}, bf16[512,1152]{1,0:T(8,128)(2,1)}, u32[]{:S(2)}) copy-start(bf16[512,1152]{1,0:T(8,128)(2,1)} %refs_0_.3) | copy-start | bytes 3538948
  8.4 3.0 %copy-start.1 = (bf16[512,1152]{1,0:T(8,128)(2,1)S(1)}, bf16[512,1152]{1,0:T(8,128)(2,1)}, u32[]{:S(2)}) copy-start(bf16[512,1152]{1,0:T(8,128)(2,1)} %refs_3_.1) | copy-start | bytes 3538948
  8.5 2.2 %collective-permute-start.3 = (bf16[256,1152]{1,0:T(8,128)(2,1)S(1)}, bf16[256,1152]{1,0:T(8,128)(2,1)S(1)}, u32[]{:S(2)}, u32[]{:S(2)}) collective-permute-start(bf16[256,1152]{1,0:T(8,128)(2,1)S(1)} %get-tuple-element.20), channel_id=1, source_target_pairs={{0,2},{2,0},{4,6},{6,4},{8,10},{10,8},{12,14},{14,12},{16,18},{18,... | collective-permute-start | bytes 1769480 | tf_op jit(solution)/shard_map/ppermute | solution.py:23
  8.6 2.8 %collective-permute-start.2 = (bf16[256,1152]{1,0:T(8,128)(2,1)S(1)}, bf16[256,1152]{1,0:T(8,128)(2,1)S(1)}, u32[]{:S(2)}, u32[]{:S(2)}) collective-permute-start(bf16[256,1152]{1,0:T(8,128)(2,1)S(1)} %get-tuple-element.21), channel_id=1, source_target_pairs={{0,2},{2,0},{4,6},{6,4},{8,10},{10,8},{12,14},{14,12},{16,18},{18,... | collective-permute-start | bytes 1769480 | tf_op jit(solution)/shard_map/ppermute | solution.py:23
  9.1 51.5 %collective-permute-start = (bf16[512,1152]{1,0:T(8,128)(2,1)S(1)}, bf16[512,1152]{1,0:T(8,128)(2,1)S(1)}, u32[]{:S(2)}, u32[]{:S(2)}) collective-permute-start(bf16[512,1152]{1,0:T(8,128)(2,1)S(1)} %get-tuple-element.10.far_own), channel_id=1, source_target_pairs={{0,26},{2,8},{4,30},{6,12},{8,2},{10,16},{12,6},{14,20},{16,10},{1... | collective-permute-start | bytes 3538952 | tf_op jit(solution)/shard_map/ppermute | solution.py:23
  54.5 6.2 %collective-permute-start.4 = (bf16[512,1152]{1,0:T(8,128)(2,1)S(1)}, bf16[512,1152]{1,0:T(8,128)(2,1)S(1)}, u32[]{:S(2)}, u32[]{:S(2)}) collective-permute-start(bf16[512,1152]{1,0:T(8,128)(2,1)S(1)} %collective-permute-done.1.refs_3_), channel_id=1, source_target_pairs={{0,2},{2,0},{4,6},{6,4},{8,10},{10,8},{12,14},{14,12},{16,18},{18,... | collective-permute-start | bytes 3538952 | tf_op jit(solution)/shard_map/ppermute | solution.py:23
  56.7 4.0 %collective-permute-start.7 = (bf16[256,1152]{1,0:T(8,128)(2,1)S(1)}, bf16[256,1152]{1,0:T(8,128)(2,1)S(1)}, u32[]{:S(2)}, u32[]{:S(2)}) collective-permute-start(bf16[256,1152]{1,0:T(8,128)(2,1)S(1)} %get-tuple-element.18), channel_id=1, source_target_pairs={{0,2},{2,0},{4,6},{6,4},{8,10},{10,8},{12,14},{14,12},{16,18},{18,... | collective-permute-start | bytes 1769480 | tf_op jit(solution)/shard_map/ppermute | solution.py:23
  56.7 3.9 %collective-permute-start.6 = (bf16[256,1152]{1,0:T(8,128)(2,1)S(1)}, bf16[256,1152]{1,0:T(8,128)(2,1)S(1)}, u32[]{:S(2)}, u32[]{:S(2)}) collective-permute-start(bf16[256,1152]{1,0:T(8,128)(2,1)S(1)} %get-tuple-element.19), channel_id=1, source_target_pairs={{0,2},{2,0},{4,6},{6,4},{8,10},{10,8},{12,14},{14,12},{16,18},{18,... | collective-permute-start | bytes 1769480 | tf_op jit(solution)/shard_map/ppermute | solution.py:23

commit v17 on v16

--- a/solution.py
+++ b/solution.py
@@ -230,12 +230,12 @@
     sums = dict(enumerate(sums))
 
     images, texts = after(images, *sums.values()), after(texts, *sums.values())
-    swapped_images, swapped_texts = swap(images, 2), swap(texts, 1)
+    swapped_images, swapped_texts = swap(images, 1), swap(texts, 1)
     sums = step([(1, text_embed, (images,)), (0, image_embed, (texts,))], sums)
     operands = (image_embed, *swapped_texts, sums[0], text_embed, *swapped_images, sums[1])
     operands = (far_own, far, *operands)
     return call(
-        functools.partial(last_kernel, factor, (1, 2)),
+        functools.partial(last_kernel, factor, (1, 1)),
         (grad, grad),
         operands,
         [kept, kept, depth((texts,)), depth((images,))]

time: 66.4 us -> 65.6 us (0.988)
  starting transfers between devices: 8.85 us -> 7.89 us
    ppermute x8 -> x7, starting transfers between devices: 8.85 us -> 7.89 us  [send(): lax.ppermute(block, AXIS, [(i, target(i) % count) for i in range(count)])]
    ppermute x8 -> x7, waiting for transfers between devices: 41.4 us -> 41.8 us  [send(): lax.ppermute(block, AXIS, [(i, target(i) % count) for i in range(count)])]
  transfers between devices with their start and end apart: 8 -> 7, of which waited for: 3 -> 5; matrix products, arithmetic and copies ran while one was open for 0% -> 0% of each run, Pallas kernels for 14% -> 14%
where the time goes in v17:
time: 65.6 us; the launch traced here: 65.5 us
  waiting for transfers between devices  41.8 us (64%)
  Pallas kernels  15 us (23%)
  starting transfers between devices  7.89 us (12%)
  between operations  0.7 us (1%)
    ppermute x7, waiting for transfers between devices, send(): lax.ppermute(block, AXIS, [(i, target(i) % count) for i in range(count)])  41.8 us
    pallas_call x4, Pallas kernels, call(): pl.pallas_call(kernel, out_shape=tuple(outs), in_specs=[in_spec] * len(op...  15 us
    ppermute x7, starting transfers between devices, send(): lax.ppermute(block, AXIS, [(i, target(i) % count) for i in range(count)])  7.89 us
  transfers between devices with their start and end apart: 7, of which 5 were waited for; matrix products, arithmetic and copies ran while one was open for 0% of the time, Pallas kernels for 14%

profile of v17, /device:TPU:0, one launch (start us, length us, event | category | flops | bytes accessed | tf_op | source)
XLA Modules:
  0.0 65.5 jit_solution(1709207719513718932)
XLA Ops:
  0.6 6.1 %collective-permute-start.5 = (bf16[512,1152]{1,0:T(8,128)(2,1)}, bf16[512,1152]{1,0:T(8,128)(2,1)S(1)}, u32[]{:S(2)}, u32[]{:S(2)}) collective-permute-start(bf16[512,1152]{1,0:T(8,128)(2,1)} %refs_0_.3), channel_id=1, source_target_pairs={{0,28},{2,30},{4,0},{6,2},{8,4},{10,6},{12,8},{14,10},{16,12},{18,... | collective-permute-start | bytes 3538952 | tf_op jit(solution)/shard_map/ppermute | solution.py:23
  6.7 0.0 collective-permute-start.1
  6.7 1.6 %shard_map.41 = (bf16[512,1152]{1,0:T(8,128)(2,1)S(1)}, bf16[512,1152]{1,0:T(8,128)(2,1)S(1)}) custom-call(bf16[512,1152]{1,0:T(8,128)(2,1)} %refs_0_.3, bf16[512,1152]{1,0:T(8,128)(2,1)} %refs_3_.1), custom_call_target="tpu_custom_call" | custom-call | flops 1 | bytes 1 | tf_op jit(solution)/shard_map/pallas_call | solution.py:177
  8.3 0.0 copy-start
  8.4 0.0 copy-start.1
  8.4 0.1 fusion
  8.5 0.1 collective-permute-start.3
  8.5 0.5 collective-permute-start.2
  9.0 0.8 %collective-permute-start = (bf16[512,1152]{1,0:T(8,128)(2,1)S(1)}, bf16[512,1152]{1,0:T(8,128)(2,1)S(1)}, u32[]{:S(2)}, u32[]{:S(2)}) collective-permute-start(bf16[512,1152]{1,0:T(8,128)(2,1)S(1)} %get-tuple-element.10.far_own), channel_id=1, source_target_pairs={{0,26},{2,8},{4,30},{6,12},{8,2},{10,16},{12,6},{14,20},{16,10},{1... | collective-permute-start | bytes 3538952 | tf_op jit(solution)/shard_map/ppermute | solution.py:23
  9.8 0.7 %collective-permute-done.3.refs_1_ = bf16[256,1152]{1,0:T(8,128)(2,1)S(1)} collective-permute-done((bf16[256,1152]{1,0:T(8,128)(2,1)S(1)}, bf16[256,1152]{1,0:T(8,128)(2,1)S(1)}, u32[]{:S(2)}, u32[]{:S(2)}) %collective-permute-start.3) | collective-permute-done | bytes 589856 | tf_op jit(solution)/shard_map/ppermute | solution.py:23
  10.5 0.8 %collective-permute-done.2.refs_0_ = bf16[256,1152]{1,0:T(8,128)(2,1)S(1)} collective-permute-done((bf16[256,1152]{1,0:T(8,128)(2,1)S(1)}, bf16[256,1152]{1,0:T(8,128)(2,1)S(1)}, u32[]{:S(2)}, u32[]{:S(2)}) %collective-permute-start.2) | collective-permute-done | bytes 589856 | tf_op jit(solution)/shard_map/ppermute | solution.py:23
  11.4 0.0 copy-done
  11.4 0.0 copy-done.1
  11.4 4.4 %shard_map.42 = (f32[512,1152]{1,0:T(8,128)S(1)}, f32[512,1152]{1,0:T(8,128)S(1)}) custom-call(bf16[512,1152]{1,0:T(8,128)(2,1)S(1)} %copy-done, bf16[512,1152]{1,0:T(8,128)(2,1)S(1)} %copy-done.1, bf16[512,1152]{1,0:T(8,128)(2,1)S(1)} %get-tuple-element.11.near_own, bf16[256,1152]{1,0:T(8,128)(2,1)S(1)} %collective-permute-done.2.refs_0_, ...), custom_call_target="tpu_custom_call" | custom-call | flops 1 | bytes 1 | tf_op jit(solution)/shard_map/pallas_call | solution.py:177
  15.8 39.3 %collective-permute-done.5.refs_1_ = bf16[512,1152]{1,0:T(8,128)(2,1)S(1)} collective-permute-done((bf16[512,1152]{1,0:T(8,128)(2,1)}, bf16[512,1152]{1,0:T(8,128)(2,1)S(1)}, u32[]{:S(2)}, u32[]{:S(2)}) %collective-permute-start.5) | collective-permute-done | bytes 1179680 | tf_op jit(solution)/shard_map/ppermute | solution.py:23
  55.1 0.3 collective-permute-done.1.refs_3_
  55.4 0.0 collective-permute-start.4
  55.4 0.5 collective-permute-start.6
  55.9 3.4 %shard_map.43 = (f32[512,1152]{1,0:T(8,128)S(1)}, f32[512,1152]{1,0:T(8,128)S(1)}) custom-call(bf16[512,1152]{1,0:T(8,128)(2,1)S(1)} %copy-done.1, bf16[512,1152]{1,0:T(8,128)(2,1)S(1)} %collective-permute-done.5.refs_1_, bf16[512,1152]{1,0:T(8,128)(2,1)S(1)} %copy-done, ...), custom_call_target="tpu_custom_call", output_to_operand_aliasing={{0}: (4, {}), {1}: (5, {})} | custom-call | flops 1 | bytes 1 | tf_op jit(solution)/shard_map/pallas_call | solution.py:177
  59.3 0.0 collective-permute-done.far
  59.3 0.0 collective-permute-done.4.refs_1_
  59.3 0.6 collective-permute-done.6.refs_4_
  59.9 5.6 %shard_map.44 = (f32[512,1152]{1,0:T(8,128)}, f32[512,1152]{1,0:T(8,128)}) custom-call(bf16[512,1152]{1,0:T(8,128)(2,1)S(1)} %get-tuple-element.10.far_own, bf16[512,1152]{1,0:T(8,128)(2,1)S(1)} %collective-permute-done.far, bf16[512,1152]{1,0:T(8,128)(2,1)S(1)} %copy-done, bf16[512,1152]{1,0:T(8,128)(2,1)S(1)} %collective-permute-done.4.refs_1_, ...), custom_call_target="tpu_custom_call" | custom-call | flops 1 | bytes 1 | tf_op jit(solution)/shard_map/pallas_call | solution.py:177
Async XLA Ops:
  0.6 54.5 %collective-permute-start.5 = (bf16[512,1152]{1,0:T(8,128)(2,1)}, bf16[512,1152]{1,0:T(8,128)(2,1)S(1)}, u32[]{:S(2)}, u32[]{:S(2)}) collective-permute-start(bf16[512,1152]{1,0:T(8,128)(2,1)} %refs_0_.3), channel_id=1, source_target_pairs={{0,28},{2,30},{4,0},{6,2},{8,4},{10,6},{12,8},{14,10},{16,12},{18,... | collective-permute-start | bytes 3538952 | tf_op jit(solution)/shard_map/ppermute | solution.py:23
  6.7 48.7 %collective-permute-start.1 = (bf16[512,1152]{1,0:T(8,128)(2,1)}, bf16[512,1152]{1,0:T(8,128)(2,1)S(1)}, u32[]{:S(2)}, u32[]{:S(2)}) collective-permute-start(bf16[512,1152]{1,0:T(8,128)(2,1)} %refs_3_.1), channel_id=1, source_target_pairs={{0,4},{2,6},{4,8},{6,10},{8,12},{10,14},{12,16},{14,18},{16,20},{1... | collective-permute-start | bytes 3538952 | tf_op jit(solution)/shard_map/ppermute | solution.py:23
  8.3 3.0 %copy-start = (bf16[512,1152]{1,0:T(8,128)(2,1)S(1)}, bf16[512,1152]{1,0:T(8,128)(2,1)}, u32[]{:S(2)}) copy-start(bf16[512,1152]{1,0:T(8,128)(2,1)} %refs_0_.3) | copy-start | bytes 3538948
  8.4 3.0 %copy-start.1 = (bf16[512,1152]{1,0:T(8,128)(2,1)S(1)}, bf16[512,1152]{1,0:T(8,128)(2,1)}, u32[]{:S(2)}) copy-start(bf16[512,1152]{1,0:T(8,128)(2,1)} %refs_3_.1) | copy-start | bytes 3538948
  8.5 2.1 %collective-permute-start.3 = (bf16[256,1152]{1,0:T(8,128)(2,1)S(1)}, bf16[256,1152]{1,0:T(8,128)(2,1)S(1)}, u32[]{:S(2)}, u32[]{:S(2)}) collective-permute-start(bf16[256,1152]{1,0:T(8,128)(2,1)S(1)} %get-tuple-element.18), channel_id=1, source_target_pairs={{0,2},{2,0},{4,6},{6,4},{8,10},{10,8},{12,14},{14,12},{16,18},{18,... | collective-permute-start | bytes 1769480 | tf_op jit(solution)/shard_map/ppermute | solution.py:23
  8.5 2.8 %collective-permute-start.2 = (bf16[256,1152]{1,0:T(8,128)(2,1)S(1)}, bf16[256,1152]{1,0:T(8,128)(2,1)S(1)}, u32[]{:S(2)}, u32[]{:S(2)}) collective-permute-start(bf16[256,1152]{1,0:T(8,128)(2,1)S(1)} %get-tuple-element.19), channel_id=1, source_target_pairs={{0,2},{2,0},{4,6},{6,4},{8,10},{10,8},{12,14},{14,12},{16,18},{18,... | collective-permute-start | bytes 1769480 | tf_op jit(solution)/shard_map/ppermute | solution.py:23
  9.0 50.2 %collective-permute-start = (bf16[512,1152]{1,0:T(8,128)(2,1)S(1)}, bf16[512,1152]{1,0:T(8,128)(2,1)S(1)}, u32[]{:S(2)}, u32[]{:S(2)}) collective-permute-start(bf16[512,1152]{1,0:T(8,128)(2,1)S(1)} %get-tuple-element.10.far_own), channel_id=1, source_target_pairs={{0,26},{2,8},{4,30},{6,12},{8,2},{10,16},{12,6},{14,20},{16,10},{1... | collective-permute-start | bytes 3538952 | tf_op jit(solution)/shard_map/ppermute | solution.py:23
  55.4 3.9 %collective-permute-start.4 = (bf16[512,1152]{1,0:T(8,128)(2,1)S(1)}, bf16[512,1152]{1,0:T(8,128)(2,1)S(1)}, u32[]{:S(2)}, u32[]{:S(2)}) collective-permute-start(bf16[512,1152]{1,0:T(8,128)(2,1)S(1)} %collective-permute-done.1.refs_3_), channel_id=1, source_target_pairs={{0,2},{2,0},{4,6},{6,4},{8,10},{10,8},{12,14},{14,12},{16,18},{18,... | collective-permute-start | bytes 3538952 | tf_op jit(solution)/shard_map/ppermute | solution.py:23
  55.4 4.5 %collective-permute-start.6 = (bf16[512,1152]{1,0:T(8,128)(2,1)S(1)}, bf16[512,1152]{1,0:T(8,128)(2,1)S(1)}, u32[]{:S(2)}, u32[]{:S(2)}) collective-permute-start(bf16[512,1152]{1,0:T(8,128)(2,1)S(1)} %collective-permute-done.5.refs_1_), channel_id=1, source_target_pairs={{0,2},{2,0},{4,6},{6,4},{8,10},{10,8},{12,14},{14,12},{16,18},{18,... | collective-permute-start | bytes 3538952 | tf_op jit(solution)/shard_map/ppermute | solution.py:23

commit v18 on v17

--- a/solution.py
+++ b/solution.py
@@ -230,12 +230,12 @@
     sums = dict(enumerate(sums))
 
     images, texts = after(images, *sums.values()), after(texts, *sums.values())
-    swapped_images, swapped_texts = swap(images, 1), swap(texts, 1)
+    swapped_images, swapped_texts = swap(images, 1), swap(texts, 2)
     sums = step([(1, text_embed, (images,)), (0, image_embed, (texts,))], sums)
     operands = (image_embed, *swapped_texts, sums[0], text_embed, *swapped_images, sums[1])
     operands = (far_own, far, *operands)
     return call(
-        functools.partial(last_kernel, factor, (1, 1)),
+        functools.partial(last_kernel, factor, (2, 1)),
         (grad, grad),
         operands,
         [kept, kept, depth((texts,)), depth((images,))]

time: 65.6 us -> 65.5 us (level)
    ppermute x7 -> x8, waiting for transfers between devices: 41.8 us -> 41.3 us  [send(): lax.ppermute(block, AXIS, [(i, target(i) % count) for i in range(count)])]
    ppermute x7 -> x8, starting transfers between devices: 7.89 us -> 7.96 us  [send(): lax.ppermute(block, AXIS, [(i, target(i) % count) for i in range(count)])]
  transfers between devices with their start and end apart: 7 -> 8, of which waited for: 5 -> 5; matrix products, arithmetic and copies ran while one was open for 0% -> 0% of each run, Pallas kernels for 14% -> 14%
where the time goes in v18:
time: 65.5 us; the launch traced here: 65.3 us
  waiting for transfers between devices  41.3 us (63%)
  Pallas kernels  15.1 us (23%)
  starting transfers between devices  7.96 us (12%)
  between operations  0.71 us (1%)
    ppermute x8, waiting for transfers between devices, send(): lax.ppermute(block, AXIS, [(i, target(i) % count) for i in range(count)])  41.3 us
    pallas_call x4, Pallas kernels, call(): pl.pallas_call(kernel, out_shape=tuple(outs), in_specs=[in_spec] * len(op...  15.1 us
    ppermute x8, starting transfers between devices, send(): lax.ppermute(block, AXIS, [(i, target(i) % count) for i in range(count)])  7.96 us
  transfers between devices with their start and end apart: 8, of which 5 were waited for; matrix products, arithmetic and copies ran while one was open for 0% of the time, Pallas kernels for 14%

profile of v18, /device:TPU:0, one launch (start us, length us, event | category | flops | bytes accessed | tf_op | source)
XLA Modules:
  0.0 65.3 jit_solution(1753367688569598790)
XLA Ops:
  0.6 6.1 %collective-permute-start.6 = (bf16[512,1152]{1,0:T(8,128)(2,1)}, bf16[512,1152]{1,0:T(8,128)(2,1)S(1)}, u32[]{:S(2)}, u32[]{:S(2)}) collective-permute-start(bf16[512,1152]{1,0:T(8,128)(2,1)} %refs_0_.3), channel_id=1, source_target_pairs={{0,28},{2,30},{4,0},{6,2},{8,4},{10,6},{12,8},{14,10},{16,12},{18,... | collective-permute-start | bytes 3538952 | tf_op jit(solution)/shard_map/ppermute | solution.py:23
  6.7 0.0 collective-permute-start.1
  6.7 1.6 %shard_map.41 = (bf16[512,1152]{1,0:T(8,128)(2,1)S(1)}, bf16[512,1152]{1,0:T(8,128)(2,1)S(1)}) custom-call(bf16[512,1152]{1,0:T(8,128)(2,1)} %refs_0_.3, bf16[512,1152]{1,0:T(8,128)(2,1)} %refs_4_.1), custom_call_target="tpu_custom_call" | custom-call | flops 1 | bytes 1 | tf_op jit(solution)/shard_map/pallas_call | solution.py:177
  8.3 0.0 copy-start
  8.4 0.0 copy-start.1
  8.4 0.1 fusion.1
  8.5 0.1 collective-permute-start.3
  8.5 0.5 collective-permute-start.2
  9.0 0.8 %collective-permute-start = (bf16[512,1152]{1,0:T(8,128)(2,1)S(1)}, bf16[512,1152]{1,0:T(8,128)(2,1)S(1)}, u32[]{:S(2)}, u32[]{:S(2)}) collective-permute-start(bf16[512,1152]{1,0:T(8,128)(2,1)S(1)} %get-tuple-element.10.far_own), channel_id=1, source_target_pairs={{0,26},{2,8},{4,30},{6,12},{8,2},{10,16},{12,6},{14,20},{16,10},{1... | collective-permute-start | bytes 3538952 | tf_op jit(solution)/shard_map/ppermute | solution.py:23
  9.8 0.7 %collective-permute-done.3.refs_1_ = bf16[256,1152]{1,0:T(8,128)(2,1)S(1)} collective-permute-done((bf16[256,1152]{1,0:T(8,128)(2,1)S(1)}, bf16[256,1152]{1,0:T(8,128)(2,1)S(1)}, u32[]{:S(2)}, u32[]{:S(2)}) %collective-permute-start.3) | collective-permute-done | bytes 589856 | tf_op jit(solution)/shard_map/ppermute | solution.py:23
  10.5 0.8 %collective-permute-done.2.refs_0_ = bf16[256,1152]{1,0:T(8,128)(2,1)S(1)} collective-permute-done((bf16[256,1152]{1,0:T(8,128)(2,1)S(1)}, bf16[256,1152]{1,0:T(8,128)(2,1)S(1)}, u32[]{:S(2)}, u32[]{:S(2)}) %collective-permute-start.2) | collective-permute-done | bytes 589856 | tf_op jit(solution)/shard_map/ppermute | solution.py:23
  11.4 0.0 copy-done
  11.4 0.0 copy-done.1
  11.4 4.4 %shard_map.42 = (f32[512,1152]{1,0:T(8,128)S(1)}, f32[512,1152]{1,0:T(8,128)S(1)}) custom-call(bf16[512,1152]{1,0:T(8,128)(2,1)S(1)} %copy-done, bf16[512,1152]{1,0:T(8,128)(2,1)S(1)} %copy-done.1, bf16[512,1152]{1,0:T(8,128)(2,1)S(1)} %get-tuple-element.11.near_own, bf16[256,1152]{1,0:T(8,128)(2,1)S(1)} %collective-permute-done.2.refs_0_, ...), custom_call_target="tpu_custom_call" | custom-call | flops 1 | bytes 1 | tf_op jit(solution)/shard_map/pallas_call | solution.py:177
  15.8 39.3 %collective-permute-done.6.refs_1_ = bf16[512,1152]{1,0:T(8,128)(2,1)S(1)} collective-permute-done((bf16[512,1152]{1,0:T(8,128)(2,1)}, bf16[512,1152]{1,0:T(8,128)(2,1)S(1)}, u32[]{:S(2)}, u32[]{:S(2)}) %collective-permute-start.6) | collective-permute-done | bytes 1179680 | tf_op jit(solution)/shard_map/ppermute | solution.py:23
  55.1 0.0 collective-permute-start.7
  55.1 0.3 collective-permute-done.1.refs_3_
  55.4 0.1 fusion
  55.5 0.3 collective-permute-start.5
  55.8 0.3 collective-permute-start.4
  56.0 3.4 %shard_map.43 = (f32[512,1152]{1,0:T(8,128)S(1)}, f32[512,1152]{1,0:T(8,128)S(1)}) custom-call(bf16[512,1152]{1,0:T(8,128)(2,1)S(1)} %copy-done.1, bf16[512,1152]{1,0:T(8,128)(2,1)S(1)} %collective-permute-done.6.refs_1_, bf16[512,1152]{1,0:T(8,128)(2,1)S(1)} %copy-done, ...), custom_call_target="tpu_custom_call", output_to_operand_aliasing={{0}: (4, {}), {1}: (5, {})} | custom-call | flops 1 | bytes 1 | tf_op jit(solution)/shard_map/pallas_call | solution.py:177
  59.4 0.0 collective-permute-done.far
  59.4 0.0 collective-permute-done.5.refs_2_
  59.4 0.2 collective-permute-done.4.refs_1_
  59.6 0.0 collective-permute-done.7.refs_5_
  59.6 5.6 %shard_map.44 = (f32[512,1152]{1,0:T(8,128)}, f32[512,1152]{1,0:T(8,128)}) custom-call(bf16[512,1152]{1,0:T(8,128)(2,1)S(1)} %get-tuple-element.10.far_own, bf16[512,1152]{1,0:T(8,128)(2,1)S(1)} %collective-permute-done.far, bf16[512,1152]{1,0:T(8,128)(2,1)S(1)} %copy-done, bf16[256,1152]{1,0:T(8,128)(2,1)S(1)} %collective-permute-done.4.refs_1_, ...), custom_call_target="tpu_custom_call" | custom-call | flops 1 | bytes 1 | tf_op jit(solution)/shard_map/pallas_call | solution.py:177
Async XLA Ops:
  0.6 54.5 %collective-permute-start.6 = (bf16[512,1152]{1,0:T(8,128)(2,1)}, bf16[512,1152]{1,0:T(8,128)(2,1)S(1)}, u32[]{:S(2)}, u32[]{:S(2)}) collective-permute-start(bf16[512,1152]{1,0:T(8,128)(2,1)} %refs_0_.3), channel_id=1, source_target_pairs={{0,28},{2,30},{4,0},{6,2},{8,4},{10,6},{12,8},{14,10},{16,12},{18,... | collective-permute-start | bytes 3538952 | tf_op jit(solution)/shard_map/ppermute | solution.py:23
  6.7 48.7 %collective-permute-start.1 = (bf16[512,1152]{1,0:T(8,128)(2,1)}, bf16[512,1152]{1,0:T(8,128)(2,1)S(1)}, u32[]{:S(2)}, u32[]{:S(2)}) collective-permute-start(bf16[512,1152]{1,0:T(8,128)(2,1)} %refs_4_.1), channel_id=1, source_target_pairs={{0,4},{2,6},{4,8},{6,10},{8,12},{10,14},{12,16},{14,18},{16,20},{1... | collective-permute-start | bytes 3538952 | tf_op jit(solution)/shard_map/ppermute | solution.py:23
  8.3 3.0 %copy-start = (bf16[512,1152]{1,0:T(8,128)(2,1)S(1)}, bf16[512,1152]{1,0:T(8,128)(2,1)}, u32[]{:S(2)}) copy-start(bf16[512,1152]{1,0:T(8,128)(2,1)} %refs_0_.3) | copy-start | bytes 3538948
  8.4 3.0 %copy-start.1 = (bf16[512,1152]{1,0:T(8,128)(2,1)S(1)}, bf16[512,1152]{1,0:T(8,128)(2,1)}, u32[]{:S(2)}) copy-start(bf16[512,1152]{1,0:T(8,128)(2,1)} %refs_4_.1) | copy-start | bytes 3538948
  8.5 2.1 %collective-permute-start.3 = (bf16[256,1152]{1,0:T(8,128)(2,1)S(1)}, bf16[256,1152]{1,0:T(8,128)(2,1)S(1)}, u32[]{:S(2)}, u32[]{:S(2)}) collective-permute-start(bf16[256,1152]{1,0:T(8,128)(2,1)S(1)} %get-tuple-element.20), channel_id=1, source_target_pairs={{0,2},{2,0},{4,6},{6,4},{8,10},{10,8},{12,14},{14,12},{16,18},{18,... | collective-permute-start | bytes 1769480 | tf_op jit(solution)/shard_map/ppermute | solution.py:23
  8.5 2.8 %collective-permute-start.2 = (bf16[256,1152]{1,0:T(8,128)(2,1)S(1)}, bf16[256,1152]{1,0:T(8,128)(2,1)S(1)}, u32[]{:S(2)}, u32[]{:S(2)}) collective-permute-start(bf16[256,1152]{1,0:T(8,128)(2,1)S(1)} %get-tuple-element.21), channel_id=1, source_target_pairs={{0,2},{2,0},{4,6},{6,4},{8,10},{10,8},{12,14},{14,12},{16,18},{18,... | collective-permute-start | bytes 1769480 | tf_op jit(solution)/shard_map/ppermute | solution.py:23
  9.0 50.4 %collective-permute-start = (bf16[512,1152]{1,0:T(8,128)(2,1)S(1)}, bf16[512,1152]{1,0:T(8,128)(2,1)S(1)}, u32[]{:S(2)}, u32[]{:S(2)}) collective-permute-start(bf16[512,1152]{1,0:T(8,128)(2,1)S(1)} %get-tuple-element.10.far_own), channel_id=1, source_target_pairs={{0,26},{2,8},{4,30},{6,12},{8,2},{10,16},{12,6},{14,20},{16,10},{1... | collective-permute-start | bytes 3538952 | tf_op jit(solution)/shard_map/ppermute | solution.py:23
  55.1 4.5 %collective-permute-start.7 = (bf16[512,1152]{1,0:T(8,128)(2,1)S(1)}, bf16[512,1152]{1,0:T(8,128)(2,1)S(1)}, u32[]{:S(2)}, u32[]{:S(2)}) collective-permute-start(bf16[512,1152]{1,0:T(8,128)(2,1)S(1)} %collective-permute-done.6.refs_1_), channel_id=1, source_target_pairs={{0,2},{2,0},{4,6},{6,4},{8,10},{10,8},{12,14},{14,12},{16,18},{18,... | collective-permute-start | bytes 3538952 | tf_op jit(solution)/shard_map/ppermute | solution.py:23
  55.5 4.0 %collective-permute-start.5 = (bf16[256,1152]{1,0:T(8,128)(2,1)S(1)}, bf16[256,1152]{1,0:T(8,128)(2,1)S(1)}, u32[]{:S(2)}, u32[]{:S(2)}) collective-permute-start(bf16[256,1152]{1,0:T(8,128)(2,1)S(1)} %get-tuple-element.18), channel_id=1, source_target_pairs={{0,2},{2,0},{4,6},{6,4},{8,10},{10,8},{12,14},{14,12},{16,18},{18,... | collective-permute-start | bytes 1769480 | tf_op jit(solution)/shard_map/ppermute | solution.py:23
  55.8 3.9 %collective-permute-start.4 = (bf16[256,1152]{1,0:T(8,128)(2,1)S(1)}, bf16[256,1152]{1,0:T(8,128)(2,1)S(1)}, u32[]{:S(2)}, u32[]{:S(2)}) collective-permute-start(bf16[256,1152]{1,0:T(8,128)(2,1)S(1)} %get-tuple-element.19), channel_id=1, source_target_pairs={{0,2},{2,0},{4,6},{6,4},{8,10},{10,8},{12,14},{14,12},{16,18},{18,... | collective-permute-start | bytes 1769480 | tf_op jit(solution)/shard_map/ppermute | solution.py:23

commit v19 on v18

--- a/solution.py
+++ b/solution.py
@@ -135,19 +135,19 @@
     for count in counts:
         parts.append((refs[0], refs[1 : 1 + count], refs[1 + count]))
         refs = refs[2 + count :]
-    outs, helds, joined, sems = refs[:2], refs[2:4], refs[4:6], refs[6]
+    outs, helds, joined, far_held, sems = refs[:2], refs[2:4], refs[4:6], refs[6], refs[7]
     starts = range(0, far_own.shape[0], LAST_TILE)
     is_1 = core().astype(jnp.float32)
+    masks = ((1.0 - is_1) * factor, is_1 * factor)
     copies = []
 
     def use_far(start, value):
+        far_held[pl.ds(start, LAST_TILE)] = value
+
+    def use(side, start, value):
         rows = pl.ds(start, LAST_TILE)
-        helds[0][rows] = parts[0][2][rows] + value * (1.0 - is_1)
-        helds[1][rows] = parts[1][2][rows] + value * is_1
-
-    def use(held, out, start, value):
-        rows = pl.ds(start, LAST_TILE)
-        held[rows] = (held[rows] + value) * factor
+        held, out = helds[side], outs[side]
+        held[rows] = (parts[side][2][rows] + value) * factor + far_held[rows] * masks[side]
         for first in range(start, start + LAST_TILE, COPY_ROWS):
             span = pl.ds(first, COPY_ROWS)
             copies.append(pltpu.make_async_copy(held.at[span], out.at[span], sems.at[len(copies)]))
@@ -157,9 +157,9 @@
         return (own.at[pl.ds(start, LAST_TILE)], others, functools.partial(act, *args, start))
 
     units = [unit(far_own, far, start, use_far) for start in starts]
-    for (own, visitors, _), held, out, scratch in zip(parts, helds, outs, joined):
+    for side, ((own, visitors, _), scratch) in enumerate(zip(parts, joined)):
         others = join(visitors, scratch)
-        units += [unit(own, others, start, use, held, out) for start in starts]
+        units += [unit(own, others, start, use, side) for start in starts]
     add_all(factor, units)
     for copy in copies:
         copy.wait()
@@ -239,7 +239,7 @@
         (grad, grad),
         operands,
         [kept, kept, depth((texts,)), depth((images,))]
-        + [pltpu.SemaphoreType.DMA((2 * rows // COPY_ROWS,))],
+        + [kept, pltpu.SemaphoreType.DMA((2 * rows // COPY_ROWS,))],
     )
 
 

time: 65.5 us -> 65.4 us (level)
  transfers between devices with their start and end apart: 8 -> 8, of which waited for: 5 -> 5; matrix products, arithmetic and copies ran while one was open for 0% -> 0% of each run, Pallas kernels for 14% -> 15%
where the time goes in v19:
time: 65.4 us; the launch traced here: 65.1 us
  waiting for transfers between devices  41.3 us (63%)
  Pallas kernels  14.9 us (23%)
  starting transfers between devices  7.96 us (12%)
  between operations  0.71 us (1%)
    ppermute x8, waiting for transfers between devices, send(): lax.ppermute(block, AXIS, [(i, target(i) % count) for i in range(count)])  41.3 us
    pallas_call x4, Pallas kernels, call(): pl.pallas_call(kernel, out_shape=tuple(outs), in_specs=[in_spec] * len(op...  14.9 us
    ppermute x8, starting transfers between devices, send(): lax.ppermute(block, AXIS, [(i, target(i) % count) for i in range(count)])  7.96 us
  transfers between devices with their start and end apart: 8, of which 5 were waited for; matrix products, arithmetic and copies ran while one was open for 0% of the time, Pallas kernels for 15%

profile of v19, /device:TPU:0, one launch (start us, length us, event | category | flops | bytes accessed | tf_op | source)
XLA Modules:
  0.0 65.1 jit_solution(16857537040918677030)
XLA Ops:
  0.6 6.1 %collective-permute-start.6 = (bf16[512,1152]{1,0:T(8,128)(2,1)}, bf16[512,1152]{1,0:T(8,128)(2,1)S(1)}, u32[]{:S(2)}, u32[]{:S(2)}) collective-permute-start(bf16[512,1152]{1,0:T(8,128)(2,1)} %refs_0_.3), channel_id=1, source_target_pairs={{0,28},{2,30},{4,0},{6,2},{8,4},{10,6},{12,8},{14,10},{16,12},{18,... | collective-permute-start | bytes 3538952 | tf_op jit(solution)/shard_map/ppermute | solution.py:23
  6.7 0.0 collective-permute-start.1
  6.7 1.6 %shard_map.41 = (bf16[512,1152]{1,0:T(8,128)(2,1)S(1)}, bf16[512,1152]{1,0:T(8,128)(2,1)S(1)}) custom-call(bf16[512,1152]{1,0:T(8,128)(2,1)} %refs_0_.3, bf16[512,1152]{1,0:T(8,128)(2,1)} %refs_4_.1), custom_call_target="tpu_custom_call" | custom-call | flops 1 | bytes 1 | tf_op jit(solution)/shard_map/pallas_call | solution.py:177
  8.3 0.0 copy-start
  8.4 0.0 copy-start.1
  8.4 0.1 fusion.1
  8.5 0.1 collective-permute-start.3
  8.5 0.5 collective-permute-start.2
  9.0 0.8 %collective-permute-start = (bf16[512,1152]{1,0:T(8,128)(2,1)S(1)}, bf16[512,1152]{1,0:T(8,128)(2,1)S(1)}, u32[]{:S(2)}, u32[]{:S(2)}) collective-permute-start(bf16[512,1152]{1,0:T(8,128)(2,1)S(1)} %get-tuple-element.10.far_own), channel_id=1, source_target_pairs={{0,26},{2,8},{4,30},{6,12},{8,2},{10,16},{12,6},{14,20},{16,10},{1... | collective-permute-start | bytes 3538952 | tf_op jit(solution)/shard_map/ppermute | solution.py:23
  9.8 0.7 %collective-permute-done.3.refs_1_ = bf16[256,1152]{1,0:T(8,128)(2,1)S(1)} collective-permute-done((bf16[256,1152]{1,0:T(8,128)(2,1)S(1)}, bf16[256,1152]{1,0:T(8,128)(2,1)S(1)}, u32[]{:S(2)}, u32[]{:S(2)}) %collective-permute-start.3) | collective-permute-done | bytes 589856 | tf_op jit(solution)/shard_map/ppermute | solution.py:23
  10.5 0.8 %collective-permute-done.2.refs_0_ = bf16[256,1152]{1,0:T(8,128)(2,1)S(1)} collective-permute-done((bf16[256,1152]{1,0:T(8,128)(2,1)S(1)}, bf16[256,1152]{1,0:T(8,128)(2,1)S(1)}, u32[]{:S(2)}, u32[]{:S(2)}) %collective-permute-start.2) | collective-permute-done | bytes 589856 | tf_op jit(solution)/shard_map/ppermute | solution.py:23
  11.4 0.0 copy-done
  11.4 0.0 copy-done.1
  11.4 4.4 %shard_map.42 = (f32[512,1152]{1,0:T(8,128)S(1)}, f32[512,1152]{1,0:T(8,128)S(1)}) custom-call(bf16[512,1152]{1,0:T(8,128)(2,1)S(1)} %copy-done, bf16[512,1152]{1,0:T(8,128)(2,1)S(1)} %copy-done.1, bf16[512,1152]{1,0:T(8,128)(2,1)S(1)} %get-tuple-element.11.near_own, bf16[256,1152]{1,0:T(8,128)(2,1)S(1)} %collective-permute-done.2.refs_0_, ...), custom_call_target="tpu_custom_call" | custom-call | flops 1 | bytes 1 | tf_op jit(solution)/shard_map/pallas_call | solution.py:177
  15.8 39.3 %collective-permute-done.6.refs_1_ = bf16[512,1152]{1,0:T(8,128)(2,1)S(1)} collective-permute-done((bf16[512,1152]{1,0:T(8,128)(2,1)}, bf16[512,1152]{1,0:T(8,128)(2,1)S(1)}, u32[]{:S(2)}, u32[]{:S(2)}) %collective-permute-start.6) | collective-permute-done | bytes 1179680 | tf_op jit(solution)/shard_map/ppermute | solution.py:23
  55.1 0.0 collective-permute-start.7
  55.1 0.3 collective-permute-done.1.refs_3_
  55.4 0.1 fusion
  55.5 0.3 collective-permute-start.5
  55.8 0.3 collective-permute-start.4
  56.0 3.4 %shard_map.43 = (f32[512,1152]{1,0:T(8,128)S(1)}, f32[512,1152]{1,0:T(8,128)S(1)}) custom-call(bf16[512,1152]{1,0:T(8,128)(2,1)S(1)} %copy-done.1, bf16[512,1152]{1,0:T(8,128)(2,1)S(1)} %collective-permute-done.6.refs_1_, bf16[512,1152]{1,0:T(8,128)(2,1)S(1)} %copy-done, ...), custom_call_target="tpu_custom_call", output_to_operand_aliasing={{0}: (4, {}), {1}: (5, {})} | custom-call | flops 1 | bytes 1 | tf_op jit(solution)/shard_map/pallas_call | solution.py:177
  59.4 0.0 collective-permute-done.far
  59.4 0.0 collective-permute-done.5.refs_2_
  59.4 0.2 collective-permute-done.4.refs_1_
  59.6 0.0 collective-permute-done.7.refs_5_
  59.6 5.5 %shard_map.44 = (f32[512,1152]{1,0:T(8,128)}, f32[512,1152]{1,0:T(8,128)}) custom-call(bf16[512,1152]{1,0:T(8,128)(2,1)S(1)} %get-tuple-element.10.far_own, bf16[512,1152]{1,0:T(8,128)(2,1)S(1)} %collective-permute-done.far, bf16[512,1152]{1,0:T(8,128)(2,1)S(1)} %copy-done, bf16[256,1152]{1,0:T(8,128)(2,1)S(1)} %collective-permute-done.4.refs_1_, ...), custom_call_target="tpu_custom_call" | custom-call | flops 1 | bytes 1 | tf_op jit(solution)/shard_map/pallas_call | solution.py:177
Async XLA Ops:
  0.6 54.5 %collective-permute-start.6 = (bf16[512,1152]{1,0:T(8,128)(2,1)}, bf16[512,1152]{1,0:T(8,128)(2,1)S(1)}, u32[]{:S(2)}, u32[]{:S(2)}) collective-permute-start(bf16[512,1152]{1,0:T(8,128)(2,1)} %refs_0_.3), channel_id=1, source_target_pairs={{0,28},{2,30},{4,0},{6,2},{8,4},{10,6},{12,8},{14,10},{16,12},{18,... | collective-permute-start | bytes 3538952 | tf_op jit(solution)/shard_map/ppermute | solution.py:23
  6.7 48.7 %collective-permute-start.1 = (bf16[512,1152]{1,0:T(8,128)(2,1)}, bf16[512,1152]{1,0:T(8,128)(2,1)S(1)}, u32[]{:S(2)}, u32[]{:S(2)}) collective-permute-start(bf16[512,1152]{1,0:T(8,128)(2,1)} %refs_4_.1), channel_id=1, source_target_pairs={{0,4},{2,6},{4,8},{6,10},{8,12},{10,14},{12,16},{14,18},{16,20},{1... | collective-permute-start | bytes 3538952 | tf_op jit(solution)/shard_map/ppermute | solution.py:23
  8.3 3.0 %copy-start = (bf16[512,1152]{1,0:T(8,128)(2,1)S(1)}, bf16[512,1152]{1,0:T(8,128)(2,1)}, u32[]{:S(2)}) copy-start(bf16[512,1152]{1,0:T(8,128)(2,1)} %refs_0_.3) | copy-start | bytes 3538948
  8.4 3.0 %copy-start.1 = (bf16[512,1152]{1,0:T(8,128)(2,1)S(1)}, bf16[512,1152]{1,0:T(8,128)(2,1)}, u32[]{:S(2)}) copy-start(bf16[512,1152]{1,0:T(8,128)(2,1)} %refs_4_.1) | copy-start | bytes 3538948
  8.5 2.1 %collective-permute-start.3 = (bf16[256,1152]{1,0:T(8,128)(2,1)S(1)}, bf16[256,1152]{1,0:T(8,128)(2,1)S(1)}, u32[]{:S(2)}, u32[]{:S(2)}) collective-permute-start(bf16[256,1152]{1,0:T(8,128)(2,1)S(1)} %get-tuple-element.20), channel_id=1, source_target_pairs={{0,2},{2,0},{4,6},{6,4},{8,10},{10,8},{12,14},{14,12},{16,18},{18,... | collective-permute-start | bytes 1769480 | tf_op jit(solution)/shard_map/ppermute | solution.py:23
  8.5 2.8 %collective-permute-start.2 = (bf16[256,1152]{1,0:T(8,128)(2,1)S(1)}, bf16[256,1152]{1,0:T(8,128)(2,1)S(1)}, u32[]{:S(2)}, u32[]{:S(2)}) collective-permute-start(bf16[256,1152]{1,0:T(8,128)(2,1)S(1)} %get-tuple-element.21), channel_id=1, source_target_pairs={{0,2},{2,0},{4,6},{6,4},{8,10},{10,8},{12,14},{14,12},{16,18},{18,... | collective-permute-start | bytes 1769480 | tf_op jit(solution)/shard_map/ppermute | solution.py:23
  9.0 50.4 %collective-permute-start = (bf16[512,1152]{1,0:T(8,128)(2,1)S(1)}, bf16[512,1152]{1,0:T(8,128)(2,1)S(1)}, u32[]{:S(2)}, u32[]{:S(2)}) collective-permute-start(bf16[512,1152]{1,0:T(8,128)(2,1)S(1)} %get-tuple-element.10.far_own), channel_id=1, source_target_pairs={{0,26},{2,8},{4,30},{6,12},{8,2},{10,16},{12,6},{14,20},{16,10},{1... | collective-permute-start | bytes 3538952 | tf_op jit(solution)/shard_map/ppermute | solution.py:23
  55.1 4.5 %collective-permute-start.7 = (bf16[512,1152]{1,0:T(8,128)(2,1)S(1)}, bf16[512,1152]{1,0:T(8,128)(2,1)S(1)}, u32[]{:S(2)}, u32[]{:S(2)}) collective-permute-start(bf16[512,1152]{1,0:T(8,128)(2,1)S(1)} %collective-permute-done.6.refs_1_), channel_id=1, source_target_pairs={{0,2},{2,0},{4,6},{6,4},{8,10},{10,8},{12,14},{14,12},{16,18},{18,... | collective-permute-start | bytes 3538952 | tf_op jit(solution)/shard_map/ppermute | solution.py:23
  55.5 4.0 %collective-permute-start.5 = (bf16[256,1152]{1,0:T(8,128)(2,1)S(1)}, bf16[256,1152]{1,0:T(8,128)(2,1)S(1)}, u32[]{:S(2)}, u32[]{:S(2)}) collective-permute-start(bf16[256,1152]{1,0:T(8,128)(2,1)S(1)} %get-tuple-element.18), channel_id=1, source_target_pairs={{0,2},{2,0},{4,6},{6,4},{8,10},{10,8},{12,14},{14,12},{16,18},{18,... | collective-permute-start | bytes 1769480 | tf_op jit(solution)/shard_map/ppermute | solution.py:23
  55.8 3.9 %collective-permute-start.4 = (bf16[256,1152]{1,0:T(8,128)(2,1)S(1)}, bf16[256,1152]{1,0:T(8,128)(2,1)S(1)}, u32[]{:S(2)}, u32[]{:S(2)}) collective-permute-start(bf16[256,1152]{1,0:T(8,128)(2,1)S(1)} %get-tuple-element.19), channel_id=1, source_target_pairs={{0,2},{2,0},{4,6},{6,4},{8,10},{10,8},{12,14},{14,12},{16,18},{18,... | collective-permute-start | bytes 1769480 | tf_op jit(solution)/shard_map/ppermute | solution.py:23

commit v20 on v19

--- a/solution.py
+++ b/solution.py
@@ -156,10 +156,12 @@
     def unit(own, others, start, act, *args):
         return (own.at[pl.ds(start, LAST_TILE)], others, functools.partial(act, *args, start))
 
-    units = [unit(far_own, far, start, use_far) for start in starts]
-    for side, ((own, visitors, _), scratch) in enumerate(zip(parts, joined)):
-        others = join(visitors, scratch)
-        units += [unit(own, others, start, use, side) for start in starts]
+    met = [join(visitors, scratch) for (_, visitors, _), scratch in zip(parts, joined)]
+    units = []
+    for start in starts:
+        units.append(unit(far_own, far, start, use_far))
+        for side in (0, 1):
+            units.append(unit(parts[side][0], met[side], start, use, side))
     add_all(factor, units)
     for copy in copies:
         copy.wait()

time: 65.4 us -> 65.8 us (level)
  transfers between devices with their start and end apart: 8 -> 8, of which waited for: 5 -> 5; matrix products, arithmetic and copies ran while one was open for 0% -> 0% of each run, Pallas kernels for 15% -> 14%
where the time goes in v20:
time: 65.8 us; the launch traced here: 65.5 us
  waiting for transfers between devices  41.3 us (63%)
  Pallas kernels  15.3 us (23%)
  starting transfers between devices  7.96 us (12%)
  between operations  0.71 us (1%)
    ppermute x8, waiting for transfers between devices, send(): lax.ppermute(block, AXIS, [(i, target(i) % count) for i in range(count)])  41.3 us
    pallas_call x4, Pallas kernels, call(): pl.pallas_call(kernel, out_shape=tuple(outs), in_specs=[in_spec] * len(op...  15.3 us
    ppermute x8, starting transfers between devices, send(): lax.ppermute(block, AXIS, [(i, target(i) % count) for i in range(count)])  7.96 us
  transfers between devices with their start and end apart: 8, of which 5 were waited for; matrix products, arithmetic and copies ran while one was open for 0% of the time, Pallas kernels for 14%

profile of v20, /device:TPU:0, one launch (start us, length us, event | category | flops | bytes accessed | tf_op | source)
XLA Modules:
  0.0 65.5 jit_solution(9677188148060112243)
XLA Ops:
  0.6 6.1 %collective-permute-start.6 = (bf16[512,1152]{1,0:T(8,128)(2,1)}, bf16[512,1152]{1,0:T(8,128)(2,1)S(1)}, u32[]{:S(2)}, u32[]{:S(2)}) collective-permute-start(bf16[512,1152]{1,0:T(8,128)(2,1)} %refs_0_.3), channel_id=1, source_target_pairs={{0,28},{2,30},{4,0},{6,2},{8,4},{10,6},{12,8},{14,10},{16,12},{18,... | collective-permute-start | bytes 3538952 | tf_op jit(solution)/shard_map/ppermute | solution.py:23
  6.7 0.0 collective-permute-start.1
  6.7 1.6 %shard_map.41 = (bf16[512,1152]{1,0:T(8,128)(2,1)S(1)}, bf16[512,1152]{1,0:T(8,128)(2,1)S(1)}) custom-call(bf16[512,1152]{1,0:T(8,128)(2,1)} %refs_0_.3, bf16[512,1152]{1,0:T(8,128)(2,1)} %refs_4_.1), custom_call_target="tpu_custom_call" | custom-call | flops 1 | bytes 1 | tf_op jit(solution)/shard_map/pallas_call | solution.py:179
  8.3 0.0 copy-start
  8.4 0.0 copy-start.1
  8.4 0.1 fusion.1
  8.5 0.1 collective-permute-start.3
  8.5 0.5 collective-permute-start.2
  9.0 0.8 %collective-permute-start = (bf16[512,1152]{1,0:T(8,128)(2,1)S(1)}, bf16[512,1152]{1,0:T(8,128)(2,1)S(1)}, u32[]{:S(2)}, u32[]{:S(2)}) collective-permute-start(bf16[512,1152]{1,0:T(8,128)(2,1)S(1)} %get-tuple-element.10.far_own), channel_id=1, source_target_pairs={{0,26},{2,8},{4,30},{6,12},{8,2},{10,16},{12,6},{14,20},{16,10},{1... | collective-permute-start | bytes 3538952 | tf_op jit(solution)/shard_map/ppermute | solution.py:23
  9.8 0.7 %collective-permute-done.3.refs_1_ = bf16[256,1152]{1,0:T(8,128)(2,1)S(1)} collective-permute-done((bf16[256,1152]{1,0:T(8,128)(2,1)S(1)}, bf16[256,1152]{1,0:T(8,128)(2,1)S(1)}, u32[]{:S(2)}, u32[]{:S(2)}) %collective-permute-start.3) | collective-permute-done | bytes 589856 | tf_op jit(solution)/shard_map/ppermute | solution.py:23
  10.5 0.8 %collective-permute-done.2.refs_0_ = bf16[256,1152]{1,0:T(8,128)(2,1)S(1)} collective-permute-done((bf16[256,1152]{1,0:T(8,128)(2,1)S(1)}, bf16[256,1152]{1,0:T(8,128)(2,1)S(1)}, u32[]{:S(2)}, u32[]{:S(2)}) %collective-permute-start.2) | collective-permute-done | bytes 589856 | tf_op jit(solution)/shard_map/ppermute | solution.py:23
  11.4 0.0 copy-done
  11.4 0.0 copy-done.1
  11.4 4.4 %shard_map.42 = (f32[512,1152]{1,0:T(8,128)S(1)}, f32[512,1152]{1,0:T(8,128)S(1)}) custom-call(bf16[512,1152]{1,0:T(8,128)(2,1)S(1)} %copy-done, bf16[512,1152]{1,0:T(8,128)(2,1)S(1)} %copy-done.1, bf16[512,1152]{1,0:T(8,128)(2,1)S(1)} %get-tuple-element.11.near_own, bf16[256,1152]{1,0:T(8,128)(2,1)S(1)} %collective-permute-done.2.refs_0_, ...), custom_call_target="tpu_custom_call" | custom-call | flops 1 | bytes 1 | tf_op jit(solution)/shard_map/pallas_call | solution.py:179
  15.8 39.3 %collective-permute-done.6.refs_1_ = bf16[512,1152]{1,0:T(8,128)(2,1)S(1)} collective-permute-done((bf16[512,1152]{1,0:T(8,128)(2,1)}, bf16[512,1152]{1,0:T(8,128)(2,1)S(1)}, u32[]{:S(2)}, u32[]{:S(2)}) %collective-permute-start.6) | collective-permute-done | bytes 1179680 | tf_op jit(solution)/shard_map/ppermute | solution.py:23
  55.1 0.0 collective-permute-start.7
  55.1 0.3 collective-permute-done.1.refs_3_
  55.4 0.1 fusion
  55.5 0.3 collective-permute-start.5
  55.8 0.3 collective-permute-start.4
  56.0 3.4 %shard_map.43 = (f32[512,1152]{1,0:T(8,128)S(1)}, f32[512,1152]{1,0:T(8,128)S(1)}) custom-call(bf16[512,1152]{1,0:T(8,128)(2,1)S(1)} %copy-done.1, bf16[512,1152]{1,0:T(8,128)(2,1)S(1)} %collective-permute-done.6.refs_1_, bf16[512,1152]{1,0:T(8,128)(2,1)S(1)} %copy-done, ...), custom_call_target="tpu_custom_call", output_to_operand_aliasing={{0}: (4, {}), {1}: (5, {})} | custom-call | flops 1 | bytes 1 | tf_op jit(solution)/shard_map/pallas_call | solution.py:179
  59.4 0.0 collective-permute-done.far
  59.4 0.0 collective-permute-done.5.refs_2_
  59.4 0.2 collective-permute-done.4.refs_1_
  59.6 0.0 collective-permute-done.7.refs_5_
  59.6 5.9 %shard_map.44 = (f32[512,1152]{1,0:T(8,128)}, f32[512,1152]{1,0:T(8,128)}) custom-call(bf16[512,1152]{1,0:T(8,128)(2,1)S(1)} %get-tuple-element.10.far_own, bf16[512,1152]{1,0:T(8,128)(2,1)S(1)} %collective-permute-done.far, bf16[512,1152]{1,0:T(8,128)(2,1)S(1)} %copy-done, bf16[256,1152]{1,0:T(8,128)(2,1)S(1)} %collective-permute-done.4.refs_1_, ...), custom_call_target="tpu_custom_call" | custom-call | flops 1 | bytes 1 | tf_op jit(solution)/shard_map/pallas_call | solution.py:179
Async XLA Ops:
  0.6 54.5 %collective-permute-start.6 = (bf16[512,1152]{1,0:T(8,128)(2,1)}, bf16[512,1152]{1,0:T(8,128)(2,1)S(1)}, u32[]{:S(2)}, u32[]{:S(2)}) collective-permute-start(bf16[512,1152]{1,0:T(8,128)(2,1)} %refs_0_.3), channel_id=1, source_target_pairs={{0,28},{2,30},{4,0},{6,2},{8,4},{10,6},{12,8},{14,10},{16,12},{18,... | collective-permute-start | bytes 3538952 | tf_op jit(solution)/shard_map/ppermute | solution.py:23
  6.7 48.7 %collective-permute-start.1 = (bf16[512,1152]{1,0:T(8,128)(2,1)}, bf16[512,1152]{1,0:T(8,128)(2,1)S(1)}, u32[]{:S(2)}, u32[]{:S(2)}) collective-permute-start(bf16[512,1152]{1,0:T(8,128)(2,1)} %refs_4_.1), channel_id=1, source_target_pairs={{0,4},{2,6},{4,8},{6,10},{8,12},{10,14},{12,16},{14,18},{16,20},{1... | collective-permute-start | bytes 3538952 | tf_op jit(solution)/shard_map/ppermute | solution.py:23
  8.3 3.0 %copy-start = (bf16[512,1152]{1,0:T(8,128)(2,1)S(1)}, bf16[512,1152]{1,0:T(8,128)(2,1)}, u32[]{:S(2)}) copy-start(bf16[512,1152]{1,0:T(8,128)(2,1)} %refs_0_.3) | copy-start | bytes 3538948
  8.4 3.0 %copy-start.1 = (bf16[512,1152]{1,0:T(8,128)(2,1)S(1)}, bf16[512,1152]{1,0:T(8,128)(2,1)}, u32[]{:S(2)}) copy-start(bf16[512,1152]{1,0:T(8,128)(2,1)} %refs_4_.1) | copy-start | bytes 3538948
  8.5 2.1 %collective-permute-start.3 = (bf16[256,1152]{1,0:T(8,128)(2,1)S(1)}, bf16[256,1152]{1,0:T(8,128)(2,1)S(1)}, u32[]{:S(2)}, u32[]{:S(2)}) collective-permute-start(bf16[256,1152]{1,0:T(8,128)(2,1)S(1)} %get-tuple-element.20), channel_id=1, source_target_pairs={{0,2},{2,0},{4,6},{6,4},{8,10},{10,8},{12,14},{14,12},{16,18},{18,... | collective-permute-start | bytes 1769480 | tf_op jit(solution)/shard_map/ppermute | solution.py:23
  8.5 2.8 %collective-permute-start.2 = (bf16[256,1152]{1,0:T(8,128)(2,1)S(1)}, bf16[256,1152]{1,0:T(8,128)(2,1)S(1)}, u32[]{:S(2)}, u32[]{:S(2)}) collective-permute-start(bf16[256,1152]{1,0:T(8,128)(2,1)S(1)} %get-tuple-element.21), channel_id=1, source_target_pairs={{0,2},{2,0},{4,6},{6,4},{8,10},{10,8},{12,14},{14,12},{16,18},{18,... | collective-permute-start | bytes 1769480 | tf_op jit(solution)/shard_map/ppermute | solution.py:23
  9.0 50.4 %collective-permute-start = (bf16[512,1152]{1,0:T(8,128)(2,1)S(1)}, bf16[512,1152]{1,0:T(8,128)(2,1)S(1)}, u32[]{:S(2)}, u32[]{:S(2)}) collective-permute-start(bf16[512,1152]{1,0:T(8,128)(2,1)S(1)} %get-tuple-element.10.far_own), channel_id=1, source_target_pairs={{0,26},{2,8},{4,30},{6,12},{8,2},{10,16},{12,6},{14,20},{16,10},{1... | collective-permute-start | bytes 3538952 | tf_op jit(solution)/shard_map/ppermute | solution.py:23
  55.1 4.5 %collective-permute-start.7 = (bf16[512,1152]{1,0:T(8,128)(2,1)S(1)}, bf16[512,1152]{1,0:T(8,128)(2,1)S(1)}, u32[]{:S(2)}, u32[]{:S(2)}) collective-permute-start(bf16[512,1152]{1,0:T(8,128)(2,1)S(1)} %collective-permute-done.6.refs_1_), channel_id=1, source_target_pairs={{0,2},{2,0},{4,6},{6,4},{8,10},{10,8},{12,14},{14,12},{16,18},{18,... | collective-permute-start | bytes 3538952 | tf_op jit(solution)/shard_map/ppermute | solution.py:23
  55.5 4.0 %collective-permute-start.5 = (bf16[256,1152]{1,0:T(8,128)(2,1)S(1)}, bf16[256,1152]{1,0:T(8,128)(2,1)S(1)}, u32[]{:S(2)}, u32[]{:S(2)}) collective-permute-start(bf16[256,1152]{1,0:T(8,128)(2,1)S(1)} %get-tuple-element.18), channel_id=1, source_target_pairs={{0,2},{2,0},{4,6},{6,4},{8,10},{10,8},{12,14},{14,12},{16,18},{18,... | collective-permute-start | bytes 1769480 | tf_op jit(solution)/shard_map/ppermute | solution.py:23
  55.8 3.9 %collective-permute-start.4 = (bf16[256,1152]{1,0:T(8,128)(2,1)S(1)}, bf16[256,1152]{1,0:T(8,128)(2,1)S(1)}, u32[]{:S(2)}, u32[]{:S(2)}) collective-permute-start(bf16[256,1152]{1,0:T(8,128)(2,1)S(1)} %get-tuple-element.19), channel_id=1, source_target_pairs={{0,2},{2,0},{4,6},{6,4},{8,10},{10,8},{12,14},{14,12},{16,18},{18,... | collective-permute-start | bytes 1769480 | tf_op jit(solution)/shard_map/ppermute | solution.py:23
